TPU v7x, 32 devices: a whole 2x2x4 slice. The times are simulated.
32 devices in a mesh: cfg: 2 (over core), patch: 8 (over z, x), req: 2 (over y).
Axes of the slice: x: 2, y: 2, z: 4, core: 2. Of those that a mesh axis runs over, the one named last changes fastest.
Arguments:
- latents: bfloat16 [2, 2, 32, 256, 320], P('cfg', 'req', 'patch'), may hold values from -60 to 60
- time_embed: bfloat16 [2, 1280], P('req'), may hold values from -6 to 6
- steer_scale: float32 [2], P('req'), may hold values from 0.5 to 4
- gain_one: float32 [320], replicated, may hold values from 0.5 to 1.5
- shift_one: float32 [320], replicated, may hold values from -3 to 3
- conv_one: bfloat16 [3, 3, 320, 320], replicated, may hold values from -0.109375 to 0.109375
- bias_one: float32 [320], replicated, may hold values from -3 to 3
- time_weight: bfloat16 [1280, 320], P('patch'), may hold values from -0.15625 to 0.15625
- time_bias: float32 [320], replicated, may hold values from -3 to 3
- gain_two: float32 [320], replicated, may hold values from 0.5 to 1.5
- shift_two: float32 [320], replicated, may hold values from -3 to 3
- conv_two: bfloat16 [3, 3, 320, 320], replicated, may hold values from -0.109375 to 0.109375
- bias_two: float32 [320], replicated, may hold values from -3 to 3
Outputs:
- block_out: bfloat16 [2, 2, 32, 256, 320], P('cfg', 'req', 'patch')
All inputs are finite; a program needn't handle non-finite values.
Results may differ from a plain program's by a relative error of at most 0.0034.
Values may be sent and summed in bfloat16 or wider, within the bound.
No kernel may reach another device: no remote copies, remote signals or barrier semaphores. Data moves between devices by JAX's collectives and lax.ppermute only.
A program may use at most 64 MiB of HBM per device.

v0:
```python
import jax
import jax.numpy as jnp
from jax import lax
from jax.sharding import PartitionSpec as P

GROUPS = 32


EPS = 1e-05


def extended(array, sides, width):
    for axis, dim in sides:
        peers, length = (lax.axis_size(axis), array.shape[dim])
        up = [(i, (i + 1) % peers) for i in range(peers - 1)]
        down = [(j, i) for i, j in up]
        last = lax.slice_in_dim(array, length - width, length, axis=dim)
        first = lax.slice_in_dim(array, 0, width, axis=dim)
        before = lax.ppermute(last, axis, up)
        after = lax.ppermute(first, axis, down)
        array = jnp.concatenate([before, array, after], axis=dim)
    return array


def from_partner(value, axis, stride):
    mask = 2**stride
    pairs = [(source, source ^ mask) for source in range(lax.axis_size(axis))]
    return lax.ppermute(value, axis, pairs)


def moments(values, total):
    batch_rows, rows, cols, chans = values.shape
    view = values.reshape(batch_rows, rows, cols, GROUPS, chans // GROUPS)
    mean = lax.psum(jnp.sum(view, axis=(1, 2, 4)), "patch") / total
    centred = view - mean[:, None, None, :, None]
    spread = lax.psum(jnp.sum(centred * centred, axis=(1, 2, 4)), "patch") / total
    return (mean, spread)


def activate(values, mean, spread, gain, shift):
    batch_rows, rows, cols, chans = values.shape
    view = values.reshape(batch_rows, rows, cols, GROUPS, chans // GROUPS)
    normed = (view - mean[:, None, None, :, None]) * lax.rsqrt(spread + EPS)[:, None, None, :, None]
    return jax.nn.silu(normed.reshape(values.shape) * gain + shift)


def pad_columns(acts):
    return jnp.pad(acts, ((0, 0), (0, 0), (1, 1), (0, 0)))


def surround(acts):
    return pad_columns(extended(acts, (("patch", 1),), 1))


def convolve(padded, weight):
    rows = padded.shape[1] - 2
    cols = padded.shape[2] - 2
    total = None
    for shift_y in range(3):
        for shift_x in range(3):
            term = jnp.einsum(
                "rhwc,cd->rhwd",
                padded[:, shift_y : shift_y + rows, shift_x : shift_x + cols],
                weight[shift_y, shift_x],
                preferred_element_type=jnp.float32,
            )
            total = term if total is None else total + term
    return total


def body(
    latents,
    time_embed,
    steer_scale,
    gain_one,
    shift_one,
    conv_one,
    bias_one,
    time_weight,
    time_bias,
    gain_two,
    shift_two,
    conv_two,
    bias_two,
):
    latent_rows = latents[0]
    batch_rows, own_rows, cols, chans = latent_rows.shape
    patches = lax.axis_size("patch")
    total = float(own_rows * patches * cols * (chans // GROUPS))
    time_act = jax.nn.silu(time_embed.astype(jnp.float32)).astype(jnp.bfloat16)
    embed_rows = time_weight.shape[0]
    own_embed = lax.dynamic_slice_in_dim(
        time_act, lax.axis_index("patch") * embed_rows, embed_rows, 1
    )
    time_part = jnp.dot(own_embed, time_weight, preferred_element_type=jnp.float32)
    time_shift = (lax.psum(time_part, "patch") + time_bias)[:, None, None, :]
    is_cond = lax.axis_index("cfg") == 0
    steer = steer_scale[:, None, None, None]
    source = latent_rows.astype(jnp.float32)
    mean_one, spread_one = moments(source, total)
    act_one = activate(source, mean_one, spread_one, gain_one, shift_one).astype(jnp.bfloat16)
    hidden = (convolve(surround(act_one), conv_one) + bias_one + time_shift).astype(jnp.bfloat16)
    partner_rows = from_partner(hidden, "cfg", 0)
    own_vals = hidden.astype(jnp.float32)
    far_vals = partner_rows.astype(jnp.float32)
    steered = own_vals + steer * jnp.where(is_cond, own_vals - far_vals, far_vals - own_vals)
    mean_two, spread_two = moments(steered, total)
    act_two = activate(steered, mean_two, spread_two, gain_two, shift_two).astype(jnp.bfloat16)
    image = convolve(surround(act_two), conv_two)
    block_out = (source + image + bias_two).astype(jnp.bfloat16)
    return block_out[None]


def solution(mesh):
    placed = (
        P("cfg", "req", "patch", None, None),
        P("req", None),
        P("req"),
        P(),
        P(),
        P(),
        P(),
        P("patch", None),
        P(),
        P(),
        P(),
        P(),
        P(),
    )
    return jax.shard_map(
        body,
        mesh=mesh,
        in_specs=placed,
        out_specs=P("cfg", "req", "patch", None, None),
        check_vma=False,
    )
```

profile of v0, /device:TPU:0, one launch (start us, length us, event | category | flops | bytes accessed | tf_op | source)
XLA Modules:
  0.0 122.1 jit_solution(7702669299954549867)
XLA Ops:
  0.0 0.8 convert_element_type.87
  0.8 1.3 %convert_reduce_fusion = f32[320]{0:T(512)S(1)} fusion(bf16[1,1,4,256,320]{3,4,2,1,0:T(8,128)(2,1)} %param.13), kind=kLoop, calls=%fused_computation.4 | loop fusion | flops 655040 | bytes 656640 | tf_op jit(solution)/shard_map/reduce_sum | solution.py:34
  2.3 23.1 %psum.35 = f32[1,32]{1,0:T(1,128)S(1)} all-reduce(f32[1,32]{1,0:T(1,128)S(1)} %bitcast.218), channel_id=1, replica_groups=mesh['cfg'=2,'patch'=8,'req'=2] {'patch'}, use_global_device_ids=true, to_apply=%region_2.3 | all-reduce | flops 32 | bytes 256 | tf_op jit(solution)/shard_map/psum | solution.py:34
  25.6 1.6 %fusion.20 = f32[320]{0:T(512)S(1)} fusion(bf16[1,1,4,256,320]{3,4,2,1,0:T(8,128)(2,1)} %param.13, f32[320]{0:T(512)S(1)} %sub.68), kind=kLoop, calls=%fused_computation.33 | loop fusion | flops 1310400 | bytes 657920 | tf_op jit(solution)/shard_map/reduce_sum | solution.py:36
  27.6 17.1 %all-reduce.2 = (f32[1,32]{1,0:T(1,128)S(1)}, f32[1,320]{1,0:T(1,128)S(1)}) all-reduce(f32[1,32]{1,0:T(1,128)S(1)} %bitcast.216, f32[1,320]{1,0:T(1,128)S(1)} %fusion.116), channel_id=1, replica_groups=mesh['cfg'=2,'patch'=8,'req'=2] {'patch'}, use_global_device_ids=true, to_apply=%region_5.6 | all-reduce | flops 352 | bytes 2816 | tf_op jit(solution)/shard_map/psum | solution.py:36
  45.6 3.9 %collective-permute-start = (bf16[1,1,256,320]{2,3,1,0:T(8,128)(2,1)S(1)}, bf16[1,1,256,320]{2,3,1,0:T(8,128)(2,1)S(1)}, u32[]{:S(2)}, u32[]{:S(2)}) collective-permute-start(bf16[1,1,256,320]{2,3,1,0:T(8,128)(2,1)S(1)} %get-tuple-element.9), channel_id=1, source_target_pairs={{0,2},{2,4},{4,6},{6,8},{8,10},{10,12},{12,14},{1,3},{3,5},{5,7},{... | collective-permute-start | bytes 491528 | tf_op jit(solution)/shard_map/ppermute | solution.py:19
  49.6 1.3 %collective-permute-start.1 = (bf16[1,1,256,320]{2,3,1,0:T(8,128)(2,1)S(1)}, bf16[1,1,256,320]{2,3,1,0:T(8,128)(2,1)S(1)}, u32[]{:S(2)}, u32[]{:S(2)}) collective-permute-start(bf16[1,1,256,320]{2,3,1,0:T(8,128)(2,1)S(1)} %get-tuple-element.10), channel_id=1, source_target_pairs={{2,0},{4,2},{6,4},{8,6},{10,8},{12,10},{14,12},{3,1},{5,3},{7,5},{... | collective-permute-start | bytes 491528 | tf_op jit(solution)/shard_map/ppermute | solution.py:20
  50.9 0.9 fusion.44
  52.4 4.4 %collective-permute-done.1 = bf16[1,1,256,320]{2,3,1,0:T(8,128)(2,1)S(1)} collective-permute-done((bf16[1,1,256,320]{2,3,1,0:T(8,128)(2,1)S(1)}, bf16[1,1,256,320]{2,3,1,0:T(8,128)(2,1)S(1)}, u32[]{:S(2)}, u32[]{:S(2)}) %collective-permute-start.1) | collective-permute-done | bytes 163872 | tf_op jit(solution)/shard_map/ppermute | solution.py:20
  56.8 0.8 fusion.7
  57.6 0.7 fusion.59
  59.4 0.7 fusion.66
  61.8 2.0 %fusion.41 = bf16[1,4,256,320]{2,3,1,0:T(8,128)(2,1)S(1)} fusion(f32[4,256,320]{1,2,0:T(8,128)S(1)} %fusion.59, f32[4,256,320]{1,2,0:T(8,128)S(1)} %fusion.61, f32[4,256,320]{1,2,0:T(8,128)S(1)} %fusion.64, f32[4,256,320]{1,2,0:T(8,128)S(1)} %fusion.44, f32[4,256,320]{1,2,0:T(8,128)S(1)} %fusion.65, f32[4,256,320]{1,2,0:T(8,128)S(1)} %fusion.66, ...), kind=kOutput, calls=%fused_computation.56 | convolution fusion | flops 213319680 | bytes 12046336 | tf_op jit(solution)/shard_map/rhwc,cd->rhwd/dot_general | solution.py:61
  64.6 1.4 %collective-permute-done.2 = bf16[1,4,256,320]{2,3,1,0:T(8,128)(2,1)S(1)} collective-permute-done((bf16[1,4,256,320]{2,3,1,0:T(8,128)(2,1)S(1)}, bf16[1,4,256,320]{2,3,1,0:T(8,128)(2,1)S(1)}, u32[]{:S(2)}, u32[]{:S(2)}) %collective-permute-start.2) | collective-permute-done | bytes 655392 | tf_op jit(solution)/shard_map/ppermute | solution.py:28
  66.7 18.0 %psum.38 = f32[1,32]{1,0:T(1,128)S(1)} all-reduce(f32[1,32]{1,0:T(1,128)S(1)} %bitcast.219), channel_id=1, replica_groups=mesh['cfg'=2,'patch'=8,'req'=2] {'patch'}, use_global_device_ids=true, to_apply=%region_9.10 | all-reduce | flops 32 | bytes 256 | tf_op jit(solution)/shard_map/psum | solution.py:34
  85.6 18.2 %psum.39 = f32[1,32]{1,0:T(1,128)S(1)} all-reduce(f32[1,32]{1,0:T(1,128)S(1)} %bitcast.217), channel_id=1, replica_groups=mesh['cfg'=2,'patch'=8,'req'=2] {'patch'}, use_global_device_ids=true, to_apply=%region_12.13 | all-reduce | flops 32 | bytes 256 | tf_op jit(solution)/shard_map/psum | solution.py:36
  104.1 0.9 multiply_convert_fusion
  105.0 2.9 %collective-permute-start.3 = (bf16[1,1,256,320]{2,3,1,0:T(8,128)(2,1)S(1)}, bf16[1,1,256,320]{2,3,1,0:T(8,128)(2,1)S(1)}, u32[]{:S(2)}, u32[]{:S(2)}) collective-permute-start(bf16[1,1,256,320]{2,3,1,0:T(8,128)(2,1)S(1)} %get-tuple-element.7), channel_id=1, source_target_pairs={{0,2},{2,4},{4,6},{6,8},{8,10},{10,12},{12,14},{1,3},{3,5},{5,7},{... | collective-permute-start | bytes 491528 | tf_op jit(solution)/shard_map/ppermute | solution.py:19
  108.0 1.5 %collective-permute-start.4 = (bf16[1,1,256,320]{2,3,1,0:T(8,128)(2,1)S(1)}, bf16[1,1,256,320]{2,3,1,0:T(8,128)(2,1)S(1)}, u32[]{:S(2)}, u32[]{:S(2)}) collective-permute-start(bf16[1,1,256,320]{2,3,1,0:T(8,128)(2,1)S(1)} %get-tuple-element.8), channel_id=1, source_target_pairs={{2,0},{4,2},{6,4},{8,6},{10,8},{12,10},{14,12},{3,1},{5,3},{7,5},{... | collective-permute-start | bytes 491528 | tf_op jit(solution)/shard_map/ppermute | solution.py:20
  110.0 0.8 collective-permute-done.3
  110.8 4.4 %collective-permute-done.4 = bf16[1,1,256,320]{2,3,1,0:T(8,128)(2,1)S(1)} collective-permute-done((bf16[1,1,256,320]{2,3,1,0:T(8,128)(2,1)S(1)}, bf16[1,1,256,320]{2,3,1,0:T(8,128)(2,1)S(1)}, u32[]{:S(2)}, u32[]{:S(2)}) %collective-permute-start.4) | collective-permute-done | bytes 163872 | tf_op jit(solution)/shard_map/ppermute | solution.py:20
  115.2 0.8 select_maximum_fusion
  116.0 0.7 fusion.46
  120.2 1.9 %fusion.42 = bf16[1,1,4,256,320]{3,4,2,1,0:T(8,128)(2,1)} fusion(f32[4,256,320]{1,2,0:T(8,128)S(1)} %fusion.46, f32[4,256,320]{1,2,0:T(8,128)S(1)} %fusion.48, f32[4,256,320]{1,2,0:T(8,128)S(1)} %fusion.51, f32[4,256,320]{1,2,0:T(8,128)S(1)} %fusion.72, f32[4,256,320]{1,2,0:T(8,128)S(1)} %fusion.52, f32[4,256,320]{1,2,0:T(8,128)S(1)} %fusion.53, ...), kind=kOutput, calls=%fused_computation.57 | convolution fusion | flops 213647360 | bytes 12699648 | tf_op jit(solution)/shard_map/rhwc,cd->rhwd/dot_general | solution.py:61
  (63 shorter events, 11.0 us)
Async XLA Ops:
  0.0 27.4 %copy-start = (bf16[160,320]{1,0:T(8,128)(2,1)S(1)}, bf16[160,320]{1,0:T(8,128)(2,1)}, u32[]{:S(2)}) copy-start(bf16[160,320]{1,0:T(8,128)(2,1)} %param.20) | copy-start | bytes 307204
  0.0 44.9 %copy-start.1 = (bf16[1,1,4,256,320]{3,4,2,1,0:T(8,128)(2,1)S(1)}, bf16[1,1,4,256,320]{3,4,2,1,0:T(8,128)(2,1)}, u32[]{:S(2)}) copy-start(bf16[1,1,4,256,320]{3,4,2,1,0:T(8,128)(2,1)} %param.13) | copy-start | bytes 1966084
  0.0 44.9 %copy-start.5 = (f32[320]{0:T(512)S(1)}, f32[320]{0:T(512)}, u32[]{:S(2)}) copy-start(f32[320]{0:T(512)} %param.16) | copy-start | bytes 3844
  0.0 44.9 %copy-start.4 = (f32[320]{0:T(512)S(1)}, f32[320]{0:T(512)}, u32[]{:S(2)}) copy-start(f32[320]{0:T(512)} %param.17) | copy-start | bytes 3844
  25.6 25.3 %copy-start.3 = (bf16[3,3,320,320]{3,2,1,0:T(8,128)(2,1)S(1)}, bf16[3,3,320,320]{3,2,1,0:T(8,128)(2,1)}, u32[]{:S(2)}) copy-start(bf16[3,3,320,320]{3,2,1,0:T(8,128)(2,1)} %param.18) | copy-start | bytes 5529604
  45.6 6.7 %collective-permute-start = (bf16[1,1,256,320]{2,3,1,0:T(8,128)(2,1)S(1)}, bf16[1,1,256,320]{2,3,1,0:T(8,128)(2,1)S(1)}, u32[]{:S(2)}, u32[]{:S(2)}) collective-permute-start(bf16[1,1,256,320]{2,3,1,0:T(8,128)(2,1)S(1)} %get-tuple-element.9), channel_id=1, source_target_pairs={{0,2},{2,4},{4,6},{6,8},{8,10},{10,12},{12,14},{1,3},{3,5},{5,7},{... | collective-permute-start | bytes 491528 | tf_op jit(solution)/shard_map/ppermute | solution.py:19
  49.5 2.2 %copy-start.8 = (f32[320]{0:T(512)S(1)}, f32[320]{0:T(512)}, u32[]{:S(2)}) copy-start(f32[320]{0:T(512)} %param.21) | copy-start | bytes 3844
  49.6 7.2 %collective-permute-start.1 = (bf16[1,1,256,320]{2,3,1,0:T(8,128)(2,1)S(1)}, bf16[1,1,256,320]{2,3,1,0:T(8,128)(2,1)S(1)}, u32[]{:S(2)}, u32[]{:S(2)}) collective-permute-start(bf16[1,1,256,320]{2,3,1,0:T(8,128)(2,1)S(1)} %get-tuple-element.10), channel_id=1, source_target_pairs={{2,0},{4,2},{6,4},{8,6},{10,8},{12,10},{14,12},{3,1},{5,3},{7,5},{... | collective-permute-start | bytes 491528 | tf_op jit(solution)/shard_map/ppermute | solution.py:20
  61.1 0.7 copy-start.9
  63.8 2.2 %collective-permute-start.2 = (bf16[1,4,256,320]{2,3,1,0:T(8,128)(2,1)S(1)}, bf16[1,4,256,320]{2,3,1,0:T(8,128)(2,1)S(1)}, u32[]{:S(2)}, u32[]{:S(2)}) collective-permute-start(bf16[1,4,256,320]{2,3,1,0:T(8,128)(2,1)S(1)} %fusion.41), channel_id=1, source_target_pairs={{0,16},{16,0},{1,17},{17,1},{2,18},{18,2},{3,19},{19,3},{4,20},{20... | collective-permute-start | bytes 1966088 | tf_op jit(solution)/shard_map/ppermute | solution.py:28
  66.0 38.1 %copy-start.6 = (f32[320]{0:T(512)S(1)}, f32[320]{0:T(512)}, u32[]{:S(2)}) copy-start(f32[320]{0:T(512)} %param.23) | copy-start | bytes 3844
  66.0 38.1 %copy-start.7 = (f32[320]{0:T(512)S(1)}, f32[320]{0:T(512)}, u32[]{:S(2)}) copy-start(f32[320]{0:T(512)} %param.22) | copy-start | bytes 3844
  104.1 5.4 %copy-start.2 = (bf16[3,3,320,320]{3,2,1,0:T(8,128)(2,1)S(1)}, bf16[3,3,320,320]{3,2,1,0:T(8,128)(2,1)}, u32[]{:S(2)}) copy-start(bf16[3,3,320,320]{3,2,1,0:T(8,128)(2,1)} %param.24) | copy-start | bytes 5529604
  105.0 5.7 %collective-permute-start.3 = (bf16[1,1,256,320]{2,3,1,0:T(8,128)(2,1)S(1)}, bf16[1,1,256,320]{2,3,1,0:T(8,128)(2,1)S(1)}, u32[]{:S(2)}, u32[]{:S(2)}) collective-permute-start(bf16[1,1,256,320]{2,3,1,0:T(8,128)(2,1)S(1)} %get-tuple-element.7), channel_id=1, source_target_pairs={{0,2},{2,4},{4,6},{6,8},{8,10},{10,12},{12,14},{1,3},{3,5},{5,7},{... | collective-permute-start | bytes 491528 | tf_op jit(solution)/shard_map/ppermute | solution.py:19
  108.0 7.2 %collective-permute-start.4 = (bf16[1,1,256,320]{2,3,1,0:T(8,128)(2,1)S(1)}, bf16[1,1,256,320]{2,3,1,0:T(8,128)(2,1)S(1)}, u32[]{:S(2)}, u32[]{:S(2)}) collective-permute-start(bf16[1,1,256,320]{2,3,1,0:T(8,128)(2,1)S(1)} %get-tuple-element.8), channel_id=1, source_target_pairs={{2,0},{4,2},{6,4},{8,6},{10,8},{12,10},{14,12},{3,1},{5,3},{7,5},{... | collective-permute-start | bytes 491528 | tf_op jit(solution)/shard_map/ppermute | solution.py:20
  119.5 0.7 copy-start.10
where the time goes:
time: 123 us; the launch traced here: 122 us
  blocking collectives  76.5 us (62%)
  matrix products  13.5 us (11%)
  waiting for transfers between devices  11.6 us (9%)
  starting transfers between devices  9.68 us (8%)
  other arithmetic  8.27 us (7%)
  local copies, waits for them, and re-layouts  1.52 us (1%)
    psum x2, blocking collectives, moments(): mean = lax.psum(jnp.sum(view, axis=(1, 2, 4)), 'patch') / total  41.1 us
    psum x2, blocking collectives, moments(): lax.psum(jnp.sum(centred * centred, axis=(1, 2, 4)), 'patch') / total  35.4 us
    dot_general x18, matrix products, convolve(): jnp.einsum('rhwc,cd->rhwd', padded[:, shift_y:shift_y + rows, shift_x:shi...  13.3 us
    ppermute x2, waiting for transfers between devices, extended(): after = lax.ppermute(first, axis, down)  8.82 us
    ppermute x2, starting transfers between devices, extended(): before = lax.ppermute(last, axis, up)  6.85 us
    ppermute x2, starting transfers between devices, extended(): after = lax.ppermute(first, axis, down)  2.76 us
  transfers between devices with their start and end apart: 5, of which 5 were waited for; matrix products, arithmetic and copies ran while one was open for 1% of the time, Pallas kernels for 0%

commit v1 on v0

--- a/solution.py
+++ b/solution.py
@@ -28,12 +28,24 @@
     return lax.ppermute(value, axis, pairs)
 
 
-def moments(values, total):
+def gathered(rows, axes):
+    peers = lax.axis_size(axes)
+    return lax.all_to_all(jnp.broadcast_to(rows[None], (peers,) + rows.shape), axes, 0, 0)
+
+
+def local_moments(values):
     batch_rows, rows, cols, chans = values.shape
     view = values.reshape(batch_rows, rows, cols, GROUPS, chans // GROUPS)
-    mean = lax.psum(jnp.sum(view, axis=(1, 2, 4)), "patch") / total
+    count = float(rows * cols * (chans // GROUPS))
+    mean = jnp.sum(view, axis=(1, 2, 4)) / count
     centred = view - mean[:, None, None, :, None]
-    spread = lax.psum(jnp.sum(centred * centred, axis=(1, 2, 4)), "patch") / total
+    return (mean, jnp.sum(centred * centred, axis=(1, 2, 4)), count)
+
+
+def combined(means, squares, count):
+    mean = jnp.mean(means, axis=0)
+    off = means - mean
+    spread = jnp.sum(squares + count * off * off, axis=0) / (count * means.shape[0])
     return (mean, spread)
 
 
@@ -85,26 +97,28 @@
 ):
     latent_rows = latents[0]
     batch_rows, own_rows, cols, chans = latent_rows.shape
-    patches = lax.axis_size("patch")
-    total = float(own_rows * patches * cols * (chans // GROUPS))
     time_act = jax.nn.silu(time_embed.astype(jnp.float32)).astype(jnp.bfloat16)
     embed_rows = time_weight.shape[0]
     own_embed = lax.dynamic_slice_in_dim(
         time_act, lax.axis_index("patch") * embed_rows, embed_rows, 1
     )
     time_part = jnp.dot(own_embed, time_weight, preferred_element_type=jnp.float32)
-    time_shift = (lax.psum(time_part, "patch") + time_bias)[:, None, None, :]
     is_cond = lax.axis_index("cfg") == 0
     steer = steer_scale[:, None, None, None]
     source = latent_rows.astype(jnp.float32)
-    mean_one, spread_one = moments(source, total)
+    mean_part, square_part, count = local_moments(source)
+    seen = gathered(jnp.concatenate([mean_part, square_part, time_part], axis=1), "patch")
+    mean_one, spread_one = combined(seen[:, :, :GROUPS], seen[:, :, GROUPS : 2 * GROUPS], count)
+    time_shift = (jnp.sum(seen[:, :, 2 * GROUPS :], axis=0) + time_bias)[:, None, None, :]
     act_one = activate(source, mean_one, spread_one, gain_one, shift_one).astype(jnp.bfloat16)
     hidden = (convolve(surround(act_one), conv_one) + bias_one + time_shift).astype(jnp.bfloat16)
     partner_rows = from_partner(hidden, "cfg", 0)
     own_vals = hidden.astype(jnp.float32)
     far_vals = partner_rows.astype(jnp.float32)
     steered = own_vals + steer * jnp.where(is_cond, own_vals - far_vals, far_vals - own_vals)
-    mean_two, spread_two = moments(steered, total)
+    mean_part, square_part, count = local_moments(steered)
+    seen = gathered(jnp.concatenate([mean_part, square_part], axis=1), "patch")
+    mean_two, spread_two = combined(seen[:, :, :GROUPS], seen[:, :, GROUPS:], count)
     act_two = activate(steered, mean_two, spread_two, gain_two, shift_two).astype(jnp.bfloat16)
     image = convolve(surround(act_two), conv_two)
     block_out = (source + image + bias_two).astype(jnp.bfloat16)

time: 123 us -> 68.5 us (0.56)
  blocking collectives: 76.5 us -> 23.7 us
  starting transfers between devices: 9.68 us -> 7.75 us
    psum x4 -> x0, blocking collectives: 76.5 us -> none  [the longest x2 41.1 us: moments(): mean = lax.psum(jnp.sum(view, axis=(1, 2, 4)), 'patch') / total]
    all_to_all x0 -> x2, blocking collectives: none -> 23.7 us  [gathered(): lax.all_to_all(jnp.broadcast_to(rows[None], (peers,) + rows.shape), axes,...]
    ppermute x2, starting transfers between devices: 6.85 us -> 4.91 us  [extended(): before = lax.ppermute(last, axis, up)]
    ppermute x2, waiting for transfers between devices: 8.82 us -> 7.03 us  [extended(): after = lax.ppermute(first, axis, down)]
    ppermute x2, waiting for transfers between devices: 1.38 us -> 3.07 us  [extended(): before = lax.ppermute(last, axis, up)]
    reduce_sum x8 -> x13, other arithmetic: 4.26 us -> 4.37 us  [the longest x4 2.18 us: local_moments(): return (mean, jnp.sum(centred * centred, axis=(1, 2, 4)), count)]
  transfers between devices with their start and end apart: 5 -> 5, of which waited for: 5 -> 5; matrix products, arithmetic and copies ran while one was open for 1% -> 2% of each run, Pallas kernels for 0% -> 0%
where the time goes in v1:
time: 68.5 us; the launch traced here: 68 us
  blocking collectives  23.7 us (35%)
  matrix products  13.5 us (20%)
  waiting for transfers between devices  11.5 us (17%)
  other arithmetic  8.54 us (12%)
  starting transfers between devices  7.75 us (11%)
  local copies, waits for them, and re-layouts  1.97 us (3%)
  between operations  1.04 us (2%)
    all_to_all x2, blocking collectives, gathered(): lax.all_to_all(jnp.broadcast_to(rows[None], (peers,) + rows.shape), axes,...  23.7 us
    dot_general x18, matrix products, convolve(): jnp.einsum('rhwc,cd->rhwd', padded[:, shift_y:shift_y + rows, shift_x:shi...  13.3 us
    ppermute x2, waiting for transfers between devices, extended(): after = lax.ppermute(first, axis, down)  7.03 us
    ppermute x2, starting transfers between devices, extended(): before = lax.ppermute(last, axis, up)  4.91 us
    ppermute x2, waiting for transfers between devices, extended(): before = lax.ppermute(last, axis, up)  3.07 us
    ppermute x2, starting transfers between devices, extended(): after = lax.ppermute(first, axis, down)  2.76 us
    reduce_sum x4, other arithmetic, local_moments(): return (mean, jnp.sum(centred * centred, axis=(1, 2, 4)), count)  2.18 us
    reduce_sum x4, other arithmetic, local_moments(): mean = jnp.sum(view, axis=(1, 2, 4)) / count  1.93 us
  transfers between devices with their start and end apart: 5, of which 5 were waited for; matrix products, arithmetic and copies ran while one was open for 2% of the time, Pallas kernels for 0%

profile of v1, /device:TPU:0, one launch (start us, length us, event | category | flops | bytes accessed | tf_op | source)
XLA Modules:
  0.0 68.0 jit_solution(15667132421779211525)
XLA Ops:
  0.0 0.8 %convert_element_type.85 = f32[1,1280]{1,0:T(1,128)S(1)} convert(bf16[1,1280]{1,0:T(2,128)(2,1)} %param.14) | non-fusion elementwise | flops 1280 | bytes 7680 | tf_op jit(solution)/shard_map/convert_element_type | solution.py:100
  0.8 1.3 %convert_reduce_fusion = f32[320]{0:T(512)S(1)} fusion(bf16[1,1,4,256,320]{3,4,2,1,0:T(8,128)(2,1)} %param.13), kind=kLoop, calls=%fused_computation.5 | loop fusion | flops 655040 | bytes 656640 | tf_op jit(solution)/shard_map/reduce_sum | solution.py:40
  2.5 1.4 %fusion.31 = f32[320]{0:T(512)S(1)} fusion(bf16[1,1,4,256,320]{3,4,2,1,0:T(8,128)(2,1)} %param.13, f32[320]{0:T(512)S(1)} %sub.97), kind=kLoop, calls=%fused_computation.45 | loop fusion | flops 1310400 | bytes 657920 | tf_op jit(solution)/shard_map/reduce_sum | solution.py:42
  4.4 13.7 %all_to_all.10 = f32[8,1,384]{2,1,0:T(1,128)S(1)} all-to-all(f32[8,1,384]{2,1,0:T(1,128)S(1)} %broadcast_in_dim.11), channel_id=1, replica_groups=mesh['cfg'=2,'patch'=8,'req'=2] {'patch'}, dimensions={0} | all-to-all | bytes 24576 | tf_op jit(solution)/shard_map/all_to_all | solution.py:33
  19.4 2.4 %collective-permute-start = (bf16[1,1,256,320]{2,3,1,0:T(8,128)(2,1)S(1)}, bf16[1,1,256,320]{2,3,1,0:T(8,128)(2,1)S(1)}, u32[]{:S(2)}, u32[]{:S(2)}) collective-permute-start(bf16[1,1,256,320]{2,3,1,0:T(8,128)(2,1)S(1)} %get-tuple-element.7), channel_id=1, source_target_pairs={{0,2},{2,4},{4,6},{6,8},{8,10},{10,12},{12,14},{1,3},{3,5},{5,7},{... | collective-permute-start | bytes 491528 | tf_op jit(solution)/shard_map/ppermute | solution.py:19
  21.9 1.3 %collective-permute-start.1 = (bf16[1,1,256,320]{2,3,1,0:T(8,128)(2,1)S(1)}, bf16[1,1,256,320]{2,3,1,0:T(8,128)(2,1)S(1)}, u32[]{:S(2)}, u32[]{:S(2)}) collective-permute-start(bf16[1,1,256,320]{2,3,1,0:T(8,128)(2,1)S(1)} %get-tuple-element.8), channel_id=1, source_target_pairs={{2,0},{4,2},{6,4},{8,6},{10,8},{12,10},{14,12},{3,1},{5,3},{7,5},{... | collective-permute-start | bytes 491528 | tf_op jit(solution)/shard_map/ppermute | solution.py:20
  23.2 0.9 %fusion.44 = f32[4,256,320]{1,2,0:T(8,128)S(1)} fusion(bf16[1,1,4,256,320]{3,4,2,1,0:T(8,128)(2,1)S(1)} %copy-done.1, f32[320]{0:T(512)S(1)} %copy-done.4, f32[320]{0:T(512)S(1)} %copy-done.5, f32[320]{0:T(512)S(1)} %mul.144, f32[320]{0:T(512)S(1)} %sub.101, bf16[3,3,320,320]{3,2,1,0:T(8,128)(2,1)S(1)} %copy-done.3), kind=kOutput, calls=%fused_computation.60 | convolution fusion | flops 212992000 | bytes 2220032 | tf_op jit(solution)/shard_map/rhwc,cd->rhwd/dot_general | solution.py:73
  24.2 2.3 %collective-permute-done = bf16[1,1,256,320]{2,3,1,0:T(8,128)(2,1)S(1)} collective-permute-done((bf16[1,1,256,320]{2,3,1,0:T(8,128)(2,1)S(1)}, bf16[1,1,256,320]{2,3,1,0:T(8,128)(2,1)S(1)}, u32[]{:S(2)}, u32[]{:S(2)}) %collective-permute-start) | collective-permute-done | bytes 163872 | tf_op jit(solution)/shard_map/ppermute | solution.py:19
  26.5 2.6 %collective-permute-done.1 = bf16[1,1,256,320]{2,3,1,0:T(8,128)(2,1)S(1)} collective-permute-done((bf16[1,1,256,320]{2,3,1,0:T(8,128)(2,1)S(1)}, bf16[1,1,256,320]{2,3,1,0:T(8,128)(2,1)S(1)}, u32[]{:S(2)}, u32[]{:S(2)}) %collective-permute-start.1) | collective-permute-done | bytes 163872 | tf_op jit(solution)/shard_map/ppermute | solution.py:20
  29.1 0.8 %fusion.5 = bf16[1,6,258,320]{2,3,1,0:T(8,128)(2,1)S(1)} fusion(bf16[1,1,256,320]{2,3,1,0:T(8,128)(2,1)S(1)} %collective-permute-done.1, bf16[1,4,256,320]{2,3,1,0:T(8,128)(2,1)S(1)} %fusion.29, bf16[1,1,256,320]{2,3,1,0:T(8,128)(2,1)S(1)} %collective-permute-done), kind=kLoop, calls=%fused_computation.17 | loop fusion | flops 5944320 | bytes 1973760 | tf_op jit(solution)/shard_map/concatenate | solution.py:21
  29.9 0.7 fusion.59
  31.7 0.7 %fusion.66 = f32[4,256,320]{1,2,0:T(8,128)S(1)} fusion(bf16[1,6,258,320]{2,3,1,0:T(8,128)(2,1)S(1)} %fusion.5, bf16[3,3,320,320]{3,2,1,0:T(8,128)(2,1)S(1)} %copy-done.3), kind=kOutput, calls=%fused_computation.92 | convolution fusion | flops 209715200 | bytes 2211840 | tf_op jit(solution)/shard_map/rhwc,cd->rhwd/dot_general | solution.py:73
  34.1 2.0 %fusion.41 = bf16[1,4,256,320]{2,3,1,0:T(8,128)(2,1)S(1)} fusion(f32[4,256,320]{1,2,0:T(8,128)S(1)} %fusion.59, f32[4,256,320]{1,2,0:T(8,128)S(1)} %fusion.61, f32[4,256,320]{1,2,0:T(8,128)S(1)} %fusion.64, f32[4,256,320]{1,2,0:T(8,128)S(1)} %fusion.44, f32[4,256,320]{1,2,0:T(8,128)S(1)} %fusion.65, f32[4,256,320]{1,2,0:T(8,128)S(1)} %fusion.66, ...), kind=kOutput, calls=%fused_computation.57 | convolution fusion | flops 213319680 | bytes 12046336 | tf_op jit(solution)/shard_map/rhwc,cd->rhwd/dot_general | solution.py:73
  36.9 1.4 %collective-permute-done.2 = bf16[1,4,256,320]{2,3,1,0:T(8,128)(2,1)S(1)} collective-permute-done((bf16[1,4,256,320]{2,3,1,0:T(8,128)(2,1)S(1)}, bf16[1,4,256,320]{2,3,1,0:T(8,128)(2,1)S(1)}, u32[]{:S(2)}, u32[]{:S(2)}) %collective-permute-start.2) | collective-permute-done | bytes 655392 | tf_op jit(solution)/shard_map/ppermute | solution.py:28
  40.0 9.9 %all_to_all.11 = f32[8,1,64]{2,1,0:T(1,128)S(1)} all-to-all(f32[8,1,64]{2,1,0:T(1,128)S(1)} %broadcast_in_dim.13), channel_id=1, replica_groups=mesh['cfg'=2,'patch'=8,'req'=2] {'patch'}, dimensions={0} | all-to-all | bytes 4096 | tf_op jit(solution)/shard_map/all_to_all | solution.py:33
  50.4 0.9 %multiply_convert_fusion = bf16[1,4,256,320]{2,3,1,0:T(8,128)(2,1)S(1)} fusion(f32[320]{0:T(512)S(1)} %copy-done.6, f32[320]{0:T(512)S(1)} %copy-done.7, f32[320]{0:T(512)S(1)} %mul.162, f32[320]{0:T(512)S(1)} %sub.115, bf16[1,4,256,320]{2,3,1,0:T(8,128)(2,1)S(1)} %collective-permute-done.2, pred[]{:T(512)S(6)} %eq.3, f32[]{:T(128)} %bitcast.214, ...), kind=kLoop, calls=%fused_computation.55 | loop fusion | flops 5242880 | bytes 1971205 | tf_op jit(solution)/shard_map/convert_element_type | solution.py:122
  51.4 2.5 %collective-permute-start.3 = (bf16[1,1,256,320]{2,3,1,0:T(8,128)(2,1)S(1)}, bf16[1,1,256,320]{2,3,1,0:T(8,128)(2,1)S(1)}, u32[]{:S(2)}, u32[]{:S(2)}) collective-permute-start(bf16[1,1,256,320]{2,3,1,0:T(8,128)(2,1)S(1)} %get-tuple-element.5), channel_id=1, source_target_pairs={{0,2},{2,4},{4,6},{6,8},{8,10},{10,12},{12,14},{1,3},{3,5},{5,7},{... | collective-permute-start | bytes 491528 | tf_op jit(solution)/shard_map/ppermute | solution.py:19
  53.9 1.5 %collective-permute-start.4 = (bf16[1,1,256,320]{2,3,1,0:T(8,128)(2,1)S(1)}, bf16[1,1,256,320]{2,3,1,0:T(8,128)(2,1)S(1)}, u32[]{:S(2)}, u32[]{:S(2)}) collective-permute-start(bf16[1,1,256,320]{2,3,1,0:T(8,128)(2,1)S(1)} %get-tuple-element.6), channel_id=1, source_target_pairs={{2,0},{4,2},{6,4},{8,6},{10,8},{12,10},{14,12},{3,1},{5,3},{7,5},{... | collective-permute-start | bytes 491528 | tf_op jit(solution)/shard_map/ppermute | solution.py:20
  55.9 0.8 %collective-permute-done.3 = bf16[1,1,256,320]{2,3,1,0:T(8,128)(2,1)S(1)} collective-permute-done((bf16[1,1,256,320]{2,3,1,0:T(8,128)(2,1)S(1)}, bf16[1,1,256,320]{2,3,1,0:T(8,128)(2,1)S(1)}, u32[]{:S(2)}, u32[]{:S(2)}) %collective-permute-start.3) | collective-permute-done | bytes 163872 | tf_op jit(solution)/shard_map/ppermute | solution.py:19
  56.7 4.4 %collective-permute-done.4 = bf16[1,1,256,320]{2,3,1,0:T(8,128)(2,1)S(1)} collective-permute-done((bf16[1,1,256,320]{2,3,1,0:T(8,128)(2,1)S(1)}, bf16[1,1,256,320]{2,3,1,0:T(8,128)(2,1)S(1)}, u32[]{:S(2)}, u32[]{:S(2)}) %collective-permute-start.4) | collective-permute-done | bytes 163872 | tf_op jit(solution)/shard_map/ppermute | solution.py:20
  61.1 0.8 %select_maximum_fusion = bf16[1,6,258,320]{2,3,1,0:T(8,128)(2,1)S(1)} fusion(bf16[1,1,256,320]{2,3,1,0:T(8,128)(2,1)S(1)} %collective-permute-done.4, bf16[1,4,256,320]{2,3,1,0:T(8,128)(2,1)S(1)} %multiply_convert_fusion, bf16[1,1,256,320]{2,3,1,0:T(8,128)(2,1)S(1)} %collective-permute-done.3), kind=kLoop, calls=%fused_computation.11 | loop fusion | flops 5944320 | bytes 1973760 | tf_op jit(solution)/shard_map/concatenate | solution.py:21
  61.9 0.7 fusion.46
  63.6 0.7 %fusion.53 = f32[4,256,320]{1,2,0:T(8,128)S(1)} fusion(bf16[1,6,258,320]{2,3,1,0:T(8,128)(2,1)S(1)} %select_maximum_fusion, bf16[3,3,320,320]{3,2,1,0:T(8,128)(2,1)S(1)} %copy-done.2), kind=kOutput, calls=%fused_computation.73 | convolution fusion | flops 209715200 | bytes 2211840 | tf_op jit(solution)/shard_map/rhwc,cd->rhwd/dot_general | solution.py:73
  66.1 1.9 %fusion.42 = bf16[1,1,4,256,320]{3,4,2,1,0:T(8,128)(2,1)} fusion(f32[4,256,320]{1,2,0:T(8,128)S(1)} %fusion.46, f32[4,256,320]{1,2,0:T(8,128)S(1)} %fusion.48, f32[4,256,320]{1,2,0:T(8,128)S(1)} %fusion.51, f32[4,256,320]{1,2,0:T(8,128)S(1)} %fusion.72, f32[4,256,320]{1,2,0:T(8,128)S(1)} %fusion.52, f32[4,256,320]{1,2,0:T(8,128)S(1)} %fusion.53, ...), kind=kOutput, calls=%fused_computation.58 | convolution fusion | flops 213647360 | bytes 12699648 | tf_op jit(solution)/shard_map/rhwc,cd->rhwd/dot_general | solution.py:73
  (77 shorter events, 10.5 us)
Async XLA Ops:
  0.0 4.1 %copy-start = (bf16[160,320]{1,0:T(8,128)(2,1)S(1)}, bf16[160,320]{1,0:T(8,128)(2,1)}, u32[]{:S(2)}) copy-start(bf16[160,320]{1,0:T(8,128)(2,1)} %param.20) | copy-start | bytes 307204
  0.0 18.7 %copy-start.1 = (bf16[1,1,4,256,320]{3,4,2,1,0:T(8,128)(2,1)S(1)}, bf16[1,1,4,256,320]{3,4,2,1,0:T(8,128)(2,1)}, u32[]{:S(2)}) copy-start(bf16[1,1,4,256,320]{3,4,2,1,0:T(8,128)(2,1)} %param.13) | copy-start | bytes 1966084
  0.0 18.7 %copy-start.5 = (f32[320]{0:T(512)S(1)}, f32[320]{0:T(512)}, u32[]{:S(2)}) copy-start(f32[320]{0:T(512)} %param.16) | copy-start | bytes 3844
  0.0 18.7 %copy-start.4 = (f32[320]{0:T(512)S(1)}, f32[320]{0:T(512)}, u32[]{:S(2)}) copy-start(f32[320]{0:T(512)} %param.17) | copy-start | bytes 3844
  3.9 19.3 %copy-start.3 = (bf16[3,3,320,320]{3,2,1,0:T(8,128)(2,1)S(1)}, bf16[3,3,320,320]{3,2,1,0:T(8,128)(2,1)}, u32[]{:S(2)}) copy-start(bf16[3,3,320,320]{3,2,1,0:T(8,128)(2,1)} %param.18) | copy-start | bytes 5529604
  19.4 7.1 %collective-permute-start = (bf16[1,1,256,320]{2,3,1,0:T(8,128)(2,1)S(1)}, bf16[1,1,256,320]{2,3,1,0:T(8,128)(2,1)S(1)}, u32[]{:S(2)}, u32[]{:S(2)}) collective-permute-start(bf16[1,1,256,320]{2,3,1,0:T(8,128)(2,1)S(1)} %get-tuple-element.7), channel_id=1, source_target_pairs={{0,2},{2,4},{4,6},{6,8},{8,10},{10,12},{12,14},{1,3},{3,5},{5,7},{... | collective-permute-start | bytes 491528 | tf_op jit(solution)/shard_map/ppermute | solution.py:19
  21.9 2.3 %copy-start.8 = (f32[320]{0:T(512)S(1)}, f32[320]{0:T(512)}, u32[]{:S(2)}) copy-start(f32[320]{0:T(512)} %param.21) | copy-start | bytes 3844
  21.9 7.2 %collective-permute-start.1 = (bf16[1,1,256,320]{2,3,1,0:T(8,128)(2,1)S(1)}, bf16[1,1,256,320]{2,3,1,0:T(8,128)(2,1)S(1)}, u32[]{:S(2)}, u32[]{:S(2)}) collective-permute-start(bf16[1,1,256,320]{2,3,1,0:T(8,128)(2,1)S(1)} %get-tuple-element.8), channel_id=1, source_target_pairs={{2,0},{4,2},{6,4},{8,6},{10,8},{12,10},{14,12},{3,1},{5,3},{7,5},{... | collective-permute-start | bytes 491528 | tf_op jit(solution)/shard_map/ppermute | solution.py:20
  33.4 0.7 %copy-start.9 = (f32[320]{0:T(512)S(1)}, f32[320]{0:T(512)}, u32[]{:S(2)}) copy-start(f32[320]{0:T(512)} %param.19) | copy-start | bytes 3844
  36.1 2.2 %collective-permute-start.2 = (bf16[1,4,256,320]{2,3,1,0:T(8,128)(2,1)S(1)}, bf16[1,4,256,320]{2,3,1,0:T(8,128)(2,1)S(1)}, u32[]{:S(2)}, u32[]{:S(2)}) collective-permute-start(bf16[1,4,256,320]{2,3,1,0:T(8,128)(2,1)S(1)} %fusion.41), channel_id=1, source_target_pairs={{0,16},{16,0},{1,17},{17,1},{2,18},{18,2},{3,19},{19,3},{4,20},{20... | collective-permute-start | bytes 1966088 | tf_op jit(solution)/shard_map/ppermute | solution.py:28
  38.3 12.1 %copy-start.6 = (f32[320]{0:T(512)S(1)}, f32[320]{0:T(512)}, u32[]{:S(2)}) copy-start(f32[320]{0:T(512)} %param.23) | copy-start | bytes 3844
  38.3 12.1 %copy-start.7 = (f32[320]{0:T(512)S(1)}, f32[320]{0:T(512)}, u32[]{:S(2)}) copy-start(f32[320]{0:T(512)} %param.22) | copy-start | bytes 3844
  50.4 4.9 %copy-start.2 = (bf16[3,3,320,320]{3,2,1,0:T(8,128)(2,1)S(1)}, bf16[3,3,320,320]{3,2,1,0:T(8,128)(2,1)}, u32[]{:S(2)}) copy-start(bf16[3,3,320,320]{3,2,1,0:T(8,128)(2,1)} %param.24) | copy-start | bytes 5529604
  51.4 5.3 %collective-permute-start.3 = (bf16[1,1,256,320]{2,3,1,0:T(8,128)(2,1)S(1)}, bf16[1,1,256,320]{2,3,1,0:T(8,128)(2,1)S(1)}, u32[]{:S(2)}, u32[]{:S(2)}) collective-permute-start(bf16[1,1,256,320]{2,3,1,0:T(8,128)(2,1)S(1)} %get-tuple-element.5), channel_id=1, source_target_pairs={{0,2},{2,4},{4,6},{6,8},{8,10},{10,12},{12,14},{1,3},{3,5},{5,7},{... | collective-permute-start | bytes 491528 | tf_op jit(solution)/shard_map/ppermute | solution.py:19
  53.9 7.2 %collective-permute-start.4 = (bf16[1,1,256,320]{2,3,1,0:T(8,128)(2,1)S(1)}, bf16[1,1,256,320]{2,3,1,0:T(8,128)(2,1)S(1)}, u32[]{:S(2)}, u32[]{:S(2)}) collective-permute-start(bf16[1,1,256,320]{2,3,1,0:T(8,128)(2,1)S(1)} %get-tuple-element.6), channel_id=1, source_target_pairs={{2,0},{4,2},{6,4},{8,6},{10,8},{12,10},{14,12},{3,1},{5,3},{7,5},{... | collective-permute-start | bytes 491528 | tf_op jit(solution)/shard_map/ppermute | solution.py:20
  65.4 0.7 %copy-start.10 = (f32[320]{0:T(512)S(1)}, f32[320]{0:T(512)}, u32[]{:S(2)}) copy-start(f32[320]{0:T(512)} %param.25) | copy-start | bytes 3844

commit v2 on v1

--- a/solution.py
+++ b/solution.py
@@ -29,8 +29,7 @@
 
 
 def gathered(rows, axes):
-    peers = lax.axis_size(axes)
-    return lax.all_to_all(jnp.broadcast_to(rows[None], (peers,) + rows.shape), axes, 0, 0)
+    return lax.all_gather(rows, axes)
 
 
 def local_moments(values):

time: 68.5 us -> 91.1 us (1.33)
  blocking collectives: 23.7 us -> 45 us
  starting transfers between devices: 7.75 us -> 9.08 us
    all_gather x0 -> x2, blocking collectives: none -> 45 us  [gathered(): return lax.all_gather(rows, axes)]
    all_to_all x2 -> x0, blocking collectives: 23.7 us -> none  [gathered(): lax.all_to_all(jnp.broadcast_to(rows[None], (peers,) + rows.shape), axes,...]
    ppermute x2, waiting for transfers between devices: 7.03 us -> 8.82 us  [extended(): after = lax.ppermute(first, axis, down)]
    ppermute x2, waiting for transfers between devices: 3.07 us -> 1.29 us  [extended(): before = lax.ppermute(last, axis, up)]
    ppermute x2, starting transfers between devices: 4.91 us -> 6.25 us  [extended(): before = lax.ppermute(last, axis, up)]
where the time goes in v2:
time: 91.1 us; the launch traced here: 90.8 us
  blocking collectives  45 us (49%)
  matrix products  13.5 us (15%)
  waiting for transfers between devices  11.5 us (13%)
  starting transfers between devices  9.08 us (10%)
  other arithmetic  8.67 us (10%)
  local copies, waits for them, and re-layouts  1.97 us (2%)
  between operations  1.02 us (1%)
    all_gather x2, blocking collectives, gathered(): return lax.all_gather(rows, axes)  45 us
    dot_general x18, matrix products, convolve(): jnp.einsum('rhwc,cd->rhwd', padded[:, shift_y:shift_y + rows, shift_x:shi...  13.3 us
    ppermute x2, waiting for transfers between devices, extended(): after = lax.ppermute(first, axis, down)  8.82 us
    ppermute x2, starting transfers between devices, extended(): before = lax.ppermute(last, axis, up)  6.25 us
    ppermute x2, starting transfers between devices, extended(): after = lax.ppermute(first, axis, down)  2.76 us
    reduce_sum x4, other arithmetic, local_moments(): return (mean, jnp.sum(centred * centred, axis=(1, 2, 4)), count)  2.33 us
    reduce_sum x4, other arithmetic, local_moments(): mean = jnp.sum(view, axis=(1, 2, 4)) / count  1.93 us
  transfers between devices with their start and end apart: 5, of which 5 were waited for; matrix products, arithmetic and copies ran while one was open for 2% of the time, Pallas kernels for 0%

profile of v2, /device:TPU:0, one launch (start us, length us, event | category | flops | bytes accessed | tf_op | source)
XLA Modules:
  0.0 90.8 jit_solution(13541359147096120050)
XLA Ops:
  0.0 0.8 convert_element_type.85
  0.8 1.3 %convert_reduce_fusion = f32[320]{0:T(512)S(1)} fusion(bf16[1,1,4,256,320]{3,4,2,1,0:T(8,128)(2,1)} %param.13), kind=kLoop, calls=%fused_computation.5 | loop fusion | flops 655040 | bytes 656640 | tf_op jit(solution)/shard_map/reduce_sum | solution.py:39
  2.5 1.6 %fusion.31 = f32[320]{0:T(512)S(1)} fusion(bf16[1,1,4,256,320]{3,4,2,1,0:T(8,128)(2,1)} %param.13, f32[320]{0:T(512)S(1)} %sub.97), kind=kLoop, calls=%fused_computation.45 | loop fusion | flops 1310400 | bytes 657920 | tf_op jit(solution)/shard_map/reduce_sum | solution.py:41
  4.6 27.7 %all-gather.2 = f32[8,1,384]{2,1,0:T(1,128)S(1)} all-gather(f32[1,1,384]{2,1,0:T(1,128)S(1)} %maximum_bitcast_fusion), channel_id=2, replica_groups=mesh['cfg'=2,'patch'=8,'req'=2] {'patch'}, dimensions={0}, use_global_device_ids=true | all-gather | bytes 13824 | tf_op jit(solution)/shard_map/all_gather | solution.py:32
  32.8 0.6 fusion.29
  33.5 3.4 %collective-permute-start = (bf16[1,1,256,320]{2,3,1,0:T(8,128)(2,1)S(1)}, bf16[1,1,256,320]{2,3,1,0:T(8,128)(2,1)S(1)}, u32[]{:S(2)}, u32[]{:S(2)}) collective-permute-start(bf16[1,1,256,320]{2,3,1,0:T(8,128)(2,1)S(1)} %get-tuple-element.7), channel_id=1, source_target_pairs={{0,2},{2,4},{4,6},{6,8},{8,10},{10,12},{12,14},{1,3},{3,5},{5,7},{... | collective-permute-start | bytes 491528 | tf_op jit(solution)/shard_map/ppermute | solution.py:19
  36.9 1.3 %collective-permute-start.1 = (bf16[1,1,256,320]{2,3,1,0:T(8,128)(2,1)S(1)}, bf16[1,1,256,320]{2,3,1,0:T(8,128)(2,1)S(1)}, u32[]{:S(2)}, u32[]{:S(2)}) collective-permute-start(bf16[1,1,256,320]{2,3,1,0:T(8,128)(2,1)S(1)} %get-tuple-element.8), channel_id=1, source_target_pairs={{2,0},{4,2},{6,4},{8,6},{10,8},{12,10},{14,12},{3,1},{5,3},{7,5},{... | collective-permute-start | bytes 491528 | tf_op jit(solution)/shard_map/ppermute | solution.py:20
  38.2 0.9 fusion.44
  39.7 4.4 %collective-permute-done.1 = bf16[1,1,256,320]{2,3,1,0:T(8,128)(2,1)S(1)} collective-permute-done((bf16[1,1,256,320]{2,3,1,0:T(8,128)(2,1)S(1)}, bf16[1,1,256,320]{2,3,1,0:T(8,128)(2,1)S(1)}, u32[]{:S(2)}, u32[]{:S(2)}) %collective-permute-start.1) | collective-permute-done | bytes 163872 | tf_op jit(solution)/shard_map/ppermute | solution.py:20
  44.1 0.8 fusion.5
  45.0 0.7 fusion.59
  46.7 0.7 fusion.66
  49.2 2.0 %fusion.41 = bf16[1,4,256,320]{2,3,1,0:T(8,128)(2,1)S(1)} fusion(f32[4,256,320]{1,2,0:T(8,128)S(1)} %fusion.59, f32[4,256,320]{1,2,0:T(8,128)S(1)} %fusion.61, f32[4,256,320]{1,2,0:T(8,128)S(1)} %fusion.64, f32[4,256,320]{1,2,0:T(8,128)S(1)} %fusion.44, f32[4,256,320]{1,2,0:T(8,128)S(1)} %fusion.65, f32[4,256,320]{1,2,0:T(8,128)S(1)} %fusion.66, ...), kind=kOutput, calls=%fused_computation.57 | convolution fusion | flops 213319680 | bytes 12046336 | tf_op jit(solution)/shard_map/rhwc,cd->rhwd/dot_general | solution.py:72
  51.9 1.4 %collective-permute-done.2 = bf16[1,4,256,320]{2,3,1,0:T(8,128)(2,1)S(1)} collective-permute-done((bf16[1,4,256,320]{2,3,1,0:T(8,128)(2,1)S(1)}, bf16[1,4,256,320]{2,3,1,0:T(8,128)(2,1)S(1)}, u32[]{:S(2)}, u32[]{:S(2)}) %collective-permute-start.2) | collective-permute-done | bytes 655392 | tf_op jit(solution)/shard_map/ppermute | solution.py:28
  55.0 17.3 %all-gather.3 = f32[8,1,64]{2,1,0:T(1,128)S(1)} all-gather(f32[1,1,64]{2,1,0:T(1,128)S(1)} %maximum_bitcast_fusion.1), channel_id=3, replica_groups=mesh['cfg'=2,'patch'=8,'req'=2] {'patch'}, dimensions={0}, use_global_device_ids=true | all-gather | bytes 2304 | tf_op jit(solution)/shard_map/all_gather | solution.py:32
  72.8 0.9 multiply_convert_fusion
  73.8 2.8 %collective-permute-start.3 = (bf16[1,1,256,320]{2,3,1,0:T(8,128)(2,1)S(1)}, bf16[1,1,256,320]{2,3,1,0:T(8,128)(2,1)S(1)}, u32[]{:S(2)}, u32[]{:S(2)}) collective-permute-start(bf16[1,1,256,320]{2,3,1,0:T(8,128)(2,1)S(1)} %get-tuple-element.5), channel_id=1, source_target_pairs={{0,2},{2,4},{4,6},{6,8},{8,10},{10,12},{12,14},{1,3},{3,5},{5,7},{... | collective-permute-start | bytes 491528 | tf_op jit(solution)/shard_map/ppermute | solution.py:19
  76.6 1.5 %collective-permute-start.4 = (bf16[1,1,256,320]{2,3,1,0:T(8,128)(2,1)S(1)}, bf16[1,1,256,320]{2,3,1,0:T(8,128)(2,1)S(1)}, u32[]{:S(2)}, u32[]{:S(2)}) collective-permute-start(bf16[1,1,256,320]{2,3,1,0:T(8,128)(2,1)S(1)} %get-tuple-element.6), channel_id=1, source_target_pairs={{2,0},{4,2},{6,4},{8,6},{10,8},{12,10},{14,12},{3,1},{5,3},{7,5},{... | collective-permute-start | bytes 491528 | tf_op jit(solution)/shard_map/ppermute | solution.py:20
  78.6 0.8 collective-permute-done.3
  79.4 4.4 %collective-permute-done.4 = bf16[1,1,256,320]{2,3,1,0:T(8,128)(2,1)S(1)} collective-permute-done((bf16[1,1,256,320]{2,3,1,0:T(8,128)(2,1)S(1)}, bf16[1,1,256,320]{2,3,1,0:T(8,128)(2,1)S(1)}, u32[]{:S(2)}, u32[]{:S(2)}) %collective-permute-start.4) | collective-permute-done | bytes 163872 | tf_op jit(solution)/shard_map/ppermute | solution.py:20
  83.8 0.8 select_maximum_fusion
  84.6 0.7 fusion.46
  86.4 0.7 fusion.53
  88.8 1.9 %fusion.42 = bf16[1,1,4,256,320]{3,4,2,1,0:T(8,128)(2,1)} fusion(f32[4,256,320]{1,2,0:T(8,128)S(1)} %fusion.46, f32[4,256,320]{1,2,0:T(8,128)S(1)} %fusion.48, f32[4,256,320]{1,2,0:T(8,128)S(1)} %fusion.51, f32[4,256,320]{1,2,0:T(8,128)S(1)} %fusion.72, f32[4,256,320]{1,2,0:T(8,128)S(1)} %fusion.52, f32[4,256,320]{1,2,0:T(8,128)S(1)} %fusion.53, ...), kind=kOutput, calls=%fused_computation.58 | convolution fusion | flops 213647360 | bytes 12699648 | tf_op jit(solution)/shard_map/rhwc,cd->rhwd/dot_general | solution.py:72
  (75 shorter events, 10.4 us)
Async XLA Ops:
  0.0 4.3 %copy-start = (bf16[160,320]{1,0:T(8,128)(2,1)S(1)}, bf16[160,320]{1,0:T(8,128)(2,1)}, u32[]{:S(2)}) copy-start(bf16[160,320]{1,0:T(8,128)(2,1)} %param.20) | copy-start | bytes 307204
  0.0 32.8 %copy-start.1 = (bf16[1,1,4,256,320]{3,4,2,1,0:T(8,128)(2,1)S(1)}, bf16[1,1,4,256,320]{3,4,2,1,0:T(8,128)(2,1)}, u32[]{:S(2)}) copy-start(bf16[1,1,4,256,320]{3,4,2,1,0:T(8,128)(2,1)} %param.13) | copy-start | bytes 1966084
  0.0 32.8 %copy-start.5 = (f32[320]{0:T(512)S(1)}, f32[320]{0:T(512)}, u32[]{:S(2)}) copy-start(f32[320]{0:T(512)} %param.16) | copy-start | bytes 3844
  0.0 32.8 %copy-start.4 = (f32[320]{0:T(512)S(1)}, f32[320]{0:T(512)}, u32[]{:S(2)}) copy-start(f32[320]{0:T(512)} %param.17) | copy-start | bytes 3844
  2.5 35.7 %copy-start.3 = (bf16[3,3,320,320]{3,2,1,0:T(8,128)(2,1)S(1)}, bf16[3,3,320,320]{3,2,1,0:T(8,128)(2,1)}, u32[]{:S(2)}) copy-start(bf16[3,3,320,320]{3,2,1,0:T(8,128)(2,1)} %param.18) | copy-start | bytes 5529604
  33.5 6.2 %collective-permute-start = (bf16[1,1,256,320]{2,3,1,0:T(8,128)(2,1)S(1)}, bf16[1,1,256,320]{2,3,1,0:T(8,128)(2,1)S(1)}, u32[]{:S(2)}, u32[]{:S(2)}) collective-permute-start(bf16[1,1,256,320]{2,3,1,0:T(8,128)(2,1)S(1)} %get-tuple-element.7), channel_id=1, source_target_pairs={{0,2},{2,4},{4,6},{6,8},{8,10},{10,12},{12,14},{1,3},{3,5},{5,7},{... | collective-permute-start | bytes 491528 | tf_op jit(solution)/shard_map/ppermute | solution.py:19
  36.9 2.3 %copy-start.8 = (f32[320]{0:T(512)S(1)}, f32[320]{0:T(512)}, u32[]{:S(2)}) copy-start(f32[320]{0:T(512)} %param.21) | copy-start | bytes 3844
  36.9 7.2 %collective-permute-start.1 = (bf16[1,1,256,320]{2,3,1,0:T(8,128)(2,1)S(1)}, bf16[1,1,256,320]{2,3,1,0:T(8,128)(2,1)S(1)}, u32[]{:S(2)}, u32[]{:S(2)}) collective-permute-start(bf16[1,1,256,320]{2,3,1,0:T(8,128)(2,1)S(1)} %get-tuple-element.8), channel_id=1, source_target_pairs={{2,0},{4,2},{6,4},{8,6},{10,8},{12,10},{14,12},{3,1},{5,3},{7,5},{... | collective-permute-start | bytes 491528 | tf_op jit(solution)/shard_map/ppermute | solution.py:20
  48.5 0.7 copy-start.9
  51.2 2.2 %collective-permute-start.2 = (bf16[1,4,256,320]{2,3,1,0:T(8,128)(2,1)S(1)}, bf16[1,4,256,320]{2,3,1,0:T(8,128)(2,1)S(1)}, u32[]{:S(2)}, u32[]{:S(2)}) collective-permute-start(bf16[1,4,256,320]{2,3,1,0:T(8,128)(2,1)S(1)} %fusion.41), channel_id=1, source_target_pairs={{0,16},{16,0},{1,17},{17,1},{2,18},{18,2},{3,19},{19,3},{4,20},{20... | collective-permute-start | bytes 1966088 | tf_op jit(solution)/shard_map/ppermute | solution.py:28
  53.4 19.4 %copy-start.6 = (f32[320]{0:T(512)S(1)}, f32[320]{0:T(512)}, u32[]{:S(2)}) copy-start(f32[320]{0:T(512)} %param.23) | copy-start | bytes 3844
  53.4 19.4 %copy-start.7 = (f32[320]{0:T(512)S(1)}, f32[320]{0:T(512)}, u32[]{:S(2)}) copy-start(f32[320]{0:T(512)} %param.22) | copy-start | bytes 3844
  72.8 5.3 %copy-start.2 = (bf16[3,3,320,320]{3,2,1,0:T(8,128)(2,1)S(1)}, bf16[3,3,320,320]{3,2,1,0:T(8,128)(2,1)}, u32[]{:S(2)}) copy-start(bf16[3,3,320,320]{3,2,1,0:T(8,128)(2,1)} %param.24) | copy-start | bytes 5529604
  73.8 5.7 %collective-permute-start.3 = (bf16[1,1,256,320]{2,3,1,0:T(8,128)(2,1)S(1)}, bf16[1,1,256,320]{2,3,1,0:T(8,128)(2,1)S(1)}, u32[]{:S(2)}, u32[]{:S(2)}) collective-permute-start(bf16[1,1,256,320]{2,3,1,0:T(8,128)(2,1)S(1)} %get-tuple-element.5), channel_id=1, source_target_pairs={{0,2},{2,4},{4,6},{6,8},{8,10},{10,12},{12,14},{1,3},{3,5},{5,7},{... | collective-permute-start | bytes 491528 | tf_op jit(solution)/shard_map/ppermute | solution.py:19
  76.6 7.2 %collective-permute-start.4 = (bf16[1,1,256,320]{2,3,1,0:T(8,128)(2,1)S(1)}, bf16[1,1,256,320]{2,3,1,0:T(8,128)(2,1)S(1)}, u32[]{:S(2)}, u32[]{:S(2)}) collective-permute-start(bf16[1,1,256,320]{2,3,1,0:T(8,128)(2,1)S(1)} %get-tuple-element.6), channel_id=1, source_target_pairs={{2,0},{4,2},{6,4},{8,6},{10,8},{12,10},{14,12},{3,1},{5,3},{7,5},{... | collective-permute-start | bytes 491528 | tf_op jit(solution)/shard_map/ppermute | solution.py:20
  88.1 0.7 copy-start.10

commit v3 on v0

v3 whole, which is shorter than its diff:
```python
import functools

import jax
import jax.numpy as jnp
from jax import lax
from jax.experimental import pallas as pl
from jax.experimental.pallas import tpu as pltpu
from jax.sharding import PartitionSpec as P

GROUPS = 32
EPS = 1e-05
REACH = 2
LANES = 128
F32 = jnp.float32
BF16 = jnp.bfloat16


def padded_lanes(chans):
    return -(-chans // LANES) * LANES


def widen(row, wide):
    short = wide - row.shape[1]
    if not short:
        return row
    return jnp.concatenate([row, jnp.zeros((row.shape[0], short), row.dtype)], axis=1)


def same_group(wide, size):
    left = lax.broadcasted_iota(jnp.int32, (wide, wide), 0).astype(F32)
    right = lax.broadcasted_iota(jnp.int32, (wide, wide), 1).astype(F32)
    group = lambda at: jnp.floor((at + 0.5) * (1.0 / size))
    return jnp.where(group(left) == group(right), 1.0, 0.0).astype(BF16)


def group_sum(rows, mask):
    high = rows.astype(BF16).astype(F32)
    rest = rows - high
    middle = rest.astype(BF16).astype(F32)
    pieces = jnp.concatenate([high, middle, rest - middle, jnp.zeros_like(rows)], axis=0).astype(BF16)
    sums = jnp.dot(pieces, mask, preferred_element_type=F32)
    return sums[0:8] + sums[8:16] + sums[16:24]


def stack_rows(rows, wide):
    filler = [jnp.zeros((8 - len(rows), wide), F32)] if len(rows) < 8 else []
    return jnp.concatenate(list(rows) + filler, axis=0)


def group_stats(means, squares, count, mask, size):
    wide = mask.shape[0]
    peers = means[0].shape[0]
    mean_rows = [jnp.sum(m, axis=0, keepdims=True) * (1.0 / peers) for m in means]
    mean_rows = group_sum(stack_rows(mean_rows, wide), mask) * (1.0 / size)
    spread = []
    for k, (m, q) in enumerate(zip(means, squares)):
        off = m - mean_rows[k : k + 1]
        spread.append(jnp.sum(q + count * (off * off), axis=0, keepdims=True))
    var_rows = group_sum(stack_rows(spread, wide), mask) * (1.0 / (size * count * peers))
    return mean_rows, var_rows


def fold(values):
    total = values[:, :LANES]
    for at in range(LANES, values.shape[1], LANES):
        total = total + values[:, at : at + LANES]
    return total


def channel_moments(rows, chans):
    count = 0
    total = None
    for row in rows():
        part = fold(row)
        count += row.shape[1]
        total = part if total is None else total + part
    mean = jnp.sum(total, axis=1, keepdims=True) * (1.0 / count)
    squares = None
    for row in rows():
        off = row - mean
        part = fold(off * off)
        squares = part if squares is None else squares + part
    squares = jnp.sum(squares, axis=1, keepdims=True)
    lane = lax.broadcasted_iota(jnp.int32, (chans, LANES), 1)
    both = jnp.where(lane == 0, mean, jnp.where(lane == 1, squares, 0.0))
    wide = padded_lanes(chans)
    both = jnp.concatenate([both, jnp.zeros((wide - chans, LANES), F32)], axis=0)
    turned = both.T
    return turned[0:1], turned[1:2]


def put_rows(tile_rows, out_ref):
    peers, height, _ = out_ref.shape
    lines = [row[:, at : at + LANES] for row in tile_rows for at in range(0, row.shape[1], LANES)]
    if len(lines) < height:
        lines.append(jnp.zeros((height - len(lines), LANES), F32))
    tile = jnp.concatenate(lines, axis=0)
    out_ref[...] = jnp.broadcast_to(tile[None], out_ref.shape)


def get_rows(seen_ref, first, peers, which, wide):
    lines = wide // LANES
    return jnp.concatenate(
        [seen_ref[pl.ds(first, peers), which * lines + k, :] for k in range(lines)], axis=1
    )


def stats_kernel(lat_ref, embed_ref, weight_ref, out_ref):
    rows, chans, _ = lat_ref.shape
    wide = padded_lanes(chans)
    mean, squares = channel_moments(lambda: (lat_ref[k].astype(F32) for k in range(rows)), chans)
    own = weight_ref.shape[0]
    length = embed_ref.shape[1]
    embed = jnp.broadcast_to(embed_ref[...].astype(F32), (8, length))
    embed = pltpu.roll(embed, length - lax.axis_index("patch") * own, 1)[:, :own]
    act = (embed / (1.0 + jnp.exp(-embed))).astype(BF16)
    time_part = jnp.dot(act, weight_ref[...], preferred_element_type=F32)[0:1]
    put_rows([mean, squares, widen(time_part, wide)], out_ref)


def turn_kernel(one_ref, two_ref, one_out, two_out):
    for source, target in ((one_ref, one_out), (two_ref, two_out)):
        deep = source.shape[0]
        step = 320 if deep % 320 == 0 else deep
        step = 2 * step if deep % (2 * step) == 0 else step
        for at in range(0, deep, 640):
            target[:, at : min(at + 640, deep)] = source[at : min(at + 640, deep), :].T


def spread_columns(rows, chans, cols_ref):
    turned = stack_rows(rows, rows[0].shape[1]).T
    for k in range(len(rows)):
        cols_ref[k] = jnp.broadcast_to(turned[:chans, k : k + 1], (chans, LANES))


def half_act(values, mean, scale, shift):
    half = (values - mean) * scale + shift
    return half * jnp.tanh(half) + half


def twice(column):
    return jnp.concatenate([column, column], axis=1)


def put_taps(taps_ref, at, row):
    chans, cols = row.shape
    lane = lax.broadcasted_iota(jnp.int32, (chans, cols), 1)
    before = jnp.where(lane == 0, 0.0, pltpu.roll(row, 1, 1))
    after = jnp.where(lane == cols - 1, 0.0, pltpu.roll(row, cols - 1, 1))
    for k, value in enumerate((before, row, after)):
        taps_ref[pl.ds((at * 3 + k) * chans, chans), :] = value.astype(BF16)


def edge_keep(at, rows, reach):
    patch, patches = lax.axis_index("patch"), lax.axis_size("patch")
    if at < reach:
        return jnp.where(patch == 0, 0.0, 1.0).astype(F32)
    if at >= reach + rows:
        return jnp.where(patch == patches - 1, 0.0, 1.0).astype(F32)
    return None


def first_kernel(
    own_ref, far_ref, near_ref, next_ref, far_near_ref, far_next_ref, seen_ref, steer_ref,
    gain_ref, shift_ref, bias_ref, time_bias_ref, weight_hbm,
    steered_ref, out_ref,
    weight_ref, taps_ref, cols_ref, edge_ref, sem,
):
    copy = pltpu.make_async_copy(weight_hbm, weight_ref, sem)
    copy.start()
    rows, chans, cols = own_ref.shape
    reach = near_ref.shape[0]
    wide = padded_lanes(chans)
    size = chans // GROUPS
    cfg, patches = lax.axis_index("cfg"), lax.axis_size("patch")
    even = lax.rem(lax.axis_index("patch"), 2) == 0
    mask = same_group(wide, size)
    peers = patches
    starts = (cfg * peers, (1 - cfg) * peers)
    means = [get_rows(seen_ref, s, peers, 0, wide) for s in starts]
    squares = [get_rows(seen_ref, s, peers, 1, wide) for s in starts]
    mean_rows, var_rows = group_stats(means, squares, float(rows * cols), mask, size)
    scale_rows = lax.rsqrt(var_rows + EPS) * (0.5 * widen(gain_ref[...], wide))
    times = jnp.sum(get_rows(seen_ref, 0, peers, 2, wide), axis=0, keepdims=True)
    added = times + widen(time_bias_ref[...] + bias_ref[...], wide)
    spread_columns(
        [mean_rows[0:1], scale_rows[0:1], mean_rows[1:2], scale_rows[1:2],
         0.5 * widen(shift_ref[...], wide), added],
        chans, cols_ref,
    )
    above = jnp.where(even, reach, 0)
    edge_ref[0, pl.ds(reach - above, reach)] = near_ref[...]
    edge_ref[0, pl.ds(above, reach)] = next_ref[...]
    edge_ref[1, pl.ds(reach - above, reach)] = far_near_ref[...]
    edge_ref[1, pl.ds(above, reach)] = far_next_ref[...]
    sign = jnp.where(cfg == 0, 1.0, -1.0).astype(F32) * steer_ref[0]

    def inputs(at):
        if at < reach:
            return edge_ref[0, reach + at], edge_ref[1, reach + at]
        if at >= reach + rows:
            return edge_ref[0, at - reach - rows], edge_ref[1, at - reach - rows]
        return own_ref[at - reach], far_ref[at - reach]

    for at in range(rows + 2 * reach):
        mine, other = inputs(at)
        shift = twice(cols_ref[4])
        mine = half_act(mine.astype(F32), twice(cols_ref[0]), twice(cols_ref[1]), shift)
        other = half_act(other.astype(F32), twice(cols_ref[2]), twice(cols_ref[3]), shift)
        mixed = mine + sign * (mine - other)
        keep = edge_keep(at, rows, reach)
        put_taps(taps_ref, at, mixed if keep is None else mixed * keep)
    copy.wait()
    deep = 9 * chans
    for at in range(rows + 2 * reach - 2):
        total = jnp.dot(
            weight_ref[...], taps_ref[pl.ds(at * 3 * chans, deep), :], preferred_element_type=F32
        )
        steered_ref[at] = total + twice(cols_ref[5])
    skip = reach - 1
    mean, square = channel_moments(lambda: (steered_ref[skip + k] for k in range(rows)), chans)
    put_rows([mean, square], out_ref)


def second_kernel(
    steered_ref, lat_ref, seen_ref, gain_ref, shift_ref, bias_ref, weight_hbm,
    out_ref,
    weight_ref, taps_ref, cols_ref, sem,
):
    copy = pltpu.make_async_copy(weight_hbm, weight_ref, sem)
    copy.start()
    rows, chans, cols = lat_ref.shape
    wide = padded_lanes(chans)
    size = chans // GROUPS
    peers = lax.axis_size("patch")
    mask = same_group(wide, size)
    mean_rows, var_rows = group_stats(
        [get_rows(seen_ref, 0, peers, 0, wide)], [get_rows(seen_ref, 0, peers, 1, wide)],
        float(rows * cols), mask, size,
    )
    scale_rows = lax.rsqrt(var_rows + EPS) * (0.5 * widen(gain_ref[...], wide))
    spread_columns(
        [mean_rows[0:1], scale_rows[0:1], 0.5 * widen(shift_ref[...], wide), widen(bias_ref[...], wide)],
        chans, cols_ref,
    )
    for at in range(rows + 2):
        value = half_act(steered_ref[at], twice(cols_ref[0]), twice(cols_ref[1]), twice(cols_ref[2]))
        keep = edge_keep(at, rows, 1)
        put_taps(taps_ref, at, value if keep is None else value * keep)
    copy.wait()
    deep = 9 * chans
    for at in range(rows):
        total = jnp.dot(
            weight_ref[...], taps_ref[pl.ds(at * 3 * chans, deep), :], preferred_element_type=F32
        )
        out_ref[at] = (lat_ref[at].astype(F32) + (total + twice(cols_ref[3]))).astype(BF16)


def everyone(tiles, axes):
    return lax.all_to_all(tiles, axes, 0, 0)


VMEM = pl.BlockSpec(memory_space=pltpu.VMEM)
SMEM = pl.BlockSpec(memory_space=pltpu.SMEM)
ANY = pl.BlockSpec(memory_space=pl.ANY)
LIMIT = pltpu.CompilerParams(vmem_limit_bytes=48 * 1024 * 1024)


def body(
    latents, time_embed, steer_scale, gain_one, shift_one, conv_one, bias_one,
    time_weight, time_bias, gain_two, shift_two, conv_two, bias_two,
):
    own = jnp.swapaxes(latents[0, 0], 1, 2)
    rows, chans, cols = own.shape
    wide = padded_lanes(chans)
    deep = 9 * chans
    patches = lax.axis_size("patch")
    even = lax.rem(lax.axis_index("patch"), 2) == 0
    near_edge = lax.dynamic_slice_in_dim(own, jnp.where(even, rows - REACH, 0), REACH, 0)
    next_edge = lax.dynamic_slice_in_dim(own, jnp.where(even, 0, rows - REACH), REACH, 0)
    near = lax.ppermute(near_edge, "patch", [(i, i ^ 1) for i in range(patches)])
    steps = [(i, i + 1) for i in range(1, patches - 1, 2)]
    following = lax.ppermute(next_edge, "patch", steps + [(j, i) for i, j in steps])
    swap = [(0, 1), (1, 0)]
    far = lax.ppermute(own, "cfg", swap)
    far_near = lax.ppermute(near, "cfg", swap)
    far_next = lax.ppermute(following, "cfg", swap)
    line = lambda vector: vector.reshape(1, chans)

    tile_one = -(-3 * wide // LANES // 8) * 8
    sent = pl.pallas_call(
        stats_kernel,
        out_shape=jax.ShapeDtypeStruct((2 * patches, tile_one, LANES), F32),
        in_specs=[VMEM] * 3,
        out_specs=VMEM,
        compiler_params=LIMIT,
        name="stats",
    )(own, time_embed, time_weight)
    seen = everyone(sent, ("cfg", "patch"))

    turned_one, turned_two = pl.pallas_call(
        turn_kernel,
        out_shape=[jax.ShapeDtypeStruct((chans, deep), BF16)] * 2,
        in_specs=[VMEM] * 2,
        out_specs=[VMEM] * 2,
        compiler_params=LIMIT,
        name="turn",
    )(conv_one.reshape(deep, chans), conv_two.reshape(deep, chans))

    tile_two = -(-2 * wide // LANES // 8) * 8
    inside = rows + 2 * REACH - 2
    steered, sent = pl.pallas_call(
        first_kernel,
        out_shape=[
            jax.ShapeDtypeStruct((inside, chans, cols), F32),
            jax.ShapeDtypeStruct((patches, tile_two, LANES), F32),
        ],
        in_specs=[VMEM] * 7 + [SMEM] + [VMEM] * 4 + [ANY],
        out_specs=[VMEM] * 2,
        scratch_shapes=[
            pltpu.VMEM((chans, deep), BF16),
            pltpu.VMEM(((rows + 2 * REACH) * 3 * chans, cols), BF16),
            pltpu.VMEM((6, chans, LANES), F32),
            pltpu.VMEM((2, 2 * REACH, chans, cols), BF16),
            pltpu.SemaphoreType.DMA,
        ],
        compiler_params=LIMIT,
        name="first",
    )(
        own, far, near, following, far_near, far_next, seen, steer_scale,
        line(gain_one), line(shift_one), line(bias_one), line(time_bias), turned_one,
    )
    seen = everyone(sent, "patch")
    image = pl.pallas_call(
        second_kernel,
        out_shape=jax.ShapeDtypeStruct((rows, chans, cols), BF16),
        in_specs=[VMEM] * 6 + [ANY],
        out_specs=VMEM,
        scratch_shapes=[
            pltpu.VMEM((chans, deep), BF16),
            pltpu.VMEM(((rows + 2) * 3 * chans, cols), BF16),
            pltpu.VMEM((4, chans, LANES), F32),
            pltpu.SemaphoreType.DMA,
        ],
        compiler_params=LIMIT,
        name="second",
    )(steered, own, seen, line(gain_two), line(shift_two), line(bias_two), turned_two)
    return jnp.swapaxes(image, 1, 2)[None, None]


def solution(mesh):
    placed = (
        P("cfg", "req", "patch", None, None), P("req", None), P("req"), P(), P(), P(), P(),
        P("patch", None), P(), P(), P(), P(), P(),
    )
    return jax.shard_map(
        body,
        mesh=mesh,
        in_specs=placed,
        out_specs=P("cfg", "req", "patch", None, None),
        check_vma=False,
    )
```

time: 123 us -> 64.8 us (0.53)
  blocking collectives: 76.5 us -> 0 us
  Pallas kernels: 0 us -> 17.4 us
  matrix products: 13.5 us -> 0 us
  waiting for transfers between devices: 11.6 us -> 20.4 us
  local copies, waits for them, and re-layouts: 1.52 us -> 9.83 us
  other arithmetic: 8.27 us -> 0 us
  starting transfers between devices: 9.68 us -> 15.8 us
    psum x4 -> x0, blocking collectives: 76.5 us -> none  [the longest x2 41.1 us: moments(): mean = lax.psum(jnp.sum(view, axis=(1, 2, 4)), 'patch') / total]
    pallas_call x0 -> x4, Pallas kernels: none -> 17.4 us  [the longest x1 8.75 us: body(): pl.pallas_call(first_kernel, out_shape=[jax.ShapeDtypeStruct((inside, cha...]
    dot_general x19 -> x0, matrix products: 13.5 us -> none  [the longest x18 13.3 us: convolve(): jnp.einsum('rhwc,cd->rhwd', padded[:, shift_y:shift_y + rows, shift_x:shi...]
    all_to_all x0 -> x2, starting transfers between devices: none -> 10.9 us  [everyone(): return lax.all_to_all(tiles, axes, 0, 0)]
    unnamed x22 -> x30, local copies, waits for them, and re-layouts: 0.34 us -> 8.64 us
    all_to_all x0 -> x2, waiting for transfers between devices: none -> 7.76 us  [everyone(): return lax.all_to_all(tiles, axes, 0, 0)]
    ppermute x5, starting transfers between devices: 9.68 us -> 4.9 us  [the longest x1 3 us: body(): lax.ppermute(near_edge, 'patch', [(i, i ^ 1) for i in range(patches)])]
    reduce_sum x8 -> x0, other arithmetic: 4.26 us -> none  [the longest x4 2.33 us: moments(): jnp.sum(centred * centred, axis=(1, 2, 4))]
  transfers between devices with their start and end apart: 5 -> 7, of which waited for: 5 -> 3; matrix products, arithmetic and copies ran while one was open for 1% -> 0% of each run, Pallas kernels for 0% -> 6%
where the time goes in v3:
time: 64.8 us; the launch traced here: 64.2 us
  waiting for transfers between devices  20.4 us (31%)
  Pallas kernels  17.4 us (27%)
  starting transfers between devices  15.8 us (24%)
  local copies, waits for them, and re-layouts  9.83 us (15%)
  between operations  0.83 us (1%)
    ppermute x1, waiting for transfers between devices, body(): lax.ppermute(near_edge, 'patch', [(i, i ^ 1) for i in range(patches)])  12.6 us
    all_to_all x2, starting transfers between devices, everyone(): return lax.all_to_all(tiles, axes, 0, 0)  10.9 us
    pallas_call x1, Pallas kernels, body(): pl.pallas_call(first_kernel, out_shape=[jax.ShapeDtypeStruct((inside, cha...  8.75 us
    unnamed x30, local copies, waits for them, and re-layouts  8.64 us
    all_to_all x2, waiting for transfers between devices, everyone(): return lax.all_to_all(tiles, axes, 0, 0)  7.76 us
    pallas_call x1, Pallas kernels, body(): pl.pallas_call(second_kernel, out_shape=jax.ShapeDtypeStruct((rows, chans...  4.66 us
    ppermute x1, starting transfers between devices, body(): lax.ppermute(near_edge, 'patch', [(i, i ^ 1) for i in range(patches)])  3 us
    pallas_call x1, Pallas kernels, body(): pl.pallas_call(turn_kernel, out_shape=[jax.ShapeDtypeStruct((chans, deep)...  2.9 us
  transfers between devices with their start and end apart: 7, of which 3 were waited for; matrix products, arithmetic and copies ran while one was open for 0% of the time, Pallas kernels for 6%

profile of v3, /device:TPU:0, one launch (start us, length us, event | category | flops | bytes accessed | tf_op | source)
XLA Modules:
  0.0 64.2 jit_solution(4579274071589779924)
XLA Ops:
  0.0 1.2 %dynamic-slice_bitcast_fusion = (bf16[2,320,256]{2,1,0:T(8,128)(2,1)S(1)}, bf16[2,320,256]{2,1,0:T(8,128)(2,1)S(1)}) fusion(bf16[1,1,4,256,320]{3,4,2,1,0:T(8,128)(2,1)} %param.13, s32[]{:T(128)S(6)} %select_n.10, s32[]{:T(128)S(6)} %select_n.9), kind=kLoop, calls=%fused_computation | loop fusion | bytes 1310728 | tf_op jit(solution)/shard_map/dynamic_slice | solution.py:280
  1.2 3.0 %collective-permute-start.1 = (bf16[2,320,256]{2,1,0:T(8,128)(2,1)S(1)}, bf16[2,320,256]{2,1,0:T(8,128)(2,1)}, u32[]{:S(2)}, u32[]{:S(2)}) collective-permute-start(bf16[2,320,256]{2,1,0:T(8,128)(2,1)S(1)} %get-tuple-element.14), channel_id=1, source_target_pairs={{0,2},{2,0},{4,6},{6,4},{8,10},{10,8},{12,14},{14,12},{1,3},{3,1},... | collective-permute-start | bytes 983048 | tf_op jit(solution)/shard_map/ppermute | solution.py:281
  4.2 1.4 %collective-permute-start.2 = (bf16[2,320,256]{2,1,0:T(8,128)(2,1)S(1)}, bf16[2,320,256]{2,1,0:T(8,128)(2,1)}, u32[]{:S(2)}, u32[]{:S(2)}) collective-permute-start(bf16[2,320,256]{2,1,0:T(8,128)(2,1)S(1)} %get-tuple-element.13), channel_id=1, source_target_pairs={{2,4},{6,8},{10,12},{4,2},{8,6},{12,10},{3,5},{7,9},{11,13},{5,3},... | collective-permute-start | bytes 983048 | tf_op jit(solution)/shard_map/ppermute | solution.py:283
  5.6 12.6 %collective-permute-done.1.near_ref = bf16[2,320,256]{2,1,0:T(8,128)(2,1)} collective-permute-done((bf16[2,320,256]{2,1,0:T(8,128)(2,1)S(1)}, bf16[2,320,256]{2,1,0:T(8,128)(2,1)}, u32[]{:S(2)}, u32[]{:S(2)}) %collective-permute-start.1) | collective-permute-done | bytes 327712 | tf_op jit(solution)/shard_map/ppermute | solution.py:281
  18.2 0.5 collective-permute-start.4
  18.7 1.1 %copy-done = bf16[1,1,4,256,320]{3,4,2,1,0:T(8,128)(2,1)S(1)} copy-done((bf16[1,1,4,256,320]{3,4,2,1,0:T(8,128)(2,1)S(1)}, bf16[1,1,4,256,320]{3,4,2,1,0:T(8,128)(2,1)}, u32[]{:S(2)}) %copy-start) | copy-done | bytes 655384
  19.8 0.9 %copy-done.6 = bf16[160,320]{1,0:T(8,128)(2,1)S(1)} copy-done((bf16[160,320]{1,0:T(8,128)(2,1)S(1)}, bf16[160,320]{1,0:T(8,128)(2,1)}, u32[]{:S(2)}) %copy-start.6) | copy-done | bytes 102424
  20.7 0.7 %copy-done.7 = bf16[1,1280]{1,0:T(2,128)(2,1)S(1)} copy-done((bf16[1,1280]{1,0:T(2,128)(2,1)S(1)}, bf16[1,1280]{1,0:T(2,128)(2,1)}, u32[]{:S(2)}) %copy-start.7) | copy-done | bytes 2584
  21.4 1.1 %stats.1 = f32[16,16,128]{2,1,0:T(8,128)} custom-call(bf16[4,320,256]{2,1,0:T(8,128)(2,1)S(1)} %bitcast.17, bf16[1,1280]{1,0:T(2,128)(2,1)S(1)} %copy-done.7, bf16[160,320]{1,0:T(8,128)(2,1)S(1)} %copy-done.6), custom_call_target="tpu_custom_call" | custom-call | tf_op jit(solution)/shard_map/stats/pallas_call | solution.py:291
  22.5 6.1 %all-to-all-start = ((f32[16,16,128]{2,1,0:T(8,128)}), f32[16,16,128]{2,1,0:T(8,128)S(1)}, u32[]{:S(2)}, u32[]{:S(2)}) async-start(f32[16,16,128]{2,1,0:T(8,128)} %stats.1), calls=%async_computation | async-start | bytes 262144 | tf_op jit(solution)/shard_map/all_to_all | solution.py:260
  29.3 0.0 copy-start.2
  29.3 1.6 %copy-done.2 = bf16[3,3,320,320]{3,2,1,0:T(8,128)(2,1)S(1)} copy-done((bf16[3,3,320,320]{3,2,1,0:T(8,128)(2,1)S(1)}, bf16[3,3,320,320]{3,2,1,0:T(8,128)(2,1)}, u32[]{:S(2)}) %copy-start.2) | copy-done | bytes 1843224
  30.9 2.9 %turn.1 = (bf16[320,2880]{1,0:T(8,128)(2,1)S(1)}, bf16[320,2880]{1,0:T(8,128)(2,1)S(1)}) custom-call(bf16[2880,320]{1,0:T(8,128)(2,1)S(1)} %bitcast.20, bf16[2880,320]{1,0:T(8,128)(2,1)} %bitcast.21), custom_call_target="tpu_custom_call" | custom-call | tf_op jit(solution)/shard_map/turn/pallas_call | solution.py:301
  33.9 1.3 %copy-done.4 = bf16[320,2880]{1,0:T(8,128)(2,1)} copy-done((bf16[320,2880]{1,0:T(8,128)(2,1)}, bf16[320,2880]{1,0:T(8,128)(2,1)S(1)}, u32[]{:S(2)}) %copy-start.4) | copy-done | bytes 1843224
  35.1 1.1 %all-to-all-done.seen_ref = f32[16,16,128]{2,1,0:T(8,128)S(1)} async-done(((f32[16,16,128]{2,1,0:T(8,128)}), f32[16,16,128]{2,1,0:T(8,128)S(1)}, u32[]{:S(2)}, u32[]{:S(2)}) %all-to-all-start) | async-done | bytes 131104 | tf_op jit(solution)/shard_map/all_to_all | solution.py:260
  36.2 0.0 collective-permute-done.3.far_near_ref
  36.2 0.0 collective-permute-done.4.far_next_ref
  36.2 0.0 collective-permute-done.far_ref
  36.3 1.5 %copy-done.5 = bf16[320,2880]{1,0:T(8,128)(2,1)S(1)} copy-done((bf16[320,2880]{1,0:T(8,128)(2,1)S(1)}, bf16[320,2880]{1,0:T(8,128)(2,1)}, u32[]{:S(2)}) %copy-start.5) | copy-done | bytes 1843224
  37.8 8.8 %first.1 = (f32[6,320,256]{2,1,0:T(8,128)}, f32[8,8,128]{2,1,0:T(8,128)}) custom-call(bf16[4,320,256]{2,1,0:T(8,128)(2,1)S(1)} %bitcast.18, bf16[4,320,256]{2,1,0:T(8,128)(2,1)S(1)} %collective-permute-done.far_ref, bf16[2,320,256]{2,1,0:T(8,128)(2,1)} %collective-permute-done.1.near_ref, bf16[2,320,256]{2,1,0:T(8,128)(2,1)} %collective-permute-done.2.next_ref, ...), custom_call_target="tpu_custom_call" | custom-call | tf_op jit(solution)/shard_map/first/pallas_call | solution.py:312
  46.5 4.8 %all-to-all-start.1 = ((f32[8,8,128]{2,1,0:T(8,128)}), f32[8,8,128]{2,1,0:T(8,128)S(1)}, u32[]{:S(2)}, u32[]{:S(2)}) async-start(f32[8,8,128]{2,1,0:T(8,128)} %get-tuple-element.11), calls=%async_computation.1 | async-start | bytes 65536 | tf_op jit(solution)/shard_map/all_to_all | solution.py:260
  51.4 6.6 %all-to-all-done.1.seen_ref = f32[8,8,128]{2,1,0:T(8,128)S(1)} async-done(((f32[8,8,128]{2,1,0:T(8,128)}), f32[8,8,128]{2,1,0:T(8,128)S(1)}, u32[]{:S(2)}, u32[]{:S(2)}) %all-to-all-start.1) | async-done | bytes 32800 | tf_op jit(solution)/shard_map/all_to_all | solution.py:260
  58.0 1.5 %copy-done.3 = f32[6,320,256]{2,1,0:T(8,128)S(1)} copy-done((f32[6,320,256]{2,1,0:T(8,128)S(1)}, f32[6,320,256]{2,1,0:T(8,128)}, u32[]{:S(2)}) %copy-start.3) | copy-done | bytes 1966104
  59.6 4.7 %second.1 = bf16[4,320,256]{2,1,0:T(8,128)(2,1)} custom-call(f32[6,320,256]{2,1,0:T(8,128)S(1)} %copy-done.3, bf16[4,320,256]{2,1,0:T(8,128)(2,1)S(1)} %bitcast.19, f32[8,8,128]{2,1,0:T(8,128)S(1)} %all-to-all-done.1.seen_ref, f32[1,320]{1,0:T(1,128)S(1)} %reshape.41.gain_ref, f32[1,320]{1,0:T(1,128)S(1)} %reshape.42.shift_ref, ...), custom_call_target="tpu_custom_call" | custom-call | tf_op jit(solution)/shard_map/second/pallas_call | solution.py:334
  (32 shorter events, 0.1 us)
Async XLA Ops:
  0.0 28.6 %copy-start.8 = (f32[320]{0:T(512)S(1)}, f32[320]{0:T(512)}, u32[]{:S(2)}) copy-start(f32[320]{0:T(512)} %param.16) | copy-start | bytes 3844
  0.0 28.6 %copy-start.9 = (f32[320]{0:T(512)S(1)}, f32[320]{0:T(512)}, u32[]{:S(2)}) copy-start(f32[320]{0:T(512)} %param.17) | copy-start | bytes 3844
  0.0 28.6 %copy-start.10 = (f32[320]{0:T(512)S(1)}, f32[320]{0:T(512)}, u32[]{:S(2)}) copy-start(f32[320]{0:T(512)} %param.19) | copy-start | bytes 3844
  0.0 28.6 %copy-start.11 = (f32[320]{0:T(512)S(1)}, f32[320]{0:T(512)}, u32[]{:S(2)}) copy-start(f32[320]{0:T(512)} %param.21) | copy-start | bytes 3844
  1.2 17.0 %collective-permute-start.1 = (bf16[2,320,256]{2,1,0:T(8,128)(2,1)S(1)}, bf16[2,320,256]{2,1,0:T(8,128)(2,1)}, u32[]{:S(2)}, u32[]{:S(2)}) collective-permute-start(bf16[2,320,256]{2,1,0:T(8,128)(2,1)S(1)} %get-tuple-element.14), channel_id=1, source_target_pairs={{0,2},{2,0},{4,6},{6,4},{8,10},{10,8},{12,14},{14,12},{1,3},{3,1},... | collective-permute-start | bytes 983048 | tf_op jit(solution)/shard_map/ppermute | solution.py:281
  4.2 14.0 %collective-permute-start.2 = (bf16[2,320,256]{2,1,0:T(8,128)(2,1)S(1)}, bf16[2,320,256]{2,1,0:T(8,128)(2,1)}, u32[]{:S(2)}, u32[]{:S(2)}) collective-permute-start(bf16[2,320,256]{2,1,0:T(8,128)(2,1)S(1)} %get-tuple-element.13), channel_id=1, source_target_pairs={{2,4},{6,8},{10,12},{4,2},{8,6},{12,10},{3,5},{7,9},{11,13},{5,3},... | collective-permute-start | bytes 983048 | tf_op jit(solution)/shard_map/ppermute | solution.py:283
  5.6 30.7 %collective-permute-start = (bf16[4,320,256]{2,1,0:T(8,128)(2,1)}, bf16[4,320,256]{2,1,0:T(8,128)(2,1)S(1)}, u32[]{:S(2)}, u32[]{:S(2)}) collective-permute-start(bf16[4,320,256]{2,1,0:T(8,128)(2,1)} %bitcast.16), channel_id=1, source_target_pairs={{0,16},{16,0},{1,17},{17,1},{2,18},{18,2},{3,19},{19,3},{4,20},{20... | collective-permute-start | bytes 1966088 | tf_op jit(solution)/shard_map/ppermute | solution.py:285
  18.2 18.1 %collective-permute-start.3 = (bf16[2,320,256]{2,1,0:T(8,128)(2,1)}, bf16[2,320,256]{2,1,0:T(8,128)(2,1)}, u32[]{:S(2)}, u32[]{:S(2)}) collective-permute-start(bf16[2,320,256]{2,1,0:T(8,128)(2,1)} %collective-permute-done.1.near_ref), channel_id=1, source_target_pairs={{0,16},{16,0},{1,17},{17,1},{2,18},{18,2},{3,19},{19,3},{4,20},{20... | collective-permute-start | bytes 983048 | tf_op jit(solution)/shard_map/ppermute | solution.py:286
  18.2 18.1 %collective-permute-start.4 = (bf16[2,320,256]{2,1,0:T(8,128)(2,1)}, bf16[2,320,256]{2,1,0:T(8,128)(2,1)}, u32[]{:S(2)}, u32[]{:S(2)}) collective-permute-start(bf16[2,320,256]{2,1,0:T(8,128)(2,1)} %collective-permute-done.2.next_ref), channel_id=1, source_target_pairs={{0,16},{16,0},{1,17},{17,1},{2,18},{18,2},{3,19},{19,3},{4,20},{20... | collective-permute-start | bytes 983048 | tf_op jit(solution)/shard_map/ppermute | solution.py:287
  18.7 1.1 %copy-start = (bf16[1,1,4,256,320]{3,4,2,1,0:T(8,128)(2,1)S(1)}, bf16[1,1,4,256,320]{3,4,2,1,0:T(8,128)(2,1)}, u32[]{:S(2)}) copy-start(bf16[1,1,4,256,320]{3,4,2,1,0:T(8,128)(2,1)} %param.13) | copy-start | bytes 1966084
  19.8 0.9 %copy-start.6 = (bf16[160,320]{1,0:T(8,128)(2,1)S(1)}, bf16[160,320]{1,0:T(8,128)(2,1)}, u32[]{:S(2)}) copy-start(bf16[160,320]{1,0:T(8,128)(2,1)} %weight_ref.1) | copy-start | bytes 307204
  20.7 0.7 %copy-start.7 = (bf16[1,1280]{1,0:T(2,128)(2,1)S(1)}, bf16[1,1280]{1,0:T(2,128)(2,1)}, u32[]{:S(2)}) copy-start(bf16[1,1280]{1,0:T(2,128)(2,1)} %embed_ref.1) | copy-start | bytes 7684
  22.5 13.8 %all-to-all-start = ((f32[16,16,128]{2,1,0:T(8,128)}), f32[16,16,128]{2,1,0:T(8,128)S(1)}, u32[]{:S(2)}, u32[]{:S(2)}) async-start(f32[16,16,128]{2,1,0:T(8,128)} %stats.1), calls=%async_computation | async-start | bytes 262144 | tf_op jit(solution)/shard_map/all_to_all | solution.py:260
  29.3 1.6 %copy-start.2 = (bf16[3,3,320,320]{3,2,1,0:T(8,128)(2,1)S(1)}, bf16[3,3,320,320]{3,2,1,0:T(8,128)(2,1)}, u32[]{:S(2)}) copy-start(bf16[3,3,320,320]{3,2,1,0:T(8,128)(2,1)} %param.18) | copy-start | bytes 5529604
  30.9 5.3 %copy-start.1 = (bf16[1,1,4,256,320]{3,4,2,1,0:T(8,128)(2,1)S(1)}, bf16[1,1,4,256,320]{3,4,2,1,0:T(8,128)(2,1)}, u32[]{:S(2)}) copy-start(bf16[1,1,4,256,320]{3,4,2,1,0:T(8,128)(2,1)} %param.13) | copy-start | bytes 1966084
  33.8 1.3 %copy-start.4 = (bf16[320,2880]{1,0:T(8,128)(2,1)}, bf16[320,2880]{1,0:T(8,128)(2,1)S(1)}, u32[]{:S(2)}) copy-start(bf16[320,2880]{1,0:T(8,128)(2,1)S(1)} %get-tuple-element.9.weight_hbm) | copy-start | bytes 5529604
  36.3 1.5 %copy-start.5 = (bf16[320,2880]{1,0:T(8,128)(2,1)S(1)}, bf16[320,2880]{1,0:T(8,128)(2,1)}, u32[]{:S(2)}) copy-start(bf16[320,2880]{1,0:T(8,128)(2,1)} %copy-done.4) | copy-start | bytes 5529604
  37.8 13.5 %copy-start.12 = (f32[320]{0:T(512)S(1)}, f32[320]{0:T(512)}, u32[]{:S(2)}) copy-start(f32[320]{0:T(512)} %param.22) | copy-start | bytes 3844
  37.8 13.6 %copy-start.13 = (f32[320]{0:T(512)S(1)}, f32[320]{0:T(512)}, u32[]{:S(2)}) copy-start(f32[320]{0:T(512)} %param.23) | copy-start | bytes 3844
  37.8 13.6 %copy-start.14 = (f32[320]{0:T(512)S(1)}, f32[320]{0:T(512)}, u32[]{:S(2)}) copy-start(f32[320]{0:T(512)} %param.25) | copy-start | bytes 3844
  46.5 11.5 %all-to-all-start.1 = ((f32[8,8,128]{2,1,0:T(8,128)}), f32[8,8,128]{2,1,0:T(8,128)S(1)}, u32[]{:S(2)}, u32[]{:S(2)}) async-start(f32[8,8,128]{2,1,0:T(8,128)} %get-tuple-element.11), calls=%async_computation.1 | async-start | bytes 65536 | tf_op jit(solution)/shard_map/all_to_all | solution.py:260
  58.0 1.5 %copy-start.3 = (f32[6,320,256]{2,1,0:T(8,128)S(1)}, f32[6,320,256]{2,1,0:T(8,128)}, u32[]{:S(2)}) copy-start(f32[6,320,256]{2,1,0:T(8,128)} %get-tuple-element.10.steered_ref) | copy-start | bytes 5898244

commit v4 on v3

--- a/solution.py
+++ b/solution.py
@@ -105,10 +105,27 @@
     )
 
 
-def stats_kernel(lat_ref, embed_ref, weight_ref, out_ref):
+def stats_kernel(lat_hbm, embed_hbm, weight_hbm, lat_ref, out_ref, embed_ref, weight_ref, sems):
     rows, chans, _ = lat_ref.shape
+    copies = [
+        pltpu.make_async_copy(lat_hbm.at[k], lat_ref.at[k], sems.at[k]) for k in range(rows)
+    ]
+    copies.append(pltpu.make_async_copy(embed_hbm, embed_ref, sems.at[rows]))
+    copies.append(pltpu.make_async_copy(weight_hbm, weight_ref, sems.at[rows + 1]))
+    for copy in copies:
+        copy.start()
+    waits = list(copies[:rows])
+
+    def values():
+        for k in range(rows):
+            if waits:
+                waits.pop(0).wait()
+            yield lat_ref[k].astype(F32)
+
     wide = padded_lanes(chans)
-    mean, squares = channel_moments(lambda: (lat_ref[k].astype(F32) for k in range(rows)), chans)
+    mean, squares = channel_moments(values, chans)
+    copies[rows].wait()
+    copies[rows + 1].wait()
     own = weight_ref.shape[0]
     length = embed_ref.shape[1]
     embed = jnp.broadcast_to(embed_ref[...].astype(F32), (8, length))
@@ -118,13 +135,29 @@
     put_rows([mean, squares, widen(time_part, wide)], out_ref)
 
 
-def turn_kernel(one_ref, two_ref, one_out, two_out):
-    for source, target in ((one_ref, one_out), (two_ref, two_out)):
-        deep = source.shape[0]
-        step = 320 if deep % 320 == 0 else deep
-        step = 2 * step if deep % (2 * step) == 0 else step
-        for at in range(0, deep, 640):
-            target[:, at : min(at + 640, deep)] = source[at : min(at + 640, deep), :].T
+PARTS = 3
+
+
+def prepare_kernel(
+    one_hbm, two_hbm, gain_one, shift_one, bias_one, time_bias, gain_two, shift_two, bias_two, steer,
+    one_out, two_out, rows_ref, one_ref, two_ref, sems,
+):
+    deep = one_ref.shape[0]
+    part = deep // PARTS
+    jobs = []
+    for k, (source, held, target) in enumerate(((one_hbm, one_ref, one_out), (two_hbm, two_ref, two_out))):
+        for at in range(PARTS):
+            here = pl.ds(at * part, part)
+            copy = pltpu.make_async_copy(source.at[here], held.at[here], sems.at[k * PARTS + at])
+            copy.start()
+            jobs.append((copy, held, target, at * part))
+    wide = rows_ref.shape[1]
+    vectors = (gain_one, shift_one, bias_one, time_bias, gain_two, shift_two, bias_two)
+    lines = [widen(v[...], wide) for v in vectors]
+    rows_ref[...] = jnp.concatenate(lines + [jnp.broadcast_to(steer[...], (1, wide))], axis=0)
+    for copy, held, target, at in jobs:
+        copy.wait()
+        target[:, at : at + part] = held[at : at + part, :].T
 
 
 def spread_columns(rows, chans, cols_ref):
@@ -160,75 +193,122 @@
     return None
 
 
-def first_kernel(
-    own_ref, far_ref, near_ref, next_ref, far_near_ref, far_next_ref, seen_ref, steer_ref,
-    gain_ref, shift_ref, bias_ref, time_bias_ref, weight_hbm,
-    steered_ref, out_ref,
-    weight_ref, taps_ref, cols_ref, edge_ref, sem,
+def mixer(cols_ref, rows_ref, chans):
+    sign = jnp.where(lax.axis_index("cfg") == 0, 1.0, -1.0).astype(F32)
+    steer = rows_ref[7:8, 0:1] * sign
+
+    def mix(mine, other):
+        shift = twice(cols_ref[4])
+        mine = half_act(mine.astype(F32), twice(cols_ref[0]), twice(cols_ref[1]), shift)
+        other = half_act(other.astype(F32), twice(cols_ref[2]), twice(cols_ref[3]), shift)
+        return mine + steer * (mine - other)
+
+    return mix
+
+
+def matmul(weight_ref, taps, first_tap):
+    depth = taps.shape[0]
+    start = first_tap * (weight_ref.shape[1] // 3)
+    return jnp.dot(weight_ref[:, start : start + depth], taps, preferred_element_type=F32)
+
+
+def inner_kernel(
+    own_ref, far_ref, seen_ref, rows_ref, weight_ref,
+    steered_ref, taps_ref, cols_ref,
 ):
-    copy = pltpu.make_async_copy(weight_hbm, weight_ref, sem)
-    copy.start()
     rows, chans, cols = own_ref.shape
-    reach = near_ref.shape[0]
     wide = padded_lanes(chans)
     size = chans // GROUPS
-    cfg, patches = lax.axis_index("cfg"), lax.axis_size("patch")
-    even = lax.rem(lax.axis_index("patch"), 2) == 0
+    cfg, peers = lax.axis_index("cfg"), lax.axis_size("patch")
     mask = same_group(wide, size)
-    peers = patches
     starts = (cfg * peers, (1 - cfg) * peers)
     means = [get_rows(seen_ref, s, peers, 0, wide) for s in starts]
     squares = [get_rows(seen_ref, s, peers, 1, wide) for s in starts]
     mean_rows, var_rows = group_stats(means, squares, float(rows * cols), mask, size)
-    scale_rows = lax.rsqrt(var_rows + EPS) * (0.5 * widen(gain_ref[...], wide))
+    scale_rows = lax.rsqrt(var_rows + EPS) * (0.5 * rows_ref[0:1])
     times = jnp.sum(get_rows(seen_ref, 0, peers, 2, wide), axis=0, keepdims=True)
-    added = times + widen(time_bias_ref[...] + bias_ref[...], wide)
+    added = times + (rows_ref[3:4] + rows_ref[2:3])
     spread_columns(
-        [mean_rows[0:1], scale_rows[0:1], mean_rows[1:2], scale_rows[1:2],
-         0.5 * widen(shift_ref[...], wide), added],
+        [mean_rows[0:1], scale_rows[0:1], mean_rows[1:2], scale_rows[1:2], 0.5 * rows_ref[1:2], added],
         chans, cols_ref,
     )
-    above = jnp.where(even, reach, 0)
+    mix = mixer(cols_ref, rows_ref, chans)
+    line = 3 * chans
+    if rows < 3:
+        steered_ref[...] = jnp.zeros_like(steered_ref)
+    for at in range(rows):
+        put_taps(taps_ref, at, mix(own_ref[at], far_ref[at]))
+        if at >= 2:
+            total = matmul(weight_ref, taps_ref[(at - 2) * line : (at + 1) * line, :], 0)
+            steered_ref[at - 2] = total + twice(cols_ref[5])
+
+
+def outer_kernel(
+    near_ref, next_ref, far_near_ref, far_next_ref, inner_ref, inner_taps_ref, cols_ref, rows_ref, weight_ref,
+    steered_ref, out_ref,
+    taps_ref, edge_ref,
+):
+    reach, chans, cols = near_ref.shape
+    line = 3 * chans
+    rows = inner_taps_ref.shape[0] // line
+    above = jnp.where(lax.rem(lax.axis_index("patch"), 2) == 0, reach, 0)
+    edge_ref[0, pl.ds(above, reach)] = next_ref[...]
+    edge_ref[1, pl.ds(above, reach)] = far_next_ref[...]
     edge_ref[0, pl.ds(reach - above, reach)] = near_ref[...]
-    edge_ref[0, pl.ds(above, reach)] = next_ref[...]
     edge_ref[1, pl.ds(reach - above, reach)] = far_near_ref[...]
-    edge_ref[1, pl.ds(above, reach)] = far_next_ref[...]
-    sign = jnp.where(cfg == 0, 1.0, -1.0).astype(F32) * steer_ref[0]
-
-    def inputs(at):
-        if at < reach:
-            return edge_ref[0, reach + at], edge_ref[1, reach + at]
-        if at >= reach + rows:
-            return edge_ref[0, at - reach - rows], edge_ref[1, at - reach - rows]
-        return own_ref[at - reach], far_ref[at - reach]
-
-    for at in range(rows + 2 * reach):
-        mine, other = inputs(at)
-        shift = twice(cols_ref[4])
-        mine = half_act(mine.astype(F32), twice(cols_ref[0]), twice(cols_ref[1]), shift)
-        other = half_act(other.astype(F32), twice(cols_ref[2]), twice(cols_ref[3]), shift)
-        mixed = mine + sign * (mine - other)
+    mix = mixer(cols_ref, rows_ref, chans)
+
+    def taps(at):
+        if reach <= at < reach + rows:
+            return inner_taps_ref, at - reach
+        return taps_ref, at if at < reach else at - rows
+
+    def rows_of(first, count):
+        ref, at = taps(first)
+        return ref[at * line : (at + count) * line, :]
+
+    def conv(at):
+        total, tap = None, 0
+        while tap < 3:
+            ref, _ = taps(at + tap)
+            count = 1
+            while tap + count < 3 and taps(at + tap + count)[0] is ref:
+                count += 1
+            part = matmul(weight_ref, rows_of(at + tap, count), tap)
+            total = part if total is None else total + part
+            tap += count
+        return total
+
+    def enter(at):
+        k = reach + at if at < reach else at - reach - rows
         keep = edge_keep(at, rows, reach)
-        put_taps(taps_ref, at, mixed if keep is None else mixed * keep)
-    copy.wait()
-    deep = 9 * chans
-    for at in range(rows + 2 * reach - 2):
-        total = jnp.dot(
-            weight_ref[...], taps_ref[pl.ds(at * 3 * chans, deep), :], preferred_element_type=F32
-        )
-        steered_ref[at] = total + twice(cols_ref[5])
-    skip = reach - 1
-    mean, square = channel_moments(lambda: (steered_ref[skip + k] for k in range(rows)), chans)
+        put_taps(taps_ref, taps(at)[1], mix(edge_ref[0, k], edge_ref[1, k]) * keep)
+
+    for at in range(reach):
+        enter(at)
+    outside = [at for at in range(rows + 2 * reach - 2) if not reach <= at < reach + rows - 2]
+    place = {at: k for k, at in enumerate(outside)}
+    ready = reach + rows
+    for at in outside:
+        while ready < at + 3:
+            enter(ready)
+            ready += 1
+        steered_ref[place[at]] = conv(at) + twice(cols_ref[5])
+
+    def own_rows():
+        for k in range(rows):
+            at = reach - 1 + k
+            yield steered_ref[place[at]] if at in place else inner_ref[at - reach]
+
+    mean, square = channel_moments(own_rows, chans)
     put_rows([mean, square], out_ref)
 
 
 def second_kernel(
-    steered_ref, lat_ref, seen_ref, gain_ref, shift_ref, bias_ref, weight_hbm,
+    inner_ref, outer_ref, lat_ref, seen_ref, rows_ref, weight_ref,
     out_ref,
-    weight_ref, taps_ref, cols_ref, sem,
+    taps_ref, cols_ref,
 ):
-    copy = pltpu.make_async_copy(weight_hbm, weight_ref, sem)
-    copy.start()
     rows, chans, cols = lat_ref.shape
     wide = padded_lanes(chans)
     size = chans // GROUPS
@@ -238,22 +318,24 @@
         [get_rows(seen_ref, 0, peers, 0, wide)], [get_rows(seen_ref, 0, peers, 1, wide)],
         float(rows * cols), mask, size,
     )
-    scale_rows = lax.rsqrt(var_rows + EPS) * (0.5 * widen(gain_ref[...], wide))
+    scale_rows = lax.rsqrt(var_rows + EPS) * (0.5 * rows_ref[4:5])
     spread_columns(
-        [mean_rows[0:1], scale_rows[0:1], 0.5 * widen(shift_ref[...], wide), widen(bias_ref[...], wide)],
-        chans, cols_ref,
-    )
+        [mean_rows[0:1], scale_rows[0:1], 0.5 * rows_ref[5:6], rows_ref[6:7]], chans, cols_ref
+    )
+    line = 3 * chans
+    inside = max(rows - 2, 0)
+    half = outer_ref.shape[0] // 2
     for at in range(rows + 2):
-        value = half_act(steered_ref[at], twice(cols_ref[0]), twice(cols_ref[1]), twice(cols_ref[2]))
+        if half <= at < half + inside:
+            value = inner_ref[at - half]
+        else:
+            value = outer_ref[at if at < half else at - inside]
+        value = half_act(value, twice(cols_ref[0]), twice(cols_ref[1]), twice(cols_ref[2]))
         keep = edge_keep(at, rows, 1)
         put_taps(taps_ref, at, value if keep is None else value * keep)
-    copy.wait()
-    deep = 9 * chans
-    for at in range(rows):
-        total = jnp.dot(
-            weight_ref[...], taps_ref[pl.ds(at * 3 * chans, deep), :], preferred_element_type=F32
-        )
-        out_ref[at] = (lat_ref[at].astype(F32) + (total + twice(cols_ref[3]))).astype(BF16)
+        if at >= 2:
+            total = matmul(weight_ref, taps_ref[(at - 2) * line : (at + 1) * line, :], 0)
+            out_ref[at - 2] = (lat_ref[at - 2].astype(F32) + (total + twice(cols_ref[3]))).astype(BF16)
 
 
 def everyone(tiles, axes):
@@ -261,9 +343,12 @@
 
 
 VMEM = pl.BlockSpec(memory_space=pltpu.VMEM)
-SMEM = pl.BlockSpec(memory_space=pltpu.SMEM)
 ANY = pl.BlockSpec(memory_space=pl.ANY)
-LIMIT = pltpu.CompilerParams(vmem_limit_bytes=48 * 1024 * 1024)
+LIMIT = pltpu.CompilerParams(vmem_limit_bytes=12 * 1024 * 1024)
+
+
+def in_hbm(value):
+    return pltpu.with_memory_space_constraint(value, pltpu.HBM)
 
 
 def body(
@@ -283,68 +368,86 @@
     following = lax.ppermute(next_edge, "patch", steps + [(j, i) for i, j in steps])
     swap = [(0, 1), (1, 0)]
     far = lax.ppermute(own, "cfg", swap)
+    line = lambda vector: vector.reshape(1, -1)
+
+    tile_one = -(-3 * wide // LANES // 8) * 8
+    held, sent = pl.pallas_call(
+        stats_kernel,
+        out_shape=[
+            pltpu.VMEM((rows, chans, cols), BF16),
+            pltpu.VMEM((2 * patches, tile_one, LANES), F32),
+        ],
+        in_specs=[ANY] * 3,
+        out_specs=[VMEM] * 2,
+        scratch_shapes=[
+            pltpu.VMEM(time_embed.shape, BF16),
+            pltpu.VMEM(time_weight.shape, BF16),
+            pltpu.SemaphoreType.DMA((rows + 2,)),
+        ],
+        compiler_params=LIMIT,
+        name="stats",
+    )(in_hbm(own), in_hbm(time_embed), in_hbm(time_weight))
+    seen = everyone(sent, ("cfg", "patch"))
+
+    weights = (conv_one.reshape(deep, chans), conv_two.reshape(deep, chans))
+    *weights, _ = lax.optimization_barrier((*weights, sent))
+    turned_one, turned_two, vectors = pl.pallas_call(
+        prepare_kernel,
+        out_shape=[pltpu.VMEM((chans, deep), BF16)] * 2 + [pltpu.VMEM((8, wide), F32)],
+        in_specs=[ANY] * 2 + [VMEM] * 8,
+        out_specs=[VMEM] * 3,
+        scratch_shapes=[pltpu.VMEM((deep, chans), BF16)] * 2 + [pltpu.SemaphoreType.DMA((2 * PARTS,))],
+        compiler_params=LIMIT,
+        name="prepare",
+    )(
+        in_hbm(weights[0]), in_hbm(weights[1]), line(gain_one), line(shift_one), line(bias_one),
+        line(time_bias), line(gain_two), line(shift_two), line(bias_two), line(steer_scale),
+    )
+    near, following, vectors, seen = lax.optimization_barrier((near, following, vectors, seen))
     far_near = lax.ppermute(near, "cfg", swap)
     far_next = lax.ppermute(following, "cfg", swap)
-    line = lambda vector: vector.reshape(1, chans)
-
-    tile_one = -(-3 * wide // LANES // 8) * 8
-    sent = pl.pallas_call(
-        stats_kernel,
-        out_shape=jax.ShapeDtypeStruct((2 * patches, tile_one, LANES), F32),
-        in_specs=[VMEM] * 3,
-        out_specs=VMEM,
+
+    inner, taps, columns = pl.pallas_call(
+        inner_kernel,
+        out_shape=[
+            pltpu.VMEM((max(rows - 2, 1), chans, cols), F32),
+            pltpu.VMEM((rows * 3 * chans, cols), BF16),
+            pltpu.VMEM((6, chans, LANES), F32),
+        ],
+        in_specs=[VMEM] * 5,
+        out_specs=[VMEM] * 3,
         compiler_params=LIMIT,
-        name="stats",
-    )(own, time_embed, time_weight)
-    seen = everyone(sent, ("cfg", "patch"))
-
-    turned_one, turned_two = pl.pallas_call(
-        turn_kernel,
-        out_shape=[jax.ShapeDtypeStruct((chans, deep), BF16)] * 2,
-        in_specs=[VMEM] * 2,
-        out_specs=[VMEM] * 2,
-        compiler_params=LIMIT,
-        name="turn",
-    )(conv_one.reshape(deep, chans), conv_two.reshape(deep, chans))
-
+        name="inner",
+    )(held, far, seen, vectors, turned_one)
     tile_two = -(-2 * wide // LANES // 8) * 8
-    inside = rows + 2 * REACH - 2
-    steered, sent = pl.pallas_call(
-        first_kernel,
+    outer, sent = pl.pallas_call(
+        outer_kernel,
         out_shape=[
-            jax.ShapeDtypeStruct((inside, chans, cols), F32),
-            jax.ShapeDtypeStruct((patches, tile_two, LANES), F32),
-        ],
-        in_specs=[VMEM] * 7 + [SMEM] + [VMEM] * 4 + [ANY],
+            pltpu.VMEM((2 * REACH, chans, cols), F32),
+            pltpu.VMEM((patches, tile_two, LANES), F32),
+        ],
+        in_specs=[VMEM] * 9,
         out_specs=[VMEM] * 2,
         scratch_shapes=[
-            pltpu.VMEM((chans, deep), BF16),
-            pltpu.VMEM(((rows + 2 * REACH) * 3 * chans, cols), BF16),
-            pltpu.VMEM((6, chans, LANES), F32),
+            pltpu.VMEM((2 * REACH * 3 * chans, cols), BF16),
             pltpu.VMEM((2, 2 * REACH, chans, cols), BF16),
-            pltpu.SemaphoreType.DMA,
         ],
         compiler_params=LIMIT,
-        name="first",
-    )(
-        own, far, near, following, far_near, far_next, seen, steer_scale,
-        line(gain_one), line(shift_one), line(bias_one), line(time_bias), turned_one,
-    )
+        name="outer",
+    )(near, following, far_near, far_next, inner, taps, columns, vectors, turned_one)
     seen = everyone(sent, "patch")
     image = pl.pallas_call(
         second_kernel,
         out_shape=jax.ShapeDtypeStruct((rows, chans, cols), BF16),
-        in_specs=[VMEM] * 6 + [ANY],
+        in_specs=[VMEM] * 6,
         out_specs=VMEM,
         scratch_shapes=[
-            pltpu.VMEM((chans, deep), BF16),
             pltpu.VMEM(((rows + 2) * 3 * chans, cols), BF16),
             pltpu.VMEM((4, chans, LANES), F32),
-            pltpu.SemaphoreType.DMA,
         ],
         compiler_params=LIMIT,
         name="second",
-    )(steered, own, seen, line(gain_two), line(shift_two), line(bias_two), turned_two)
+    )(inner, outer, held, seen, vectors, turned_two)
     return jnp.swapaxes(image, 1, 2)[None, None]
 
 

time: 64.8 us -> 47.5 us (0.73)
  waiting for transfers between devices: 20.4 us -> 2.49 us
  blocking collectives: 0 us -> 12.1 us
  local copies, waits for them, and re-layouts: 9.83 us -> 3.33 us
  starting transfers between devices: 15.8 us -> 11.9 us
  Pallas kernels: 17.4 us -> 16.5 us
    ppermute x1, waiting for transfers between devices: 12.6 us -> 0.01 us  [body(): lax.ppermute(near_edge, 'patch', [(i, i ^ 1) for i in range(patches)])]
    all_to_all x0 -> x1, blocking collectives: none -> 12.1 us  [everyone(): return lax.all_to_all(tiles, axes, 0, 0)]
    unnamed x30 -> x18, local copies, waits for them, and re-layouts: 8.64 us -> 1.31 us
    all_to_all x2 -> x1, starting transfers between devices: 10.9 us -> 4.91 us  [everyone(): return lax.all_to_all(tiles, axes, 0, 0)]
    all_to_all x2 -> x1, waiting for transfers between devices: 7.76 us -> 2.48 us  [everyone(): return lax.all_to_all(tiles, axes, 0, 0)]
    ppermute x1, starting transfers between devices: 3 us -> 5.05 us  [body(): lax.ppermute(near_edge, 'patch', [(i, i ^ 1) for i in range(patches)])]
    dynamic_slice x1, local copies, waits for them, and re-layouts: 1.17 us -> 2 us  [body(): lax.dynamic_slice_in_dim(own, jnp.where(even, 0, rows - REACH), REACH, 0)]
    pallas_call x3 -> x4, Pallas kernels: 12.8 us -> 12.3 us  [the longest x1 4.1 us: body(): pl.pallas_call(outer_kernel, out_shape=[pltpu.VMEM((2 * REACH, chans, col...]
  transfers between devices with their start and end apart: 7 -> 6, of which waited for: 3 -> 1; matrix products, arithmetic and copies ran while one was open for 0% -> 0% of each run, Pallas kernels for 6% -> 17%
where the time goes in v4:
time: 47.5 us; the launch traced here: 47.2 us
  Pallas kernels  16.5 us (35%)
  blocking collectives  12.1 us (25%)
  starting transfers between devices  11.9 us (25%)
  local copies, waits for them, and re-layouts  3.33 us (7%)
  waiting for transfers between devices  2.49 us (5%)
  between operations  0.87 us (2%)
    all_to_all x1, blocking collectives, everyone(): return lax.all_to_all(tiles, axes, 0, 0)  12.1 us
    ppermute x1, starting transfers between devices, body(): lax.ppermute(near_edge, 'patch', [(i, i ^ 1) for i in range(patches)])  5.05 us
    all_to_all x1, starting transfers between devices, everyone(): return lax.all_to_all(tiles, axes, 0, 0)  4.91 us
    pallas_call x1, Pallas kernels, body(): pl.pallas_call(second_kernel, out_shape=jax.ShapeDtypeStruct((rows, chans...  4.17 us
    pallas_call x1, Pallas kernels, body(): pl.pallas_call(outer_kernel, out_shape=[pltpu.VMEM((2 * REACH, chans, col...  4.1 us
    pallas_call x1, Pallas kernels, body(): pl.pallas_call(prepare_kernel, out_shape=[pltpu.VMEM((chans, deep), BF16)...  3.1 us
    pallas_call x1, Pallas kernels, body(): pl.pallas_call(inner_kernel, out_shape=[pltpu.VMEM((max(rows - 2, 1), cha...  2.66 us
    all_to_all x1, waiting for transfers between devices, everyone(): return lax.all_to_all(tiles, axes, 0, 0)  2.48 us
  transfers between devices with their start and end apart: 6, of which 1 were waited for; matrix products, arithmetic and copies ran while one was open for 0% of the time, Pallas kernels for 17%

profile of v4, /device:TPU:0, one launch (start us, length us, event | category | flops | bytes accessed | tf_op | source)
XLA Modules:
  0.0 47.2 jit_solution(17509756627943021463)
XLA Ops:
  0.0 0.0 copy-start.7
  0.0 0.0 copy-start.8
  0.0 2.0 %dynamic-slice_bitcast_fusion = (bf16[2,320,256]{2,1,0:T(8,128)(2,1)}, bf16[2,320,256]{2,1,0:T(8,128)(2,1)}) fusion(bf16[1,1,4,256,320]{3,4,2,1,0:T(8,128)(2,1)} %param.13, s32[]{:T(128)S(6)} %select_n.10, s32[]{:T(128)S(6)} %select_n.9), kind=kLoop, calls=%fused_computation | loop fusion | bytes 1310728 | tf_op jit(solution)/shard_map/dynamic_slice | solution.py:365
  2.0 1.4 %collective-permute-start.2 = (bf16[2,320,256]{2,1,0:T(8,128)(2,1)}, bf16[2,320,256]{2,1,0:T(8,128)(2,1)}, u32[]{:S(2)}, u32[]{:S(2)}) collective-permute-start(bf16[2,320,256]{2,1,0:T(8,128)(2,1)} %get-tuple-element.37), channel_id=1, source_target_pairs={{2,4},{6,8},{10,12},{4,2},{8,6},{12,10},{3,5},{7,9},{11,13},{5,3},... | collective-permute-start | bytes 983048 | tf_op jit(solution)/shard_map/ppermute | solution.py:368
  3.5 5.0 %collective-permute-start.1 = (bf16[2,320,256]{2,1,0:T(8,128)(2,1)}, bf16[2,320,256]{2,1,0:T(8,128)(2,1)}, u32[]{:S(2)}, u32[]{:S(2)}) collective-permute-start(bf16[2,320,256]{2,1,0:T(8,128)(2,1)} %get-tuple-element.38), channel_id=1, source_target_pairs={{0,2},{2,0},{4,6},{6,4},{8,10},{10,8},{12,14},{14,12},{1,3},{3,1},... | collective-permute-start | bytes 983048 | tf_op jit(solution)/shard_map/ppermute | solution.py:366
  8.5 0.0 collective-permute-start
  8.5 2.5 %stats.1 = (bf16[4,320,256]{2,1,0:T(8,128)(2,1)S(1)}, f32[16,16,128]{2,1,0:T(8,128)}) custom-call(bf16[4,320,256]{2,1,0:T(8,128)(2,1)} %bitcast.19, bf16[1,1280]{1,0:T(2,128)(2,1)} %embed_hbm.1, bf16[160,320]{1,0:T(8,128)(2,1)} %weight_hbm.1), custom_call_target="tpu_custom_call" | custom-call | tf_op jit(solution)/shard_map/stats/pallas_call | solution.py:374
  11.0 4.9 %all-to-all-start = ((f32[16,16,128]{2,1,0:T(8,128)}), f32[16,16,128]{2,1,0:T(8,128)S(1)}, u32[]{:S(2)}, u32[]{:S(2)}) async-start(f32[16,16,128]{2,1,0:T(8,128)} %get-tuple-element.22), calls=%async_computation | async-start | bytes 262144 | tf_op jit(solution)/shard_map/all_to_all | solution.py:342
  16.6 0.0 copy-done.3
  16.7 0.0 copy-done.8
  16.7 3.1 %prepare.1 = (bf16[320,2880]{1,0:T(8,128)(2,1)S(1)}, bf16[320,2880]{1,0:T(8,128)(2,1)S(1)}, f32[8,384]{1,0:T(8,128)S(1)}) custom-call(bf16[2880,320]{1,0:T(8,128)(2,1)} %bitcast.20, bf16[2880,320]{1,0:T(8,128)(2,1)} %bitcast.21, f32[1,320]{1,0:T(1,128)S(1)} %reshape.40.gain_one, f32[1,320]{1,0:T(1,128)S(1)} %reshape.41.shift_one, ...), custom_call_target="tpu_custom_call" | custom-call | tf_op jit(solution)/shard_map/prepare/pallas_call | solution.py:394
  19.8 1.3 %copy-done = bf16[320,2880]{1,0:T(8,128)(2,1)} copy-done((bf16[320,2880]{1,0:T(8,128)(2,1)}, bf16[320,2880]{1,0:T(8,128)(2,1)S(1)}, u32[]{:S(2)}) %copy-start) | copy-done | bytes 1843224
  21.1 2.5 %all-to-all-done.seen_ref = f32[16,16,128]{2,1,0:T(8,128)S(1)} async-done(((f32[16,16,128]{2,1,0:T(8,128)}), f32[16,16,128]{2,1,0:T(8,128)S(1)}, u32[]{:S(2)}, u32[]{:S(2)}) %all-to-all-start) | async-done | bytes 131104 | tf_op jit(solution)/shard_map/all_to_all | solution.py:342
  23.6 0.0 collective-permute-done.2.next_ref
  23.6 0.0 collective-permute-done.1.near_ref
  23.6 0.0 collective-permute-start.3
  23.6 0.5 %collective-permute-start.4 = (bf16[2,320,256]{2,1,0:T(8,128)(2,1)}, bf16[2,320,256]{2,1,0:T(8,128)(2,1)S(1)}, u32[]{:S(2)}, u32[]{:S(2)}) collective-permute-start(bf16[2,320,256]{2,1,0:T(8,128)(2,1)} %collective-permute-done.2.next_ref), channel_id=1, source_target_pairs={{0,16},{16,0},{1,17},{17,1},{2,18},{18,2},{3,19},{19,3},{4,20},{20... | collective-permute-start | bytes 983048 | tf_op jit(solution)/shard_map/ppermute | solution.py:408
  24.1 0.0 collective-permute-done.far_ref
  24.1 2.7 %inner.1 = (f32[2,320,256]{2,1,0:T(8,128)S(1)}, bf16[3840,256]{1,0:T(8,128)(2,1)S(1)}, f32[6,320,128]{2,1,0:T(8,128)S(1)}) custom-call(bf16[4,320,256]{2,1,0:T(8,128)(2,1)S(1)} %get-tuple-element.21.own_ref.lat_ref, bf16[4,320,256]{2,1,0:T(8,128)(2,1)S(1)} %collective-permute-done.far_ref, f32[16,16,128]{2,1,0:T(8,128)S(1)} %all-to-all-done.seen_ref, ...), custom_call_target="tpu_custom_call" | custom-call | tf_op jit(solution)/shard_map/inner/pallas_call | solution.py:410
  26.8 0.0 collective-permute-done.3.far_near_ref
  26.8 0.0 collective-permute-done.4.far_next_ref
  26.8 4.1 %outer.1 = (f32[4,320,256]{2,1,0:T(8,128)S(1)}, f32[8,8,128]{2,1,0:T(8,128)S(1)}) custom-call(bf16[2,320,256]{2,1,0:T(8,128)(2,1)} %collective-permute-done.1.near_ref, bf16[2,320,256]{2,1,0:T(8,128)(2,1)} %collective-permute-done.2.next_ref, bf16[2,320,256]{2,1,0:T(8,128)(2,1)S(1)} %collective-permute-done.3.far_near_ref, ...), custom_call_target="tpu_custom_call" | custom-call | tf_op jit(solution)/shard_map/outer/pallas_call | solution.py:423
  30.9 12.1 %all_to_all.10.seen_ref = f32[8,8,128]{2,1,0:T(8,128)S(1)} all-to-all(f32[8,8,128]{2,1,0:T(8,128)S(1)} %get-tuple-element.35), channel_id=1, replica_groups=mesh['cfg'=2,'patch'=8,'req'=2] {'patch'}, dimensions={0} | all-to-all | bytes 65536 | tf_op jit(solution)/shard_map/all_to_all | solution.py:342
  43.0 4.2 %second.1 = bf16[4,320,256]{2,1,0:T(8,128)(2,1)} custom-call(f32[2,320,256]{2,1,0:T(8,128)S(1)} %get-tuple-element.29.inner_ref, f32[4,320,256]{2,1,0:T(8,128)S(1)} %get-tuple-element.34.outer_ref, bf16[4,320,256]{2,1,0:T(8,128)(2,1)S(1)} %get-tuple-element.21.own_ref.lat_ref, f32[8,8,128]{2,1,0:T(8,128)S(1)} %all_to_all.10.seen_ref, ...), custom_call_target="tpu_custom_call" | custom-call | tf_op jit(solution)/shard_map/second/pallas_call | solution.py:439
  (20 shorter events, 0.0 us)
Async XLA Ops:
  0.0 16.6 %copy-start.2 = (f32[320]{0:T(512)S(1)}, f32[320]{0:T(512)}, u32[]{:S(2)}) copy-start(f32[320]{0:T(512)} %param.16) | copy-start | bytes 3844
  0.0 16.6 %copy-start.3 = (f32[320]{0:T(512)S(1)}, f32[320]{0:T(512)}, u32[]{:S(2)}) copy-start(f32[320]{0:T(512)} %param.17) | copy-start | bytes 3844
  0.0 16.6 %copy-start.4 = (f32[320]{0:T(512)S(1)}, f32[320]{0:T(512)}, u32[]{:S(2)}) copy-start(f32[320]{0:T(512)} %param.19) | copy-start | bytes 3844
  0.0 16.6 %copy-start.5 = (f32[320]{0:T(512)S(1)}, f32[320]{0:T(512)}, u32[]{:S(2)}) copy-start(f32[320]{0:T(512)} %param.21) | copy-start | bytes 3844
  0.0 16.6 %copy-start.6 = (f32[320]{0:T(512)S(1)}, f32[320]{0:T(512)}, u32[]{:S(2)}) copy-start(f32[320]{0:T(512)} %param.22) | copy-start | bytes 3844
  0.0 16.6 %copy-start.7 = (f32[320]{0:T(512)S(1)}, f32[320]{0:T(512)}, u32[]{:S(2)}) copy-start(f32[320]{0:T(512)} %param.23) | copy-start | bytes 3844
  0.0 16.7 %copy-start.8 = (f32[320]{0:T(512)S(1)}, f32[320]{0:T(512)}, u32[]{:S(2)}) copy-start(f32[320]{0:T(512)} %param.25) | copy-start | bytes 3844
  2.0 21.5 %collective-permute-start.2 = (bf16[2,320,256]{2,1,0:T(8,128)(2,1)}, bf16[2,320,256]{2,1,0:T(8,128)(2,1)}, u32[]{:S(2)}, u32[]{:S(2)}) collective-permute-start(bf16[2,320,256]{2,1,0:T(8,128)(2,1)} %get-tuple-element.37), channel_id=1, source_target_pairs={{2,4},{6,8},{10,12},{4,2},{8,6},{12,10},{3,5},{7,9},{11,13},{5,3},... | collective-permute-start | bytes 983048 | tf_op jit(solution)/shard_map/ppermute | solution.py:368
  3.5 20.1 %collective-permute-start.1 = (bf16[2,320,256]{2,1,0:T(8,128)(2,1)}, bf16[2,320,256]{2,1,0:T(8,128)(2,1)}, u32[]{:S(2)}, u32[]{:S(2)}) collective-permute-start(bf16[2,320,256]{2,1,0:T(8,128)(2,1)} %get-tuple-element.38), channel_id=1, source_target_pairs={{0,2},{2,0},{4,6},{6,4},{8,10},{10,8},{12,14},{14,12},{1,3},{3,1},... | collective-permute-start | bytes 983048 | tf_op jit(solution)/shard_map/ppermute | solution.py:366
  8.5 15.6 %collective-permute-start = (bf16[4,320,256]{2,1,0:T(8,128)(2,1)}, bf16[4,320,256]{2,1,0:T(8,128)(2,1)S(1)}, u32[]{:S(2)}, u32[]{:S(2)}) collective-permute-start(bf16[4,320,256]{2,1,0:T(8,128)(2,1)} %bitcast.18), channel_id=1, source_target_pairs={{0,16},{16,0},{1,17},{17,1},{2,18},{18,2},{3,19},{19,3},{4,20},{20... | collective-permute-start | bytes 1966088 | tf_op jit(solution)/shard_map/ppermute | solution.py:370
  11.0 12.6 %all-to-all-start = ((f32[16,16,128]{2,1,0:T(8,128)}), f32[16,16,128]{2,1,0:T(8,128)S(1)}, u32[]{:S(2)}, u32[]{:S(2)}) async-start(f32[16,16,128]{2,1,0:T(8,128)} %get-tuple-element.22), calls=%async_computation | async-start | bytes 262144 | tf_op jit(solution)/shard_map/all_to_all | solution.py:342
  19.8 1.3 %copy-start = (bf16[320,2880]{1,0:T(8,128)(2,1)}, bf16[320,2880]{1,0:T(8,128)(2,1)S(1)}, u32[]{:S(2)}) copy-start(bf16[320,2880]{1,0:T(8,128)(2,1)S(1)} %get-tuple-element.36.weight_ref) | copy-start | bytes 5529604
  23.6 3.2 %collective-permute-start.3 = (bf16[2,320,256]{2,1,0:T(8,128)(2,1)}, bf16[2,320,256]{2,1,0:T(8,128)(2,1)S(1)}, u32[]{:S(2)}, u32[]{:S(2)}) collective-permute-start(bf16[2,320,256]{2,1,0:T(8,128)(2,1)} %collective-permute-done.1.near_ref), channel_id=1, source_target_pairs={{0,16},{16,0},{1,17},{17,1},{2,18},{18,2},{3,19},{19,3},{4,20},{20... | collective-permute-start | bytes 983048 | tf_op jit(solution)/shard_map/ppermute | solution.py:407
  23.6 3.2 %collective-permute-start.4 = (bf16[2,320,256]{2,1,0:T(8,128)(2,1)}, bf16[2,320,256]{2,1,0:T(8,128)(2,1)S(1)}, u32[]{:S(2)}, u32[]{:S(2)}) collective-permute-start(bf16[2,320,256]{2,1,0:T(8,128)(2,1)} %collective-permute-done.2.next_ref), channel_id=1, source_target_pairs={{0,16},{16,0},{1,17},{17,1},{2,18},{18,2},{3,19},{19,3},{4,20},{20... | collective-permute-start | bytes 983048 | tf_op jit(solution)/shard_map/ppermute | solution.py:408
  26.8 16.3 %copy-start.1 = (bf16[320,2880]{1,0:T(8,128)(2,1)S(1)}, bf16[320,2880]{1,0:T(8,128)(2,1)}, u32[]{:S(2)}) copy-start(bf16[320,2880]{1,0:T(8,128)(2,1)} %copy-done) | copy-start | bytes 5529604

commit v5 on v4

--- a/solution.py
+++ b/solution.py
@@ -138,26 +138,51 @@
 PARTS = 3
 
 
+def edges_kernel(lat_hbm, near_ref, next_ref, sems):
+    reach = near_ref.shape[0]
+    last = lat_hbm.shape[0] - reach
+    near_at = jnp.where(lax.rem(lax.axis_index("patch"), 2) == 0, last, 0)
+    copies = [
+        pltpu.make_async_copy(lat_hbm.at[pl.ds(near_at, reach)], near_ref, sems.at[0]),
+        pltpu.make_async_copy(lat_hbm.at[pl.ds(last - near_at, reach)], next_ref, sems.at[1]),
+    ]
+    for copy in copies:
+        copy.start()
+    for copy in copies:
+        copy.wait()
+
+
+def turn(source, held, target, sems):
+    part = held.shape[0] // PARTS
+    jobs = []
+    for k in range(PARTS):
+        here = pl.ds(k * part, part)
+        copy = pltpu.make_async_copy(source.at[here], held.at[here], sems.at[k])
+        copy.start()
+        jobs.append((copy, k * part))
+
+    def finish():
+        for copy, at in jobs:
+            copy.wait()
+            target[:, at : at + part] = held[at : at + part, :].T
+
+    return finish
+
+
 def prepare_kernel(
-    one_hbm, two_hbm, gain_one, shift_one, bias_one, time_bias, gain_two, shift_two, bias_two, steer,
-    one_out, two_out, rows_ref, one_ref, two_ref, sems,
+    weight_hbm, gain_one, shift_one, bias_one, time_bias, gain_two, shift_two, bias_two, steer,
+    out_ref, rows_ref, held_ref, sems,
 ):
-    deep = one_ref.shape[0]
-    part = deep // PARTS
-    jobs = []
-    for k, (source, held, target) in enumerate(((one_hbm, one_ref, one_out), (two_hbm, two_ref, two_out))):
-        for at in range(PARTS):
-            here = pl.ds(at * part, part)
-            copy = pltpu.make_async_copy(source.at[here], held.at[here], sems.at[k * PARTS + at])
-            copy.start()
-            jobs.append((copy, held, target, at * part))
+    finish = turn(weight_hbm, held_ref, out_ref, sems)
     wide = rows_ref.shape[1]
     vectors = (gain_one, shift_one, bias_one, time_bias, gain_two, shift_two, bias_two)
     lines = [widen(v[...], wide) for v in vectors]
     rows_ref[...] = jnp.concatenate(lines + [jnp.broadcast_to(steer[...], (1, wide))], axis=0)
-    for copy, held, target, at in jobs:
-        copy.wait()
-        target[:, at : at + part] = held[at : at + part, :].T
+    finish()
+
+
+def turn_kernel(weight_hbm, out_ref, held_ref, sems):
+    turn(weight_hbm, held_ref, out_ref, sems)()
 
 
 def spread_columns(rows, chans, cols_ref):
@@ -360,14 +385,19 @@
     wide = padded_lanes(chans)
     deep = 9 * chans
     patches = lax.axis_size("patch")
-    even = lax.rem(lax.axis_index("patch"), 2) == 0
-    near_edge = lax.dynamic_slice_in_dim(own, jnp.where(even, rows - REACH, 0), REACH, 0)
-    next_edge = lax.dynamic_slice_in_dim(own, jnp.where(even, 0, rows - REACH), REACH, 0)
+    near_edge, next_edge = pl.pallas_call(
+        edges_kernel,
+        out_shape=[pltpu.VMEM((REACH, chans, cols), BF16)] * 2,
+        in_specs=[ANY],
+        out_specs=[VMEM] * 2,
+        scratch_shapes=[pltpu.SemaphoreType.DMA((2,))],
+        compiler_params=LIMIT,
+        name="edges",
+    )(in_hbm(own))
     near = lax.ppermute(near_edge, "patch", [(i, i ^ 1) for i in range(patches)])
     steps = [(i, i + 1) for i in range(1, patches - 1, 2)]
     following = lax.ppermute(next_edge, "patch", steps + [(j, i) for i, j in steps])
     swap = [(0, 1), (1, 0)]
-    far = lax.ppermute(own, "cfg", swap)
     line = lambda vector: vector.reshape(1, -1)
 
     tile_one = -(-3 * wide // LANES // 8) * 8
@@ -389,18 +419,20 @@
     )(in_hbm(own), in_hbm(time_embed), in_hbm(time_weight))
     seen = everyone(sent, ("cfg", "patch"))
 
-    weights = (conv_one.reshape(deep, chans), conv_two.reshape(deep, chans))
-    *weights, _ = lax.optimization_barrier((*weights, sent))
-    turned_one, turned_two, vectors = pl.pallas_call(
+    source, weight_one, _ = lax.optimization_barrier((own, conv_one.reshape(deep, chans), sent))
+    far = lax.ppermute(source, "cfg", swap)
+    turned_one, vectors = pl.pallas_call(
         prepare_kernel,
-        out_shape=[pltpu.VMEM((chans, deep), BF16)] * 2 + [pltpu.VMEM((8, wide), F32)],
-        in_specs=[ANY] * 2 + [VMEM] * 8,
-        out_specs=[VMEM] * 3,
-        scratch_shapes=[pltpu.VMEM((deep, chans), BF16)] * 2 + [pltpu.SemaphoreType.DMA((2 * PARTS,))],
+        out_shape=[pltpu.VMEM((chans, deep), BF16), pltpu.VMEM((8, wide), F32)],
+        in_specs=[ANY] + [VMEM] * 8,
+        out_specs=[VMEM] * 2,
+        scratch_shapes=[
+            pltpu.VMEM((deep, chans), BF16), pltpu.SemaphoreType.DMA((PARTS,)),
+        ],
         compiler_params=LIMIT,
         name="prepare",
     )(
-        in_hbm(weights[0]), in_hbm(weights[1]), line(gain_one), line(shift_one), line(bias_one),
+        in_hbm(weight_one), line(gain_one), line(shift_one), line(bias_one),
         line(time_bias), line(gain_two), line(shift_two), line(bias_two), line(steer_scale),
     )
     near, following, vectors, seen = lax.optimization_barrier((near, following, vectors, seen))
@@ -436,6 +468,16 @@
         name="outer",
     )(near, following, far_near, far_next, inner, taps, columns, vectors, turned_one)
     seen = everyone(sent, "patch")
+    weight_two, _ = lax.optimization_barrier((conv_two.reshape(deep, chans), sent))
+    turned_two = pl.pallas_call(
+        turn_kernel,
+        out_shape=pltpu.VMEM((chans, deep), BF16),
+        in_specs=[ANY],
+        out_specs=VMEM,
+        scratch_shapes=[pltpu.VMEM((deep, chans), BF16), pltpu.SemaphoreType.DMA((PARTS,))],
+        compiler_params=LIMIT,
+        name="turn",
+    )(in_hbm(weight_two))
     image = pl.pallas_call(
         second_kernel,
         out_shape=jax.ShapeDtypeStruct((rows, chans, cols), BF16),

time: 47.5 us -> 53 us (1.12)
  blocking collectives: 12.1 us -> 0 us
  starting transfers between devices: 11.9 us -> 17.9 us
  local copies, waits for them, and re-layouts: 3.33 us -> 9.1 us
  Pallas kernels: 16.5 us -> 19.9 us
  waiting for transfers between devices: 2.49 us -> 4.71 us
    all_to_all x1 -> x0, blocking collectives: 12.1 us -> none  [everyone(): return lax.all_to_all(tiles, axes, 0, 0)]
    all_to_all x1 -> x2, starting transfers between devices: 4.91 us -> 12.9 us  [everyone(): return lax.all_to_all(tiles, axes, 0, 0)]
    reshape x7, local copies, waits for them, and re-layouts: 0.02 us -> 4.78 us  [body(): line = lambda vector: vector.reshape(1, -1)]
    pallas_call x0 -> x2, Pallas kernels: none -> 4.01 us  [the longest x1 2.1 us: body(): pl.pallas_call(turn_kernel, out_shape=pltpu.VMEM((chans, deep), BF16), in...]
    unnamed x18 -> x8, local copies, waits for them, and re-layouts: 1.31 us -> 4.32 us
    all_to_all x1 -> x2, waiting for transfers between devices: 2.48 us -> 4.69 us  [everyone(): return lax.all_to_all(tiles, axes, 0, 0)]
    ppermute x1, starting transfers between devices: 5.05 us -> 3 us  [body(): lax.ppermute(near_edge, 'patch', [(i, i ^ 1) for i in range(patches)])]
    dynamic_slice x1 -> x0, local copies, waits for them, and re-layouts: 2 us -> none  [body(): lax.dynamic_slice_in_dim(own, jnp.where(even, 0, rows - REACH), REACH, 0)]
  transfers between devices with their start and end apart: 6 -> 7, of which waited for: 1 -> 2; matrix products, arithmetic and copies ran while one was open for 0% -> 9% of each run, Pallas kernels for 17% -> 18%
where the time goes in v5:
time: 53 us; the launch traced here: 52.4 us
  Pallas kernels  19.9 us (38%)
  starting transfers between devices  17.9 us (34%)
  local copies, waits for them, and re-layouts  9.1 us (17%)
  waiting for transfers between devices  4.71 us (9%)
  between operations  0.73 us (1%)
    all_to_all x2, starting transfers between devices, everyone(): return lax.all_to_all(tiles, axes, 0, 0)  12.9 us
    reshape x7, local copies, waits for them, and re-layouts, body(): line = lambda vector: vector.reshape(1, -1)  4.78 us
    all_to_all x2, waiting for transfers between devices, everyone(): return lax.all_to_all(tiles, axes, 0, 0)  4.69 us
    pallas_call x1, Pallas kernels, body(): pl.pallas_call(outer_kernel, out_shape=[pltpu.VMEM((2 * REACH, chans, col...  4.58 us
    unnamed x8, local copies, waits for them, and re-layouts  4.32 us
    pallas_call x1, Pallas kernels, body(): pl.pallas_call(second_kernel, out_shape=jax.ShapeDtypeStruct((rows, chans...  4.11 us
    ppermute x1, starting transfers between devices, body(): lax.ppermute(near_edge, 'patch', [(i, i ^ 1) for i in range(patches)])  3 us
    pallas_call x1, Pallas kernels, body(): pl.pallas_call(inner_kernel, out_shape=[pltpu.VMEM((max(rows - 2, 1), cha...  2.65 us
  transfers between devices with their start and end apart: 7, of which 2 were waited for; matrix products, arithmetic and copies ran while one was open for 9% of the time, Pallas kernels for 18%

profile of v5, /device:TPU:0, one launch (start us, length us, event | category | flops | bytes accessed | tf_op | source)
XLA Modules:
  0.0 52.4 jit_solution(3221784639563222049)
XLA Ops:
  0.0 1.9 %edges.1 = (bf16[2,320,256]{2,1,0:T(8,128)(2,1)}, bf16[2,320,256]{2,1,0:T(8,128)(2,1)}) custom-call(bf16[4,320,256]{2,1,0:T(8,128)(2,1)} %bitcast.10), custom_call_target="tpu_custom_call" | custom-call | tf_op jit(solution)/shard_map/edges/pallas_call | solution.py:388
  1.9 3.0 %collective-permute-start.1 = (bf16[2,320,256]{2,1,0:T(8,128)(2,1)}, bf16[2,320,256]{2,1,0:T(8,128)(2,1)}, u32[]{:S(2)}, u32[]{:S(2)}) collective-permute-start(bf16[2,320,256]{2,1,0:T(8,128)(2,1)} %get-tuple-element.26), channel_id=1, source_target_pairs={{0,2},{2,0},{4,6},{6,4},{8,10},{10,8},{12,14},{14,12},{1,3},{3,1},... | collective-permute-start | bytes 983048 | tf_op jit(solution)/shard_map/ppermute | solution.py:397
  4.9 1.4 %collective-permute-start.2 = (bf16[2,320,256]{2,1,0:T(8,128)(2,1)}, bf16[2,320,256]{2,1,0:T(8,128)(2,1)}, u32[]{:S(2)}, u32[]{:S(2)}) collective-permute-start(bf16[2,320,256]{2,1,0:T(8,128)(2,1)} %get-tuple-element.27), channel_id=1, source_target_pairs={{2,4},{6,8},{10,12},{4,2},{8,6},{12,10},{3,5},{7,9},{11,13},{5,3},... | collective-permute-start | bytes 983048 | tf_op jit(solution)/shard_map/ppermute | solution.py:399
  6.3 2.5 %stats.1 = (bf16[4,320,256]{2,1,0:T(8,128)(2,1)S(1)}, f32[16,16,128]{2,1,0:T(8,128)}) custom-call(bf16[4,320,256]{2,1,0:T(8,128)(2,1)} %bitcast.11, bf16[1,1280]{1,0:T(2,128)(2,1)} %embed_hbm.1, bf16[160,320]{1,0:T(8,128)(2,1)} %weight_hbm.1), custom_call_target="tpu_custom_call" | custom-call | tf_op jit(solution)/shard_map/stats/pallas_call | solution.py:404
  8.9 7.1 %all-to-all-start = ((f32[16,16,128]{2,1,0:T(8,128)}), f32[16,16,128]{2,1,0:T(8,128)S(1)}, u32[]{:S(2)}, u32[]{:S(2)}) async-start(f32[16,16,128]{2,1,0:T(8,128)} %get-tuple-element.24), calls=%async_computation | async-start | bytes 262144 | tf_op jit(solution)/shard_map/all_to_all | solution.py:367
  16.6 0.7 %reshape.31.gain_one = f32[1,320]{1,0:T(1,128)S(1)} reshape(f32[320]{0:T(512)} %param.16) | data formatting | bytes 2560 | tf_op jit(solution)/shard_map/reshape | solution.py:401
  17.3 0.7 %reshape.32.shift_one = f32[1,320]{1,0:T(1,128)S(1)} reshape(f32[320]{0:T(512)} %param.17) | data formatting | bytes 2560 | tf_op jit(solution)/shard_map/reshape | solution.py:401
  18.0 0.7 %reshape.33.bias_one = f32[1,320]{1,0:T(1,128)S(1)} reshape(f32[320]{0:T(512)} %param.19) | data formatting | bytes 2560 | tf_op jit(solution)/shard_map/reshape | solution.py:401
  18.7 0.7 %reshape.34.time_bias = f32[1,320]{1,0:T(1,128)S(1)} reshape(f32[320]{0:T(512)} %param.21) | data formatting | bytes 2560 | tf_op jit(solution)/shard_map/reshape | solution.py:401
  19.3 0.7 %reshape.35.gain_two = f32[1,320]{1,0:T(1,128)S(1)} reshape(f32[320]{0:T(512)} %param.22) | data formatting | bytes 2560 | tf_op jit(solution)/shard_map/reshape | solution.py:401
  20.0 0.7 %reshape.36.shift_two = f32[1,320]{1,0:T(1,128)S(1)} reshape(f32[320]{0:T(512)} %param.23) | data formatting | bytes 2560 | tf_op jit(solution)/shard_map/reshape | solution.py:401
  20.7 0.7 %reshape.37.bias_two = f32[1,320]{1,0:T(1,128)S(1)} reshape(f32[320]{0:T(512)} %param.25) | data formatting | bytes 2560 | tf_op jit(solution)/shard_map/reshape | solution.py:401
  21.4 2.1 %prepare.1 = (bf16[320,2880]{1,0:T(8,128)(2,1)S(1)}, f32[8,384]{1,0:T(8,128)S(1)}) custom-call(bf16[2880,320]{1,0:T(8,128)(2,1)} %bitcast.13, f32[1,320]{1,0:T(1,128)S(1)} %reshape.31.gain_one, f32[1,320]{1,0:T(1,128)S(1)} %reshape.32.shift_one, f32[1,320]{1,0:T(1,128)S(1)} %reshape.33.bias_one, f32[1,320]{1,0:T(1,128)S(1)} %reshape.34.time_bias, ...), custom_call_target="tpu_custom_call" | custom-call | tf_op jit(solution)/shard_map/prepare/pallas_call | solution.py:424
  23.6 0.4 collective-permute-start.3
  24.2 0.8 %copy-done.2 = bf16[4,320,256]{2,1,0:T(8,128)(2,1)} copy-done((bf16[4,320,256]{2,1,0:T(8,128)(2,1)}, bf16[4,320,256]{2,1,0:T(8,128)(2,1)S(1)}, u32[]{:S(2)}) %copy-start.2) | copy-done | bytes 655384
  25.0 1.1 %copy-done.3 = bf16[4,320,256]{2,1,0:T(8,128)(2,1)S(1)} copy-done((bf16[4,320,256]{2,1,0:T(8,128)(2,1)S(1)}, bf16[4,320,256]{2,1,0:T(8,128)(2,1)}, u32[]{:S(2)}) %copy-start.3) | copy-done | bytes 655384
  26.1 2.7 %inner.1 = (f32[2,320,256]{2,1,0:T(8,128)S(1)}, bf16[3840,256]{1,0:T(8,128)(2,1)S(1)}, f32[6,320,128]{2,1,0:T(8,128)S(1)}) custom-call(bf16[4,320,256]{2,1,0:T(8,128)(2,1)S(1)} %get-tuple-element.23.own_ref.lat_ref, bf16[4,320,256]{2,1,0:T(8,128)(2,1)S(1)} %copy-done.3, f32[16,16,128]{2,1,0:T(8,128)S(1)} %all-to-all-done.seen_ref, ...), custom_call_target="tpu_custom_call" | custom-call | tf_op jit(solution)/shard_map/inner/pallas_call | solution.py:442
  28.8 4.6 %outer.1 = (f32[4,320,256]{2,1,0:T(8,128)S(1)}, f32[8,8,128]{2,1,0:T(8,128)}) custom-call(bf16[2,320,256]{2,1,0:T(8,128)(2,1)} %collective-permute-done.1.near_ref, bf16[2,320,256]{2,1,0:T(8,128)(2,1)} %collective-permute-done.2.next_ref, bf16[2,320,256]{2,1,0:T(8,128)(2,1)S(1)} %collective-permute-done.3.far_near_ref, ...), custom_call_target="tpu_custom_call" | custom-call | tf_op jit(solution)/shard_map/outer/pallas_call | solution.py:455
  33.4 1.1 %copy-done = f32[4,320,256]{2,1,0:T(8,128)} copy-done((f32[4,320,256]{2,1,0:T(8,128)}, f32[4,320,256]{2,1,0:T(8,128)S(1)}, u32[]{:S(2)}) %copy-start) | copy-done | bytes 1310744
  34.4 5.9 %all-to-all-start.1 = ((f32[8,8,128]{2,1,0:T(8,128)}), f32[8,8,128]{2,1,0:T(8,128)S(1)}, u32[]{:S(2)}, u32[]{:S(2)}) async-start(f32[8,8,128]{2,1,0:T(8,128)} %get-tuple-element.39), calls=%async_computation.1 | async-start | bytes 65536 | tf_op jit(solution)/shard_map/all_to_all | solution.py:367
  40.3 2.1 %turn.1.weight_ref = bf16[320,2880]{1,0:T(8,128)(2,1)S(1)} custom-call(bf16[2880,320]{1,0:T(8,128)(2,1)} %bitcast.14), custom_call_target="tpu_custom_call" | custom-call | tf_op jit(solution)/shard_map/turn/pallas_call | solution.py:472
  42.4 4.6 %all-to-all-done.1.seen_ref = f32[8,8,128]{2,1,0:T(8,128)S(1)} async-done(((f32[8,8,128]{2,1,0:T(8,128)}), f32[8,8,128]{2,1,0:T(8,128)S(1)}, u32[]{:S(2)}, u32[]{:S(2)}) %all-to-all-start.1) | async-done | bytes 32800 | tf_op jit(solution)/shard_map/all_to_all | solution.py:367
  47.0 1.3 %copy-done.1 = f32[4,320,256]{2,1,0:T(8,128)S(1)} copy-done((f32[4,320,256]{2,1,0:T(8,128)S(1)}, f32[4,320,256]{2,1,0:T(8,128)}, u32[]{:S(2)}) %copy-start.1) | copy-done | bytes 1310744
  48.3 4.1 %second.1 = bf16[4,320,256]{2,1,0:T(8,128)(2,1)} custom-call(f32[2,320,256]{2,1,0:T(8,128)S(1)} %get-tuple-element.33.inner_ref, f32[4,320,256]{2,1,0:T(8,128)S(1)} %copy-done.1, bf16[4,320,256]{2,1,0:T(8,128)(2,1)S(1)} %get-tuple-element.23.own_ref.lat_ref, f32[8,8,128]{2,1,0:T(8,128)S(1)} %all-to-all-done.1.seen_ref, ...), custom_call_target="tpu_custom_call" | custom-call | tf_op jit(solution)/shard_map/second/pallas_call | solution.py:481
  (12 shorter events, 0.3 us)
Async XLA Ops:
  1.9 21.7 %collective-permute-start.1 = (bf16[2,320,256]{2,1,0:T(8,128)(2,1)}, bf16[2,320,256]{2,1,0:T(8,128)(2,1)}, u32[]{:S(2)}, u32[]{:S(2)}) collective-permute-start(bf16[2,320,256]{2,1,0:T(8,128)(2,1)} %get-tuple-element.26), channel_id=1, source_target_pairs={{0,2},{2,0},{4,6},{6,4},{8,10},{10,8},{12,14},{14,12},{1,3},{3,1},... | collective-permute-start | bytes 983048 | tf_op jit(solution)/shard_map/ppermute | solution.py:397
  4.9 18.7 %collective-permute-start.2 = (bf16[2,320,256]{2,1,0:T(8,128)(2,1)}, bf16[2,320,256]{2,1,0:T(8,128)(2,1)}, u32[]{:S(2)}, u32[]{:S(2)}) collective-permute-start(bf16[2,320,256]{2,1,0:T(8,128)(2,1)} %get-tuple-element.27), channel_id=1, source_target_pairs={{2,4},{6,8},{10,12},{4,2},{8,6},{12,10},{3,5},{7,9},{11,13},{5,3},... | collective-permute-start | bytes 983048 | tf_op jit(solution)/shard_map/ppermute | solution.py:399
  8.8 15.4 %collective-permute-start = (bf16[4,320,256]{2,1,0:T(8,128)(2,1)}, bf16[4,320,256]{2,1,0:T(8,128)(2,1)S(1)}, u32[]{:S(2)}, u32[]{:S(2)}) collective-permute-start(bf16[4,320,256]{2,1,0:T(8,128)(2,1)} %bitcast.12), channel_id=1, source_target_pairs={{0,16},{16,0},{1,17},{17,1},{2,18},{18,2},{3,19},{19,3},{4,20},{20... | collective-permute-start | bytes 1966088 | tf_op jit(solution)/shard_map/ppermute | solution.py:423
  8.9 14.7 %all-to-all-start = ((f32[16,16,128]{2,1,0:T(8,128)}), f32[16,16,128]{2,1,0:T(8,128)S(1)}, u32[]{:S(2)}, u32[]{:S(2)}) async-start(f32[16,16,128]{2,1,0:T(8,128)} %get-tuple-element.24), calls=%async_computation | async-start | bytes 262144 | tf_op jit(solution)/shard_map/all_to_all | solution.py:367
  23.6 5.1 %collective-permute-start.3 = (bf16[2,320,256]{2,1,0:T(8,128)(2,1)}, bf16[2,320,256]{2,1,0:T(8,128)(2,1)S(1)}, u32[]{:S(2)}, u32[]{:S(2)}) collective-permute-start(bf16[2,320,256]{2,1,0:T(8,128)(2,1)} %collective-permute-done.1.near_ref), channel_id=1, source_target_pairs={{0,16},{16,0},{1,17},{17,1},{2,18},{18,2},{3,19},{19,3},{4,20},{20... | collective-permute-start | bytes 983048 | tf_op jit(solution)/shard_map/ppermute | solution.py:439
  24.0 4.7 %collective-permute-start.4 = (bf16[2,320,256]{2,1,0:T(8,128)(2,1)}, bf16[2,320,256]{2,1,0:T(8,128)(2,1)S(1)}, u32[]{:S(2)}, u32[]{:S(2)}) collective-permute-start(bf16[2,320,256]{2,1,0:T(8,128)(2,1)} %collective-permute-done.2.next_ref), channel_id=1, source_target_pairs={{0,16},{16,0},{1,17},{17,1},{2,18},{18,2},{3,19},{19,3},{4,20},{20... | collective-permute-start | bytes 983048 | tf_op jit(solution)/shard_map/ppermute | solution.py:440
  24.2 0.8 %copy-start.2 = (bf16[4,320,256]{2,1,0:T(8,128)(2,1)}, bf16[4,320,256]{2,1,0:T(8,128)(2,1)S(1)}, u32[]{:S(2)}) copy-start(bf16[4,320,256]{2,1,0:T(8,128)(2,1)S(1)} %collective-permute-done.far_ref) | copy-start | bytes 1966084
  25.0 1.1 %copy-start.3 = (bf16[4,320,256]{2,1,0:T(8,128)(2,1)S(1)}, bf16[4,320,256]{2,1,0:T(8,128)(2,1)}, u32[]{:S(2)}) copy-start(bf16[4,320,256]{2,1,0:T(8,128)(2,1)} %copy-done.2) | copy-start | bytes 1966084
  33.3 1.1 %copy-start = (f32[4,320,256]{2,1,0:T(8,128)}, f32[4,320,256]{2,1,0:T(8,128)S(1)}, u32[]{:S(2)}) copy-start(f32[4,320,256]{2,1,0:T(8,128)S(1)} %get-tuple-element.38.outer_ref) | copy-start | bytes 3932164
  34.4 12.5 %all-to-all-start.1 = ((f32[8,8,128]{2,1,0:T(8,128)}), f32[8,8,128]{2,1,0:T(8,128)S(1)}, u32[]{:S(2)}, u32[]{:S(2)}) async-start(f32[8,8,128]{2,1,0:T(8,128)} %get-tuple-element.39), calls=%async_computation.1 | async-start | bytes 65536 | tf_op jit(solution)/shard_map/all_to_all | solution.py:367
  47.0 1.3 %copy-start.1 = (f32[4,320,256]{2,1,0:T(8,128)S(1)}, f32[4,320,256]{2,1,0:T(8,128)}, u32[]{:S(2)}) copy-start(f32[4,320,256]{2,1,0:T(8,128)} %copy-done) | copy-start | bytes 3932164

commit v6 on v4

--- a/solution.py
+++ b/solution.py
@@ -105,14 +105,25 @@
     )
 
 
-def stats_kernel(lat_hbm, embed_hbm, weight_hbm, lat_ref, out_ref, embed_ref, weight_ref, sems):
+def stats_kernel(
+    lat_hbm, embed_hbm, weight_hbm,
+    lat_ref, out_ref, near_hbm, next_hbm,
+    embed_ref, weight_ref, sems, edge_sems,
+):
     rows, chans, _ = lat_ref.shape
     copies = [
         pltpu.make_async_copy(lat_hbm.at[k], lat_ref.at[k], sems.at[k]) for k in range(rows)
     ]
     copies.append(pltpu.make_async_copy(embed_hbm, embed_ref, sems.at[rows]))
     copies.append(pltpu.make_async_copy(weight_hbm, weight_ref, sems.at[rows + 1]))
-    for copy in copies:
+    reach = near_hbm.shape[0]
+    last = rows - reach
+    near_at = jnp.where(lax.rem(lax.axis_index("patch"), 2) == 0, last, 0)
+    edges = [
+        pltpu.make_async_copy(lat_hbm.at[pl.ds(near_at, reach)], near_hbm, edge_sems.at[0]),
+        pltpu.make_async_copy(lat_hbm.at[pl.ds(last - near_at, reach)], next_hbm, edge_sems.at[1]),
+    ]
+    for copy in copies + edges:
         copy.start()
     waits = list(copies[:rows])
 
@@ -133,31 +144,54 @@
     act = (embed / (1.0 + jnp.exp(-embed))).astype(BF16)
     time_part = jnp.dot(act, weight_ref[...], preferred_element_type=F32)[0:1]
     put_rows([mean, squares, widen(time_part, wide)], out_ref)
-
-
-PARTS = 3
+    for copy in edges:
+        copy.wait()
+
+
+def turn(source, target, held_ref, turned_ref, sems):
+    part = held_ref.shape[0] // 3
+    copies = []
+    for k in range(3):
+        here = pl.ds(k * part, part)
+        copies.append(pltpu.make_async_copy(source.at[here], held_ref.at[here], sems.at[k]))
+        copies[k].start()
+
+    def finish():
+        out = []
+        for k in range(3):
+            copies[k].wait()
+            turned_ref[k] = held_ref[k * part : (k + 1) * part, :].T
+            out.append(pltpu.make_async_copy(turned_ref.at[k], target.at[k], sems.at[3 + k]))
+            out[k].start()
+        for copy in out:
+            copy.wait()
+
+    return finish
 
 
 def prepare_kernel(
-    one_hbm, two_hbm, gain_one, shift_one, bias_one, time_bias, gain_two, shift_two, bias_two, steer,
-    one_out, two_out, rows_ref, one_ref, two_ref, sems,
+    weight_hbm, gain_one, shift_one, bias_one, time_bias, gain_two, shift_two, bias_two, steer,
+    out_hbm, rows_ref, held_ref, turned_ref, sems, row_sems, *vector_refs,
 ):
-    deep = one_ref.shape[0]
-    part = deep // PARTS
-    jobs = []
-    for k, (source, held, target) in enumerate(((one_hbm, one_ref, one_out), (two_hbm, two_ref, two_out))):
-        for at in range(PARTS):
-            here = pl.ds(at * part, part)
-            copy = pltpu.make_async_copy(source.at[here], held.at[here], sems.at[k * PARTS + at])
-            copy.start()
-            jobs.append((copy, held, target, at * part))
+    finish = turn(weight_hbm, out_hbm, held_ref, turned_ref, sems)
     wide = rows_ref.shape[1]
     vectors = (gain_one, shift_one, bias_one, time_bias, gain_two, shift_two, bias_two)
-    lines = [widen(v[...], wide) for v in vectors]
-    rows_ref[...] = jnp.concatenate(lines + [jnp.broadcast_to(steer[...], (1, wide))], axis=0)
-    for copy, held, target, at in jobs:
+    for copy in fetch(zip(vectors, vector_refs), row_sems):
         copy.wait()
-        target[:, at : at + part] = held[at : at + part, :].T
+    rows = [widen(v[...].reshape(1, -1), wide) for v in vector_refs]
+    rows_ref[...] = jnp.concatenate(rows + [jnp.broadcast_to(steer[...], (1, wide))], axis=0)
+    finish()
+
+
+def turn_kernel(weight_hbm, out_hbm, held_ref, turned_ref, sems):
+    turn(weight_hbm, out_hbm, held_ref, turned_ref, sems)()
+
+
+def fetch(pairs, sems):
+    copies = [pltpu.make_async_copy(a, b, sems.at[k]) for k, (a, b) in enumerate(pairs)]
+    for copy in copies:
+        copy.start()
+    return copies
 
 
 def spread_columns(rows, chans, cols_ref):
@@ -206,17 +240,29 @@
     return mix
 
 
-def matmul(weight_ref, taps, first_tap):
-    depth = taps.shape[0]
-    start = first_tap * (weight_ref.shape[1] // 3)
-    return jnp.dot(weight_ref[:, start : start + depth], taps, preferred_element_type=F32)
+def conv_row(weight_ref, taps):
+    total = None
+    for k, tap in enumerate(taps):
+        part = jnp.dot(weight_ref[k], tap, preferred_element_type=F32)
+        total = part if total is None else total + part
+    return total
+
+
+def line_of(taps_ref, at, chans):
+    return taps_ref[at * 3 * chans : (at + 1) * 3 * chans, :]
 
 
 def inner_kernel(
-    own_ref, far_ref, seen_ref, rows_ref, weight_ref,
+    own_ref, far_hbm, seen_ref, rows_ref, weight_hbm,
     steered_ref, taps_ref, cols_ref,
+    far_ref, weight_ref, sems,
 ):
     rows, chans, cols = own_ref.shape
+    copies = fetch(
+        [(far_hbm.at[k], far_ref.at[k]) for k in range(rows)]
+        + [(weight_hbm.at[k], weight_ref.at[k]) for k in range(3)],
+        sems,
+    )
     wide = padded_lanes(chans)
     size = chans // GROUPS
     cfg, peers = lax.axis_index("cfg"), lax.axis_size("patch")
@@ -233,59 +279,56 @@
         chans, cols_ref,
     )
     mix = mixer(cols_ref, rows_ref, chans)
-    line = 3 * chans
     if rows < 3:
         steered_ref[...] = jnp.zeros_like(steered_ref)
     for at in range(rows):
+        copies[at].wait()
         put_taps(taps_ref, at, mix(own_ref[at], far_ref[at]))
+        if at == min(1, rows - 1):
+            for copy in copies[rows:]:
+                copy.wait()
         if at >= 2:
-            total = matmul(weight_ref, taps_ref[(at - 2) * line : (at + 1) * line, :], 0)
+            total = conv_row(weight_ref, [line_of(taps_ref, at - 2 + k, chans) for k in range(3)])
             steered_ref[at - 2] = total + twice(cols_ref[5])
 
 
 def outer_kernel(
-    near_ref, next_ref, far_near_ref, far_next_ref, inner_ref, inner_taps_ref, cols_ref, rows_ref, weight_ref,
+    near_hbm, next_hbm, far_near_hbm, far_next_hbm, inner_ref, inner_taps_ref, cols_ref, rows_ref, weight_hbm,
     steered_ref, out_ref,
-    taps_ref, edge_ref,
+    taps_ref, edge_ref, weight_ref, sems,
 ):
-    reach, chans, cols = near_ref.shape
-    line = 3 * chans
-    rows = inner_taps_ref.shape[0] // line
+    reach, chans, cols = near_hbm.shape
+    rows = inner_taps_ref.shape[0] // (3 * chans)
     above = jnp.where(lax.rem(lax.axis_index("patch"), 2) == 0, reach, 0)
-    edge_ref[0, pl.ds(above, reach)] = next_ref[...]
-    edge_ref[1, pl.ds(above, reach)] = far_next_ref[...]
-    edge_ref[0, pl.ds(reach - above, reach)] = near_ref[...]
-    edge_ref[1, pl.ds(reach - above, reach)] = far_near_ref[...]
+    below = reach - above
+    copies = fetch(
+        [
+            (next_hbm, edge_ref.at[0, pl.ds(above, reach)]),
+            (far_next_hbm, edge_ref.at[1, pl.ds(above, reach)]),
+            (near_hbm, edge_ref.at[0, pl.ds(below, reach)]),
+            (far_near_hbm, edge_ref.at[1, pl.ds(below, reach)]),
+        ]
+        + [(weight_hbm.at[k], weight_ref.at[k]) for k in range(3)],
+        sems,
+    )
     mix = mixer(cols_ref, rows_ref, chans)
 
     def taps(at):
         if reach <= at < reach + rows:
-            return inner_taps_ref, at - reach
-        return taps_ref, at if at < reach else at - rows
-
-    def rows_of(first, count):
-        ref, at = taps(first)
-        return ref[at * line : (at + count) * line, :]
-
-    def conv(at):
-        total, tap = None, 0
-        while tap < 3:
-            ref, _ = taps(at + tap)
-            count = 1
-            while tap + count < 3 and taps(at + tap + count)[0] is ref:
-                count += 1
-            part = matmul(weight_ref, rows_of(at + tap, count), tap)
-            total = part if total is None else total + part
-            tap += count
-        return total
+            return line_of(inner_taps_ref, at - reach, chans)
+        return line_of(taps_ref, at if at < reach else at - rows, chans)
 
     def enter(at):
         k = reach + at if at < reach else at - reach - rows
         keep = edge_keep(at, rows, reach)
-        put_taps(taps_ref, taps(at)[1], mix(edge_ref[0, k], edge_ref[1, k]) * keep)
-
+        put_taps(taps_ref, at if at < reach else at - rows, mix(edge_ref[0, k], edge_ref[1, k]) * keep)
+
+    for copy in copies[:4]:
+        copy.wait()
     for at in range(reach):
         enter(at)
+    for copy in copies[4:]:
+        copy.wait()
     outside = [at for at in range(rows + 2 * reach - 2) if not reach <= at < reach + rows - 2]
     place = {at: k for k, at in enumerate(outside)}
     ready = reach + rows
@@ -293,7 +336,8 @@
         while ready < at + 3:
             enter(ready)
             ready += 1
-        steered_ref[place[at]] = conv(at) + twice(cols_ref[5])
+        total = conv_row(weight_ref, [taps(at + k) for k in range(3)])
+        steered_ref[place[at]] = total + twice(cols_ref[5])
 
     def own_rows():
         for k in range(rows):
@@ -305,10 +349,11 @@
 
 
 def second_kernel(
-    inner_ref, outer_ref, lat_ref, seen_ref, rows_ref, weight_ref,
+    inner_ref, outer_ref, lat_ref, seen_ref, rows_ref, weight_hbm,
     out_ref,
-    taps_ref, cols_ref,
+    taps_ref, cols_ref, weight_ref, sems,
 ):
+    copies = fetch([(weight_hbm.at[k], weight_ref.at[k]) for k in range(3)], sems)
     rows, chans, cols = lat_ref.shape
     wide = padded_lanes(chans)
     size = chans // GROUPS
@@ -322,7 +367,6 @@
     spread_columns(
         [mean_rows[0:1], scale_rows[0:1], 0.5 * rows_ref[5:6], rows_ref[6:7]], chans, cols_ref
     )
-    line = 3 * chans
     inside = max(rows - 2, 0)
     half = outer_ref.shape[0] // 2
     for at in range(rows + 2):
@@ -333,8 +377,11 @@
         value = half_act(value, twice(cols_ref[0]), twice(cols_ref[1]), twice(cols_ref[2]))
         keep = edge_keep(at, rows, 1)
         put_taps(taps_ref, at, value if keep is None else value * keep)
+        if at == 1:
+            for copy in copies:
+                copy.wait()
         if at >= 2:
-            total = matmul(weight_ref, taps_ref[(at - 2) * line : (at + 1) * line, :], 0)
+            total = conv_row(weight_ref, [line_of(taps_ref, at - 2 + k, chans) for k in range(3)])
             out_ref[at - 2] = (lat_ref[at - 2].astype(F32) + (total + twice(cols_ref[3]))).astype(BF16)
 
 
@@ -360,49 +407,51 @@
     wide = padded_lanes(chans)
     deep = 9 * chans
     patches = lax.axis_size("patch")
-    even = lax.rem(lax.axis_index("patch"), 2) == 0
-    near_edge = lax.dynamic_slice_in_dim(own, jnp.where(even, rows - REACH, 0), REACH, 0)
-    next_edge = lax.dynamic_slice_in_dim(own, jnp.where(even, 0, rows - REACH), REACH, 0)
-    near = lax.ppermute(near_edge, "patch", [(i, i ^ 1) for i in range(patches)])
-    steps = [(i, i + 1) for i in range(1, patches - 1, 2)]
-    following = lax.ppermute(next_edge, "patch", steps + [(j, i) for i, j in steps])
     swap = [(0, 1), (1, 0)]
-    far = lax.ppermute(own, "cfg", swap)
-    line = lambda vector: vector.reshape(1, -1)
+    dma = pltpu.SemaphoreType.DMA
+    turned = (3, chans, 3 * chans)
 
     tile_one = -(-3 * wide // LANES // 8) * 8
-    held, sent = pl.pallas_call(
+    held, sent, near_edge, next_edge = pl.pallas_call(
         stats_kernel,
         out_shape=[
             pltpu.VMEM((rows, chans, cols), BF16),
             pltpu.VMEM((2 * patches, tile_one, LANES), F32),
+            pltpu.HBM((REACH, chans, cols), BF16),
+            pltpu.HBM((REACH, chans, cols), BF16),
         ],
         in_specs=[ANY] * 3,
-        out_specs=[VMEM] * 2,
+        out_specs=[VMEM] * 2 + [ANY] * 2,
         scratch_shapes=[
             pltpu.VMEM(time_embed.shape, BF16),
             pltpu.VMEM(time_weight.shape, BF16),
-            pltpu.SemaphoreType.DMA((rows + 2,)),
+            dma((rows + 2,)),
+            dma((2,)),
         ],
         compiler_params=LIMIT,
         name="stats",
     )(in_hbm(own), in_hbm(time_embed), in_hbm(time_weight))
+    near = lax.ppermute(near_edge, "patch", [(i, i ^ 1) for i in range(patches)])
+    steps = [(i, i + 1) for i in range(1, patches - 1, 2)]
+    following = lax.ppermute(next_edge, "patch", steps + [(j, i) for i, j in steps])
     seen = everyone(sent, ("cfg", "patch"))
 
-    weights = (conv_one.reshape(deep, chans), conv_two.reshape(deep, chans))
-    *weights, _ = lax.optimization_barrier((*weights, sent))
-    turned_one, turned_two, vectors = pl.pallas_call(
+    weight_one, _ = lax.optimization_barrier((conv_one.reshape(deep, chans), sent))
+    turning = [pltpu.VMEM((deep, chans), BF16), pltpu.VMEM(turned, BF16)]
+    turned_one, vectors = pl.pallas_call(
         prepare_kernel,
-        out_shape=[pltpu.VMEM((chans, deep), BF16)] * 2 + [pltpu.VMEM((8, wide), F32)],
-        in_specs=[ANY] * 2 + [VMEM] * 8,
-        out_specs=[VMEM] * 3,
-        scratch_shapes=[pltpu.VMEM((deep, chans), BF16)] * 2 + [pltpu.SemaphoreType.DMA((2 * PARTS,))],
+        out_shape=[pltpu.HBM(turned, BF16), pltpu.VMEM((8, wide), F32)],
+        in_specs=[ANY] * 8 + [VMEM],
+        out_specs=[ANY, VMEM],
+        scratch_shapes=turning + [dma((6,)), dma((7,))] + [pltpu.VMEM((chans,), F32)] * 7,
         compiler_params=LIMIT,
         name="prepare",
     )(
-        in_hbm(weights[0]), in_hbm(weights[1]), line(gain_one), line(shift_one), line(bias_one),
-        line(time_bias), line(gain_two), line(shift_two), line(bias_two), line(steer_scale),
-    )
+        in_hbm(weight_one), *(in_hbm(v) for v in (gain_one, shift_one, bias_one,
+        time_bias, gain_two, shift_two, bias_two)), steer_scale.reshape(1, 1),
+    )
+    source, vectors = lax.optimization_barrier((own, vectors))
+    far = lax.ppermute(source, "cfg", swap)
     near, following, vectors, seen = lax.optimization_barrier((near, following, vectors, seen))
     far_near = lax.ppermute(near, "cfg", swap)
     far_next = lax.ppermute(following, "cfg", swap)
@@ -414,11 +463,14 @@
             pltpu.VMEM((rows * 3 * chans, cols), BF16),
             pltpu.VMEM((6, chans, LANES), F32),
         ],
-        in_specs=[VMEM] * 5,
+        in_specs=[VMEM, ANY, VMEM, VMEM, ANY],
         out_specs=[VMEM] * 3,
+        scratch_shapes=[
+            pltpu.VMEM((rows, chans, cols), BF16), pltpu.VMEM(turned, BF16), dma((rows + 3,)),
+        ],
         compiler_params=LIMIT,
         name="inner",
-    )(held, far, seen, vectors, turned_one)
+    )(held, far, seen, vectors, in_hbm(turned_one))
     tile_two = -(-2 * wide // LANES // 8) * 8
     outer, sent = pl.pallas_call(
         outer_kernel,
@@ -426,28 +478,44 @@
             pltpu.VMEM((2 * REACH, chans, cols), F32),
             pltpu.VMEM((patches, tile_two, LANES), F32),
         ],
-        in_specs=[VMEM] * 9,
+        in_specs=[ANY] * 4 + [VMEM] * 4 + [ANY],
         out_specs=[VMEM] * 2,
         scratch_shapes=[
             pltpu.VMEM((2 * REACH * 3 * chans, cols), BF16),
             pltpu.VMEM((2, 2 * REACH, chans, cols), BF16),
+            pltpu.VMEM(turned, BF16),
+            dma((7,)),
         ],
         compiler_params=LIMIT,
         name="outer",
-    )(near, following, far_near, far_next, inner, taps, columns, vectors, turned_one)
+    )(
+        near, following, far_near, far_next, inner, taps, columns, vectors, in_hbm(turned_one),
+    )
     seen = everyone(sent, "patch")
+    weight_two, _ = lax.optimization_barrier((conv_two.reshape(deep, chans), sent))
+    turned_two = pl.pallas_call(
+        turn_kernel,
+        out_shape=pltpu.HBM(turned, BF16),
+        in_specs=[ANY],
+        out_specs=ANY,
+        scratch_shapes=turning + [dma((6,))],
+        compiler_params=LIMIT,
+        name="turn",
+    )(in_hbm(weight_two))
     image = pl.pallas_call(
         second_kernel,
         out_shape=jax.ShapeDtypeStruct((rows, chans, cols), BF16),
-        in_specs=[VMEM] * 6,
+        in_specs=[VMEM] * 5 + [ANY],
         out_specs=VMEM,
         scratch_shapes=[
             pltpu.VMEM(((rows + 2) * 3 * chans, cols), BF16),
             pltpu.VMEM((4, chans, LANES), F32),
+            pltpu.VMEM(turned, BF16),
+            dma((3,)),
         ],
         compiler_params=LIMIT,
         name="second",
-    )(inner, outer, held, seen, vectors, turned_two)
+    )(inner, outer, held, seen, vectors, in_hbm(turned_two))
     return jnp.swapaxes(image, 1, 2)[None, None]
 
 

time: 47.5 us -> 70.3 us (1.48)
  Pallas kernels: 16.5 us -> 42.5 us
  starting transfers between devices: 11.9 us -> 7.6 us
  local copies, waits for them, and re-layouts: 3.33 us -> 0.01 us
  blocking collectives: 12.1 us -> 15.2 us
  waiting for transfers between devices: 2.49 us -> 3.85 us
    pallas_call x1, Pallas kernels: 2.48 us -> 21 us  [body(): pl.pallas_call(stats_kernel, out_shape=[pltpu.VMEM((rows, chans, cols), B...]
    all_to_all x1, blocking collectives: 12.1 us -> 15.2 us  [everyone(): return lax.all_to_all(tiles, axes, 0, 0)]
    pallas_call x1 -> x2, Pallas kernels: 3.1 us -> 6.02 us  [the longest x1 3.24 us: body(): pl.pallas_call(prepare_kernel, out_shape=[pltpu.HBM(turned, BF16), pltpu....]
    pallas_call x1, Pallas kernels: 2.66 us -> 5.05 us  [body(): pl.pallas_call(inner_kernel, out_shape=[pltpu.VMEM((max(rows - 2, 1), cha...]
    ppermute x1, starting transfers between devices: 5.05 us -> 3 us  [body(): lax.ppermute(near_edge, 'patch', [(i, i ^ 1) for i in range(patches)])]
    dynamic_slice x1 -> x0, local copies, waits for them, and re-layouts: 2 us -> none  [body(): lax.dynamic_slice_in_dim(own, jnp.where(even, 0, rows - REACH), REACH, 0)]
    all_to_all x1, starting transfers between devices: 4.91 us -> 3.35 us  [everyone(): return lax.all_to_all(tiles, axes, 0, 0)]
    all_to_all x1, waiting for transfers between devices: 2.48 us -> 3.83 us  [everyone(): return lax.all_to_all(tiles, axes, 0, 0)]
  transfers between devices with their start and end apart: 6 -> 6, of which waited for: 1 -> 1; matrix products, arithmetic and copies ran while one was open for 0% -> 0% of each run, Pallas kernels for 17% -> 16%
where the time goes in v6:
time: 70.3 us; the launch traced here: 69.9 us
  Pallas kernels  42.5 us (60%)
  blocking collectives  15.2 us (22%)
  starting transfers between devices  7.6 us (11%)
  waiting for transfers between devices  3.85 us (5%)
  between operations  0.75 us (1%)
    pallas_call x1, Pallas kernels, body(): pl.pallas_call(stats_kernel, out_shape=[pltpu.VMEM((rows, chans, cols), B...  21 us
    all_to_all x1, blocking collectives, everyone(): return lax.all_to_all(tiles, axes, 0, 0)  15.2 us
    pallas_call x1, Pallas kernels, body(): pl.pallas_call(outer_kernel, out_shape=[pltpu.VMEM((2 * REACH, chans, col...  5.25 us
    pallas_call x1, Pallas kernels, body(): pl.pallas_call(second_kernel, out_shape=jax.ShapeDtypeStruct((rows, chans...  5.17 us
    pallas_call x1, Pallas kernels, body(): pl.pallas_call(inner_kernel, out_shape=[pltpu.VMEM((max(rows - 2, 1), cha...  5.05 us
    all_to_all x1, waiting for transfers between devices, everyone(): return lax.all_to_all(tiles, axes, 0, 0)  3.83 us
    all_to_all x1, starting transfers between devices, everyone(): return lax.all_to_all(tiles, axes, 0, 0)  3.35 us
    pallas_call x1, Pallas kernels, body(): pl.pallas_call(prepare_kernel, out_shape=[pltpu.HBM(turned, BF16), pltpu....  3.24 us
  transfers between devices with their start and end apart: 6, of which 1 were waited for; matrix products, arithmetic and copies ran while one was open for 0% of the time, Pallas kernels for 16%

profile of v6, /device:TPU:0, one launch (start us, length us, event | category | flops | bytes accessed | tf_op | source)
XLA Modules:
  0.0 69.9 jit_solution(439586670858491552)
XLA Ops:
  0.0 0.0 copy-start
  0.0 21.0 %stats.1 = (bf16[4,320,256]{2,1,0:T(8,128)(2,1)S(1)}, f32[16,16,128]{2,1,0:T(8,128)S(1)}, bf16[2,320,256]{2,1,0:T(8,128)(2,1)}, bf16[2,320,256]{2,1,0:T(8,128)(2,1)}) custom-call(bf16[4,320,256]{2,1,0:T(8,128)(2,1)} %bitcast.12, bf16[1,1280]{1,0:T(2,128)(2,1)} %embed_hbm.1, bf16[160,320]{1,0:T(8,128)(2,1)} %weight_hbm.1), custom_call_target="tpu_custom_call" | custom-call | tf_op jit(solution)/shard_map/stats/pallas_call | solution.py:415
  21.0 3.0 %collective-permute-start.1 = (bf16[2,320,256]{2,1,0:T(8,128)(2,1)}, bf16[2,320,256]{2,1,0:T(8,128)(2,1)S(1)}, u32[]{:S(2)}, u32[]{:S(2)}) collective-permute-start(bf16[2,320,256]{2,1,0:T(8,128)(2,1)} %get-tuple-element.29), channel_id=1, source_target_pairs={{0,2},{2,0},{4,6},{6,4},{8,10},{10,8},{12,14},{14,12},{1,3},{3,1},... | collective-permute-start | bytes 983048 | tf_op jit(solution)/shard_map/ppermute | solution.py:434
  24.0 0.7 collective-permute-start.2
  25.4 3.2 %prepare.1 = (bf16[3,320,960]{2,1,0:T(8,128)(2,1)}, f32[8,384]{1,0:T(8,128)S(1)}) custom-call(bf16[2880,320]{1,0:T(8,128)(2,1)} %bitcast.10, f32[320]{0:T(512)} %gain_one.1, f32[320]{0:T(512)} %shift_one.1, f32[320]{0:T(512)} %bias_one.1, f32[320]{0:T(512)} %time_bias.1, f32[320]{0:T(512)} %gain_two.1, f32[320]{0:T(512)} %shift_two.1, f32[320]{0:T(512)} %bias_two.1, ...), custom_call_target="tpu_custom_call" | custom-call | tf_op jit(solution)/shard_map/prepare/pallas_call | solution.py:441
  28.6 0.0 copy-done
  28.6 0.1 collective-permute-start
  28.7 15.2 %all_to_all.10.seen_ref = f32[16,16,128]{2,1,0:T(8,128)S(1)} all-to-all(f32[16,16,128]{2,1,0:T(8,128)S(1)} %get-tuple-element.25), channel_id=1, replica_groups=mesh['cfg'=2,'patch'=8,'req'=2] {'cfg','patch'}, dimensions={0} | all-to-all | bytes 262144 | tf_op jit(solution)/shard_map/all_to_all | solution.py:389
  43.9 0.0 collective-permute-done.1.near_hbm
  43.9 0.0 collective-permute-done.2.next_hbm
  43.9 0.0 collective-permute-start.3
  43.9 0.5 collective-permute-start.4
  44.5 0.0 collective-permute-done.far_hbm
  44.5 5.0 %inner.1 = (f32[2,320,256]{2,1,0:T(8,128)S(1)}, bf16[3840,256]{1,0:T(8,128)(2,1)S(1)}, f32[6,320,128]{2,1,0:T(8,128)S(1)}) custom-call(bf16[4,320,256]{2,1,0:T(8,128)(2,1)S(1)} %get-tuple-element.24.own_ref.lat_ref, bf16[4,320,256]{2,1,0:T(8,128)(2,1)S(1)} %collective-permute-done.far_hbm, f32[16,16,128]{2,1,0:T(8,128)S(1)} %all_to_all.10.seen_ref, ...), custom_call_target="tpu_custom_call" | custom-call | tf_op jit(solution)/shard_map/inner/pallas_call | solution.py:459
  49.5 0.0 collective-permute-done.3.far_near_hbm
  49.5 0.0 collective-permute-done.4.far_next_hbm
  49.5 5.2 %outer.1 = (f32[4,320,256]{2,1,0:T(8,128)S(1)}, f32[8,8,128]{2,1,0:T(8,128)}) custom-call(bf16[2,320,256]{2,1,0:T(8,128)(2,1)S(1)} %collective-permute-done.1.near_hbm, bf16[2,320,256]{2,1,0:T(8,128)(2,1)S(1)} %collective-permute-done.2.next_hbm, bf16[2,320,256]{2,1,0:T(8,128)(2,1)S(1)} %collective-permute-done.3.far_near_hbm, ...), custom_call_target="tpu_custom_call" | custom-call | tf_op jit(solution)/shard_map/outer/pallas_call | solution.py:475
  54.8 3.4 %all-to-all-start.1 = ((f32[8,8,128]{2,1,0:T(8,128)}), f32[8,8,128]{2,1,0:T(8,128)S(1)}, u32[]{:S(2)}, u32[]{:S(2)}) async-start(f32[8,8,128]{2,1,0:T(8,128)} %get-tuple-element.41), calls=%async_computation.1 | async-start | bytes 65536 | tf_op jit(solution)/shard_map/all_to_all | solution.py:389
  58.1 2.8 %turn.1.weight_hbm = bf16[3,320,960]{2,1,0:T(8,128)(2,1)} custom-call(bf16[2880,320]{1,0:T(8,128)(2,1)} %bitcast.11), custom_call_target="tpu_custom_call" | custom-call | tf_op jit(solution)/shard_map/turn/pallas_call | solution.py:496
  60.9 3.8 %all-to-all-done.1.seen_ref = f32[8,8,128]{2,1,0:T(8,128)S(1)} async-done(((f32[8,8,128]{2,1,0:T(8,128)}), f32[8,8,128]{2,1,0:T(8,128)S(1)}, u32[]{:S(2)}, u32[]{:S(2)}) %all-to-all-start.1) | async-done | bytes 32800 | tf_op jit(solution)/shard_map/all_to_all | solution.py:389
  64.8 5.2 %second.1 = bf16[4,320,256]{2,1,0:T(8,128)(2,1)} custom-call(f32[2,320,256]{2,1,0:T(8,128)S(1)} %get-tuple-element.35.inner_ref, f32[4,320,256]{2,1,0:T(8,128)S(1)} %get-tuple-element.40.outer_ref, bf16[4,320,256]{2,1,0:T(8,128)(2,1)S(1)} %get-tuple-element.24.own_ref.lat_ref, f32[8,8,128]{2,1,0:T(8,128)S(1)} %all-to-all-done.1.seen_ref, ...), custom_call_target="tpu_custom_call" | custom-call | tf_op jit(solution)/shard_map/second/pallas_call | solution.py:505
Async XLA Ops:
  0.0 28.6 %copy-start = (bf16[1,1,4,256,320]{3,4,2,1,0:T(8,128)(2,1)S(1)}, bf16[1,1,4,256,320]{3,4,2,1,0:T(8,128)(2,1)}, u32[]{:S(2)}) copy-start(bf16[1,1,4,256,320]{3,4,2,1,0:T(8,128)(2,1)} %param.13) | copy-start | bytes 1966084
  21.0 22.9 %collective-permute-start.1 = (bf16[2,320,256]{2,1,0:T(8,128)(2,1)}, bf16[2,320,256]{2,1,0:T(8,128)(2,1)S(1)}, u32[]{:S(2)}, u32[]{:S(2)}) collective-permute-start(bf16[2,320,256]{2,1,0:T(8,128)(2,1)} %get-tuple-element.29), channel_id=1, source_target_pairs={{0,2},{2,0},{4,6},{6,4},{8,10},{10,8},{12,14},{14,12},{1,3},{3,1},... | collective-permute-start | bytes 983048 | tf_op jit(solution)/shard_map/ppermute | solution.py:434
  24.0 19.9 %collective-permute-start.2 = (bf16[2,320,256]{2,1,0:T(8,128)(2,1)}, bf16[2,320,256]{2,1,0:T(8,128)(2,1)S(1)}, u32[]{:S(2)}, u32[]{:S(2)}) collective-permute-start(bf16[2,320,256]{2,1,0:T(8,128)(2,1)} %get-tuple-element.30), channel_id=1, source_target_pairs={{2,4},{6,8},{10,12},{4,2},{8,6},{12,10},{3,5},{7,9},{11,13},{5,3},... | collective-permute-start | bytes 983048 | tf_op jit(solution)/shard_map/ppermute | solution.py:436
  28.6 15.8 %collective-permute-start = (bf16[4,320,256]{2,1,0:T(8,128)(2,1)S(1)}, bf16[4,320,256]{2,1,0:T(8,128)(2,1)S(1)}, u32[]{:S(2)}, u32[]{:S(2)}) collective-permute-start(bf16[4,320,256]{2,1,0:T(8,128)(2,1)S(1)} %bitcast.13), channel_id=1, source_target_pairs={{0,16},{16,0},{1,17},{17,1},{2,18},{18,2},{3,19},{19,3},{4,20},{20... | collective-permute-start | bytes 1966088 | tf_op jit(solution)/shard_map/ppermute | solution.py:454
  43.9 5.6 %collective-permute-start.3 = (bf16[2,320,256]{2,1,0:T(8,128)(2,1)S(1)}, bf16[2,320,256]{2,1,0:T(8,128)(2,1)S(1)}, u32[]{:S(2)}, u32[]{:S(2)}) collective-permute-start(bf16[2,320,256]{2,1,0:T(8,128)(2,1)S(1)} %collective-permute-done.1.near_hbm), channel_id=1, source_target_pairs={{0,16},{16,0},{1,17},{17,1},{2,18},{18,2},{3,19},{19,3},{4,20},{20... | collective-permute-start | bytes 983048 | tf_op jit(solution)/shard_map/ppermute | solution.py:456
  43.9 5.6 %collective-permute-start.4 = (bf16[2,320,256]{2,1,0:T(8,128)(2,1)S(1)}, bf16[2,320,256]{2,1,0:T(8,128)(2,1)S(1)}, u32[]{:S(2)}, u32[]{:S(2)}) collective-permute-start(bf16[2,320,256]{2,1,0:T(8,128)(2,1)S(1)} %collective-permute-done.2.next_hbm), channel_id=1, source_target_pairs={{0,16},{16,0},{1,17},{17,1},{2,18},{18,2},{3,19},{19,3},{4,20},{20... | collective-permute-start | bytes 983048 | tf_op jit(solution)/shard_map/ppermute | solution.py:457
  54.8 10.0 %all-to-all-start.1 = ((f32[8,8,128]{2,1,0:T(8,128)}), f32[8,8,128]{2,1,0:T(8,128)S(1)}, u32[]{:S(2)}, u32[]{:S(2)}) async-start(f32[8,8,128]{2,1,0:T(8,128)} %get-tuple-element.41), calls=%async_computation.1 | async-start | bytes 65536 | tf_op jit(solution)/shard_map/all_to_all | solution.py:389

commit v7 on v4

--- a/solution.py
+++ b/solution.py
@@ -105,14 +105,25 @@
     )
 
 
-def stats_kernel(lat_hbm, embed_hbm, weight_hbm, lat_ref, out_ref, embed_ref, weight_ref, sems):
+def stats_kernel(
+    lat_hbm, embed_hbm, weight_hbm,
+    lat_ref, out_ref, near_ref, next_ref,
+    embed_ref, weight_ref, sems, edge_sems,
+):
     rows, chans, _ = lat_ref.shape
     copies = [
         pltpu.make_async_copy(lat_hbm.at[k], lat_ref.at[k], sems.at[k]) for k in range(rows)
     ]
     copies.append(pltpu.make_async_copy(embed_hbm, embed_ref, sems.at[rows]))
     copies.append(pltpu.make_async_copy(weight_hbm, weight_ref, sems.at[rows + 1]))
-    for copy in copies:
+    reach = near_ref.shape[0]
+    last = rows - reach
+    near_at = jnp.where(lax.rem(lax.axis_index("patch"), 2) == 0, last, 0)
+    edges = [
+        pltpu.make_async_copy(lat_hbm.at[pl.ds(near_at, reach)], near_ref, edge_sems.at[0]),
+        pltpu.make_async_copy(lat_hbm.at[pl.ds(last - near_at, reach)], next_ref, edge_sems.at[1]),
+    ]
+    for copy in copies + edges:
         copy.start()
     waits = list(copies[:rows])
 
@@ -133,6 +144,8 @@
     act = (embed / (1.0 + jnp.exp(-embed))).astype(BF16)
     time_part = jnp.dot(act, weight_ref[...], preferred_element_type=F32)[0:1]
     put_rows([mean, squares, widen(time_part, wide)], out_ref)
+    for copy in edges:
+        copy.wait()
 
 
 PARTS = 3
@@ -360,33 +373,32 @@
     wide = padded_lanes(chans)
     deep = 9 * chans
     patches = lax.axis_size("patch")
-    even = lax.rem(lax.axis_index("patch"), 2) == 0
-    near_edge = lax.dynamic_slice_in_dim(own, jnp.where(even, rows - REACH, 0), REACH, 0)
-    next_edge = lax.dynamic_slice_in_dim(own, jnp.where(even, 0, rows - REACH), REACH, 0)
-    near = lax.ppermute(near_edge, "patch", [(i, i ^ 1) for i in range(patches)])
-    steps = [(i, i + 1) for i in range(1, patches - 1, 2)]
-    following = lax.ppermute(next_edge, "patch", steps + [(j, i) for i, j in steps])
     swap = [(0, 1), (1, 0)]
-    far = lax.ppermute(own, "cfg", swap)
     line = lambda vector: vector.reshape(1, -1)
 
     tile_one = -(-3 * wide // LANES // 8) * 8
-    held, sent = pl.pallas_call(
+    held, sent, near_edge, next_edge = pl.pallas_call(
         stats_kernel,
         out_shape=[
             pltpu.VMEM((rows, chans, cols), BF16),
             pltpu.VMEM((2 * patches, tile_one, LANES), F32),
+            pltpu.VMEM((REACH, chans, cols), BF16),
+            pltpu.VMEM((REACH, chans, cols), BF16),
         ],
         in_specs=[ANY] * 3,
-        out_specs=[VMEM] * 2,
+        out_specs=[VMEM] * 4,
         scratch_shapes=[
             pltpu.VMEM(time_embed.shape, BF16),
             pltpu.VMEM(time_weight.shape, BF16),
             pltpu.SemaphoreType.DMA((rows + 2,)),
+            pltpu.SemaphoreType.DMA((2,)),
         ],
         compiler_params=LIMIT,
         name="stats",
     )(in_hbm(own), in_hbm(time_embed), in_hbm(time_weight))
+    near = lax.ppermute(near_edge, "patch", [(i, i ^ 1) for i in range(patches)])
+    steps = [(i, i + 1) for i in range(1, patches - 1, 2)]
+    following = lax.ppermute(next_edge, "patch", steps + [(j, i) for i, j in steps])
     seen = everyone(sent, ("cfg", "patch"))
 
     weights = (conv_one.reshape(deep, chans), conv_two.reshape(deep, chans))
@@ -403,6 +415,8 @@
         in_hbm(weights[0]), in_hbm(weights[1]), line(gain_one), line(shift_one), line(bias_one),
         line(time_bias), line(gain_two), line(shift_two), line(bias_two), line(steer_scale),
     )
+    source, vectors = lax.optimization_barrier((own, vectors))
+    far = lax.ppermute(source, "cfg", swap)
     near, following, vectors, seen = lax.optimization_barrier((near, following, vectors, seen))
     far_near = lax.ppermute(near, "cfg", swap)
     far_next = lax.ppermute(following, "cfg", swap)

time: 47.5 us -> 49.3 us (1.038)
  blocking collectives: 12.1 us -> 24.3 us
  starting transfers between devices: 11.9 us -> 4.25 us
  waiting for transfers between devices: 2.49 us -> 0.01 us
  Pallas kernels: 16.5 us -> 14.8 us
  local copies, waits for them, and re-layouts: 3.33 us -> 4.79 us
    all_to_all x1 -> x2, blocking collectives: 12.1 us -> 24.3 us  [everyone(): return lax.all_to_all(tiles, axes, 0, 0)]
    all_to_all x1 -> x0, starting transfers between devices: 4.91 us -> none  [everyone(): return lax.all_to_all(tiles, axes, 0, 0)]
    reshape x7, local copies, waits for them, and re-layouts: 0.02 us -> 4.78 us  [body(): line = lambda vector: vector.reshape(1, -1)]
    all_to_all x1 -> x0, waiting for transfers between devices: 2.48 us -> none  [everyone(): return lax.all_to_all(tiles, axes, 0, 0)]
    ppermute x1, starting transfers between devices: 5.05 us -> 3 us  [body(): lax.ppermute(near_edge, 'patch', [(i, i ^ 1) for i in range(patches)])]
    dynamic_slice x1 -> x0, local copies, waits for them, and re-layouts: 2 us -> none  [body(): lax.dynamic_slice_in_dim(own, jnp.where(even, 0, rows - REACH), REACH, 0)]
    unnamed x18 -> x2, local copies, waits for them, and re-layouts: 1.31 us -> 0.01 us
    pallas_call x1, Pallas kernels: 4.1 us -> 3.01 us  [body(): pl.pallas_call(outer_kernel, out_shape=[pltpu.VMEM((2 * REACH, chans, col...]
  transfers between devices with their start and end apart: 6 -> 5, of which waited for: 1 -> 0; matrix products, arithmetic and copies ran while one was open for 0% -> 10% of each run, Pallas kernels for 17% -> 12%
where the time goes in v7:
time: 49.3 us; the launch traced here: 48.9 us
  blocking collectives  24.3 us (49%)
  Pallas kernels  14.8 us (30%)
  local copies, waits for them, and re-layouts  4.79 us (10%)
  starting transfers between devices  4.25 us (9%)
  between operations  0.73 us (1%)
    all_to_all x2, blocking collectives, everyone(): return lax.all_to_all(tiles, axes, 0, 0)  24.3 us
    reshape x7, local copies, waits for them, and re-layouts, body(): line = lambda vector: vector.reshape(1, -1)  4.78 us
    pallas_call x1, Pallas kernels, body(): pl.pallas_call(second_kernel, out_shape=jax.ShapeDtypeStruct((rows, chans...  4.18 us
    pallas_call x1, Pallas kernels, body(): pl.pallas_call(prepare_kernel, out_shape=[pltpu.VMEM((chans, deep), BF16)...  3.16 us
    pallas_call x1, Pallas kernels, body(): pl.pallas_call(outer_kernel, out_shape=[pltpu.VMEM((2 * REACH, chans, col...  3.01 us
    ppermute x1, starting transfers between devices, body(): lax.ppermute(near_edge, 'patch', [(i, i ^ 1) for i in range(patches)])  3 us
    pallas_call x1, Pallas kernels, body(): pl.pallas_call(inner_kernel, out_shape=[pltpu.VMEM((max(rows - 2, 1), cha...  2.65 us
    pallas_call x1, Pallas kernels, body(): pl.pallas_call(stats_kernel, out_shape=[pltpu.VMEM((rows, chans, cols), B...  1.85 us
  transfers between devices with their start and end apart: 5, of which 0 were waited for; matrix products, arithmetic and copies ran while one was open for 10% of the time, Pallas kernels for 12%

profile of v7, /device:TPU:0, one launch (start us, length us, event | category | flops | bytes accessed | tf_op | source)
XLA Modules:
  0.0 48.9 jit_solution(12611449545057254258)
XLA Ops:
  0.0 1.8 %stats.1 = (bf16[4,320,256]{2,1,0:T(8,128)(2,1)S(1)}, f32[16,16,128]{2,1,0:T(8,128)S(1)}, bf16[2,320,256]{2,1,0:T(8,128)(2,1)S(1)}, bf16[2,320,256]{2,1,0:T(8,128)(2,1)S(1)}) custom-call(bf16[4,320,256]{2,1,0:T(8,128)(2,1)} %bitcast.12, bf16[1,1280]{1,0:T(2,128)(2,1)} %embed_hbm.1, bf16[160,320]{1,0:T(8,128)(2,1)} %weight_hbm.1), custom_call_target="tpu_custom_call" | custom-call | tf_op jit(solution)/shard_map/stats/pallas_call | solution.py:380
  1.9 3.0 %collective-permute-start.1 = (bf16[2,320,256]{2,1,0:T(8,128)(2,1)S(1)}, bf16[2,320,256]{2,1,0:T(8,128)(2,1)S(1)}, u32[]{:S(2)}, u32[]{:S(2)}) collective-permute-start(bf16[2,320,256]{2,1,0:T(8,128)(2,1)S(1)} %get-tuple-element.31), channel_id=1, source_target_pairs={{0,2},{2,0},{4,6},{6,4},{8,10},{10,8},{12,14},{14,12},{1,3},{3,1},... | collective-permute-start | bytes 983048 | tf_op jit(solution)/shard_map/ppermute | solution.py:399
  4.9 0.7 %collective-permute-start.2 = (bf16[2,320,256]{2,1,0:T(8,128)(2,1)S(1)}, bf16[2,320,256]{2,1,0:T(8,128)(2,1)S(1)}, u32[]{:S(2)}, u32[]{:S(2)}) collective-permute-start(bf16[2,320,256]{2,1,0:T(8,128)(2,1)S(1)} %get-tuple-element.32), channel_id=1, source_target_pairs={{2,4},{6,8},{10,12},{4,2},{8,6},{12,10},{3,5},{7,9},{11,13},{5,3},... | collective-permute-start | bytes 983048 | tf_op jit(solution)/shard_map/ppermute | solution.py:401
  6.2 0.7 %reshape.32.gain_one = f32[1,320]{1,0:T(1,128)S(1)} reshape(f32[320]{0:T(512)} %param.16) | data formatting | bytes 2560 | tf_op jit(solution)/shard_map/reshape | solution.py:377
  6.9 0.7 %reshape.33.shift_one = f32[1,320]{1,0:T(1,128)S(1)} reshape(f32[320]{0:T(512)} %param.17) | data formatting | bytes 2560 | tf_op jit(solution)/shard_map/reshape | solution.py:377
  7.6 0.7 %reshape.34.bias_one = f32[1,320]{1,0:T(1,128)S(1)} reshape(f32[320]{0:T(512)} %param.19) | data formatting | bytes 2560 | tf_op jit(solution)/shard_map/reshape | solution.py:377
  8.2 0.7 %reshape.35.time_bias = f32[1,320]{1,0:T(1,128)S(1)} reshape(f32[320]{0:T(512)} %param.21) | data formatting | bytes 2560 | tf_op jit(solution)/shard_map/reshape | solution.py:377
  8.9 0.7 %reshape.36.gain_two = f32[1,320]{1,0:T(1,128)S(1)} reshape(f32[320]{0:T(512)} %param.22) | data formatting | bytes 2560 | tf_op jit(solution)/shard_map/reshape | solution.py:377
  9.6 0.7 %reshape.37.shift_two = f32[1,320]{1,0:T(1,128)S(1)} reshape(f32[320]{0:T(512)} %param.23) | data formatting | bytes 2560 | tf_op jit(solution)/shard_map/reshape | solution.py:377
  10.3 0.7 %reshape.38.bias_two = f32[1,320]{1,0:T(1,128)S(1)} reshape(f32[320]{0:T(512)} %param.25) | data formatting | bytes 2560 | tf_op jit(solution)/shard_map/reshape | solution.py:377
  11.0 3.2 %prepare.1 = (bf16[320,2880]{1,0:T(8,128)(2,1)S(1)}, bf16[320,2880]{1,0:T(8,128)(2,1)S(1)}, f32[8,384]{1,0:T(8,128)S(1)}) custom-call(bf16[2880,320]{1,0:T(8,128)(2,1)} %bitcast.10, bf16[2880,320]{1,0:T(8,128)(2,1)} %bitcast.11, f32[1,320]{1,0:T(1,128)S(1)} %reshape.32.gain_one, f32[1,320]{1,0:T(1,128)S(1)} %reshape.33.shift_one, ...), custom_call_target="tpu_custom_call" | custom-call | tf_op jit(solution)/shard_map/prepare/pallas_call | solution.py:406
  14.1 0.1 collective-permute-start
  14.2 15.2 %all_to_all.10.seen_ref = f32[16,16,128]{2,1,0:T(8,128)S(1)} all-to-all(f32[16,16,128]{2,1,0:T(8,128)S(1)} %get-tuple-element.26), channel_id=1, replica_groups=mesh['cfg'=2,'patch'=8,'req'=2] {'cfg','patch'}, dimensions={0} | all-to-all | bytes 262144 | tf_op jit(solution)/shard_map/all_to_all | solution.py:355
  29.5 0.0 collective-permute-done.1.near_ref
  29.5 0.0 collective-permute-done.2.next_ref
  29.5 0.0 collective-permute-start.3
  29.5 0.5 %collective-permute-start.4 = (bf16[2,320,256]{2,1,0:T(8,128)(2,1)S(1)}, bf16[2,320,256]{2,1,0:T(8,128)(2,1)S(1)}, u32[]{:S(2)}, u32[]{:S(2)}) collective-permute-start(bf16[2,320,256]{2,1,0:T(8,128)(2,1)S(1)} %collective-permute-done.2.next_ref), channel_id=1, source_target_pairs={{0,16},{16,0},{1,17},{17,1},{2,18},{18,2},{3,19},{19,3},{4,20},{20... | collective-permute-start | bytes 983048 | tf_op jit(solution)/shard_map/ppermute | solution.py:422
  30.0 0.0 collective-permute-done.far_ref
  30.0 2.6 %inner.1 = (f32[2,320,256]{2,1,0:T(8,128)S(1)}, bf16[3840,256]{1,0:T(8,128)(2,1)S(1)}, f32[6,320,128]{2,1,0:T(8,128)S(1)}) custom-call(bf16[4,320,256]{2,1,0:T(8,128)(2,1)S(1)} %get-tuple-element.25.own_ref.lat_ref, bf16[4,320,256]{2,1,0:T(8,128)(2,1)S(1)} %collective-permute-done.far_ref, f32[16,16,128]{2,1,0:T(8,128)S(1)} %all_to_all.10.seen_ref, ...), custom_call_target="tpu_custom_call" | custom-call | tf_op jit(solution)/shard_map/inner/pallas_call | solution.py:424
  32.6 0.0 collective-permute-done.3.far_near_ref
  32.6 0.0 collective-permute-done.4.far_next_ref
  32.7 3.0 %outer.1 = (f32[4,320,256]{2,1,0:T(8,128)S(1)}, f32[8,8,128]{2,1,0:T(8,128)S(1)}) custom-call(bf16[2,320,256]{2,1,0:T(8,128)(2,1)S(1)} %collective-permute-done.1.near_ref, bf16[2,320,256]{2,1,0:T(8,128)(2,1)S(1)} %collective-permute-done.2.next_ref, bf16[2,320,256]{2,1,0:T(8,128)(2,1)S(1)} %collective-permute-done.3.far_near_ref, ...), custom_call_target="tpu_custom_call" | custom-call | tf_op jit(solution)/shard_map/outer/pallas_call | solution.py:437
  35.7 9.1 %all_to_all.11.seen_ref = f32[8,8,128]{2,1,0:T(8,128)S(1)} all-to-all(f32[8,8,128]{2,1,0:T(8,128)S(1)} %get-tuple-element.43), channel_id=1, replica_groups=mesh['cfg'=2,'patch'=8,'req'=2] {'patch'}, dimensions={0} | all-to-all | bytes 65536 | tf_op jit(solution)/shard_map/all_to_all | solution.py:355
  44.7 4.2 %second.1 = bf16[4,320,256]{2,1,0:T(8,128)(2,1)} custom-call(f32[2,320,256]{2,1,0:T(8,128)S(1)} %get-tuple-element.37.inner_ref, f32[4,320,256]{2,1,0:T(8,128)S(1)} %get-tuple-element.42.outer_ref, bf16[4,320,256]{2,1,0:T(8,128)(2,1)S(1)} %get-tuple-element.25.own_ref.lat_ref, f32[8,8,128]{2,1,0:T(8,128)S(1)} %all_to_all.11.seen_ref, ...), custom_call_target="tpu_custom_call" | custom-call | tf_op jit(solution)/shard_map/second/pallas_call | solution.py:453
  (2 shorter events, 0.0 us)
Async XLA Ops:
  1.9 27.6 %collective-permute-start.1 = (bf16[2,320,256]{2,1,0:T(8,128)(2,1)S(1)}, bf16[2,320,256]{2,1,0:T(8,128)(2,1)S(1)}, u32[]{:S(2)}, u32[]{:S(2)}) collective-permute-start(bf16[2,320,256]{2,1,0:T(8,128)(2,1)S(1)} %get-tuple-element.31), channel_id=1, source_target_pairs={{0,2},{2,0},{4,6},{6,4},{8,10},{10,8},{12,14},{14,12},{1,3},{3,1},... | collective-permute-start | bytes 983048 | tf_op jit(solution)/shard_map/ppermute | solution.py:399
  4.9 24.6 %collective-permute-start.2 = (bf16[2,320,256]{2,1,0:T(8,128)(2,1)S(1)}, bf16[2,320,256]{2,1,0:T(8,128)(2,1)S(1)}, u32[]{:S(2)}, u32[]{:S(2)}) collective-permute-start(bf16[2,320,256]{2,1,0:T(8,128)(2,1)S(1)} %get-tuple-element.32), channel_id=1, source_target_pairs={{2,4},{6,8},{10,12},{4,2},{8,6},{12,10},{3,5},{7,9},{11,13},{5,3},... | collective-permute-start | bytes 983048 | tf_op jit(solution)/shard_map/ppermute | solution.py:401
  11.0 3.2 %copy-start = (bf16[1,1,4,256,320]{3,4,2,1,0:T(8,128)(2,1)S(1)}, bf16[1,1,4,256,320]{3,4,2,1,0:T(8,128)(2,1)}, u32[]{:S(2)}) copy-start(bf16[1,1,4,256,320]{3,4,2,1,0:T(8,128)(2,1)} %param.13) | copy-start | bytes 1966084
  14.1 15.8 %collective-permute-start = (bf16[4,320,256]{2,1,0:T(8,128)(2,1)S(1)}, bf16[4,320,256]{2,1,0:T(8,128)(2,1)S(1)}, u32[]{:S(2)}, u32[]{:S(2)}) collective-permute-start(bf16[4,320,256]{2,1,0:T(8,128)(2,1)S(1)} %bitcast.13), channel_id=1, source_target_pairs={{0,16},{16,0},{1,17},{17,1},{2,18},{18,2},{3,19},{19,3},{4,20},{20... | collective-permute-start | bytes 1966088 | tf_op jit(solution)/shard_map/ppermute | solution.py:419
  29.5 3.2 %collective-permute-start.3 = (bf16[2,320,256]{2,1,0:T(8,128)(2,1)S(1)}, bf16[2,320,256]{2,1,0:T(8,128)(2,1)S(1)}, u32[]{:S(2)}, u32[]{:S(2)}) collective-permute-start(bf16[2,320,256]{2,1,0:T(8,128)(2,1)S(1)} %collective-permute-done.1.near_ref), channel_id=1, source_target_pairs={{0,16},{16,0},{1,17},{17,1},{2,18},{18,2},{3,19},{19,3},{4,20},{20... | collective-permute-start | bytes 983048 | tf_op jit(solution)/shard_map/ppermute | solution.py:421
  29.5 3.2 %collective-permute-start.4 = (bf16[2,320,256]{2,1,0:T(8,128)(2,1)S(1)}, bf16[2,320,256]{2,1,0:T(8,128)(2,1)S(1)}, u32[]{:S(2)}, u32[]{:S(2)}) collective-permute-start(bf16[2,320,256]{2,1,0:T(8,128)(2,1)S(1)} %collective-permute-done.2.next_ref), channel_id=1, source_target_pairs={{0,16},{16,0},{1,17},{17,1},{2,18},{18,2},{3,19},{19,3},{4,20},{20... | collective-permute-start | bytes 983048 | tf_op jit(solution)/shard_map/ppermute | solution.py:422

commit v8 on v7

--- a/solution.py
+++ b/solution.py
@@ -86,23 +86,26 @@
     wide = padded_lanes(chans)
     both = jnp.concatenate([both, jnp.zeros((wide - chans, LANES), F32)], axis=0)
     turned = both.T
-    return turned[0:1], turned[1:2]
+    return turned[0:1, :chans], turned[1:2, :chans]
 
 
 def put_rows(tile_rows, out_ref):
-    peers, height, _ = out_ref.shape
-    lines = [row[:, at : at + LANES] for row in tile_rows for at in range(0, row.shape[1], LANES)]
-    if len(lines) < height:
-        lines.append(jnp.zeros((height - len(lines), LANES), F32))
-    tile = jnp.concatenate(lines, axis=0)
+    height = out_ref.shape[1]
+    flat = widen(jnp.concatenate(tile_rows, axis=1), height * LANES)
+    tile = jnp.concatenate([flat[:, at : at + LANES] for at in range(0, height * LANES, LANES)], axis=0)
     out_ref[...] = jnp.broadcast_to(tile[None], out_ref.shape)
 
 
-def get_rows(seen_ref, first, peers, which, wide):
-    lines = wide // LANES
-    return jnp.concatenate(
-        [seen_ref[pl.ds(first, peers), which * lines + k, :] for k in range(lines)], axis=1
-    )
+def get_rows(seen_ref, first, peers, which, chans):
+    start, end = which * chans, (which + 1) * chans
+    lines = range(start // LANES, -(-end // LANES))
+    flat = jnp.concatenate([seen_ref[pl.ds(first, peers), k, :] for k in lines], axis=1)
+    start -= lines[0] * LANES
+    return widen(flat[:, start : start + chans], padded_lanes(chans))
+
+
+def tile_height(chans, rows):
+    return -(-rows * chans // LANES // 8) * 8
 
 
 def stats_kernel(
@@ -133,7 +136,6 @@
                 waits.pop(0).wait()
             yield lat_ref[k].astype(F32)
 
-    wide = padded_lanes(chans)
     mean, squares = channel_moments(values, chans)
     copies[rows].wait()
     copies[rows + 1].wait()
@@ -143,34 +145,43 @@
     embed = pltpu.roll(embed, length - lax.axis_index("patch") * own, 1)[:, :own]
     act = (embed / (1.0 + jnp.exp(-embed))).astype(BF16)
     time_part = jnp.dot(act, weight_ref[...], preferred_element_type=F32)[0:1]
-    put_rows([mean, squares, widen(time_part, wide)], out_ref)
+    put_rows([mean, squares, time_part], out_ref)
     for copy in edges:
         copy.wait()
 
 
-PARTS = 3
+def parts_of(deep, part=8 * LANES):
+    return [(at, min(part, deep - at)) for at in range(0, deep, part)]
+
+
+def fetch(pairs, sems, first=0):
+    copies = [pltpu.make_async_copy(a, b, sems.at[first + k]) for k, (a, b) in enumerate(pairs)]
+    for copy in copies:
+        copy.start()
+    return copies
 
 
 def prepare_kernel(
     one_hbm, two_hbm, gain_one, shift_one, bias_one, time_bias, gain_two, shift_two, bias_two, steer,
-    one_out, two_out, rows_ref, one_ref, two_ref, sems,
-):
-    deep = one_ref.shape[0]
-    part = deep // PARTS
-    jobs = []
-    for k, (source, held, target) in enumerate(((one_hbm, one_ref, one_out), (two_hbm, two_ref, two_out))):
-        for at in range(PARTS):
-            here = pl.ds(at * part, part)
-            copy = pltpu.make_async_copy(source.at[here], held.at[here], sems.at[k * PARTS + at])
-            copy.start()
-            jobs.append((copy, held, target, at * part))
+    one_out, two_out, rows_ref, one_ref, two_ref, sems, row_sems, *vector_refs,
+):
+    vectors = (gain_one, shift_one, bias_one, time_bias, gain_two, shift_two, bias_two)
+    lines = fetch(zip(vectors, vector_refs), row_sems)
+    parts = parts_of(one_ref.shape[0])
+    sides = ((one_hbm, one_ref, one_out), (two_hbm, two_ref, two_out))
+    copies = [
+        fetch([(a.at[pl.ds(*p)], b.at[pl.ds(*p)]) for p in parts], sems, k * len(parts))
+        for k, (a, b, _) in enumerate(sides)
+    ]
+    for line in lines:
+        line.wait()
     wide = rows_ref.shape[1]
-    vectors = (gain_one, shift_one, bias_one, time_bias, gain_two, shift_two, bias_two)
-    lines = [widen(v[...], wide) for v in vectors]
-    rows_ref[...] = jnp.concatenate(lines + [jnp.broadcast_to(steer[...], (1, wide))], axis=0)
-    for copy, held, target, at in jobs:
-        copy.wait()
-        target[:, at : at + part] = held[at : at + part, :].T
+    rows = [widen(v[...].reshape(1, -1), wide) for v in vector_refs]
+    rows_ref[...] = jnp.concatenate(rows + [jnp.broadcast_to(steer[...], (1, wide))], axis=0)
+    for waits, (_, held, target) in zip(copies, sides):
+        for wait, (at, size) in zip(waits, parts):
+            wait.wait()
+            target[:, at : at + size] = held[at : at + size, :].T
 
 
 def spread_columns(rows, chans, cols_ref):
@@ -235,11 +246,11 @@
     cfg, peers = lax.axis_index("cfg"), lax.axis_size("patch")
     mask = same_group(wide, size)
     starts = (cfg * peers, (1 - cfg) * peers)
-    means = [get_rows(seen_ref, s, peers, 0, wide) for s in starts]
-    squares = [get_rows(seen_ref, s, peers, 1, wide) for s in starts]
+    means = [get_rows(seen_ref, s, peers, 0, chans) for s in starts]
+    squares = [get_rows(seen_ref, s, peers, 1, chans) for s in starts]
     mean_rows, var_rows = group_stats(means, squares, float(rows * cols), mask, size)
     scale_rows = lax.rsqrt(var_rows + EPS) * (0.5 * rows_ref[0:1])
-    times = jnp.sum(get_rows(seen_ref, 0, peers, 2, wide), axis=0, keepdims=True)
+    times = jnp.sum(get_rows(seen_ref, 0, peers, 2, chans), axis=0, keepdims=True)
     added = times + (rows_ref[3:4] + rows_ref[2:3])
     spread_columns(
         [mean_rows[0:1], scale_rows[0:1], mean_rows[1:2], scale_rows[1:2], 0.5 * rows_ref[1:2], added],
@@ -328,7 +339,7 @@
     peers = lax.axis_size("patch")
     mask = same_group(wide, size)
     mean_rows, var_rows = group_stats(
-        [get_rows(seen_ref, 0, peers, 0, wide)], [get_rows(seen_ref, 0, peers, 1, wide)],
+        [get_rows(seen_ref, 0, peers, 0, chans)], [get_rows(seen_ref, 0, peers, 1, chans)],
         float(rows * cols), mask, size,
     )
     scale_rows = lax.rsqrt(var_rows + EPS) * (0.5 * rows_ref[4:5])
@@ -376,7 +387,7 @@
     swap = [(0, 1), (1, 0)]
     line = lambda vector: vector.reshape(1, -1)
 
-    tile_one = -(-3 * wide // LANES // 8) * 8
+    tile_one = tile_height(chans, 3)
     held, sent, near_edge, next_edge = pl.pallas_call(
         stats_kernel,
         out_shape=[
@@ -402,20 +413,21 @@
     seen = everyone(sent, ("cfg", "patch"))
 
     weights = (conv_one.reshape(deep, chans), conv_two.reshape(deep, chans))
-    *weights, _ = lax.optimization_barrier((*weights, sent))
+    source, *weights, _ = lax.optimization_barrier((own, *weights, sent))
     turned_one, turned_two, vectors = pl.pallas_call(
         prepare_kernel,
         out_shape=[pltpu.VMEM((chans, deep), BF16)] * 2 + [pltpu.VMEM((8, wide), F32)],
-        in_specs=[ANY] * 2 + [VMEM] * 8,
+        in_specs=[ANY] * 9 + [VMEM],
         out_specs=[VMEM] * 3,
-        scratch_shapes=[pltpu.VMEM((deep, chans), BF16)] * 2 + [pltpu.SemaphoreType.DMA((2 * PARTS,))],
+        scratch_shapes=[pltpu.VMEM((deep, chans), BF16)] * 2
+        + [pltpu.SemaphoreType.DMA((2 * len(parts_of(deep)),)), pltpu.SemaphoreType.DMA((7,))]
+        + [pltpu.VMEM((chans,), F32)] * 7,
         compiler_params=LIMIT,
         name="prepare",
     )(
-        in_hbm(weights[0]), in_hbm(weights[1]), line(gain_one), line(shift_one), line(bias_one),
-        line(time_bias), line(gain_two), line(shift_two), line(bias_two), line(steer_scale),
-    )
-    source, vectors = lax.optimization_barrier((own, vectors))
+        in_hbm(weights[0]), in_hbm(weights[1]), in_hbm(gain_one), in_hbm(shift_one), in_hbm(bias_one),
+        in_hbm(time_bias), in_hbm(gain_two), in_hbm(shift_two), in_hbm(bias_two), line(steer_scale),
+    )
     far = lax.ppermute(source, "cfg", swap)
     near, following, vectors, seen = lax.optimization_barrier((near, following, vectors, seen))
     far_near = lax.ppermute(near, "cfg", swap)
@@ -433,7 +445,7 @@
         compiler_params=LIMIT,
         name="inner",
     )(held, far, seen, vectors, turned_one)
-    tile_two = -(-2 * wide // LANES // 8) * 8
+    tile_two = tile_height(chans, 2)
     outer, sent = pl.pallas_call(
         outer_kernel,
         out_shape=[

time: 49.3 us -> 45.6 us (0.925)
  blocking collectives: 24.3 us -> 12 us
  starting transfers between devices: 4.25 us -> 12.1 us
  local copies, waits for them, and re-layouts: 4.79 us -> 1.29 us
  Pallas kernels: 14.8 us -> 17.9 us
  waiting for transfers between devices: 0.01 us -> 1.29 us
    all_to_all x2 -> x1, blocking collectives: 24.3 us -> 12 us  [everyone(): return lax.all_to_all(tiles, axes, 0, 0)]
    all_to_all x0 -> x1, starting transfers between devices: none -> 7.16 us  [everyone(): return lax.all_to_all(tiles, axes, 0, 0)]
    reshape x7 -> x0, local copies, waits for them, and re-layouts: 4.78 us -> none  [body(): line = lambda vector: vector.reshape(1, -1)]
    unnamed x2 -> x4, local copies, waits for them, and re-layouts: 0.01 us -> 1.29 us
    all_to_all x0 -> x1, waiting for transfers between devices: none -> 1.28 us  [everyone(): return lax.all_to_all(tiles, axes, 0, 0)]
    pallas_call x1, Pallas kernels: 3.01 us -> 4.14 us  [body(): pl.pallas_call(outer_kernel, out_shape=[pltpu.VMEM((2 * REACH, chans, col...]
    pallas_call x1, Pallas kernels: 1.85 us -> 2.7 us  [body(): pl.pallas_call(stats_kernel, out_shape=[pltpu.VMEM((rows, chans, cols), B...]
    pallas_call x1, Pallas kernels: 2.65 us -> 3.42 us  [body(): pl.pallas_call(inner_kernel, out_shape=[pltpu.VMEM((max(rows - 2, 1), cha...]
  transfers between devices with their start and end apart: 5 -> 6, of which waited for: 0 -> 1; matrix products, arithmetic and copies ran while one was open for 10% -> 0% of each run, Pallas kernels for 12% -> 15%
where the time goes in v8:
time: 45.6 us; the launch traced here: 45.3 us
  Pallas kernels  17.9 us (39%)
  starting transfers between devices  12.1 us (27%)
  blocking collectives  12 us (26%)
  local copies, waits for them, and re-layouts  1.29 us (3%)
  waiting for transfers between devices  1.29 us (3%)
  between operations  0.72 us (2%)
    all_to_all x1, blocking collectives, everyone(): return lax.all_to_all(tiles, axes, 0, 0)  12 us
    all_to_all x1, starting transfers between devices, everyone(): return lax.all_to_all(tiles, axes, 0, 0)  7.16 us
    pallas_call x1, Pallas kernels, body(): pl.pallas_call(outer_kernel, out_shape=[pltpu.VMEM((2 * REACH, chans, col...  4.14 us
    pallas_call x1, Pallas kernels, body(): pl.pallas_call(second_kernel, out_shape=jax.ShapeDtypeStruct((rows, chans...  4.07 us
    pallas_call x1, Pallas kernels, body(): pl.pallas_call(prepare_kernel, out_shape=[pltpu.VMEM((chans, deep), BF16)...  3.59 us
    pallas_call x1, Pallas kernels, body(): pl.pallas_call(inner_kernel, out_shape=[pltpu.VMEM((max(rows - 2, 1), cha...  3.42 us
    ppermute x1, starting transfers between devices, body(): lax.ppermute(near_edge, 'patch', [(i, i ^ 1) for i in range(patches)])  3 us
    pallas_call x1, Pallas kernels, body(): pl.pallas_call(stats_kernel, out_shape=[pltpu.VMEM((rows, chans, cols), B...  2.7 us
  transfers between devices with their start and end apart: 6, of which 1 were waited for; matrix products, arithmetic and copies ran while one was open for 0% of the time, Pallas kernels for 15%

profile of v8, /device:TPU:0, one launch (start us, length us, event | category | flops | bytes accessed | tf_op | source)
XLA Modules:
  0.0 45.3 jit_solution(5077787449924669972)
XLA Ops:
  0.0 2.7 %stats.1 = (bf16[4,320,256]{2,1,0:T(8,128)(2,1)S(1)}, f32[16,8,128]{2,1,0:T(8,128)}, bf16[2,320,256]{2,1,0:T(8,128)(2,1)}, bf16[2,320,256]{2,1,0:T(8,128)(2,1)}) custom-call(bf16[4,320,256]{2,1,0:T(8,128)(2,1)} %bitcast.12, bf16[1,1280]{1,0:T(2,128)(2,1)} %embed_hbm.1, bf16[160,320]{1,0:T(8,128)(2,1)} %weight_hbm.1), custom_call_target="tpu_custom_call" | custom-call | tf_op jit(solution)/shard_map/stats/pallas_call | solution.py:391
  2.7 3.0 %collective-permute-start.1 = (bf16[2,320,256]{2,1,0:T(8,128)(2,1)}, bf16[2,320,256]{2,1,0:T(8,128)(2,1)S(1)}, u32[]{:S(2)}, u32[]{:S(2)}) collective-permute-start(bf16[2,320,256]{2,1,0:T(8,128)(2,1)} %get-tuple-element.27), channel_id=1, source_target_pairs={{0,2},{2,0},{4,6},{6,4},{8,10},{10,8},{12,14},{14,12},{1,3},{3,1},... | collective-permute-start | bytes 983048 | tf_op jit(solution)/shard_map/ppermute | solution.py:410
  5.7 1.4 %collective-permute-start.2 = (bf16[2,320,256]{2,1,0:T(8,128)(2,1)}, bf16[2,320,256]{2,1,0:T(8,128)(2,1)}, u32[]{:S(2)}, u32[]{:S(2)}) collective-permute-start(bf16[2,320,256]{2,1,0:T(8,128)(2,1)} %get-tuple-element.28), channel_id=1, source_target_pairs={{2,4},{6,8},{10,12},{4,2},{8,6},{12,10},{3,5},{7,9},{11,13},{5,3},... | collective-permute-start | bytes 983048 | tf_op jit(solution)/shard_map/ppermute | solution.py:412
  7.1 0.0 collective-permute-start
  7.1 7.2 %all-to-all-start = ((f32[16,8,128]{2,1,0:T(8,128)}), f32[16,8,128]{2,1,0:T(8,128)}, u32[]{:S(2)}, u32[]{:S(2)}) async-start(f32[16,8,128]{2,1,0:T(8,128)} %get-tuple-element.25), calls=%async_computation | async-start | bytes 131072 | tf_op jit(solution)/shard_map/all_to_all | solution.py:366
  14.9 3.6 %prepare.1 = (bf16[320,2880]{1,0:T(8,128)(2,1)S(1)}, bf16[320,2880]{1,0:T(8,128)(2,1)S(1)}, f32[8,384]{1,0:T(8,128)S(1)}) custom-call(bf16[2880,320]{1,0:T(8,128)(2,1)} %bitcast.10, bf16[2880,320]{1,0:T(8,128)(2,1)} %bitcast.11, f32[320]{0:T(512)} %gain_one.1, f32[320]{0:T(512)} %shift_one.1, f32[320]{0:T(512)} %bias_one.1, f32[320]{0:T(512)} %time_bias.1, ...), custom_call_target="tpu_custom_call" | custom-call | tf_op jit(solution)/shard_map/prepare/pallas_call | solution.py:417
  18.5 0.0 copy-start
  18.6 1.3 %copy-done = bf16[320,2880]{1,0:T(8,128)(2,1)} copy-done((bf16[320,2880]{1,0:T(8,128)(2,1)}, bf16[320,2880]{1,0:T(8,128)(2,1)S(1)}, u32[]{:S(2)}) %copy-start) | copy-done | bytes 1843224
  19.8 1.3 %all-to-all-done.seen_ref = f32[16,8,128]{2,1,0:T(8,128)} async-done(((f32[16,8,128]{2,1,0:T(8,128)}), f32[16,8,128]{2,1,0:T(8,128)}, u32[]{:S(2)}, u32[]{:S(2)}) %all-to-all-start) | async-done | bytes 65568 | tf_op jit(solution)/shard_map/all_to_all | solution.py:366
  21.1 0.0 collective-permute-done.1.near_ref
  21.1 0.0 collective-permute-done.2.next_ref
  21.1 0.0 collective-permute-start.3
  21.1 0.5 %collective-permute-start.4 = (bf16[2,320,256]{2,1,0:T(8,128)(2,1)}, bf16[2,320,256]{2,1,0:T(8,128)(2,1)S(1)}, u32[]{:S(2)}, u32[]{:S(2)}) collective-permute-start(bf16[2,320,256]{2,1,0:T(8,128)(2,1)} %collective-permute-done.2.next_ref), channel_id=1, source_target_pairs={{0,16},{16,0},{1,17},{17,1},{2,18},{18,2},{3,19},{19,3},{4,20},{20... | collective-permute-start | bytes 983048 | tf_op jit(solution)/shard_map/ppermute | solution.py:434
  21.6 0.0 collective-permute-done.far_ref
  21.6 3.4 %inner.1 = (f32[2,320,256]{2,1,0:T(8,128)S(1)}, bf16[3840,256]{1,0:T(8,128)(2,1)S(1)}, f32[6,320,128]{2,1,0:T(8,128)S(1)}) custom-call(bf16[4,320,256]{2,1,0:T(8,128)(2,1)S(1)} %get-tuple-element.24.own_ref.lat_ref, bf16[4,320,256]{2,1,0:T(8,128)(2,1)S(1)} %collective-permute-done.far_ref, f32[16,8,128]{2,1,0:T(8,128)} %all-to-all-done.seen_ref, ...), custom_call_target="tpu_custom_call" | custom-call | tf_op jit(solution)/shard_map/inner/pallas_call | solution.py:436
  25.1 0.0 collective-permute-done.3.far_near_ref
  25.1 0.0 collective-permute-done.4.far_next_ref
  25.1 0.0 copy-start.1
  25.1 4.1 %outer.1 = (f32[4,320,256]{2,1,0:T(8,128)S(1)}, f32[8,8,128]{2,1,0:T(8,128)S(1)}) custom-call(bf16[2,320,256]{2,1,0:T(8,128)(2,1)S(1)} %collective-permute-done.1.near_ref, bf16[2,320,256]{2,1,0:T(8,128)(2,1)} %collective-permute-done.2.next_ref, bf16[2,320,256]{2,1,0:T(8,128)(2,1)S(1)} %collective-permute-done.3.far_near_ref, ...), custom_call_target="tpu_custom_call" | custom-call | tf_op jit(solution)/shard_map/outer/pallas_call | solution.py:449
  29.2 12.0 %all_to_all.10.seen_ref = f32[8,8,128]{2,1,0:T(8,128)S(1)} all-to-all(f32[8,8,128]{2,1,0:T(8,128)S(1)} %get-tuple-element.41), channel_id=1, replica_groups=mesh['cfg'=2,'patch'=8,'req'=2] {'patch'}, dimensions={0} | all-to-all | bytes 65536 | tf_op jit(solution)/shard_map/all_to_all | solution.py:366
  41.2 0.0 copy-done.1
  41.2 4.1 %second.1 = bf16[4,320,256]{2,1,0:T(8,128)(2,1)} custom-call(f32[2,320,256]{2,1,0:T(8,128)S(1)} %get-tuple-element.35.inner_ref, f32[4,320,256]{2,1,0:T(8,128)S(1)} %get-tuple-element.40.outer_ref, bf16[4,320,256]{2,1,0:T(8,128)(2,1)S(1)} %get-tuple-element.24.own_ref.lat_ref, f32[8,8,128]{2,1,0:T(8,128)S(1)} %all_to_all.10.seen_ref, ...), custom_call_target="tpu_custom_call" | custom-call | tf_op jit(solution)/shard_map/second/pallas_call | solution.py:465
Async XLA Ops:
  2.7 18.4 %collective-permute-start.1 = (bf16[2,320,256]{2,1,0:T(8,128)(2,1)}, bf16[2,320,256]{2,1,0:T(8,128)(2,1)S(1)}, u32[]{:S(2)}, u32[]{:S(2)}) collective-permute-start(bf16[2,320,256]{2,1,0:T(8,128)(2,1)} %get-tuple-element.27), channel_id=1, source_target_pairs={{0,2},{2,0},{4,6},{6,4},{8,10},{10,8},{12,14},{14,12},{1,3},{3,1},... | collective-permute-start | bytes 983048 | tf_op jit(solution)/shard_map/ppermute | solution.py:410
  5.7 15.4 %collective-permute-start.2 = (bf16[2,320,256]{2,1,0:T(8,128)(2,1)}, bf16[2,320,256]{2,1,0:T(8,128)(2,1)}, u32[]{:S(2)}, u32[]{:S(2)}) collective-permute-start(bf16[2,320,256]{2,1,0:T(8,128)(2,1)} %get-tuple-element.28), channel_id=1, source_target_pairs={{2,4},{6,8},{10,12},{4,2},{8,6},{12,10},{3,5},{7,9},{11,13},{5,3},... | collective-permute-start | bytes 983048 | tf_op jit(solution)/shard_map/ppermute | solution.py:412
  7.1 14.5 %collective-permute-start = (bf16[4,320,256]{2,1,0:T(8,128)(2,1)}, bf16[4,320,256]{2,1,0:T(8,128)(2,1)S(1)}, u32[]{:S(2)}, u32[]{:S(2)}) collective-permute-start(bf16[4,320,256]{2,1,0:T(8,128)(2,1)} %bitcast.13), channel_id=1, source_target_pairs={{0,16},{16,0},{1,17},{17,1},{2,18},{18,2},{3,19},{19,3},{4,20},{20... | collective-permute-start | bytes 1966088 | tf_op jit(solution)/shard_map/ppermute | solution.py:431
  7.1 14.0 %all-to-all-start = ((f32[16,8,128]{2,1,0:T(8,128)}), f32[16,8,128]{2,1,0:T(8,128)}, u32[]{:S(2)}, u32[]{:S(2)}) async-start(f32[16,8,128]{2,1,0:T(8,128)} %get-tuple-element.25), calls=%async_computation | async-start | bytes 131072 | tf_op jit(solution)/shard_map/all_to_all | solution.py:366
  18.5 1.3 %copy-start = (bf16[320,2880]{1,0:T(8,128)(2,1)}, bf16[320,2880]{1,0:T(8,128)(2,1)S(1)}, u32[]{:S(2)}) copy-start(bf16[320,2880]{1,0:T(8,128)(2,1)S(1)} %get-tuple-element.42.weight_ref) | copy-start | bytes 5529604
  21.1 4.0 %collective-permute-start.3 = (bf16[2,320,256]{2,1,0:T(8,128)(2,1)S(1)}, bf16[2,320,256]{2,1,0:T(8,128)(2,1)S(1)}, u32[]{:S(2)}, u32[]{:S(2)}) collective-permute-start(bf16[2,320,256]{2,1,0:T(8,128)(2,1)S(1)} %collective-permute-done.1.near_ref), channel_id=1, source_target_pairs={{0,16},{16,0},{1,17},{17,1},{2,18},{18,2},{3,19},{19,3},{4,20},{20... | collective-permute-start | bytes 983048 | tf_op jit(solution)/shard_map/ppermute | solution.py:433
  21.1 4.0 %collective-permute-start.4 = (bf16[2,320,256]{2,1,0:T(8,128)(2,1)}, bf16[2,320,256]{2,1,0:T(8,128)(2,1)S(1)}, u32[]{:S(2)}, u32[]{:S(2)}) collective-permute-start(bf16[2,320,256]{2,1,0:T(8,128)(2,1)} %collective-permute-done.2.next_ref), channel_id=1, source_target_pairs={{0,16},{16,0},{1,17},{17,1},{2,18},{18,2},{3,19},{19,3},{4,20},{20... | collective-permute-start | bytes 983048 | tf_op jit(solution)/shard_map/ppermute | solution.py:434
  25.1 16.1 %copy-start.1 = (bf16[320,2880]{1,0:T(8,128)(2,1)S(1)}, bf16[320,2880]{1,0:T(8,128)(2,1)}, u32[]{:S(2)}) copy-start(bf16[320,2880]{1,0:T(8,128)(2,1)} %copy-done) | copy-start | bytes 5529604

commit v9 on v8

--- a/solution.py
+++ b/solution.py
@@ -108,32 +108,44 @@
     return -(-rows * chans // LANES // 8) * 8
 
 
+def fetch(pairs, sems, first=0):
+    copies = [pltpu.make_async_copy(a, b, sems.at[first + k]) for k, (a, b) in enumerate(pairs)]
+    for copy in copies:
+        copy.start()
+    return copies
+
+
 def stats_kernel(
     lat_hbm, embed_hbm, weight_hbm,
-    lat_ref, out_ref, near_ref, next_ref,
-    embed_ref, weight_ref, sems, edge_sems,
+    out_ref, near_hbm, next_hbm,
+    lat_ref, embed_ref, weight_ref, sems, edge_sems,
 ):
     rows, chans, _ = lat_ref.shape
-    copies = [
-        pltpu.make_async_copy(lat_hbm.at[k], lat_ref.at[k], sems.at[k]) for k in range(rows)
-    ]
-    copies.append(pltpu.make_async_copy(embed_hbm, embed_ref, sems.at[rows]))
-    copies.append(pltpu.make_async_copy(weight_hbm, weight_ref, sems.at[rows + 1]))
-    reach = near_ref.shape[0]
+    reach = near_hbm.shape[0]
     last = rows - reach
     near_at = jnp.where(lax.rem(lax.axis_index("patch"), 2) == 0, last, 0)
-    edges = [
-        pltpu.make_async_copy(lat_hbm.at[pl.ds(near_at, reach)], near_ref, edge_sems.at[0]),
-        pltpu.make_async_copy(lat_hbm.at[pl.ds(last - near_at, reach)], next_ref, edge_sems.at[1]),
-    ]
-    for copy in copies + edges:
-        copy.start()
+    copies = fetch(
+        [(lat_hbm.at[k], lat_ref.at[k]) for k in range(rows)]
+        + [(embed_hbm, embed_ref), (weight_hbm, weight_ref)],
+        sems,
+    )
+    edges = []
     waits = list(copies[:rows])
 
     def values():
         for k in range(rows):
             if waits:
                 waits.pop(0).wait()
+                if not waits:
+                    edges.extend(
+                        fetch(
+                            [
+                                (lat_ref.at[pl.ds(near_at, reach)], near_hbm),
+                                (lat_ref.at[pl.ds(last - near_at, reach)], next_hbm),
+                            ],
+                            edge_sems,
+                        )
+                    )
             yield lat_ref[k].astype(F32)
 
     mean, squares = channel_moments(values, chans)
@@ -154,21 +166,14 @@
     return [(at, min(part, deep - at)) for at in range(0, deep, part)]
 
 
-def fetch(pairs, sems, first=0):
-    copies = [pltpu.make_async_copy(a, b, sems.at[first + k]) for k, (a, b) in enumerate(pairs)]
-    for copy in copies:
-        copy.start()
-    return copies
-
-
 def prepare_kernel(
     one_hbm, two_hbm, gain_one, shift_one, bias_one, time_bias, gain_two, shift_two, bias_two, steer,
-    one_out, two_out, rows_ref, one_ref, two_ref, sems, row_sems, *vector_refs,
+    one_out, two_hbm_out, rows_ref, one_ref, two_ref, two_out, sems, row_sems, out_sem, *vector_refs,
 ):
     vectors = (gain_one, shift_one, bias_one, time_bias, gain_two, shift_two, bias_two)
     lines = fetch(zip(vectors, vector_refs), row_sems)
     parts = parts_of(one_ref.shape[0])
-    sides = ((one_hbm, one_ref, one_out), (two_hbm, two_ref, two_out))
+    sides = ((two_hbm, two_ref, two_out), (one_hbm, one_ref, one_out))
     copies = [
         fetch([(a.at[pl.ds(*p)], b.at[pl.ds(*p)]) for p in parts], sems, k * len(parts))
         for k, (a, b, _) in enumerate(sides)
@@ -182,6 +187,10 @@
         for wait, (at, size) in zip(waits, parts):
             wait.wait()
             target[:, at : at + size] = held[at : at + size, :].T
+        if target is two_out:
+            out = pltpu.make_async_copy(two_out, two_hbm_out, out_sem)
+            out.start()
+    out.wait()
 
 
 def spread_columns(rows, chans, cols_ref):
@@ -237,10 +246,12 @@
 
 
 def inner_kernel(
-    own_ref, far_ref, seen_ref, rows_ref, weight_ref,
+    own_hbm, far_ref, seen_ref, rows_ref, weight_ref,
     steered_ref, taps_ref, cols_ref,
+    own_ref, sems,
 ):
     rows, chans, cols = own_ref.shape
+    copies = fetch([(own_hbm.at[k], own_ref.at[k]) for k in range(rows)], sems)
     wide = padded_lanes(chans)
     size = chans // GROUPS
     cfg, peers = lax.axis_index("cfg"), lax.axis_size("patch")
@@ -261,6 +272,7 @@
     if rows < 3:
         steered_ref[...] = jnp.zeros_like(steered_ref)
     for at in range(rows):
+        copies[at].wait()
         put_taps(taps_ref, at, mix(own_ref[at], far_ref[at]))
         if at >= 2:
             total = matmul(weight_ref, taps_ref[(at - 2) * line : (at + 1) * line, :], 0)
@@ -329,11 +341,13 @@
 
 
 def second_kernel(
-    inner_ref, outer_ref, lat_ref, seen_ref, rows_ref, weight_ref,
-    out_ref,
-    taps_ref, cols_ref,
+    inner_ref, outer_ref, lat_hbm, seen_ref, rows_ref, weight_ref,
+    out_hbm,
+    taps_ref, cols_ref, lat_ref, out_ref, sems, out_sems,
 ):
     rows, chans, cols = lat_ref.shape
+    copies = fetch([(lat_hbm.at[k], lat_ref.at[k]) for k in range(rows)], sems)
+    outs = []
     wide = padded_lanes(chans)
     size = chans // GROUPS
     peers = lax.axis_size("patch")
@@ -359,7 +373,11 @@
         put_taps(taps_ref, at, value if keep is None else value * keep)
         if at >= 2:
             total = matmul(weight_ref, taps_ref[(at - 2) * line : (at + 1) * line, :], 0)
+            copies[at - 2].wait()
             out_ref[at - 2] = (lat_ref[at - 2].astype(F32) + (total + twice(cols_ref[3]))).astype(BF16)
+            outs += fetch([(out_ref.at[at - 2], out_hbm.at[at - 2])], out_sems, at - 2)
+    for copy in outs:
+        copy.wait()
 
 
 def everyone(tiles, axes):
@@ -388,17 +406,17 @@
     line = lambda vector: vector.reshape(1, -1)
 
     tile_one = tile_height(chans, 3)
-    held, sent, near_edge, next_edge = pl.pallas_call(
+    sent, near_edge, next_edge = pl.pallas_call(
         stats_kernel,
         out_shape=[
+            pltpu.VMEM((2 * patches, tile_one, LANES), F32),
+            pltpu.HBM((REACH, chans, cols), BF16),
+            pltpu.HBM((REACH, chans, cols), BF16),
+        ],
+        in_specs=[ANY] * 3,
+        out_specs=[VMEM, ANY, ANY],
+        scratch_shapes=[
             pltpu.VMEM((rows, chans, cols), BF16),
-            pltpu.VMEM((2 * patches, tile_one, LANES), F32),
-            pltpu.VMEM((REACH, chans, cols), BF16),
-            pltpu.VMEM((REACH, chans, cols), BF16),
-        ],
-        in_specs=[ANY] * 3,
-        out_specs=[VMEM] * 4,
-        scratch_shapes=[
             pltpu.VMEM(time_embed.shape, BF16),
             pltpu.VMEM(time_weight.shape, BF16),
             pltpu.SemaphoreType.DMA((rows + 2,)),
@@ -416,11 +434,14 @@
     source, *weights, _ = lax.optimization_barrier((own, *weights, sent))
     turned_one, turned_two, vectors = pl.pallas_call(
         prepare_kernel,
-        out_shape=[pltpu.VMEM((chans, deep), BF16)] * 2 + [pltpu.VMEM((8, wide), F32)],
+        out_shape=[
+            pltpu.VMEM((chans, deep), BF16), pltpu.HBM((chans, deep), BF16), pltpu.VMEM((8, wide), F32),
+        ],
         in_specs=[ANY] * 9 + [VMEM],
-        out_specs=[VMEM] * 3,
-        scratch_shapes=[pltpu.VMEM((deep, chans), BF16)] * 2
+        out_specs=[VMEM, ANY, VMEM],
+        scratch_shapes=[pltpu.VMEM((deep, chans), BF16)] * 2 + [pltpu.VMEM((chans, deep), BF16)]
         + [pltpu.SemaphoreType.DMA((2 * len(parts_of(deep)),)), pltpu.SemaphoreType.DMA((7,))]
+        + [pltpu.SemaphoreType.DMA]
         + [pltpu.VMEM((chans,), F32)] * 7,
         compiler_params=LIMIT,
         name="prepare",
@@ -440,11 +461,12 @@
             pltpu.VMEM((rows * 3 * chans, cols), BF16),
             pltpu.VMEM((6, chans, LANES), F32),
         ],
-        in_specs=[VMEM] * 5,
+        in_specs=[ANY] + [VMEM] * 4,
         out_specs=[VMEM] * 3,
+        scratch_shapes=[pltpu.VMEM((rows, chans, cols), BF16), pltpu.SemaphoreType.DMA((rows,))],
         compiler_params=LIMIT,
         name="inner",
-    )(held, far, seen, vectors, turned_one)
+    )(in_hbm(own), far, seen, vectors, turned_one)
     tile_two = tile_height(chans, 2)
     outer, sent = pl.pallas_call(
         outer_kernel,
@@ -464,16 +486,20 @@
     seen = everyone(sent, "patch")
     image = pl.pallas_call(
         second_kernel,
-        out_shape=jax.ShapeDtypeStruct((rows, chans, cols), BF16),
-        in_specs=[VMEM] * 6,
-        out_specs=VMEM,
+        out_shape=pltpu.HBM((rows, chans, cols), BF16),
+        in_specs=[VMEM] * 2 + [ANY] + [VMEM] * 3,
+        out_specs=ANY,
         scratch_shapes=[
             pltpu.VMEM(((rows + 2) * 3 * chans, cols), BF16),
             pltpu.VMEM((4, chans, LANES), F32),
+            pltpu.VMEM((rows, chans, cols), BF16),
+            pltpu.VMEM((rows, chans, cols), BF16),
+            pltpu.SemaphoreType.DMA((rows,)),
+            pltpu.SemaphoreType.DMA((rows,)),
         ],
         compiler_params=LIMIT,
         name="second",
-    )(inner, outer, held, seen, vectors, turned_two)
+    )(inner, outer, in_hbm(own), seen, vectors, turned_two)
     return jnp.swapaxes(image, 1, 2)[None, None]
 
 

time: 45.6 us -> 47.7 us (1.046)
  Pallas kernels: 17.9 us -> 20.7 us
  local copies, waits for them, and re-layouts: 1.29 us -> 0.01 us
  waiting for transfers between devices: 1.29 us -> 1.98 us
    pallas_call x2, Pallas kernels: 6.77 us -> 9.44 us  [the longest x1 6.73 us: body(): pl.pallas_call(second_kernel, out_shape=pltpu.HBM((rows, chans, cols), BF...]
    unnamed x4 -> x2, local copies, waits for them, and re-layouts: 1.29 us -> 0.01 us
    pallas_call x1, Pallas kernels: 4.14 us -> 3.04 us  [body(): pl.pallas_call(outer_kernel, out_shape=[pltpu.VMEM((2 * REACH, chans, col...]
    ppermute x1, starting transfers between devices: 1.42 us -> 0.67 us  [body(): lax.ppermute(next_edge, 'patch', steps + [(j, i) for i, j in steps])]
    pallas_call x1, Pallas kernels: 3.42 us -> 4.11 us  [body(): pl.pallas_call(inner_kernel, out_shape=[pltpu.VMEM((max(rows - 2, 1), cha...]
    all_to_all x1, waiting for transfers between devices: 1.28 us -> 1.96 us  [everyone(): return lax.all_to_all(tiles, axes, 0, 0)]
    all_to_all x1, starting transfers between devices: 7.16 us -> 7.77 us  [everyone(): return lax.all_to_all(tiles, axes, 0, 0)]
    pallas_call x1, Pallas kernels: 3.59 us -> 4.14 us  [body(): pl.pallas_call(prepare_kernel, out_shape=[pltpu.VMEM((chans, deep), BF16)...]
  transfers between devices with their start and end apart: 6 -> 6, of which waited for: 1 -> 1; matrix products, arithmetic and copies ran while one was open for 0% -> 0% of each run, Pallas kernels for 15% -> 17%
where the time goes in v9:
time: 47.7 us; the launch traced here: 47.4 us
  Pallas kernels  20.7 us (43%)
  starting transfers between devices  12 us (25%)
  blocking collectives  12 us (25%)
  waiting for transfers between devices  1.98 us (4%)
  between operations  0.73 us (2%)
    all_to_all x1, blocking collectives, everyone(): return lax.all_to_all(tiles, axes, 0, 0)  12 us
    all_to_all x1, starting transfers between devices, everyone(): return lax.all_to_all(tiles, axes, 0, 0)  7.77 us
    pallas_call x1, Pallas kernels, body(): pl.pallas_call(second_kernel, out_shape=pltpu.HBM((rows, chans, cols), BF...  6.73 us
    pallas_call x1, Pallas kernels, body(): pl.pallas_call(prepare_kernel, out_shape=[pltpu.VMEM((chans, deep), BF16)...  4.14 us
    pallas_call x1, Pallas kernels, body(): pl.pallas_call(inner_kernel, out_shape=[pltpu.VMEM((max(rows - 2, 1), cha...  4.11 us
    pallas_call x1, Pallas kernels, body(): pl.pallas_call(outer_kernel, out_shape=[pltpu.VMEM((2 * REACH, chans, col...  3.04 us
    ppermute x1, starting transfers between devices, body(): lax.ppermute(near_edge, 'patch', [(i, i ^ 1) for i in range(patches)])  3 us
    pallas_call x1, Pallas kernels, body(): pl.pallas_call(stats_kernel, out_shape=[pltpu.VMEM((2 * patches, tile_one...  2.71 us
  transfers between devices with their start and end apart: 6, of which 1 were waited for; matrix products, arithmetic and copies ran while one was open for 0% of the time, Pallas kernels for 17%

profile of v9, /device:TPU:0, one launch (start us, length us, event | category | flops | bytes accessed | tf_op | source)
XLA Modules:
  0.0 47.4 jit_solution(12097626728415718514)
XLA Ops:
  0.0 2.7 %stats.1 = (f32[16,8,128]{2,1,0:T(8,128)}, bf16[2,320,256]{2,1,0:T(8,128)(2,1)}, bf16[2,320,256]{2,1,0:T(8,128)(2,1)}) custom-call(bf16[4,320,256]{2,1,0:T(8,128)(2,1)} %bitcast.10, bf16[1,1280]{1,0:T(2,128)(2,1)} %embed_hbm.1, bf16[160,320]{1,0:T(8,128)(2,1)} %weight_hbm.1), custom_call_target="tpu_custom_call" | custom-call | tf_op jit(solution)/shard_map/stats/pallas_call | solution.py:409
  2.7 3.0 %collective-permute-start.1 = (bf16[2,320,256]{2,1,0:T(8,128)(2,1)}, bf16[2,320,256]{2,1,0:T(8,128)(2,1)S(1)}, u32[]{:S(2)}, u32[]{:S(2)}) collective-permute-start(bf16[2,320,256]{2,1,0:T(8,128)(2,1)} %get-tuple-element.25), channel_id=1, source_target_pairs={{0,2},{2,0},{4,6},{6,4},{8,10},{10,8},{12,14},{14,12},{1,3},{3,1},... | collective-permute-start | bytes 983048 | tf_op jit(solution)/shard_map/ppermute | solution.py:428
  5.7 0.7 %collective-permute-start.2 = (bf16[2,320,256]{2,1,0:T(8,128)(2,1)}, bf16[2,320,256]{2,1,0:T(8,128)(2,1)S(1)}, u32[]{:S(2)}, u32[]{:S(2)}) collective-permute-start(bf16[2,320,256]{2,1,0:T(8,128)(2,1)} %get-tuple-element.26), channel_id=1, source_target_pairs={{2,4},{6,8},{10,12},{4,2},{8,6},{12,10},{3,5},{7,9},{11,13},{5,3},... | collective-permute-start | bytes 983048 | tf_op jit(solution)/shard_map/ppermute | solution.py:430
  6.4 0.1 collective-permute-start
  6.5 7.8 %all-to-all-start = ((f32[16,8,128]{2,1,0:T(8,128)}), f32[16,8,128]{2,1,0:T(8,128)S(1)}, u32[]{:S(2)}, u32[]{:S(2)}) async-start(f32[16,8,128]{2,1,0:T(8,128)} %get-tuple-element.23), calls=%async_computation | async-start | bytes 131072 | tf_op jit(solution)/shard_map/all_to_all | solution.py:384
  14.9 4.1 %prepare.1 = (bf16[320,2880]{1,0:T(8,128)(2,1)S(1)}, bf16[320,2880]{1,0:T(8,128)(2,1)}, f32[8,384]{1,0:T(8,128)S(1)}) custom-call(bf16[2880,320]{1,0:T(8,128)(2,1)} %bitcast.14, bf16[2880,320]{1,0:T(8,128)(2,1)} %bitcast.15, f32[320]{0:T(512)} %gain_one.1, f32[320]{0:T(512)} %shift_one.1, f32[320]{0:T(512)} %bias_one.1, f32[320]{0:T(512)} %time_bias.1, ...), custom_call_target="tpu_custom_call" | custom-call | tf_op jit(solution)/shard_map/prepare/pallas_call | solution.py:435
  19.1 2.0 %all-to-all-done.seen_ref = f32[16,8,128]{2,1,0:T(8,128)S(1)} async-done(((f32[16,8,128]{2,1,0:T(8,128)}), f32[16,8,128]{2,1,0:T(8,128)S(1)}, u32[]{:S(2)}, u32[]{:S(2)}) %all-to-all-start) | async-done | bytes 65568 | tf_op jit(solution)/shard_map/all_to_all | solution.py:384
  21.0 0.0 collective-permute-done.1.near_ref
  21.0 0.0 collective-permute-done.2.next_ref
  21.0 0.0 collective-permute-start.3
  21.0 0.5 %collective-permute-start.4 = (bf16[2,320,256]{2,1,0:T(8,128)(2,1)S(1)}, bf16[2,320,256]{2,1,0:T(8,128)(2,1)S(1)}, u32[]{:S(2)}, u32[]{:S(2)}) collective-permute-start(bf16[2,320,256]{2,1,0:T(8,128)(2,1)S(1)} %collective-permute-done.2.next_ref), channel_id=1, source_target_pairs={{0,16},{16,0},{1,17},{17,1},{2,18},{18,2},{3,19},{19,3},{4,20},{20... | collective-permute-start | bytes 983048 | tf_op jit(solution)/shard_map/ppermute | solution.py:455
  21.5 0.0 collective-permute-done.far_ref
  21.5 4.1 %inner.1 = (f32[2,320,256]{2,1,0:T(8,128)S(1)}, bf16[3840,256]{1,0:T(8,128)(2,1)S(1)}, f32[6,320,128]{2,1,0:T(8,128)S(1)}) custom-call(bf16[4,320,256]{2,1,0:T(8,128)(2,1)} %bitcast.12, bf16[4,320,256]{2,1,0:T(8,128)(2,1)S(1)} %collective-permute-done.far_ref, f32[16,8,128]{2,1,0:T(8,128)S(1)} %all-to-all-done.seen_ref, ...), custom_call_target="tpu_custom_call" | custom-call | tf_op jit(solution)/shard_map/inner/pallas_call | solution.py:457
  25.7 0.0 collective-permute-done.3.far_near_ref
  25.7 0.0 collective-permute-done.4.far_next_ref
  25.7 0.0 copy-start
  25.7 3.0 %outer.1 = (f32[4,320,256]{2,1,0:T(8,128)S(1)}, f32[8,8,128]{2,1,0:T(8,128)S(1)}) custom-call(bf16[2,320,256]{2,1,0:T(8,128)(2,1)S(1)} %collective-permute-done.1.near_ref, bf16[2,320,256]{2,1,0:T(8,128)(2,1)S(1)} %collective-permute-done.2.next_ref, bf16[2,320,256]{2,1,0:T(8,128)(2,1)S(1)} %collective-permute-done.3.far_near_ref, ...), custom_call_target="tpu_custom_call" | custom-call | tf_op jit(solution)/shard_map/outer/pallas_call | solution.py:471
  28.7 12.0 %all_to_all.10.seen_ref = f32[8,8,128]{2,1,0:T(8,128)S(1)} all-to-all(f32[8,8,128]{2,1,0:T(8,128)S(1)} %get-tuple-element.39), channel_id=1, replica_groups=mesh['cfg'=2,'patch'=8,'req'=2] {'patch'}, dimensions={0} | all-to-all | bytes 65536 | tf_op jit(solution)/shard_map/all_to_all | solution.py:384
  40.7 0.0 copy-done
  40.7 6.7 %second.1 = bf16[4,320,256]{2,1,0:T(8,128)(2,1)} custom-call(f32[2,320,256]{2,1,0:T(8,128)S(1)} %get-tuple-element.33.inner_ref, f32[4,320,256]{2,1,0:T(8,128)S(1)} %get-tuple-element.38.outer_ref, bf16[4,320,256]{2,1,0:T(8,128)(2,1)} %bitcast.13, f32[8,8,128]{2,1,0:T(8,128)S(1)} %all_to_all.10.seen_ref, f32[8,384]{1,0:T(8,128)S(1)} %get-tuple-element.31.rows_ref, ...), custom_call_target="tpu_custom_call" | custom-call | tf_op jit(solution)/shard_map/second/pallas_call | solution.py:487
Async XLA Ops:
  2.7 18.3 %collective-permute-start.1 = (bf16[2,320,256]{2,1,0:T(8,128)(2,1)}, bf16[2,320,256]{2,1,0:T(8,128)(2,1)S(1)}, u32[]{:S(2)}, u32[]{:S(2)}) collective-permute-start(bf16[2,320,256]{2,1,0:T(8,128)(2,1)} %get-tuple-element.25), channel_id=1, source_target_pairs={{0,2},{2,0},{4,6},{6,4},{8,10},{10,8},{12,14},{14,12},{1,3},{3,1},... | collective-permute-start | bytes 983048 | tf_op jit(solution)/shard_map/ppermute | solution.py:428
  5.7 15.3 %collective-permute-start.2 = (bf16[2,320,256]{2,1,0:T(8,128)(2,1)}, bf16[2,320,256]{2,1,0:T(8,128)(2,1)S(1)}, u32[]{:S(2)}, u32[]{:S(2)}) collective-permute-start(bf16[2,320,256]{2,1,0:T(8,128)(2,1)} %get-tuple-element.26), channel_id=1, source_target_pairs={{2,4},{6,8},{10,12},{4,2},{8,6},{12,10},{3,5},{7,9},{11,13},{5,3},... | collective-permute-start | bytes 983048 | tf_op jit(solution)/shard_map/ppermute | solution.py:430
  6.4 15.1 %collective-permute-start = (bf16[4,320,256]{2,1,0:T(8,128)(2,1)}, bf16[4,320,256]{2,1,0:T(8,128)(2,1)S(1)}, u32[]{:S(2)}, u32[]{:S(2)}) collective-permute-start(bf16[4,320,256]{2,1,0:T(8,128)(2,1)} %bitcast.11), channel_id=1, source_target_pairs={{0,16},{16,0},{1,17},{17,1},{2,18},{18,2},{3,19},{19,3},{4,20},{20... | collective-permute-start | bytes 1966088 | tf_op jit(solution)/shard_map/ppermute | solution.py:452
  6.5 14.5 %all-to-all-start = ((f32[16,8,128]{2,1,0:T(8,128)}), f32[16,8,128]{2,1,0:T(8,128)S(1)}, u32[]{:S(2)}, u32[]{:S(2)}) async-start(f32[16,8,128]{2,1,0:T(8,128)} %get-tuple-element.23), calls=%async_computation | async-start | bytes 131072 | tf_op jit(solution)/shard_map/all_to_all | solution.py:384
  21.0 4.6 %collective-permute-start.3 = (bf16[2,320,256]{2,1,0:T(8,128)(2,1)S(1)}, bf16[2,320,256]{2,1,0:T(8,128)(2,1)S(1)}, u32[]{:S(2)}, u32[]{:S(2)}) collective-permute-start(bf16[2,320,256]{2,1,0:T(8,128)(2,1)S(1)} %collective-permute-done.1.near_ref), channel_id=1, source_target_pairs={{0,16},{16,0},{1,17},{17,1},{2,18},{18,2},{3,19},{19,3},{4,20},{20... | collective-permute-start | bytes 983048 | tf_op jit(solution)/shard_map/ppermute | solution.py:454
  21.0 4.6 %collective-permute-start.4 = (bf16[2,320,256]{2,1,0:T(8,128)(2,1)S(1)}, bf16[2,320,256]{2,1,0:T(8,128)(2,1)S(1)}, u32[]{:S(2)}, u32[]{:S(2)}) collective-permute-start(bf16[2,320,256]{2,1,0:T(8,128)(2,1)S(1)} %collective-permute-done.2.next_ref), channel_id=1, source_target_pairs={{0,16},{16,0},{1,17},{17,1},{2,18},{18,2},{3,19},{19,3},{4,20},{20... | collective-permute-start | bytes 983048 | tf_op jit(solution)/shard_map/ppermute | solution.py:455
  25.7 15.0 %copy-start = (bf16[320,2880]{1,0:T(8,128)(2,1)S(1)}, bf16[320,2880]{1,0:T(8,128)(2,1)}, u32[]{:S(2)}) copy-start(bf16[320,2880]{1,0:T(8,128)(2,1)} %get-tuple-element.40.weight_ref) | copy-start | bytes 5529604

commit v10 on v9

--- a/solution.py
+++ b/solution.py
@@ -269,10 +269,11 @@
     )
     mix = mixer(cols_ref, rows_ref, chans)
     line = 3 * chans
+    for copy in copies:
+        copy.wait()
     if rows < 3:
         steered_ref[...] = jnp.zeros_like(steered_ref)
     for at in range(rows):
-        copies[at].wait()
         put_taps(taps_ref, at, mix(own_ref[at], far_ref[at]))
         if at >= 2:
             total = matmul(weight_ref, taps_ref[(at - 2) * line : (at + 1) * line, :], 0)
@@ -342,12 +343,11 @@
 
 def second_kernel(
     inner_ref, outer_ref, lat_hbm, seen_ref, rows_ref, weight_ref,
-    out_hbm,
-    taps_ref, cols_ref, lat_ref, out_ref, sems, out_sems,
+    out_ref,
+    taps_ref, cols_ref, lat_ref, sems,
 ):
     rows, chans, cols = lat_ref.shape
     copies = fetch([(lat_hbm.at[k], lat_ref.at[k]) for k in range(rows)], sems)
-    outs = []
     wide = padded_lanes(chans)
     size = chans // GROUPS
     peers = lax.axis_size("patch")
@@ -360,6 +360,8 @@
     spread_columns(
         [mean_rows[0:1], scale_rows[0:1], 0.5 * rows_ref[5:6], rows_ref[6:7]], chans, cols_ref
     )
+    for copy in copies:
+        copy.wait()
     line = 3 * chans
     inside = max(rows - 2, 0)
     half = outer_ref.shape[0] // 2
@@ -373,11 +375,7 @@
         put_taps(taps_ref, at, value if keep is None else value * keep)
         if at >= 2:
             total = matmul(weight_ref, taps_ref[(at - 2) * line : (at + 1) * line, :], 0)
-            copies[at - 2].wait()
             out_ref[at - 2] = (lat_ref[at - 2].astype(F32) + (total + twice(cols_ref[3]))).astype(BF16)
-            outs += fetch([(out_ref.at[at - 2], out_hbm.at[at - 2])], out_sems, at - 2)
-    for copy in outs:
-        copy.wait()
 
 
 def everyone(tiles, axes):
@@ -486,15 +484,13 @@
     seen = everyone(sent, "patch")
     image = pl.pallas_call(
         second_kernel,
-        out_shape=pltpu.HBM((rows, chans, cols), BF16),
+        out_shape=jax.ShapeDtypeStruct((rows, chans, cols), BF16),
         in_specs=[VMEM] * 2 + [ANY] + [VMEM] * 3,
-        out_specs=ANY,
+        out_specs=VMEM,
         scratch_shapes=[
             pltpu.VMEM(((rows + 2) * 3 * chans, cols), BF16),
             pltpu.VMEM((4, chans, LANES), F32),
             pltpu.VMEM((rows, chans, cols), BF16),
-            pltpu.VMEM((rows, chans, cols), BF16),
-            pltpu.SemaphoreType.DMA((rows,)),
             pltpu.SemaphoreType.DMA((rows,)),
         ],
         compiler_params=LIMIT,

time: 47.7 us -> 44.9 us (0.941)
  Pallas kernels: 20.7 us -> 17.9 us
    pallas_call x1, Pallas kernels: 6.73 us -> 4.49 us  [body(): pl.pallas_call(second_kernel, out_shape=jax.ShapeDtypeStruct((rows, chans...]
    pallas_call x1, Pallas kernels: 4.11 us -> 3.51 us  [body(): pl.pallas_call(inner_kernel, out_shape=[pltpu.VMEM((max(rows - 2, 1), cha...]
where the time goes in v10:
time: 44.9 us; the launch traced here: 44.6 us
  Pallas kernels  17.9 us (40%)
  starting transfers between devices  12 us (27%)
  blocking collectives  12 us (27%)
  waiting for transfers between devices  1.98 us (4%)
  between operations  0.73 us (2%)
    all_to_all x1, blocking collectives, everyone(): return lax.all_to_all(tiles, axes, 0, 0)  12 us
    all_to_all x1, starting transfers between devices, everyone(): return lax.all_to_all(tiles, axes, 0, 0)  7.77 us
    pallas_call x1, Pallas kernels, body(): pl.pallas_call(second_kernel, out_shape=jax.ShapeDtypeStruct((rows, chans...  4.49 us
    pallas_call x1, Pallas kernels, body(): pl.pallas_call(prepare_kernel, out_shape=[pltpu.VMEM((chans, deep), BF16)...  4.14 us
    pallas_call x1, Pallas kernels, body(): pl.pallas_call(inner_kernel, out_shape=[pltpu.VMEM((max(rows - 2, 1), cha...  3.51 us
    pallas_call x1, Pallas kernels, body(): pl.pallas_call(outer_kernel, out_shape=[pltpu.VMEM((2 * REACH, chans, col...  3.04 us
    ppermute x1, starting transfers between devices, body(): lax.ppermute(near_edge, 'patch', [(i, i ^ 1) for i in range(patches)])  3 us
    pallas_call x1, Pallas kernels, body(): pl.pallas_call(stats_kernel, out_shape=[pltpu.VMEM((2 * patches, tile_one...  2.71 us
  transfers between devices with their start and end apart: 6, of which 1 were waited for; matrix products, arithmetic and copies ran while one was open for 0% of the time, Pallas kernels for 17%

profile of v10, /device:TPU:0, one launch (start us, length us, event | category | flops | bytes accessed | tf_op | source)
XLA Modules:
  0.0 44.6 jit_solution(5291418319709439507)
XLA Ops:
  0.0 2.7 %stats.1 = (f32[16,8,128]{2,1,0:T(8,128)}, bf16[2,320,256]{2,1,0:T(8,128)(2,1)}, bf16[2,320,256]{2,1,0:T(8,128)(2,1)}) custom-call(bf16[4,320,256]{2,1,0:T(8,128)(2,1)} %bitcast.10, bf16[1,1280]{1,0:T(2,128)(2,1)} %embed_hbm.1, bf16[160,320]{1,0:T(8,128)(2,1)} %weight_hbm.1), custom_call_target="tpu_custom_call" | custom-call | tf_op jit(solution)/shard_map/stats/pallas_call | solution.py:407
  2.7 3.0 %collective-permute-start.1 = (bf16[2,320,256]{2,1,0:T(8,128)(2,1)}, bf16[2,320,256]{2,1,0:T(8,128)(2,1)S(1)}, u32[]{:S(2)}, u32[]{:S(2)}) collective-permute-start(bf16[2,320,256]{2,1,0:T(8,128)(2,1)} %get-tuple-element.25), channel_id=1, source_target_pairs={{0,2},{2,0},{4,6},{6,4},{8,10},{10,8},{12,14},{14,12},{1,3},{3,1},... | collective-permute-start | bytes 983048 | tf_op jit(solution)/shard_map/ppermute | solution.py:426
  5.7 0.7 %collective-permute-start.2 = (bf16[2,320,256]{2,1,0:T(8,128)(2,1)}, bf16[2,320,256]{2,1,0:T(8,128)(2,1)S(1)}, u32[]{:S(2)}, u32[]{:S(2)}) collective-permute-start(bf16[2,320,256]{2,1,0:T(8,128)(2,1)} %get-tuple-element.26), channel_id=1, source_target_pairs={{2,4},{6,8},{10,12},{4,2},{8,6},{12,10},{3,5},{7,9},{11,13},{5,3},... | collective-permute-start | bytes 983048 | tf_op jit(solution)/shard_map/ppermute | solution.py:428
  6.4 0.1 collective-permute-start
  6.5 7.8 %all-to-all-start = ((f32[16,8,128]{2,1,0:T(8,128)}), f32[16,8,128]{2,1,0:T(8,128)S(1)}, u32[]{:S(2)}, u32[]{:S(2)}) async-start(f32[16,8,128]{2,1,0:T(8,128)} %get-tuple-element.23), calls=%async_computation | async-start | bytes 131072 | tf_op jit(solution)/shard_map/all_to_all | solution.py:382
  14.9 4.1 %prepare.1 = (bf16[320,2880]{1,0:T(8,128)(2,1)S(1)}, bf16[320,2880]{1,0:T(8,128)(2,1)}, f32[8,384]{1,0:T(8,128)S(1)}) custom-call(bf16[2880,320]{1,0:T(8,128)(2,1)} %bitcast.14, bf16[2880,320]{1,0:T(8,128)(2,1)} %bitcast.15, f32[320]{0:T(512)} %gain_one.1, f32[320]{0:T(512)} %shift_one.1, f32[320]{0:T(512)} %bias_one.1, f32[320]{0:T(512)} %time_bias.1, ...), custom_call_target="tpu_custom_call" | custom-call | tf_op jit(solution)/shard_map/prepare/pallas_call | solution.py:433
  19.1 2.0 %all-to-all-done.seen_ref = f32[16,8,128]{2,1,0:T(8,128)S(1)} async-done(((f32[16,8,128]{2,1,0:T(8,128)}), f32[16,8,128]{2,1,0:T(8,128)S(1)}, u32[]{:S(2)}, u32[]{:S(2)}) %all-to-all-start) | async-done | bytes 65568 | tf_op jit(solution)/shard_map/all_to_all | solution.py:382
  21.0 0.0 collective-permute-done.1.near_ref
  21.0 0.0 collective-permute-done.2.next_ref
  21.0 0.0 collective-permute-start.3
  21.0 0.5 %collective-permute-start.4 = (bf16[2,320,256]{2,1,0:T(8,128)(2,1)S(1)}, bf16[2,320,256]{2,1,0:T(8,128)(2,1)S(1)}, u32[]{:S(2)}, u32[]{:S(2)}) collective-permute-start(bf16[2,320,256]{2,1,0:T(8,128)(2,1)S(1)} %collective-permute-done.2.next_ref), channel_id=1, source_target_pairs={{0,16},{16,0},{1,17},{17,1},{2,18},{18,2},{3,19},{19,3},{4,20},{20... | collective-permute-start | bytes 983048 | tf_op jit(solution)/shard_map/ppermute | solution.py:453
  21.5 0.0 collective-permute-done.far_ref
  21.5 3.5 %inner.1 = (f32[2,320,256]{2,1,0:T(8,128)S(1)}, bf16[3840,256]{1,0:T(8,128)(2,1)S(1)}, f32[6,320,128]{2,1,0:T(8,128)S(1)}) custom-call(bf16[4,320,256]{2,1,0:T(8,128)(2,1)} %bitcast.12, bf16[4,320,256]{2,1,0:T(8,128)(2,1)S(1)} %collective-permute-done.far_ref, f32[16,8,128]{2,1,0:T(8,128)S(1)} %all-to-all-done.seen_ref, ...), custom_call_target="tpu_custom_call" | custom-call | tf_op jit(solution)/shard_map/inner/pallas_call | solution.py:455
  25.1 0.0 collective-permute-done.3.far_near_ref
  25.1 0.0 collective-permute-done.4.far_next_ref
  25.1 0.0 copy-start
  25.1 3.0 %outer.1 = (f32[4,320,256]{2,1,0:T(8,128)S(1)}, f32[8,8,128]{2,1,0:T(8,128)S(1)}) custom-call(bf16[2,320,256]{2,1,0:T(8,128)(2,1)S(1)} %collective-permute-done.1.near_ref, bf16[2,320,256]{2,1,0:T(8,128)(2,1)S(1)} %collective-permute-done.2.next_ref, bf16[2,320,256]{2,1,0:T(8,128)(2,1)S(1)} %collective-permute-done.3.far_near_ref, ...), custom_call_target="tpu_custom_call" | custom-call | tf_op jit(solution)/shard_map/outer/pallas_call | solution.py:469
  28.1 12.0 %all_to_all.10.seen_ref = f32[8,8,128]{2,1,0:T(8,128)S(1)} all-to-all(f32[8,8,128]{2,1,0:T(8,128)S(1)} %get-tuple-element.39), channel_id=1, replica_groups=mesh['cfg'=2,'patch'=8,'req'=2] {'patch'}, dimensions={0} | all-to-all | bytes 65536 | tf_op jit(solution)/shard_map/all_to_all | solution.py:382
  40.1 0.0 copy-done
  40.1 4.5 %second.1 = bf16[4,320,256]{2,1,0:T(8,128)(2,1)} custom-call(f32[2,320,256]{2,1,0:T(8,128)S(1)} %get-tuple-element.33.inner_ref, f32[4,320,256]{2,1,0:T(8,128)S(1)} %get-tuple-element.38.outer_ref, bf16[4,320,256]{2,1,0:T(8,128)(2,1)} %bitcast.13, f32[8,8,128]{2,1,0:T(8,128)S(1)} %all_to_all.10.seen_ref, f32[8,384]{1,0:T(8,128)S(1)} %get-tuple-element.31.rows_ref, ...), custom_call_target="tpu_custom_call" | custom-call | tf_op jit(solution)/shard_map/second/pallas_call | solution.py:485
Async XLA Ops:
  2.7 18.3 %collective-permute-start.1 = (bf16[2,320,256]{2,1,0:T(8,128)(2,1)}, bf16[2,320,256]{2,1,0:T(8,128)(2,1)S(1)}, u32[]{:S(2)}, u32[]{:S(2)}) collective-permute-start(bf16[2,320,256]{2,1,0:T(8,128)(2,1)} %get-tuple-element.25), channel_id=1, source_target_pairs={{0,2},{2,0},{4,6},{6,4},{8,10},{10,8},{12,14},{14,12},{1,3},{3,1},... | collective-permute-start | bytes 983048 | tf_op jit(solution)/shard_map/ppermute | solution.py:426
  5.7 15.3 %collective-permute-start.2 = (bf16[2,320,256]{2,1,0:T(8,128)(2,1)}, bf16[2,320,256]{2,1,0:T(8,128)(2,1)S(1)}, u32[]{:S(2)}, u32[]{:S(2)}) collective-permute-start(bf16[2,320,256]{2,1,0:T(8,128)(2,1)} %get-tuple-element.26), channel_id=1, source_target_pairs={{2,4},{6,8},{10,12},{4,2},{8,6},{12,10},{3,5},{7,9},{11,13},{5,3},... | collective-permute-start | bytes 983048 | tf_op jit(solution)/shard_map/ppermute | solution.py:428
  6.4 15.1 %collective-permute-start = (bf16[4,320,256]{2,1,0:T(8,128)(2,1)}, bf16[4,320,256]{2,1,0:T(8,128)(2,1)S(1)}, u32[]{:S(2)}, u32[]{:S(2)}) collective-permute-start(bf16[4,320,256]{2,1,0:T(8,128)(2,1)} %bitcast.11), channel_id=1, source_target_pairs={{0,16},{16,0},{1,17},{17,1},{2,18},{18,2},{3,19},{19,3},{4,20},{20... | collective-permute-start | bytes 1966088 | tf_op jit(solution)/shard_map/ppermute | solution.py:450
  6.5 14.5 %all-to-all-start = ((f32[16,8,128]{2,1,0:T(8,128)}), f32[16,8,128]{2,1,0:T(8,128)S(1)}, u32[]{:S(2)}, u32[]{:S(2)}) async-start(f32[16,8,128]{2,1,0:T(8,128)} %get-tuple-element.23), calls=%async_computation | async-start | bytes 131072 | tf_op jit(solution)/shard_map/all_to_all | solution.py:382
  21.0 4.0 %collective-permute-start.3 = (bf16[2,320,256]{2,1,0:T(8,128)(2,1)S(1)}, bf16[2,320,256]{2,1,0:T(8,128)(2,1)S(1)}, u32[]{:S(2)}, u32[]{:S(2)}) collective-permute-start(bf16[2,320,256]{2,1,0:T(8,128)(2,1)S(1)} %collective-permute-done.1.near_ref), channel_id=1, source_target_pairs={{0,16},{16,0},{1,17},{17,1},{2,18},{18,2},{3,19},{19,3},{4,20},{20... | collective-permute-start | bytes 983048 | tf_op jit(solution)/shard_map/ppermute | solution.py:452
  21.0 4.0 %collective-permute-start.4 = (bf16[2,320,256]{2,1,0:T(8,128)(2,1)S(1)}, bf16[2,320,256]{2,1,0:T(8,128)(2,1)S(1)}, u32[]{:S(2)}, u32[]{:S(2)}) collective-permute-start(bf16[2,320,256]{2,1,0:T(8,128)(2,1)S(1)} %collective-permute-done.2.next_ref), channel_id=1, source_target_pairs={{0,16},{16,0},{1,17},{17,1},{2,18},{18,2},{3,19},{19,3},{4,20},{20... | collective-permute-start | bytes 983048 | tf_op jit(solution)/shard_map/ppermute | solution.py:453
  25.1 15.0 %copy-start = (bf16[320,2880]{1,0:T(8,128)(2,1)S(1)}, bf16[320,2880]{1,0:T(8,128)(2,1)}, u32[]{:S(2)}) copy-start(bf16[320,2880]{1,0:T(8,128)(2,1)} %get-tuple-element.40.weight_ref) | copy-start | bytes 5529604

commit v11 on v8

--- a/solution.py
+++ b/solution.py
@@ -108,37 +108,40 @@
     return -(-rows * chans // LANES // 8) * 8
 
 
+def fetch(pairs, sems, first=0):
+    copies = [pltpu.make_async_copy(a, b, sems.at[first + k]) for k, (a, b) in enumerate(pairs)]
+    for copy in copies:
+        copy.start()
+    return copies
+
+
 def stats_kernel(
-    lat_hbm, embed_hbm, weight_hbm,
-    lat_ref, out_ref, near_ref, next_ref,
-    embed_ref, weight_ref, sems, edge_sems,
+    lat_hbm, embed_hbm, weight_hbm, gain_one, shift_one, bias_one, time_bias, gain_two, shift_two, bias_two, steer, conv_hbm,
+    lat_ref, out_ref, near_ref, next_ref, rows_ref, conv_ref,
+    embed_ref, weight_ref, sems, edge_sems, row_sems, *vector_refs,
 ):
     rows, chans, _ = lat_ref.shape
-    copies = [
-        pltpu.make_async_copy(lat_hbm.at[k], lat_ref.at[k], sems.at[k]) for k in range(rows)
-    ]
-    copies.append(pltpu.make_async_copy(embed_hbm, embed_ref, sems.at[rows]))
-    copies.append(pltpu.make_async_copy(weight_hbm, weight_ref, sems.at[rows + 1]))
     reach = near_ref.shape[0]
     last = rows - reach
     near_at = jnp.where(lax.rem(lax.axis_index("patch"), 2) == 0, last, 0)
-    edges = [
-        pltpu.make_async_copy(lat_hbm.at[pl.ds(near_at, reach)], near_ref, edge_sems.at[0]),
-        pltpu.make_async_copy(lat_hbm.at[pl.ds(last - near_at, reach)], next_ref, edge_sems.at[1]),
-    ]
-    for copy in copies + edges:
-        copy.start()
-    waits = list(copies[:rows])
-
-    def values():
-        for k in range(rows):
-            if waits:
-                waits.pop(0).wait()
-            yield lat_ref[k].astype(F32)
-
-    mean, squares = channel_moments(values, chans)
-    copies[rows].wait()
-    copies[rows + 1].wait()
+    copies = fetch(
+        [(lat_hbm.at[k], lat_ref.at[k]) for k in range(rows)]
+        + [(embed_hbm, embed_ref), (weight_hbm, weight_ref)],
+        sems,
+    )
+    vectors = (gain_one, shift_one, bias_one, time_bias, gain_two, shift_two, bias_two)
+    copies += fetch(zip(vectors, vector_refs), row_sems)
+    edges = fetch(
+        [
+            (lat_hbm.at[pl.ds(near_at, reach)], near_ref),
+            (lat_hbm.at[pl.ds(last - near_at, reach)], next_ref),
+            (conv_hbm, conv_ref),
+        ],
+        edge_sems,
+    )
+    for copy in copies:
+        copy.wait()
+    mean, squares = channel_moments(lambda: (lat_ref[k].astype(F32) for k in range(rows)), chans)
     own = weight_ref.shape[0]
     length = embed_ref.shape[1]
     embed = jnp.broadcast_to(embed_ref[...].astype(F32), (8, length))
@@ -146,42 +149,18 @@
     act = (embed / (1.0 + jnp.exp(-embed))).astype(BF16)
     time_part = jnp.dot(act, weight_ref[...], preferred_element_type=F32)[0:1]
     put_rows([mean, squares, time_part], out_ref)
+    wide = rows_ref.shape[1]
+    lines = [widen(v[...].reshape(1, -1), wide) for v in vector_refs]
+    rows_ref[...] = jnp.concatenate(lines + [jnp.full((1, wide), steer[0], F32)], axis=0)
     for copy in edges:
         copy.wait()
 
 
-def parts_of(deep, part=8 * LANES):
-    return [(at, min(part, deep - at)) for at in range(0, deep, part)]
-
-
-def fetch(pairs, sems, first=0):
-    copies = [pltpu.make_async_copy(a, b, sems.at[first + k]) for k, (a, b) in enumerate(pairs)]
-    for copy in copies:
-        copy.start()
-    return copies
-
-
-def prepare_kernel(
-    one_hbm, two_hbm, gain_one, shift_one, bias_one, time_bias, gain_two, shift_two, bias_two, steer,
-    one_out, two_out, rows_ref, one_ref, two_ref, sems, row_sems, *vector_refs,
-):
-    vectors = (gain_one, shift_one, bias_one, time_bias, gain_two, shift_two, bias_two)
-    lines = fetch(zip(vectors, vector_refs), row_sems)
-    parts = parts_of(one_ref.shape[0])
-    sides = ((one_hbm, one_ref, one_out), (two_hbm, two_ref, two_out))
-    copies = [
-        fetch([(a.at[pl.ds(*p)], b.at[pl.ds(*p)]) for p in parts], sems, k * len(parts))
-        for k, (a, b, _) in enumerate(sides)
-    ]
-    for line in lines:
-        line.wait()
-    wide = rows_ref.shape[1]
-    rows = [widen(v[...].reshape(1, -1), wide) for v in vector_refs]
-    rows_ref[...] = jnp.concatenate(rows + [jnp.broadcast_to(steer[...], (1, wide))], axis=0)
-    for waits, (_, held, target) in zip(copies, sides):
-        for wait, (at, size) in zip(waits, parts):
-            wait.wait()
-            target[:, at : at + size] = held[at : at + size, :].T
+def turn(source, target, part=8 * LANES):
+    deep = source.shape[0]
+    for at in range(0, deep, part):
+        size = min(part, deep - at)
+        target[:, at : at + size] = source[at : at + size, :].T
 
 
 def spread_columns(rows, chans, cols_ref):
@@ -237,10 +216,11 @@
 
 
 def inner_kernel(
-    own_ref, far_ref, seen_ref, rows_ref, weight_ref,
-    steered_ref, taps_ref, cols_ref,
+    own_ref, far_ref, seen_ref, rows_ref, raw_ref,
+    steered_ref, taps_ref, cols_ref, weight_ref,
 ):
     rows, chans, cols = own_ref.shape
+    turn(raw_ref, weight_ref)
     wide = padded_lanes(chans)
     size = chans // GROUPS
     cfg, peers = lax.axis_index("cfg"), lax.axis_size("patch")
@@ -268,8 +248,8 @@
 
 
 def outer_kernel(
-    near_ref, next_ref, far_near_ref, far_next_ref, inner_ref, inner_taps_ref, cols_ref, rows_ref, weight_ref,
-    steered_ref, out_ref,
+    near_ref, next_ref, far_near_ref, far_next_ref, inner_ref, inner_taps_ref, cols_ref, rows_ref, weight_ref, raw_ref,
+    steered_ref, out_ref, turned_ref,
     taps_ref, edge_ref,
 ):
     reach, chans, cols = near_ref.shape
@@ -318,6 +298,7 @@
             enter(ready)
             ready += 1
         steered_ref[place[at]] = conv(at) + twice(cols_ref[5])
+    turn(raw_ref, turned_ref)
 
     def own_rows():
         for k in range(rows):
@@ -367,6 +348,7 @@
 
 
 VMEM = pl.BlockSpec(memory_space=pltpu.VMEM)
+SMEM = pl.BlockSpec(memory_space=pltpu.SMEM)
 ANY = pl.BlockSpec(memory_space=pl.ANY)
 LIMIT = pltpu.CompilerParams(vmem_limit_bytes=12 * 1024 * 1024)
 
@@ -385,82 +367,78 @@
     deep = 9 * chans
     patches = lax.axis_size("patch")
     swap = [(0, 1), (1, 0)]
-    line = lambda vector: vector.reshape(1, -1)
-
     tile_one = tile_height(chans, 3)
-    held, sent, near_edge, next_edge = pl.pallas_call(
+    held, sent, near_edge, next_edge, vectors, raw_one = pl.pallas_call(
         stats_kernel,
         out_shape=[
             pltpu.VMEM((rows, chans, cols), BF16),
             pltpu.VMEM((2 * patches, tile_one, LANES), F32),
             pltpu.VMEM((REACH, chans, cols), BF16),
             pltpu.VMEM((REACH, chans, cols), BF16),
-        ],
-        in_specs=[ANY] * 3,
-        out_specs=[VMEM] * 4,
+            pltpu.VMEM((8, wide), F32),
+            pltpu.VMEM((deep, chans), BF16),
+        ],
+        in_specs=[ANY] * 10 + [SMEM, ANY],
+        out_specs=[VMEM] * 6,
         scratch_shapes=[
             pltpu.VMEM(time_embed.shape, BF16),
             pltpu.VMEM(time_weight.shape, BF16),
             pltpu.SemaphoreType.DMA((rows + 2,)),
-            pltpu.SemaphoreType.DMA((2,)),
-        ],
+            pltpu.SemaphoreType.DMA((3,)),
+            pltpu.SemaphoreType.DMA((7,)),
+        ]
+        + [pltpu.VMEM((chans,), F32)] * 7,
         compiler_params=LIMIT,
         name="stats",
-    )(in_hbm(own), in_hbm(time_embed), in_hbm(time_weight))
+    )(
+        in_hbm(own), in_hbm(time_embed), in_hbm(time_weight), in_hbm(gain_one), in_hbm(shift_one),
+        in_hbm(bias_one), in_hbm(time_bias), in_hbm(gain_two), in_hbm(shift_two), in_hbm(bias_two), steer_scale,
+        in_hbm(conv_one.reshape(deep, chans)),
+    )
     near = lax.ppermute(near_edge, "patch", [(i, i ^ 1) for i in range(patches)])
     steps = [(i, i + 1) for i in range(1, patches - 1, 2)]
     following = lax.ppermute(next_edge, "patch", steps + [(j, i) for i, j in steps])
     seen = everyone(sent, ("cfg", "patch"))
 
-    weights = (conv_one.reshape(deep, chans), conv_two.reshape(deep, chans))
-    source, *weights, _ = lax.optimization_barrier((own, *weights, sent))
-    turned_one, turned_two, vectors = pl.pallas_call(
-        prepare_kernel,
-        out_shape=[pltpu.VMEM((chans, deep), BF16)] * 2 + [pltpu.VMEM((8, wide), F32)],
-        in_specs=[ANY] * 9 + [VMEM],
-        out_specs=[VMEM] * 3,
-        scratch_shapes=[pltpu.VMEM((deep, chans), BF16)] * 2
-        + [pltpu.SemaphoreType.DMA((2 * len(parts_of(deep)),)), pltpu.SemaphoreType.DMA((7,))]
-        + [pltpu.VMEM((chans,), F32)] * 7,
-        compiler_params=LIMIT,
-        name="prepare",
-    )(
-        in_hbm(weights[0]), in_hbm(weights[1]), in_hbm(gain_one), in_hbm(shift_one), in_hbm(bias_one),
-        in_hbm(time_bias), in_hbm(gain_two), in_hbm(shift_two), in_hbm(bias_two), line(steer_scale),
-    )
+    source, _ = lax.optimization_barrier((own, sent))
     far = lax.ppermute(source, "cfg", swap)
-    near, following, vectors, seen = lax.optimization_barrier((near, following, vectors, seen))
+    near, following, seen = lax.optimization_barrier((near, following, seen))
     far_near = lax.ppermute(near, "cfg", swap)
     far_next = lax.ppermute(following, "cfg", swap)
 
-    inner, taps, columns = pl.pallas_call(
+    inner, taps, columns, turned_one = pl.pallas_call(
         inner_kernel,
         out_shape=[
             pltpu.VMEM((max(rows - 2, 1), chans, cols), F32),
             pltpu.VMEM((rows * 3 * chans, cols), BF16),
             pltpu.VMEM((6, chans, LANES), F32),
+            pltpu.VMEM((chans, deep), BF16),
         ],
         in_specs=[VMEM] * 5,
-        out_specs=[VMEM] * 3,
+        out_specs=[VMEM] * 4,
         compiler_params=LIMIT,
         name="inner",
-    )(held, far, seen, vectors, turned_one)
+    )(held, far, seen, vectors, raw_one)
     tile_two = tile_height(chans, 2)
-    outer, sent = pl.pallas_call(
+    outer, sent, turned_two = pl.pallas_call(
         outer_kernel,
         out_shape=[
             pltpu.VMEM((2 * REACH, chans, cols), F32),
             pltpu.VMEM((patches, tile_two, LANES), F32),
-        ],
-        in_specs=[VMEM] * 9,
-        out_specs=[VMEM] * 2,
+            pltpu.VMEM((chans, deep), BF16),
+        ],
+        in_specs=[VMEM] * 10,
+        out_specs=[VMEM] * 3,
         scratch_shapes=[
             pltpu.VMEM((2 * REACH * 3 * chans, cols), BF16),
             pltpu.VMEM((2, 2 * REACH, chans, cols), BF16),
         ],
         compiler_params=LIMIT,
         name="outer",
-    )(near, following, far_near, far_next, inner, taps, columns, vectors, turned_one)
+    )(
+        near, following, far_near, far_next, inner, taps, columns, vectors, turned_one,
+        conv_two.reshape(deep, chans),
+    )
     seen = everyone(sent, "patch")
     image = pl.pallas_call(
         second_kernel,

time: 45.6 us -> 44.5 us (0.976)
  blocking collectives: 12 us -> 26.4 us
  starting transfers between devices: 12.1 us -> 4.19 us
  Pallas kernels: 17.9 us -> 12.9 us
  local copies, waits for them, and re-layouts: 1.29 us -> 0.01 us
  waiting for transfers between devices: 1.29 us -> 0.01 us
    all_to_all x1 -> x2, blocking collectives: 12 us -> 26.4 us  [everyone(): return lax.all_to_all(tiles, axes, 0, 0)]
    all_to_all x1 -> x0, starting transfers between devices: 7.16 us -> none  [everyone(): return lax.all_to_all(tiles, axes, 0, 0)]
    pallas_call x1 -> x0, Pallas kernels: 3.59 us -> none  [body(): pl.pallas_call(prepare_kernel, out_shape=[pltpu.VMEM((chans, deep), BF16)...]
    all_to_all x1 -> x0, waiting for transfers between devices: 1.28 us -> none  [everyone(): return lax.all_to_all(tiles, axes, 0, 0)]
    unnamed x4, local copies, waits for them, and re-layouts: 1.29 us -> 0.01 us
    pallas_call x1, Pallas kernels: 4.14 us -> 3.19 us  [body(): pl.pallas_call(outer_kernel, out_shape=[pltpu.VMEM((2 * REACH, chans, col...]
    ppermute x1, starting transfers between devices: 1.42 us -> 0.67 us  [body(): lax.ppermute(next_edge, 'patch', steps + [(j, i) for i, j in steps])]
  transfers between devices with their start and end apart: 6 -> 5, of which waited for: 1 -> 0; matrix products, arithmetic and copies ran while one was open for 0% -> 0% of each run, Pallas kernels for 15% -> 7%
where the time goes in v11:
time: 44.5 us; the launch traced here: 44.3 us
  blocking collectives  26.4 us (59%)
  Pallas kernels  12.9 us (29%)
  starting transfers between devices  4.19 us (9%)
  between operations  0.78 us (2%)
    all_to_all x2, blocking collectives, everyone(): return lax.all_to_all(tiles, axes, 0, 0)  26.4 us
    pallas_call x1, Pallas kernels, body(): pl.pallas_call(second_kernel, out_shape=jax.ShapeDtypeStruct((rows, chans...  4.14 us
    pallas_call x1, Pallas kernels, body(): pl.pallas_call(outer_kernel, out_shape=[pltpu.VMEM((2 * REACH, chans, col...  3.19 us
    pallas_call x1, Pallas kernels, body(): pl.pallas_call(inner_kernel, out_shape=[pltpu.VMEM((max(rows - 2, 1), cha...  3.17 us
    ppermute x1, starting transfers between devices, body(): lax.ppermute(near_edge, 'patch', [(i, i ^ 1) for i in range(patches)])  3 us
    pallas_call x1, Pallas kernels, body(): pl.pallas_call(stats_kernel, out_shape=[pltpu.VMEM((rows, chans, cols), B...  2.42 us
  transfers between devices with their start and end apart: 5, of which 0 were waited for; matrix products, arithmetic and copies ran while one was open for 0% of the time, Pallas kernels for 7%

profile of v11, /device:TPU:0, one launch (start us, length us, event | category | flops | bytes accessed | tf_op | source)
XLA Modules:
  0.0 44.3 jit_solution(8866899583347861980)
XLA Ops:
  0.0 0.0 copy-start.1
  0.7 2.4 %stats.1 = (bf16[4,320,256]{2,1,0:T(8,128)(2,1)S(1)}, f32[16,8,128]{2,1,0:T(8,128)S(1)}, bf16[2,320,256]{2,1,0:T(8,128)(2,1)S(1)}, bf16[2,320,256]{2,1,0:T(8,128...) custom-call(bf16[4,320,256]{2,1,0:T(8,128)(2,1)} %bitcast.10, bf16[1,1280]{1,0:T(2,128)(2,1)} %embed_hbm.1, ...), custom_call_target="tpu_custom_call" | custom-call | tf_op jit(solution)/shard_map/stats/pallas_call | solution.py:371
  3.2 0.0 copy-start
  3.2 3.0 %collective-permute-start.1 = (bf16[2,320,256]{2,1,0:T(8,128)(2,1)S(1)}, bf16[2,320,256]{2,1,0:T(8,128)(2,1)S(1)}, u32[]{:S(2)}, u32[]{:S(2)}) collective-permute-start(bf16[2,320,256]{2,1,0:T(8,128)(2,1)S(1)} %get-tuple-element.25), channel_id=1, source_target_pairs={{0,2},{2,0},{4,6},{6,4},{8,10},{10,8},{12,14},{14,12},{1,3},{3,1},... | collective-permute-start | bytes 983048 | tf_op jit(solution)/shard_map/ppermute | solution.py:398
  6.2 0.0 copy-done.1
  6.2 0.0 collective-permute-start
  6.2 0.7 %collective-permute-start.2 = (bf16[2,320,256]{2,1,0:T(8,128)(2,1)S(1)}, bf16[2,320,256]{2,1,0:T(8,128)(2,1)S(1)}, u32[]{:S(2)}, u32[]{:S(2)}) collective-permute-start(bf16[2,320,256]{2,1,0:T(8,128)(2,1)S(1)} %get-tuple-element.26), channel_id=1, source_target_pairs={{2,4},{6,8},{10,12},{4,2},{8,6},{12,10},{3,5},{7,9},{11,13},{5,3},... | collective-permute-start | bytes 983048 | tf_op jit(solution)/shard_map/ppermute | solution.py:400
  6.9 14.2 %all_to_all.10.seen_ref = f32[16,8,128]{2,1,0:T(8,128)S(1)} all-to-all(f32[16,8,128]{2,1,0:T(8,128)S(1)} %get-tuple-element.23), channel_id=1, replica_groups=mesh['cfg'=2,'patch'=8,'req'=2] {'cfg','patch'}, dimensions={0} | all-to-all | bytes 131072 | tf_op jit(solution)/shard_map/all_to_all | solution.py:347
  21.1 0.0 collective-permute-done.1.near_ref
  21.1 0.0 collective-permute-done.2.next_ref
  21.1 0.1 collective-permute-start.3
  21.2 0.4 collective-permute-start.4
  21.6 0.0 collective-permute-done.far_ref
  21.6 3.2 %inner.1 = (f32[2,320,256]{2,1,0:T(8,128)S(1)}, bf16[3840,256]{1,0:T(8,128)(2,1)S(1)}, f32[6,320,128]{2,1,0:T(8,128)S(1)}, bf16[320,2880]{1,0:T(8,128)(2,1)S(1)}) custom-call(bf16[4,320,256]{2,1,0:T(8,128)(2,1)S(1)} %get-tuple-element.22.own_ref.lat_ref, bf16[4,320,256]{2,1,0:T(8,128)(2,1)S(1)} %collective-permute-done.far_ref, ...), custom_call_target="tpu_custom_call" | custom-call | tf_op jit(solution)/shard_map/inner/pallas_call | solution.py:409
  24.8 0.0 collective-permute-done.3.far_near_ref
  24.8 0.0 collective-permute-done.4.far_next_ref
  24.8 0.0 copy-done
  24.8 3.2 %outer.1 = (f32[4,320,256]{2,1,0:T(8,128)S(1)}, f32[8,8,128]{2,1,0:T(8,128)S(1)}, bf16[320,2880]{1,0:T(8,128)(2,1)S(1)}) custom-call(bf16[2,320,256]{2,1,0:T(8,128)(2,1)S(1)} %collective-permute-done.1.near_ref, bf16[2,320,256]{2,1,0:T(8,128)(2,1)S(1)} %collective-permute-done.2.next_ref, bf16[2,320,256]{2,1,0:T(8,128)(2,1)S(1)} %collective-permute-done.3.far_near_ref, ...), custom_call_target="tpu_custom_call" | custom-call | tf_op jit(solution)/shard_map/outer/pallas_call | solution.py:423
  28.0 12.1 %all_to_all.11.seen_ref = f32[8,8,128]{2,1,0:T(8,128)S(1)} all-to-all(f32[8,8,128]{2,1,0:T(8,128)S(1)} %get-tuple-element.37), channel_id=1, replica_groups=mesh['cfg'=2,'patch'=8,'req'=2] {'patch'}, dimensions={0} | all-to-all | bytes 65536 | tf_op jit(solution)/shard_map/all_to_all | solution.py:347
  40.1 4.1 %second.1 = bf16[4,320,256]{2,1,0:T(8,128)(2,1)} custom-call(f32[2,320,256]{2,1,0:T(8,128)S(1)} %get-tuple-element.30.inner_ref, f32[4,320,256]{2,1,0:T(8,128)S(1)} %get-tuple-element.36.outer_ref, bf16[4,320,256]{2,1,0:T(8,128)(2,1)S(1)} %get-tuple-element.22.own_ref.lat_ref, f32[8,8,128]{2,1,0:T(8,128)S(1)} %all_to_all.11.seen_ref, ...), custom_call_target="tpu_custom_call" | custom-call | tf_op jit(solution)/shard_map/second/pallas_call | solution.py:443
Async XLA Ops:
  0.0 6.2 %copy-start.1 = (bf16[1,1,4,256,320]{3,4,2,1,0:T(8,128)(2,1)S(1)}, bf16[1,1,4,256,320]{3,4,2,1,0:T(8,128)(2,1)}, u32[]{:S(2)}) copy-start(bf16[1,1,4,256,320]{3,4,2,1,0:T(8,128)(2,1)} %param.13) | copy-start | bytes 1966084
  3.2 21.7 %copy-start = (bf16[3,3,320,320]{3,2,1,0:T(8,128)(2,1)S(1)}, bf16[3,3,320,320]{3,2,1,0:T(8,128)(2,1)}, u32[]{:S(2)}) copy-start(bf16[3,3,320,320]{3,2,1,0:T(8,128)(2,1)} %param.24) | copy-start | bytes 5529604
  3.2 17.9 %collective-permute-start.1 = (bf16[2,320,256]{2,1,0:T(8,128)(2,1)S(1)}, bf16[2,320,256]{2,1,0:T(8,128)(2,1)S(1)}, u32[]{:S(2)}, u32[]{:S(2)}) collective-permute-start(bf16[2,320,256]{2,1,0:T(8,128)(2,1)S(1)} %get-tuple-element.25), channel_id=1, source_target_pairs={{0,2},{2,0},{4,6},{6,4},{8,10},{10,8},{12,14},{14,12},{1,3},{3,1},... | collective-permute-start | bytes 983048 | tf_op jit(solution)/shard_map/ppermute | solution.py:398
  6.2 15.4 %collective-permute-start = (bf16[4,320,256]{2,1,0:T(8,128)(2,1)S(1)}, bf16[4,320,256]{2,1,0:T(8,128)(2,1)S(1)}, u32[]{:S(2)}, u32[]{:S(2)}) collective-permute-start(bf16[4,320,256]{2,1,0:T(8,128)(2,1)S(1)} %bitcast.11), channel_id=1, source_target_pairs={{0,16},{16,0},{1,17},{17,1},{2,18},{18,2},{3,19},{19,3},{4,20},{20... | collective-permute-start | bytes 1966088 | tf_op jit(solution)/shard_map/ppermute | solution.py:404
  6.2 14.9 %collective-permute-start.2 = (bf16[2,320,256]{2,1,0:T(8,128)(2,1)S(1)}, bf16[2,320,256]{2,1,0:T(8,128)(2,1)S(1)}, u32[]{:S(2)}, u32[]{:S(2)}) collective-permute-start(bf16[2,320,256]{2,1,0:T(8,128)(2,1)S(1)} %get-tuple-element.26), channel_id=1, source_target_pairs={{2,4},{6,8},{10,12},{4,2},{8,6},{12,10},{3,5},{7,9},{11,13},{5,3},... | collective-permute-start | bytes 983048 | tf_op jit(solution)/shard_map/ppermute | solution.py:400
  21.1 3.7 %collective-permute-start.3 = (bf16[2,320,256]{2,1,0:T(8,128)(2,1)S(1)}, bf16[2,320,256]{2,1,0:T(8,128)(2,1)S(1)}, u32[]{:S(2)}, u32[]{:S(2)}) collective-permute-start(bf16[2,320,256]{2,1,0:T(8,128)(2,1)S(1)} %collective-permute-done.1.near_ref), channel_id=1, source_target_pairs={{0,16},{16,0},{1,17},{17,1},{2,18},{18,2},{3,19},{19,3},{4,20},{20... | collective-permute-start | bytes 983048 | tf_op jit(solution)/shard_map/ppermute | solution.py:406
  21.2 3.6 %collective-permute-start.4 = (bf16[2,320,256]{2,1,0:T(8,128)(2,1)S(1)}, bf16[2,320,256]{2,1,0:T(8,128)(2,1)S(1)}, u32[]{:S(2)}, u32[]{:S(2)}) collective-permute-start(bf16[2,320,256]{2,1,0:T(8,128)(2,1)S(1)} %collective-permute-done.2.next_ref), channel_id=1, source_target_pairs={{0,16},{16,0},{1,17},{17,1},{2,18},{18,2},{3,19},{19,3},{4,20},{20... | collective-permute-start | bytes 983048 | tf_op jit(solution)/shard_map/ppermute | solution.py:407

commit v12 on v11

--- a/solution.py
+++ b/solution.py
@@ -115,15 +115,24 @@
     return copies
 
 
+def near_at(lat_hbm, reach):
+    return jnp.where(lax.rem(lax.axis_index("patch"), 2) == 0, lat_hbm.shape[0] - reach, 0)
+
+
+def edge_kernel(lat_hbm, next_ref, sem):
+    reach = next_ref.shape[0]
+    at = lat_hbm.shape[0] - reach - near_at(lat_hbm, reach)
+    copy = pltpu.make_async_copy(lat_hbm.at[pl.ds(at, reach)], next_ref, sem)
+    copy.start()
+    copy.wait()
+
+
 def stats_kernel(
     lat_hbm, embed_hbm, weight_hbm, gain_one, shift_one, bias_one, time_bias, gain_two, shift_two, bias_two, steer, conv_hbm,
-    lat_ref, out_ref, near_ref, next_ref, rows_ref, conv_ref,
-    embed_ref, weight_ref, sems, edge_sems, row_sems, *vector_refs,
+    lat_ref, out_ref, near_ref, rows_ref, conv_ref,
+    embed_ref, weight_ref, sems, late_sems, row_sems, *vector_refs,
 ):
     rows, chans, _ = lat_ref.shape
-    reach = near_ref.shape[0]
-    last = rows - reach
-    near_at = jnp.where(lax.rem(lax.axis_index("patch"), 2) == 0, last, 0)
     copies = fetch(
         [(lat_hbm.at[k], lat_ref.at[k]) for k in range(rows)]
         + [(embed_hbm, embed_ref), (weight_hbm, weight_ref)],
@@ -131,14 +140,9 @@
     )
     vectors = (gain_one, shift_one, bias_one, time_bias, gain_two, shift_two, bias_two)
     copies += fetch(zip(vectors, vector_refs), row_sems)
-    edges = fetch(
-        [
-            (lat_hbm.at[pl.ds(near_at, reach)], near_ref),
-            (lat_hbm.at[pl.ds(last - near_at, reach)], next_ref),
-            (conv_hbm, conv_ref),
-        ],
-        edge_sems,
-    )
+    reach = near_ref.shape[0]
+    edge = lat_hbm.at[pl.ds(near_at(lat_hbm, reach), reach)]
+    late = fetch([(edge, near_ref), (conv_hbm, conv_ref)], late_sems)
     for copy in copies:
         copy.wait()
     mean, squares = channel_moments(lambda: (lat_ref[k].astype(F32) for k in range(rows)), chans)
@@ -152,7 +156,7 @@
     wide = rows_ref.shape[1]
     lines = [widen(v[...].reshape(1, -1), wide) for v in vector_refs]
     rows_ref[...] = jnp.concatenate(lines + [jnp.full((1, wide), steer[0], F32)], axis=0)
-    for copy in edges:
+    for copy in late:
         copy.wait()
 
 
@@ -248,7 +252,7 @@
 
 
 def outer_kernel(
-    near_ref, next_ref, far_near_ref, far_next_ref, inner_ref, inner_taps_ref, cols_ref, rows_ref, weight_ref, raw_ref,
+    next_ref, near_ref, far_next_ref, far_near_ref, inner_ref, inner_taps_ref, cols_ref, rows_ref, weight_ref, raw_ref,
     steered_ref, out_ref, turned_ref,
     taps_ref, edge_ref,
 ):
@@ -367,24 +371,35 @@
     deep = 9 * chans
     patches = lax.axis_size("patch")
     swap = [(0, 1), (1, 0)]
+    next_edge = pl.pallas_call(
+        edge_kernel,
+        out_shape=pltpu.VMEM((REACH, chans, cols), BF16),
+        in_specs=[ANY],
+        out_specs=VMEM,
+        scratch_shapes=[pltpu.SemaphoreType.DMA],
+        compiler_params=LIMIT,
+        name="edge",
+    )(in_hbm(own))
+    steps = [(i, i + 1) for i in range(1, patches - 1, 2)]
+    following = lax.ppermute(next_edge, "patch", steps + [(j, i) for i, j in steps])
+    steer, _ = lax.optimization_barrier((steer_scale, next_edge))
     tile_one = tile_height(chans, 3)
-    held, sent, near_edge, next_edge, vectors, raw_one = pl.pallas_call(
+    held, sent, near_edge, vectors, raw_one = pl.pallas_call(
         stats_kernel,
         out_shape=[
             pltpu.VMEM((rows, chans, cols), BF16),
             pltpu.VMEM((2 * patches, tile_one, LANES), F32),
             pltpu.VMEM((REACH, chans, cols), BF16),
-            pltpu.VMEM((REACH, chans, cols), BF16),
             pltpu.VMEM((8, wide), F32),
             pltpu.VMEM((deep, chans), BF16),
         ],
         in_specs=[ANY] * 10 + [SMEM, ANY],
-        out_specs=[VMEM] * 6,
+        out_specs=[VMEM] * 5,
         scratch_shapes=[
             pltpu.VMEM(time_embed.shape, BF16),
             pltpu.VMEM(time_weight.shape, BF16),
             pltpu.SemaphoreType.DMA((rows + 2,)),
-            pltpu.SemaphoreType.DMA((3,)),
+            pltpu.SemaphoreType.DMA((2,)),
             pltpu.SemaphoreType.DMA((7,)),
         ]
         + [pltpu.VMEM((chans,), F32)] * 7,
@@ -392,19 +407,17 @@
         name="stats",
     )(
         in_hbm(own), in_hbm(time_embed), in_hbm(time_weight), in_hbm(gain_one), in_hbm(shift_one),
-        in_hbm(bias_one), in_hbm(time_bias), in_hbm(gain_two), in_hbm(shift_two), in_hbm(bias_two), steer_scale,
+        in_hbm(bias_one), in_hbm(time_bias), in_hbm(gain_two), in_hbm(shift_two), in_hbm(bias_two), steer,
         in_hbm(conv_one.reshape(deep, chans)),
     )
     near = lax.ppermute(near_edge, "patch", [(i, i ^ 1) for i in range(patches)])
-    steps = [(i, i + 1) for i in range(1, patches - 1, 2)]
-    following = lax.ppermute(next_edge, "patch", steps + [(j, i) for i, j in steps])
-    seen = everyone(sent, ("cfg", "patch"))
-
     source, _ = lax.optimization_barrier((own, sent))
     far = lax.ppermute(source, "cfg", swap)
-    near, following, seen = lax.optimization_barrier((near, following, seen))
+    seen = everyone(sent, ("cfg", "patch"))
+
+    following, near, seen = lax.optimization_barrier((following, near, seen))
+    far_next = lax.ppermute(following, "cfg", swap)
     far_near = lax.ppermute(near, "cfg", swap)
-    far_next = lax.ppermute(following, "cfg", swap)
 
     inner, taps, columns, turned_one = pl.pallas_call(
         inner_kernel,
@@ -436,7 +449,7 @@
         compiler_params=LIMIT,
         name="outer",
     )(
-        near, following, far_near, far_next, inner, taps, columns, vectors, turned_one,
+        following, near, far_next, far_near, inner, taps, columns, vectors, turned_one,
         conv_two.reshape(deep, chans),
     )
     seen = everyone(sent, "patch")

time: 44.5 us -> 45.1 us (1.013)
  blocking collectives: 26.4 us -> 23.2 us
  starting transfers between devices: 4.19 us -> 7.04 us
  Pallas kernels: 12.9 us -> 13.9 us
    all_to_all x2, blocking collectives: 26.4 us -> 23.2 us  [everyone(): return lax.all_to_all(tiles, axes, 0, 0)]
    ppermute x1, starting transfers between devices: 3 us -> 5.34 us  [body(): lax.ppermute(near_edge, 'patch', [(i, i ^ 1) for i in range(patches)])]
    pallas_call x0 -> x1, Pallas kernels: none -> 1.05 us  [body(): pl.pallas_call(edge_kernel, out_shape=pltpu.VMEM((REACH, chans, cols), BF...]
    ppermute x1, starting transfers between devices: 0.01 us -> 0.52 us  [body(): far = lax.ppermute(source, 'cfg', swap)]
  transfers between devices with their start and end apart: 5 -> 5, of which waited for: 0 -> 0; matrix products, arithmetic and copies ran while one was open for 0% -> 0% of each run, Pallas kernels for 7% -> 12%
where the time goes in v12:
time: 45.1 us; the launch traced here: 44.9 us
  blocking collectives  23.2 us (51%)
  Pallas kernels  13.9 us (31%)
  starting transfers between devices  7.04 us (16%)
  between operations  0.73 us (2%)
    all_to_all x2, blocking collectives, everyone(): return lax.all_to_all(tiles, axes, 0, 0)  23.2 us
    ppermute x1, starting transfers between devices, body(): lax.ppermute(near_edge, 'patch', [(i, i ^ 1) for i in range(patches)])  5.34 us
    pallas_call x1, Pallas kernels, body(): pl.pallas_call(second_kernel, out_shape=jax.ShapeDtypeStruct((rows, chans...  4.14 us
    pallas_call x1, Pallas kernels, body(): pl.pallas_call(outer_kernel, out_shape=[pltpu.VMEM((2 * REACH, chans, col...  3.19 us
    pallas_call x1, Pallas kernels, body(): pl.pallas_call(inner_kernel, out_shape=[pltpu.VMEM((max(rows - 2, 1), cha...  3.18 us
    pallas_call x1, Pallas kernels, body(): pl.pallas_call(stats_kernel, out_shape=[pltpu.VMEM((rows, chans, cols), B...  2.32 us
    pallas_call x1, Pallas kernels, body(): pl.pallas_call(edge_kernel, out_shape=pltpu.VMEM((REACH, chans, cols), BF...  1.05 us
  transfers between devices with their start and end apart: 5, of which 0 were waited for; matrix products, arithmetic and copies ran while one was open for 0% of the time, Pallas kernels for 12%

profile of v12, /device:TPU:0, one launch (start us, length us, event | category | flops | bytes accessed | tf_op | source)
XLA Modules:
  0.0 44.9 jit_solution(5262394789849302295)
XLA Ops:
  0.0 0.0 copy-start.1
  0.0 1.1 %edge.1 = bf16[2,320,256]{2,1,0:T(8,128)(2,1)S(1)} custom-call(bf16[4,320,256]{2,1,0:T(8,128)(2,1)} %bitcast.9), custom_call_target="tpu_custom_call" | custom-call | tf_op jit(solution)/shard_map/edge/pallas_call | solution.py:374
  1.1 0.7 %collective-permute-start.1 = (bf16[2,320,256]{2,1,0:T(8,128)(2,1)S(1)}, bf16[2,320,256]{2,1,0:T(8,128)(2,1)S(1)}, u32[]{:S(2)}, u32[]{:S(2)}) collective-permute-start(bf16[2,320,256]{2,1,0:T(8,128)(2,1)S(1)} %edge.1), channel_id=1, source_target_pairs={{2,4},{6,8},{10,12},{4,2},{8,6},{12,10},{3,5},{7,9},{11,13},{5,3},... | collective-permute-start | bytes 983048 | tf_op jit(solution)/shard_map/ppermute | solution.py:384
  2.4 2.3 %stats.1 = (bf16[4,320,256]{2,1,0:T(8,128)(2,1)S(1)}, f32[16,8,128]{2,1,0:T(8,128)S(1)}, bf16[2,320,256]{2,1,0:T(8,128)(2,1)S(1)}, f32[8,384]{1,0:T(8,128)S(1)}, bf16[2880,320]{1,0:T(8,128)(2,1)S(1)}) custom-call(bf16[4,320,256]{2,1,0:T(8,128)(2,1)} %bitcast.10, bf16[1,1280]{1,0:T(2,128)(2,1)} %embed_hbm.1, bf16[160,320]{1,0:T(8,128)(2,1)} %weight_hbm.1, ...), custom_call_target="tpu_custom_call" | custom-call | tf_op jit(solution)/shard_map/stats/pallas_call | solution.py:387
  4.7 0.0 copy-start
  4.7 0.0 copy-done.1
  4.7 0.5 %collective-permute-start = (bf16[4,320,256]{2,1,0:T(8,128)(2,1)S(1)}, bf16[4,320,256]{2,1,0:T(8,128)(2,1)S(1)}, u32[]{:S(2)}, u32[]{:S(2)}) collective-permute-start(bf16[4,320,256]{2,1,0:T(8,128)(2,1)S(1)} %bitcast.11), channel_id=1, source_target_pairs={{0,16},{16,0},{1,17},{17,1},{2,18},{18,2},{3,19},{19,3},{4,20},{20... | collective-permute-start | bytes 1966088 | tf_op jit(solution)/shard_map/ppermute | solution.py:415
  5.3 5.3 %collective-permute-start.2 = (bf16[2,320,256]{2,1,0:T(8,128)(2,1)S(1)}, bf16[2,320,256]{2,1,0:T(8,128)(2,1)S(1)}, u32[]{:S(2)}, u32[]{:S(2)}) collective-permute-start(bf16[2,320,256]{2,1,0:T(8,128)(2,1)S(1)} %get-tuple-element.26), channel_id=1, source_target_pairs={{0,2},{2,0},{4,6},{6,4},{8,10},{10,8},{12,14},{14,12},{1,3},{3,1},... | collective-permute-start | bytes 983048 | tf_op jit(solution)/shard_map/ppermute | solution.py:413
  10.6 11.3 %all_to_all.10.seen_ref = f32[16,8,128]{2,1,0:T(8,128)S(1)} all-to-all(f32[16,8,128]{2,1,0:T(8,128)S(1)} %get-tuple-element.24), channel_id=1, replica_groups=mesh['cfg'=2,'patch'=8,'req'=2] {'cfg','patch'}, dimensions={0} | all-to-all | bytes 131072 | tf_op jit(solution)/shard_map/all_to_all | solution.py:351
  21.9 0.0 collective-permute-done.1.next_ref
  21.9 0.0 collective-permute-done.2.near_ref
  21.9 0.0 collective-permute-start.3
  22.0 0.5 %collective-permute-start.4 = (bf16[2,320,256]{2,1,0:T(8,128)(2,1)S(1)}, bf16[2,320,256]{2,1,0:T(8,128)(2,1)S(1)}, u32[]{:S(2)}, u32[]{:S(2)}) collective-permute-start(bf16[2,320,256]{2,1,0:T(8,128)(2,1)S(1)} %collective-permute-done.2.near_ref), channel_id=1, source_target_pairs={{0,16},{16,0},{1,17},{17,1},{2,18},{18,2},{3,19},{19,3},{4,20},{20... | collective-permute-start | bytes 983048 | tf_op jit(solution)/shard_map/ppermute | solution.py:420
  22.5 0.0 collective-permute-done.far_ref
  22.5 3.2 %inner.1 = (f32[2,320,256]{2,1,0:T(8,128)S(1)}, bf16[3840,256]{1,0:T(8,128)(2,1)S(1)}, f32[6,320,128]{2,1,0:T(8,128)S(1)}, bf16[320,2880]{1,0:T(8,128)(2,1)S(1)}) custom-call(bf16[4,320,256]{2,1,0:T(8,128)(2,1)S(1)} %get-tuple-element.23.own_ref.lat_ref, bf16[4,320,256]{2,1,0:T(8,128)(2,1)S(1)} %collective-permute-done.far_ref, ...), custom_call_target="tpu_custom_call" | custom-call | tf_op jit(solution)/shard_map/inner/pallas_call | solution.py:422
  25.6 0.0 collective-permute-done.3.far_next_ref
  25.7 0.0 collective-permute-done.4.far_near_ref
  25.7 0.0 copy-done
  25.7 3.2 %outer.1 = (f32[4,320,256]{2,1,0:T(8,128)S(1)}, f32[8,8,128]{2,1,0:T(8,128)S(1)}, bf16[320,2880]{1,0:T(8,128)(2,1)S(1)}) custom-call(bf16[2,320,256]{2,1,0:T(8,128)(2,1)S(1)} %collective-permute-done.1.next_ref, bf16[2,320,256]{2,1,0:T(8,128)(2,1)S(1)} %collective-permute-done.2.near_ref, bf16[2,320,256]{2,1,0:T(8,128)(2,1)S(1)} %collective-permute-done.3.far_next_ref, ...), custom_call_target="tpu_custom_call" | custom-call | tf_op jit(solution)/shard_map/outer/pallas_call | solution.py:436
  28.9 11.9 %all_to_all.11.seen_ref = f32[8,8,128]{2,1,0:T(8,128)S(1)} all-to-all(f32[8,8,128]{2,1,0:T(8,128)S(1)} %get-tuple-element.37), channel_id=1, replica_groups=mesh['cfg'=2,'patch'=8,'req'=2] {'patch'}, dimensions={0} | all-to-all | bytes 65536 | tf_op jit(solution)/shard_map/all_to_all | solution.py:351
  40.8 4.1 %second.1 = bf16[4,320,256]{2,1,0:T(8,128)(2,1)} custom-call(f32[2,320,256]{2,1,0:T(8,128)S(1)} %get-tuple-element.30.inner_ref, f32[4,320,256]{2,1,0:T(8,128)S(1)} %get-tuple-element.36.outer_ref, bf16[4,320,256]{2,1,0:T(8,128)(2,1)S(1)} %get-tuple-element.23.own_ref.lat_ref, f32[8,8,128]{2,1,0:T(8,128)S(1)} %all_to_all.11.seen_ref, ...), custom_call_target="tpu_custom_call" | custom-call | tf_op jit(solution)/shard_map/second/pallas_call | solution.py:456
Async XLA Ops:
  0.0 4.7 %copy-start.1 = (bf16[1,1,4,256,320]{3,4,2,1,0:T(8,128)(2,1)S(1)}, bf16[1,1,4,256,320]{3,4,2,1,0:T(8,128)(2,1)}, u32[]{:S(2)}) copy-start(bf16[1,1,4,256,320]{3,4,2,1,0:T(8,128)(2,1)} %param.13) | copy-start | bytes 1966084
  1.1 20.9 %collective-permute-start.1 = (bf16[2,320,256]{2,1,0:T(8,128)(2,1)S(1)}, bf16[2,320,256]{2,1,0:T(8,128)(2,1)S(1)}, u32[]{:S(2)}, u32[]{:S(2)}) collective-permute-start(bf16[2,320,256]{2,1,0:T(8,128)(2,1)S(1)} %edge.1), channel_id=1, source_target_pairs={{2,4},{6,8},{10,12},{4,2},{8,6},{12,10},{3,5},{7,9},{11,13},{5,3},... | collective-permute-start | bytes 983048 | tf_op jit(solution)/shard_map/ppermute | solution.py:384
  4.7 20.9 %copy-start = (bf16[3,3,320,320]{3,2,1,0:T(8,128)(2,1)S(1)}, bf16[3,3,320,320]{3,2,1,0:T(8,128)(2,1)}, u32[]{:S(2)}) copy-start(bf16[3,3,320,320]{3,2,1,0:T(8,128)(2,1)} %param.24) | copy-start | bytes 5529604
  4.7 17.7 %collective-permute-start = (bf16[4,320,256]{2,1,0:T(8,128)(2,1)S(1)}, bf16[4,320,256]{2,1,0:T(8,128)(2,1)S(1)}, u32[]{:S(2)}, u32[]{:S(2)}) collective-permute-start(bf16[4,320,256]{2,1,0:T(8,128)(2,1)S(1)} %bitcast.11), channel_id=1, source_target_pairs={{0,16},{16,0},{1,17},{17,1},{2,18},{18,2},{3,19},{19,3},{4,20},{20... | collective-permute-start | bytes 1966088 | tf_op jit(solution)/shard_map/ppermute | solution.py:415
  5.3 16.7 %collective-permute-start.2 = (bf16[2,320,256]{2,1,0:T(8,128)(2,1)S(1)}, bf16[2,320,256]{2,1,0:T(8,128)(2,1)S(1)}, u32[]{:S(2)}, u32[]{:S(2)}) collective-permute-start(bf16[2,320,256]{2,1,0:T(8,128)(2,1)S(1)} %get-tuple-element.26), channel_id=1, source_target_pairs={{0,2},{2,0},{4,6},{6,4},{8,10},{10,8},{12,14},{14,12},{1,3},{3,1},... | collective-permute-start | bytes 983048 | tf_op jit(solution)/shard_map/ppermute | solution.py:413
  21.9 3.7 %collective-permute-start.3 = (bf16[2,320,256]{2,1,0:T(8,128)(2,1)S(1)}, bf16[2,320,256]{2,1,0:T(8,128)(2,1)S(1)}, u32[]{:S(2)}, u32[]{:S(2)}) collective-permute-start(bf16[2,320,256]{2,1,0:T(8,128)(2,1)S(1)} %collective-permute-done.1.next_ref), channel_id=1, source_target_pairs={{0,16},{16,0},{1,17},{17,1},{2,18},{18,2},{3,19},{19,3},{4,20},{20... | collective-permute-start | bytes 983048 | tf_op jit(solution)/shard_map/ppermute | solution.py:419
  22.0 3.7 %collective-permute-start.4 = (bf16[2,320,256]{2,1,0:T(8,128)(2,1)S(1)}, bf16[2,320,256]{2,1,0:T(8,128)(2,1)S(1)}, u32[]{:S(2)}, u32[]{:S(2)}) collective-permute-start(bf16[2,320,256]{2,1,0:T(8,128)(2,1)S(1)} %collective-permute-done.2.near_ref), channel_id=1, source_target_pairs={{0,16},{16,0},{1,17},{17,1},{2,18},{18,2},{3,19},{19,3},{4,20},{20... | collective-permute-start | bytes 983048 | tf_op jit(solution)/shard_map/ppermute | solution.py:420

commit v13 on v11

--- a/solution.py
+++ b/solution.py
@@ -90,16 +90,16 @@
 
 
 def put_rows(tile_rows, out_ref):
-    height = out_ref.shape[1]
+    height = out_ref.shape[-2]
     flat = widen(jnp.concatenate(tile_rows, axis=1), height * LANES)
     tile = jnp.concatenate([flat[:, at : at + LANES] for at in range(0, height * LANES, LANES)], axis=0)
-    out_ref[...] = jnp.broadcast_to(tile[None], out_ref.shape)
-
-
-def get_rows(seen_ref, first, peers, which, chans):
+    out_ref[...] = jnp.broadcast_to(tile, out_ref.shape)
+
+
+def get_rows(seen_ref, which, chans, base=0):
     start, end = which * chans, (which + 1) * chans
     lines = range(start // LANES, -(-end // LANES))
-    flat = jnp.concatenate([seen_ref[pl.ds(first, peers), k, :] for k in lines], axis=1)
+    flat = jnp.concatenate([seen_ref[:, base + k, :] for k in lines], axis=1)
     start -= lines[0] * LANES
     return widen(flat[:, start : start + chans], padded_lanes(chans))
 
@@ -223,14 +223,13 @@
     turn(raw_ref, weight_ref)
     wide = padded_lanes(chans)
     size = chans // GROUPS
-    cfg, peers = lax.axis_index("cfg"), lax.axis_size("patch")
     mask = same_group(wide, size)
-    starts = (cfg * peers, (1 - cfg) * peers)
-    means = [get_rows(seen_ref, s, peers, 0, chans) for s in starts]
-    squares = [get_rows(seen_ref, s, peers, 1, chans) for s in starts]
+    bases = (0, seen_ref.shape[1] // 2)
+    means = [get_rows(seen_ref, 0, chans, base) for base in bases]
+    squares = [get_rows(seen_ref, 1, chans, base) for base in bases]
     mean_rows, var_rows = group_stats(means, squares, float(rows * cols), mask, size)
     scale_rows = lax.rsqrt(var_rows + EPS) * (0.5 * rows_ref[0:1])
-    times = jnp.sum(get_rows(seen_ref, 0, peers, 2, chans), axis=0, keepdims=True)
+    times = jnp.sum(get_rows(seen_ref, 2, chans), axis=0, keepdims=True)
     added = times + (rows_ref[3:4] + rows_ref[2:3])
     spread_columns(
         [mean_rows[0:1], scale_rows[0:1], mean_rows[1:2], scale_rows[1:2], 0.5 * rows_ref[1:2], added],
@@ -317,10 +316,9 @@
     rows, chans, cols = lat_ref.shape
     wide = padded_lanes(chans)
     size = chans // GROUPS
-    peers = lax.axis_size("patch")
     mask = same_group(wide, size)
     mean_rows, var_rows = group_stats(
-        [get_rows(seen_ref, 0, peers, 0, chans)], [get_rows(seen_ref, 0, peers, 1, chans)],
+        [get_rows(seen_ref, 0, chans)], [get_rows(seen_ref, 1, chans)],
         float(rows * cols), mask, size,
     )
     scale_rows = lax.rsqrt(var_rows + EPS) * (0.5 * rows_ref[4:5])
@@ -368,11 +366,11 @@
     patches = lax.axis_size("patch")
     swap = [(0, 1), (1, 0)]
     tile_one = tile_height(chans, 3)
-    held, sent, near_edge, next_edge, vectors, raw_one = pl.pallas_call(
+    held, tile, near_edge, next_edge, vectors, raw_one = pl.pallas_call(
         stats_kernel,
         out_shape=[
             pltpu.VMEM((rows, chans, cols), BF16),
-            pltpu.VMEM((2 * patches, tile_one, LANES), F32),
+            pltpu.VMEM((tile_one, LANES), F32),
             pltpu.VMEM((REACH, chans, cols), BF16),
             pltpu.VMEM((REACH, chans, cols), BF16),
             pltpu.VMEM((8, wide), F32),
@@ -398,9 +396,10 @@
     near = lax.ppermute(near_edge, "patch", [(i, i ^ 1) for i in range(patches)])
     steps = [(i, i + 1) for i in range(1, patches - 1, 2)]
     following = lax.ppermute(next_edge, "patch", steps + [(j, i) for i, j in steps])
-    seen = everyone(sent, ("cfg", "patch"))
-
-    source, _ = lax.optimization_barrier((own, sent))
+    both = jnp.concatenate([tile, lax.ppermute(tile, "cfg", swap)], axis=0)
+    seen = everyone(jnp.broadcast_to(both, (patches,) + both.shape), "patch")
+
+    source, _ = lax.optimization_barrier((own, tile))
     far = lax.ppermute(source, "cfg", swap)
     near, following, seen = lax.optimization_barrier((near, following, seen))
     far_near = lax.ppermute(near, "cfg", swap)

time: 44.5 us -> 44.5 us (level)
  blocking collectives: 26.4 us -> 24.9 us
  waiting for transfers between devices: 0.01 us -> 0.86 us
  starting transfers between devices: 4.19 us -> 4.75 us
    all_to_all x2, blocking collectives: 26.4 us -> 24.9 us  [everyone(): return lax.all_to_all(tiles, axes, 0, 0)]
    ppermute x0 -> x1, waiting for transfers between devices: none -> 0.85 us  [body(): both = jnp.concatenate([tile, lax.ppermute(tile, 'cfg', swap)], axis=0)]
    ppermute x0 -> x1, starting transfers between devices: none -> 0.57 us  [body(): both = jnp.concatenate([tile, lax.ppermute(tile, 'cfg', swap)], axis=0)]
  transfers between devices with their start and end apart: 5 -> 6, of which waited for: 0 -> 1; matrix products, arithmetic and copies ran while one was open for 0% -> 0% of each run, Pallas kernels for 7% -> 7%
where the time goes in v13:
time: 44.5 us; the launch traced here: 44.3 us
  blocking collectives  24.9 us (56%)
  Pallas kernels  12.9 us (29%)
  starting transfers between devices  4.75 us (11%)
  waiting for transfers between devices  0.86 us (2%)
  between operations  0.79 us (2%)
    all_to_all x2, blocking collectives, everyone(): return lax.all_to_all(tiles, axes, 0, 0)  24.9 us
    pallas_call x1, Pallas kernels, body(): pl.pallas_call(second_kernel, out_shape=jax.ShapeDtypeStruct((rows, chans...  4.14 us
    pallas_call x1, Pallas kernels, body(): pl.pallas_call(outer_kernel, out_shape=[pltpu.VMEM((2 * REACH, chans, col...  3.19 us
    pallas_call x1, Pallas kernels, body(): pl.pallas_call(inner_kernel, out_shape=[pltpu.VMEM((max(rows - 2, 1), cha...  3.17 us
    ppermute x1, starting transfers between devices, body(): lax.ppermute(near_edge, 'patch', [(i, i ^ 1) for i in range(patches)])  3 us
    pallas_call x1, Pallas kernels, body(): pl.pallas_call(stats_kernel, out_shape=[pltpu.VMEM((rows, chans, cols), B...  2.42 us
  transfers between devices with their start and end apart: 6, of which 1 were waited for; matrix products, arithmetic and copies ran while one was open for 0% of the time, Pallas kernels for 7%

profile of v13, /device:TPU:0, one launch (start us, length us, event | category | flops | bytes accessed | tf_op | source)
XLA Modules:
  0.0 44.3 jit_solution(5648308815486610541)
XLA Ops:
  0.0 0.0 copy-start.1
  0.7 2.4 %stats.1 = (bf16[4,320,256]{2,1,0:T(8,128)(2,1)S(1)}, f32[8,128]{1,0:T(8,128)S(1)}, bf16[2,320,256]{2,1,0:T(8,128)(2,1)S(1)}, bf16[2,320,256]{2,1,0:T(8,128)(2,1...) custom-call(bf16[4,320,256]{2,1,0:T(8,128)(2,1)} %bitcast.10, bf16[1,1280]{1,0:T(2,128)(2,1)} %embed_hbm.1, ...), custom_call_target="tpu_custom_call" | custom-call | tf_op jit(solution)/shard_map/stats/pallas_call | solution.py:369
  3.2 0.0 copy-start
  3.2 3.0 %collective-permute-start.1 = (bf16[2,320,256]{2,1,0:T(8,128)(2,1)S(1)}, bf16[2,320,256]{2,1,0:T(8,128)(2,1)S(1)}, u32[]{:S(2)}, u32[]{:S(2)}) collective-permute-start(bf16[2,320,256]{2,1,0:T(8,128)(2,1)S(1)} %get-tuple-element.25), channel_id=1, source_target_pairs={{0,2},{2,0},{4,6},{6,4},{8,10},{10,8},{12,14},{14,12},{1,3},{3,1},... | collective-permute-start | bytes 983048 | tf_op jit(solution)/shard_map/ppermute | solution.py:396
  6.2 0.0 copy-done.1
  6.2 0.0 collective-permute-start
  6.2 0.7 %collective-permute-start.2 = (bf16[2,320,256]{2,1,0:T(8,128)(2,1)S(1)}, bf16[2,320,256]{2,1,0:T(8,128)(2,1)S(1)}, u32[]{:S(2)}, u32[]{:S(2)}) collective-permute-start(bf16[2,320,256]{2,1,0:T(8,128)(2,1)S(1)} %get-tuple-element.26), channel_id=1, source_target_pairs={{2,4},{6,8},{10,12},{4,2},{8,6},{12,10},{3,5},{7,9},{11,13},{5,3},... | collective-permute-start | bytes 983048 | tf_op jit(solution)/shard_map/ppermute | solution.py:398
  6.9 0.6 %collective-permute-start.3 = (f32[8,128]{1,0:T(8,128)S(1)}, f32[8,128]{1,0:T(8,128)S(1)}, u32[]{:S(2)}, u32[]{:S(2)}) collective-permute-start(f32[8,128]{1,0:T(8,128)S(1)} %get-tuple-element.23), channel_id=1, source_target_pairs={{0,16},{16,0},{1,17},{17,1},{2,18},{18,2},{3,19},{19,3},{4,20},{20... | collective-permute-start | bytes 12296 | tf_op jit(solution)/shard_map/ppermute | solution.py:399
  7.4 0.8 %collective-permute-done.3 = f32[8,128]{1,0:T(8,128)S(1)} collective-permute-done((f32[8,128]{1,0:T(8,128)S(1)}, f32[8,128]{1,0:T(8,128)S(1)}, u32[]{:S(2)}, u32[]{:S(2)}) %collective-permute-start.3) | collective-permute-done | bytes 4128 | tf_op jit(solution)/shard_map/ppermute | solution.py:399
  8.3 14.1 %all_to_all.10.seen_ref = f32[8,16,128]{2,1,0:T(8,128)S(1)} all-to-all(f32[8,16,128]{2,1,0:T(8,128)S(1)} %broadcast_in_dim.6), channel_id=1, replica_groups=mesh['cfg'=2,'patch'=8,'req'=2] {'patch'}, dimensions={0} | all-to-all | bytes 131072 | tf_op jit(solution)/shard_map/all_to_all | solution.py:345
  22.4 0.0 collective-permute-done.1.near_ref
  22.4 0.0 collective-permute-done.2.next_ref
  22.4 0.0 collective-permute-start.4
  22.4 0.5 %collective-permute-start.5 = (bf16[2,320,256]{2,1,0:T(8,128)(2,1)S(1)}, bf16[2,320,256]{2,1,0:T(8,128)(2,1)S(1)}, u32[]{:S(2)}, u32[]{:S(2)}) collective-permute-start(bf16[2,320,256]{2,1,0:T(8,128)(2,1)S(1)} %collective-permute-done.2.next_ref), channel_id=1, source_target_pairs={{0,16},{16,0},{1,17},{17,1},{2,18},{18,2},{3,19},{19,3},{4,20},{20... | collective-permute-start | bytes 983048 | tf_op jit(solution)/shard_map/ppermute | solution.py:406
  22.9 0.0 collective-permute-done.far_ref
  22.9 3.2 %inner.1 = (f32[2,320,256]{2,1,0:T(8,128)S(1)}, bf16[3840,256]{1,0:T(8,128)(2,1)S(1)}, f32[6,320,128]{2,1,0:T(8,128)S(1)}, bf16[320,2880]{1,0:T(8,128)(2,1)S(1)}) custom-call(bf16[4,320,256]{2,1,0:T(8,128)(2,1)S(1)} %get-tuple-element.22.own_ref.lat_ref, bf16[4,320,256]{2,1,0:T(8,128)(2,1)S(1)} %collective-permute-done.far_ref, ...), custom_call_target="tpu_custom_call" | custom-call | tf_op jit(solution)/shard_map/inner/pallas_call | solution.py:408
  26.1 0.0 collective-permute-done.4.far_near_ref
  26.1 0.0 collective-permute-done.5.far_next_ref
  26.1 0.0 copy-done
  26.1 3.2 %outer.1 = (f32[4,320,256]{2,1,0:T(8,128)S(1)}, f32[8,8,128]{2,1,0:T(8,128)S(1)}, bf16[320,2880]{1,0:T(8,128)(2,1)S(1)}) custom-call(bf16[2,320,256]{2,1,0:T(8,128)(2,1)S(1)} %collective-permute-done.1.near_ref, bf16[2,320,256]{2,1,0:T(8,128)(2,1)S(1)} %collective-permute-done.2.next_ref, bf16[2,320,256]{2,1,0:T(8,128)(2,1)S(1)} %collective-permute-done.4.far_near_ref, ...), custom_call_target="tpu_custom_call" | custom-call | tf_op jit(solution)/shard_map/outer/pallas_call | solution.py:422
  29.3 10.8 %all_to_all.11.seen_ref = f32[8,8,128]{2,1,0:T(8,128)S(1)} all-to-all(f32[8,8,128]{2,1,0:T(8,128)S(1)} %get-tuple-element.37), channel_id=1, replica_groups=mesh['cfg'=2,'patch'=8,'req'=2] {'patch'}, dimensions={0} | all-to-all | bytes 65536 | tf_op jit(solution)/shard_map/all_to_all | solution.py:345
  40.1 4.1 %second.1 = bf16[4,320,256]{2,1,0:T(8,128)(2,1)} custom-call(f32[2,320,256]{2,1,0:T(8,128)S(1)} %get-tuple-element.30.inner_ref, f32[4,320,256]{2,1,0:T(8,128)S(1)} %get-tuple-element.36.outer_ref, bf16[4,320,256]{2,1,0:T(8,128)(2,1)S(1)} %get-tuple-element.22.own_ref.lat_ref, f32[8,8,128]{2,1,0:T(8,128)S(1)} %all_to_all.11.seen_ref, ...), custom_call_target="tpu_custom_call" | custom-call | tf_op jit(solution)/shard_map/second/pallas_call | solution.py:442
  (2 shorter events, 0.0 us)
Async XLA Ops:
  0.0 6.2 %copy-start.1 = (bf16[1,1,4,256,320]{3,4,2,1,0:T(8,128)(2,1)S(1)}, bf16[1,1,4,256,320]{3,4,2,1,0:T(8,128)(2,1)}, u32[]{:S(2)}) copy-start(bf16[1,1,4,256,320]{3,4,2,1,0:T(8,128)(2,1)} %param.13) | copy-start | bytes 1966084
  3.2 22.9 %copy-start = (bf16[3,3,320,320]{3,2,1,0:T(8,128)(2,1)S(1)}, bf16[3,3,320,320]{3,2,1,0:T(8,128)(2,1)}, u32[]{:S(2)}) copy-start(bf16[3,3,320,320]{3,2,1,0:T(8,128)(2,1)} %param.24) | copy-start | bytes 5529604
  3.2 19.2 %collective-permute-start.1 = (bf16[2,320,256]{2,1,0:T(8,128)(2,1)S(1)}, bf16[2,320,256]{2,1,0:T(8,128)(2,1)S(1)}, u32[]{:S(2)}, u32[]{:S(2)}) collective-permute-start(bf16[2,320,256]{2,1,0:T(8,128)(2,1)S(1)} %get-tuple-element.25), channel_id=1, source_target_pairs={{0,2},{2,0},{4,6},{6,4},{8,10},{10,8},{12,14},{14,12},{1,3},{3,1},... | collective-permute-start | bytes 983048 | tf_op jit(solution)/shard_map/ppermute | solution.py:396
  6.2 16.7 %collective-permute-start = (bf16[4,320,256]{2,1,0:T(8,128)(2,1)S(1)}, bf16[4,320,256]{2,1,0:T(8,128)(2,1)S(1)}, u32[]{:S(2)}, u32[]{:S(2)}) collective-permute-start(bf16[4,320,256]{2,1,0:T(8,128)(2,1)S(1)} %bitcast.11), channel_id=1, source_target_pairs={{0,16},{16,0},{1,17},{17,1},{2,18},{18,2},{3,19},{19,3},{4,20},{20... | collective-permute-start | bytes 1966088 | tf_op jit(solution)/shard_map/ppermute | solution.py:403
  6.2 16.2 %collective-permute-start.2 = (bf16[2,320,256]{2,1,0:T(8,128)(2,1)S(1)}, bf16[2,320,256]{2,1,0:T(8,128)(2,1)S(1)}, u32[]{:S(2)}, u32[]{:S(2)}) collective-permute-start(bf16[2,320,256]{2,1,0:T(8,128)(2,1)S(1)} %get-tuple-element.26), channel_id=1, source_target_pairs={{2,4},{6,8},{10,12},{4,2},{8,6},{12,10},{3,5},{7,9},{11,13},{5,3},... | collective-permute-start | bytes 983048 | tf_op jit(solution)/shard_map/ppermute | solution.py:398
  6.9 1.4 %collective-permute-start.3 = (f32[8,128]{1,0:T(8,128)S(1)}, f32[8,128]{1,0:T(8,128)S(1)}, u32[]{:S(2)}, u32[]{:S(2)}) collective-permute-start(f32[8,128]{1,0:T(8,128)S(1)} %get-tuple-element.23), channel_id=1, source_target_pairs={{0,16},{16,0},{1,17},{17,1},{2,18},{18,2},{3,19},{19,3},{4,20},{20... | collective-permute-start | bytes 12296 | tf_op jit(solution)/shard_map/ppermute | solution.py:399
  22.4 3.7 %collective-permute-start.4 = (bf16[2,320,256]{2,1,0:T(8,128)(2,1)S(1)}, bf16[2,320,256]{2,1,0:T(8,128)(2,1)S(1)}, u32[]{:S(2)}, u32[]{:S(2)}) collective-permute-start(bf16[2,320,256]{2,1,0:T(8,128)(2,1)S(1)} %collective-permute-done.1.near_ref), channel_id=1, source_target_pairs={{0,16},{16,0},{1,17},{17,1},{2,18},{18,2},{3,19},{19,3},{4,20},{20... | collective-permute-start | bytes 983048 | tf_op jit(solution)/shard_map/ppermute | solution.py:405
  22.4 3.7 %collective-permute-start.5 = (bf16[2,320,256]{2,1,0:T(8,128)(2,1)S(1)}, bf16[2,320,256]{2,1,0:T(8,128)(2,1)S(1)}, u32[]{:S(2)}, u32[]{:S(2)}) collective-permute-start(bf16[2,320,256]{2,1,0:T(8,128)(2,1)S(1)} %collective-permute-done.2.next_ref), channel_id=1, source_target_pairs={{0,16},{16,0},{1,17},{17,1},{2,18},{18,2},{3,19},{19,3},{4,20},{20... | collective-permute-start | bytes 983048 | tf_op jit(solution)/shard_map/ppermute | solution.py:406

commit v14 on v13

--- a/solution.py
+++ b/solution.py
@@ -105,7 +105,7 @@
 
 
 def tile_height(chans, rows):
-    return -(-rows * chans // LANES // 8) * 8
+    return -(-(rows * chans + 1) // LANES // 8) * 8
 
 
 def fetch(pairs, sems, first=0):
@@ -116,7 +116,7 @@
 
 
 def stats_kernel(
-    lat_hbm, embed_hbm, weight_hbm, gain_one, shift_one, bias_one, time_bias, gain_two, shift_two, bias_two, steer, conv_hbm,
+    lat_hbm, embed_hbm, weight_hbm, gain_one, shift_one, bias_one, time_bias, gain_two, shift_two, bias_two, conv_hbm,
     lat_ref, out_ref, near_ref, next_ref, rows_ref, conv_ref,
     embed_ref, weight_ref, sems, edge_sems, row_sems, *vector_refs,
 ):
@@ -151,7 +151,7 @@
     put_rows([mean, squares, time_part], out_ref)
     wide = rows_ref.shape[1]
     lines = [widen(v[...].reshape(1, -1), wide) for v in vector_refs]
-    rows_ref[...] = jnp.concatenate(lines + [jnp.full((1, wide), steer[0], F32)], axis=0)
+    rows_ref[...] = stack_rows(lines, wide)
     for copy in edges:
         copy.wait()
 
@@ -196,9 +196,10 @@
     return None
 
 
-def mixer(cols_ref, rows_ref, chans):
+def mixer(cols_ref, steer_ref):
+    line = steer_ref.shape[1] // 2 - 1
     sign = jnp.where(lax.axis_index("cfg") == 0, 1.0, -1.0).astype(F32)
-    steer = rows_ref[7:8, 0:1] * sign
+    steer = steer_ref[0, line : line + 1, LANES - 1 :] * sign
 
     def mix(mine, other):
         shift = twice(cols_ref[4])
@@ -235,7 +236,7 @@
         [mean_rows[0:1], scale_rows[0:1], mean_rows[1:2], scale_rows[1:2], 0.5 * rows_ref[1:2], added],
         chans, cols_ref,
     )
-    mix = mixer(cols_ref, rows_ref, chans)
+    mix = mixer(cols_ref, seen_ref)
     line = 3 * chans
     if rows < 3:
         steered_ref[...] = jnp.zeros_like(steered_ref)
@@ -247,7 +248,8 @@
 
 
 def outer_kernel(
-    near_ref, next_ref, far_near_ref, far_next_ref, inner_ref, inner_taps_ref, cols_ref, rows_ref, weight_ref, raw_ref,
+    near_ref, next_ref, far_near_ref, far_next_ref, inner_ref, inner_taps_ref, cols_ref, weight_ref, raw_ref,
+    steer_ref,
     steered_ref, out_ref, turned_ref,
     taps_ref, edge_ref,
 ):
@@ -259,7 +261,7 @@
     edge_ref[1, pl.ds(above, reach)] = far_next_ref[...]
     edge_ref[0, pl.ds(reach - above, reach)] = near_ref[...]
     edge_ref[1, pl.ds(reach - above, reach)] = far_near_ref[...]
-    mix = mixer(cols_ref, rows_ref, chans)
+    mix = mixer(cols_ref, steer_ref)
 
     def taps(at):
         if reach <= at < reach + rows:
@@ -376,7 +378,7 @@
             pltpu.VMEM((8, wide), F32),
             pltpu.VMEM((deep, chans), BF16),
         ],
-        in_specs=[ANY] * 10 + [SMEM, ANY],
+        in_specs=[ANY] * 11,
         out_specs=[VMEM] * 6,
         scratch_shapes=[
             pltpu.VMEM(time_embed.shape, BF16),
@@ -390,13 +392,17 @@
         name="stats",
     )(
         in_hbm(own), in_hbm(time_embed), in_hbm(time_weight), in_hbm(gain_one), in_hbm(shift_one),
-        in_hbm(bias_one), in_hbm(time_bias), in_hbm(gain_two), in_hbm(shift_two), in_hbm(bias_two), steer_scale,
+        in_hbm(bias_one), in_hbm(time_bias), in_hbm(gain_two), in_hbm(shift_two), in_hbm(bias_two),
         in_hbm(conv_one.reshape(deep, chans)),
     )
+    other = lax.ppermute(tile, "cfg", swap)
+    next_edge, other = lax.optimization_barrier((next_edge, other))
     near = lax.ppermute(near_edge, "patch", [(i, i ^ 1) for i in range(patches)])
     steps = [(i, i + 1) for i in range(1, patches - 1, 2)]
     following = lax.ppermute(next_edge, "patch", steps + [(j, i) for i, j in steps])
-    both = jnp.concatenate([tile, lax.ppermute(tile, "cfg", swap)], axis=0)
+    both = jnp.concatenate([tile, other], axis=0)
+    free = (jnp.arange(2 * tile_one) == tile_one - 1)[:, None] & (jnp.arange(LANES) == LANES - 1)
+    both = jnp.where(free, steer_scale[0], both)
     seen = everyone(jnp.broadcast_to(both, (patches,) + both.shape), "patch")
 
     source, _ = lax.optimization_barrier((own, tile))
@@ -435,8 +441,8 @@
         compiler_params=LIMIT,
         name="outer",
     )(
-        near, following, far_near, far_next, inner, taps, columns, vectors, turned_one,
-        conv_two.reshape(deep, chans),
+        near, following, far_near, far_next, inner, taps, columns, turned_one,
+        conv_two.reshape(deep, chans), seen,
     )
     seen = everyone(sent, "patch")
     image = pl.pallas_call(

time: 44.5 us -> 44.2 us (level)
  blocking collectives: 24.9 us -> 26 us
  waiting for transfers between devices: 0.86 us -> 0.02 us
    all_to_all x2, blocking collectives: 24.9 us -> 26 us  [everyone(): return lax.all_to_all(tiles, axes, 0, 0)]
    ppermute x1, waiting for transfers between devices: 0.85 us -> 0.01 us  [body(): other = lax.ppermute(tile, 'cfg', swap)]
  transfers between devices with their start and end apart: 6 -> 6, of which waited for: 1 -> 0; matrix products, arithmetic and copies ran while one was open for 0% -> 0% of each run, Pallas kernels for 7% -> 7%
where the time goes in v14:
time: 44.2 us; the launch traced here: 44 us
  blocking collectives  26 us (59%)
  Pallas kernels  12.6 us (29%)
  starting transfers between devices  4.44 us (10%)
  between operations  0.73 us (2%)
    all_to_all x2, blocking collectives, everyone(): return lax.all_to_all(tiles, axes, 0, 0)  26 us
    pallas_call x1, Pallas kernels, body(): pl.pallas_call(second_kernel, out_shape=jax.ShapeDtypeStruct((rows, chans...  4.01 us
    pallas_call x1, Pallas kernels, body(): pl.pallas_call(inner_kernel, out_shape=[pltpu.VMEM((max(rows - 2, 1), cha...  3.07 us
    pallas_call x1, Pallas kernels, body(): pl.pallas_call(outer_kernel, out_shape=[pltpu.VMEM((2 * REACH, chans, col...  3.07 us
    ppermute x1, starting transfers between devices, body(): lax.ppermute(near_edge, 'patch', [(i, i ^ 1) for i in range(patches)])  2.56 us
    pallas_call x1, Pallas kernels, body(): pl.pallas_call(stats_kernel, out_shape=[pltpu.VMEM((rows, chans, cols), B...  2.47 us
  transfers between devices with their start and end apart: 6, of which 0 were waited for; matrix products, arithmetic and copies ran while one was open for 0% of the time, Pallas kernels for 7%

profile of v14, /device:TPU:0, one launch (start us, length us, event | category | flops | bytes accessed | tf_op | source)
XLA Modules:
  0.0 44.0 jit_solution(12503289233637023441)
XLA Ops:
  0.0 0.0 copy-start.1
  0.0 2.5 %stats.1 = (bf16[4,320,256]{2,1,0:T(8,128)(2,1)S(1)}, f32[8,128]{1,0:T(8,128)S(1)}, bf16[2,320,256]{2,1,0:T(8,128)(2,1)S(1)}, bf16[2,320,256]{2,1,0:T(8,128)(2,1...) custom-call(bf16[4,320,256]{2,1,0:T(8,128)(2,1)} %bitcast.12, bf16[1,1280]{1,0:T(2,128)(2,1)} %embed_hbm.1, ...), custom_call_target="tpu_custom_call" | custom-call | tf_op jit(solution)/shard_map/stats/pallas_call | solution.py:371
  2.5 0.0 copy-start
  2.5 0.5 %collective-permute-start.2 = (f32[8,128]{1,0:T(8,128)S(1)}, f32[8,128]{1,0:T(8,128)S(1)}, u32[]{:S(2)}, u32[]{:S(2)}) collective-permute-start(f32[8,128]{1,0:T(8,128)S(1)} %get-tuple-element.25), channel_id=1, source_target_pairs={{0,16},{16,0},{1,17},{17,1},{2,18},{18,2},{3,19},{19,3},{4,20},{20... | collective-permute-start | bytes 12296 | tf_op jit(solution)/shard_map/ppermute | solution.py:398
  3.0 2.6 %collective-permute-start.1 = (bf16[2,320,256]{2,1,0:T(8,128)(2,1)S(1)}, bf16[2,320,256]{2,1,0:T(8,128)(2,1)S(1)}, u32[]{:S(2)}, u32[]{:S(2)}) collective-permute-start(bf16[2,320,256]{2,1,0:T(8,128)(2,1)S(1)} %get-tuple-element.27), channel_id=1, source_target_pairs={{0,2},{2,0},{4,6},{6,4},{8,10},{10,8},{12,14},{14,12},{1,3},{3,1},... | collective-permute-start | bytes 983048 | tf_op jit(solution)/shard_map/ppermute | solution.py:400
  5.6 0.0 copy-done.1
  5.6 0.2 collective-permute-start
  6.4 0.0 collective-permute-done.2
  6.4 0.7 %collective-permute-start.3 = (bf16[2,320,256]{2,1,0:T(8,128)(2,1)S(1)}, bf16[2,320,256]{2,1,0:T(8,128)(2,1)S(1)}, u32[]{:S(2)}, u32[]{:S(2)}) collective-permute-start(bf16[2,320,256]{2,1,0:T(8,128)(2,1)S(1)} %get-tuple-element.29), channel_id=1, source_target_pairs={{2,4},{6,8},{10,12},{4,2},{8,6},{12,10},{3,5},{7,9},{11,13},{5,3},... | collective-permute-start | bytes 983048 | tf_op jit(solution)/shard_map/ppermute | solution.py:402
  7.1 0.1 maximum_select_fusion
  7.2 14.3 %all_to_all.10.seen_ref.steer_ref = f32[8,16,128]{2,1,0:T(8,128)S(1)} all-to-all(f32[8,16,128]{2,1,0:T(8,128)S(1)} %broadcast_in_dim.13), channel_id=1, replica_groups=mesh['cfg'=2,'patch'=8,'req'=2] {'patch'}, dimensions={0} | all-to-all | bytes 131072 | tf_op jit(solution)/shard_map/all_to_all | solution.py:347
  21.5 0.0 collective-permute-done.1.near_ref
  21.5 0.0 collective-permute-done.3.next_ref
  21.5 0.0 collective-permute-start.4
  21.5 0.5 %collective-permute-start.5 = (bf16[2,320,256]{2,1,0:T(8,128)(2,1)S(1)}, bf16[2,320,256]{2,1,0:T(8,128)(2,1)S(1)}, u32[]{:S(2)}, u32[]{:S(2)}) collective-permute-start(bf16[2,320,256]{2,1,0:T(8,128)(2,1)S(1)} %collective-permute-done.3.next_ref), channel_id=1, source_target_pairs={{0,16},{16,0},{1,17},{17,1},{2,18},{18,2},{3,19},{19,3},{4,20},{20... | collective-permute-start | bytes 983048 | tf_op jit(solution)/shard_map/ppermute | solution.py:412
  22.0 0.0 collective-permute-done.far_ref
  22.0 3.1 %inner.1 = (f32[2,320,256]{2,1,0:T(8,128)S(1)}, bf16[3840,256]{1,0:T(8,128)(2,1)S(1)}, f32[6,320,128]{2,1,0:T(8,128)S(1)}, bf16[320,2880]{1,0:T(8,128)(2,1)S(1)}) custom-call(bf16[4,320,256]{2,1,0:T(8,128)(2,1)S(1)} %get-tuple-element.24.own_ref.lat_ref, bf16[4,320,256]{2,1,0:T(8,128)(2,1)S(1)} %collective-permute-done.far_ref, ...), custom_call_target="tpu_custom_call" | custom-call | tf_op jit(solution)/shard_map/inner/pallas_call | solution.py:414
  25.1 0.0 collective-permute-done.4.far_near_ref
  25.1 0.0 collective-permute-done.5.far_next_ref
  25.1 0.0 copy-done
  25.1 3.1 %outer.1 = (f32[4,320,256]{2,1,0:T(8,128)S(1)}, f32[8,8,128]{2,1,0:T(8,128)S(1)}, bf16[320,2880]{1,0:T(8,128)(2,1)S(1)}) custom-call(bf16[2,320,256]{2,1,0:T(8,128)(2,1)S(1)} %collective-permute-done.1.near_ref, bf16[2,320,256]{2,1,0:T(8,128)(2,1)S(1)} %collective-permute-done.3.next_ref, bf16[2,320,256]{2,1,0:T(8,128)(2,1)S(1)} %collective-permute-done.4.far_near_ref, ...), custom_call_target="tpu_custom_call" | custom-call | tf_op jit(solution)/shard_map/outer/pallas_call | solution.py:428
  28.2 11.8 %all_to_all.11.seen_ref = f32[8,8,128]{2,1,0:T(8,128)S(1)} all-to-all(f32[8,8,128]{2,1,0:T(8,128)S(1)} %get-tuple-element.41), channel_id=1, replica_groups=mesh['cfg'=2,'patch'=8,'req'=2] {'patch'}, dimensions={0} | all-to-all | bytes 65536 | tf_op jit(solution)/shard_map/all_to_all | solution.py:347
  39.9 4.0 %second.1 = bf16[4,320,256]{2,1,0:T(8,128)(2,1)} custom-call(f32[2,320,256]{2,1,0:T(8,128)S(1)} %get-tuple-element.34.inner_ref, f32[4,320,256]{2,1,0:T(8,128)S(1)} %get-tuple-element.40.outer_ref, bf16[4,320,256]{2,1,0:T(8,128)(2,1)S(1)} %get-tuple-element.24.own_ref.lat_ref, f32[8,8,128]{2,1,0:T(8,128)S(1)} %all_to_all.11.seen_ref, ...), custom_call_target="tpu_custom_call" | custom-call | tf_op jit(solution)/shard_map/second/pallas_call | solution.py:448
  (3 shorter events, 0.0 us)
Async XLA Ops:
  0.0 5.6 %copy-start.1 = (bf16[1,1,4,256,320]{3,4,2,1,0:T(8,128)(2,1)S(1)}, bf16[1,1,4,256,320]{3,4,2,1,0:T(8,128)(2,1)}, u32[]{:S(2)}) copy-start(bf16[1,1,4,256,320]{3,4,2,1,0:T(8,128)(2,1)} %param.13) | copy-start | bytes 1966084
  2.5 22.6 %copy-start = (bf16[3,3,320,320]{3,2,1,0:T(8,128)(2,1)S(1)}, bf16[3,3,320,320]{3,2,1,0:T(8,128)(2,1)}, u32[]{:S(2)}) copy-start(bf16[3,3,320,320]{3,2,1,0:T(8,128)(2,1)} %param.24) | copy-start | bytes 5529604
  2.5 3.9 %collective-permute-start.2 = (f32[8,128]{1,0:T(8,128)S(1)}, f32[8,128]{1,0:T(8,128)S(1)}, u32[]{:S(2)}, u32[]{:S(2)}) collective-permute-start(f32[8,128]{1,0:T(8,128)S(1)} %get-tuple-element.25), channel_id=1, source_target_pairs={{0,16},{16,0},{1,17},{17,1},{2,18},{18,2},{3,19},{19,3},{4,20},{20... | collective-permute-start | bytes 12296 | tf_op jit(solution)/shard_map/ppermute | solution.py:398
  3.0 18.5 %collective-permute-start.1 = (bf16[2,320,256]{2,1,0:T(8,128)(2,1)S(1)}, bf16[2,320,256]{2,1,0:T(8,128)(2,1)S(1)}, u32[]{:S(2)}, u32[]{:S(2)}) collective-permute-start(bf16[2,320,256]{2,1,0:T(8,128)(2,1)S(1)} %get-tuple-element.27), channel_id=1, source_target_pairs={{0,2},{2,0},{4,6},{6,4},{8,10},{10,8},{12,14},{14,12},{1,3},{3,1},... | collective-permute-start | bytes 983048 | tf_op jit(solution)/shard_map/ppermute | solution.py:400
  5.6 16.4 %collective-permute-start = (bf16[4,320,256]{2,1,0:T(8,128)(2,1)S(1)}, bf16[4,320,256]{2,1,0:T(8,128)(2,1)S(1)}, u32[]{:S(2)}, u32[]{:S(2)}) collective-permute-start(bf16[4,320,256]{2,1,0:T(8,128)(2,1)S(1)} %bitcast.13), channel_id=1, source_target_pairs={{0,16},{16,0},{1,17},{17,1},{2,18},{18,2},{3,19},{19,3},{4,20},{20... | collective-permute-start | bytes 1966088 | tf_op jit(solution)/shard_map/ppermute | solution.py:409
  6.4 15.1 %collective-permute-start.3 = (bf16[2,320,256]{2,1,0:T(8,128)(2,1)S(1)}, bf16[2,320,256]{2,1,0:T(8,128)(2,1)S(1)}, u32[]{:S(2)}, u32[]{:S(2)}) collective-permute-start(bf16[2,320,256]{2,1,0:T(8,128)(2,1)S(1)} %get-tuple-element.29), channel_id=1, source_target_pairs={{2,4},{6,8},{10,12},{4,2},{8,6},{12,10},{3,5},{7,9},{11,13},{5,3},... | collective-permute-start | bytes 983048 | tf_op jit(solution)/shard_map/ppermute | solution.py:402
  21.5 3.6 %collective-permute-start.4 = (bf16[2,320,256]{2,1,0:T(8,128)(2,1)S(1)}, bf16[2,320,256]{2,1,0:T(8,128)(2,1)S(1)}, u32[]{:S(2)}, u32[]{:S(2)}) collective-permute-start(bf16[2,320,256]{2,1,0:T(8,128)(2,1)S(1)} %collective-permute-done.1.near_ref), channel_id=1, source_target_pairs={{0,16},{16,0},{1,17},{17,1},{2,18},{18,2},{3,19},{19,3},{4,20},{20... | collective-permute-start | bytes 983048 | tf_op jit(solution)/shard_map/ppermute | solution.py:411
  21.5 3.6 %collective-permute-start.5 = (bf16[2,320,256]{2,1,0:T(8,128)(2,1)S(1)}, bf16[2,320,256]{2,1,0:T(8,128)(2,1)S(1)}, u32[]{:S(2)}, u32[]{:S(2)}) collective-permute-start(bf16[2,320,256]{2,1,0:T(8,128)(2,1)S(1)} %collective-permute-done.3.next_ref), channel_id=1, source_target_pairs={{0,16},{16,0},{1,17},{17,1},{2,18},{18,2},{3,19},{19,3},{4,20},{20... | collective-permute-start | bytes 983048 | tf_op jit(solution)/shard_map/ppermute | solution.py:412

commit v15 on v14

--- a/solution.py
+++ b/solution.py
@@ -115,15 +115,25 @@
     return copies
 
 
+def near_at(lat_hbm, reach):
+    return jnp.where(lax.rem(lax.axis_index("patch"), 2) == 0, lat_hbm.shape[0] - reach, 0)
+
+
+def edge_kernel(lat_hbm, near_ref, sem):
+    reach = near_ref.shape[0]
+    copy = pltpu.make_async_copy(lat_hbm.at[pl.ds(near_at(lat_hbm, reach), reach)], near_ref, sem)
+    copy.start()
+    copy.wait()
+
+
 def stats_kernel(
     lat_hbm, embed_hbm, weight_hbm, gain_one, shift_one, bias_one, time_bias, gain_two, shift_two, bias_two, conv_hbm,
-    lat_ref, out_ref, near_ref, next_ref, rows_ref, conv_ref,
+    lat_ref, out_ref, next_ref, rows_ref, conv_ref,
     embed_ref, weight_ref, sems, edge_sems, row_sems, *vector_refs,
 ):
     rows, chans, _ = lat_ref.shape
-    reach = near_ref.shape[0]
-    last = rows - reach
-    near_at = jnp.where(lax.rem(lax.axis_index("patch"), 2) == 0, last, 0)
+    reach = next_ref.shape[0]
+    next_at = rows - reach - near_at(lat_hbm, reach)
     copies = fetch(
         [(lat_hbm.at[k], lat_ref.at[k]) for k in range(rows)]
         + [(embed_hbm, embed_ref), (weight_hbm, weight_ref)],
@@ -133,8 +143,7 @@
     copies += fetch(zip(vectors, vector_refs), row_sems)
     edges = fetch(
         [
-            (lat_hbm.at[pl.ds(near_at, reach)], near_ref),
-            (lat_hbm.at[pl.ds(last - near_at, reach)], next_ref),
+            (lat_hbm.at[pl.ds(next_at, reach)], next_ref),
             (conv_hbm, conv_ref),
         ],
         edge_sems,
@@ -367,24 +376,34 @@
     deep = 9 * chans
     patches = lax.axis_size("patch")
     swap = [(0, 1), (1, 0)]
+    near_edge = pl.pallas_call(
+        edge_kernel,
+        out_shape=pltpu.VMEM((REACH, chans, cols), BF16),
+        in_specs=[ANY],
+        out_specs=VMEM,
+        scratch_shapes=[pltpu.SemaphoreType.DMA],
+        compiler_params=LIMIT,
+        name="edge",
+    )(in_hbm(own))
+    near = lax.ppermute(near_edge, "patch", [(i, i ^ 1) for i in range(patches)])
+    time_embed, _ = lax.optimization_barrier((time_embed, near_edge))
     tile_one = tile_height(chans, 3)
-    held, tile, near_edge, next_edge, vectors, raw_one = pl.pallas_call(
+    held, tile, next_edge, vectors, raw_one = pl.pallas_call(
         stats_kernel,
         out_shape=[
             pltpu.VMEM((rows, chans, cols), BF16),
             pltpu.VMEM((tile_one, LANES), F32),
             pltpu.VMEM((REACH, chans, cols), BF16),
-            pltpu.VMEM((REACH, chans, cols), BF16),
             pltpu.VMEM((8, wide), F32),
             pltpu.VMEM((deep, chans), BF16),
         ],
         in_specs=[ANY] * 11,
-        out_specs=[VMEM] * 6,
+        out_specs=[VMEM] * 5,
         scratch_shapes=[
             pltpu.VMEM(time_embed.shape, BF16),
             pltpu.VMEM(time_weight.shape, BF16),
             pltpu.SemaphoreType.DMA((rows + 2,)),
-            pltpu.SemaphoreType.DMA((3,)),
+            pltpu.SemaphoreType.DMA((2,)),
             pltpu.SemaphoreType.DMA((7,)),
         ]
         + [pltpu.VMEM((chans,), F32)] * 7,
@@ -396,8 +415,6 @@
         in_hbm(conv_one.reshape(deep, chans)),
     )
     other = lax.ppermute(tile, "cfg", swap)
-    next_edge, other = lax.optimization_barrier((next_edge, other))
-    near = lax.ppermute(near_edge, "patch", [(i, i ^ 1) for i in range(patches)])
     steps = [(i, i + 1) for i in range(1, patches - 1, 2)]
     following = lax.ppermute(next_edge, "patch", steps + [(j, i) for i, j in steps])
     both = jnp.concatenate([tile, other], axis=0)

time: 44.2 us -> 43 us (0.973)
  blocking collectives: 26 us -> 23.5 us
  Pallas kernels: 12.6 us -> 13.5 us
    all_to_all x2, blocking collectives: 26 us -> 23.5 us  [everyone(): return lax.all_to_all(tiles, axes, 0, 0)]
    pallas_call x0 -> x1, Pallas kernels: none -> 1.05 us  [body(): pl.pallas_call(edge_kernel, out_shape=pltpu.VMEM((REACH, chans, cols), BF...]
    ppermute x1, starting transfers between devices: 0.52 us -> 0.07 us  [body(): other = lax.ppermute(tile, 'cfg', swap)]
  transfers between devices with their start and end apart: 6 -> 6, of which waited for: 0 -> 0; matrix products, arithmetic and copies ran while one was open for 0% -> 0% of each run, Pallas kernels for 7% -> 13%
where the time goes in v15:
time: 43 us; the launch traced here: 42.7 us
  blocking collectives  23.5 us (55%)
  Pallas kernels  13.5 us (31%)
  starting transfers between devices  4.81 us (11%)
  between operations  0.75 us (2%)
    all_to_all x2, blocking collectives, everyone(): return lax.all_to_all(tiles, axes, 0, 0)  23.5 us
    pallas_call x1, Pallas kernels, body(): pl.pallas_call(second_kernel, out_shape=jax.ShapeDtypeStruct((rows, chans...  4.02 us
    pallas_call x1, Pallas kernels, body(): pl.pallas_call(inner_kernel, out_shape=[pltpu.VMEM((max(rows - 2, 1), cha...  3.07 us
    pallas_call x1, Pallas kernels, body(): pl.pallas_call(outer_kernel, out_shape=[pltpu.VMEM((2 * REACH, chans, col...  3.07 us
    ppermute x1, starting transfers between devices, body(): lax.ppermute(near_edge, 'patch', [(i, i ^ 1) for i in range(patches)])  3 us
    pallas_call x1, Pallas kernels, body(): pl.pallas_call(stats_kernel, out_shape=[pltpu.VMEM((rows, chans, cols), B...  2.31 us
    pallas_call x1, Pallas kernels, body(): pl.pallas_call(edge_kernel, out_shape=pltpu.VMEM((REACH, chans, cols), BF...  1.05 us
  transfers between devices with their start and end apart: 6, of which 0 were waited for; matrix products, arithmetic and copies ran while one was open for 0% of the time, Pallas kernels for 13%

profile of v15, /device:TPU:0, one launch (start us, length us, event | category | flops | bytes accessed | tf_op | source)
XLA Modules:
  0.0 42.7 jit_solution(11273171761784233288)
XLA Ops:
  0.0 0.0 copy-start.1
  0.0 1.1 %edge.1 = bf16[2,320,256]{2,1,0:T(8,128)(2,1)S(1)} custom-call(bf16[4,320,256]{2,1,0:T(8,128)(2,1)} %bitcast.11), custom_call_target="tpu_custom_call" | custom-call | tf_op jit(solution)/shard_map/edge/pallas_call | solution.py:379
  1.1 3.0 %collective-permute-start.1 = (bf16[2,320,256]{2,1,0:T(8,128)(2,1)S(1)}, bf16[2,320,256]{2,1,0:T(8,128)(2,1)S(1)}, u32[]{:S(2)}, u32[]{:S(2)}) collective-permute-start(bf16[2,320,256]{2,1,0:T(8,128)(2,1)S(1)} %edge.1), channel_id=1, source_target_pairs={{0,2},{2,0},{4,6},{6,4},{8,10},{10,8},{12,14},{14,12},{1,3},{3,1},... | collective-permute-start | bytes 983048 | tf_op jit(solution)/shard_map/ppermute | solution.py:388
  4.1 2.3 %stats.1 = (bf16[4,320,256]{2,1,0:T(8,128)(2,1)S(1)}, f32[8,128]{1,0:T(8,128)S(1)}, bf16[2,320,256]{2,1,0:T(8,128)(2,1)S(1)}, f32[8,384]{1,0:T(8,128)S(1)}, bf16[2880,320]{1,0:T(8,128)(2,1)S(1)}) custom-call(bf16[4,320,256]{2,1,0:T(8,128)(2,1)} %bitcast.12, bf16[1,1280]{1,0:T(2,128)(2,1)} %embed_hbm, bf16[160,320]{1,0:T(8,128)(2,1)} %weight_hbm.1, ...), custom_call_target="tpu_custom_call" | custom-call | tf_op jit(solution)/shard_map/stats/pallas_call | solution.py:391
  6.4 0.0 copy-start
  6.4 0.1 collective-permute-start.3
  6.5 0.8 %collective-permute-start.2 = (bf16[2,320,256]{2,1,0:T(8,128)(2,1)S(1)}, bf16[2,320,256]{2,1,0:T(8,128)(2,1)S(1)}, u32[]{:S(2)}, u32[]{:S(2)}) collective-permute-start(bf16[2,320,256]{2,1,0:T(8,128)(2,1)S(1)} %get-tuple-element.26), channel_id=1, source_target_pairs={{2,4},{6,8},{10,12},{4,2},{8,6},{12,10},{3,5},{7,9},{11,13},{5,3},... | collective-permute-start | bytes 983048 | tf_op jit(solution)/shard_map/ppermute | solution.py:419
  7.3 0.0 copy-done.1
  7.3 0.4 collective-permute-start
  8.4 0.0 collective-permute-done.3
  8.4 0.1 maximum_select_fusion
  8.5 14.0 %all_to_all.10.seen_ref.steer_ref = f32[8,16,128]{2,1,0:T(8,128)S(1)} all-to-all(f32[8,16,128]{2,1,0:T(8,128)S(1)} %broadcast_in_dim.13), channel_id=1, replica_groups=mesh['cfg'=2,'patch'=8,'req'=2] {'patch'}, dimensions={0} | all-to-all | bytes 131072 | tf_op jit(solution)/shard_map/all_to_all | solution.py:356
  22.5 0.0 collective-permute-done.1.near_ref
  22.5 0.0 collective-permute-done.2.next_ref
  22.5 0.0 collective-permute-start.4
  22.5 0.5 %collective-permute-start.5 = (bf16[2,320,256]{2,1,0:T(8,128)(2,1)S(1)}, bf16[2,320,256]{2,1,0:T(8,128)(2,1)S(1)}, u32[]{:S(2)}, u32[]{:S(2)}) collective-permute-start(bf16[2,320,256]{2,1,0:T(8,128)(2,1)S(1)} %collective-permute-done.2.next_ref), channel_id=1, source_target_pairs={{0,16},{16,0},{1,17},{17,1},{2,18},{18,2},{3,19},{19,3},{4,20},{20... | collective-permute-start | bytes 983048 | tf_op jit(solution)/shard_map/ppermute | solution.py:429
  23.0 0.0 collective-permute-done.far_ref
  23.0 3.1 %inner.1 = (f32[2,320,256]{2,1,0:T(8,128)S(1)}, bf16[3840,256]{1,0:T(8,128)(2,1)S(1)}, f32[6,320,128]{2,1,0:T(8,128)S(1)}, bf16[320,2880]{1,0:T(8,128)(2,1)S(1)}) custom-call(bf16[4,320,256]{2,1,0:T(8,128)(2,1)S(1)} %get-tuple-element.23.own_ref.lat_ref, bf16[4,320,256]{2,1,0:T(8,128)(2,1)S(1)} %collective-permute-done.far_ref, ...), custom_call_target="tpu_custom_call" | custom-call | tf_op jit(solution)/shard_map/inner/pallas_call | solution.py:431
  26.1 0.0 collective-permute-done.4.far_near_ref
  26.1 0.0 collective-permute-done.5.far_next_ref
  26.1 0.0 copy-done
  26.1 3.1 %outer.1 = (f32[4,320,256]{2,1,0:T(8,128)S(1)}, f32[8,8,128]{2,1,0:T(8,128)S(1)}, bf16[320,2880]{1,0:T(8,128)(2,1)S(1)}) custom-call(bf16[2,320,256]{2,1,0:T(8,128)(2,1)S(1)} %collective-permute-done.1.near_ref, bf16[2,320,256]{2,1,0:T(8,128)(2,1)S(1)} %collective-permute-done.2.next_ref, bf16[2,320,256]{2,1,0:T(8,128)(2,1)S(1)} %collective-permute-done.4.far_near_ref, ...), custom_call_target="tpu_custom_call" | custom-call | tf_op jit(solution)/shard_map/outer/pallas_call | solution.py:445
  29.2 9.6 %all_to_all.11.seen_ref = f32[8,8,128]{2,1,0:T(8,128)S(1)} all-to-all(f32[8,8,128]{2,1,0:T(8,128)S(1)} %get-tuple-element.37), channel_id=1, replica_groups=mesh['cfg'=2,'patch'=8,'req'=2] {'patch'}, dimensions={0} | all-to-all | bytes 65536 | tf_op jit(solution)/shard_map/all_to_all | solution.py:356
  38.7 4.0 %second.1 = bf16[4,320,256]{2,1,0:T(8,128)(2,1)} custom-call(f32[2,320,256]{2,1,0:T(8,128)S(1)} %get-tuple-element.30.inner_ref, f32[4,320,256]{2,1,0:T(8,128)S(1)} %get-tuple-element.36.outer_ref, bf16[4,320,256]{2,1,0:T(8,128)(2,1)S(1)} %get-tuple-element.23.own_ref.lat_ref, f32[8,8,128]{2,1,0:T(8,128)S(1)} %all_to_all.11.seen_ref, ...), custom_call_target="tpu_custom_call" | custom-call | tf_op jit(solution)/shard_map/second/pallas_call | solution.py:465
  (3 shorter events, 0.0 us)
Async XLA Ops:
  0.0 7.3 %copy-start.1 = (bf16[1,1,4,256,320]{3,4,2,1,0:T(8,128)(2,1)S(1)}, bf16[1,1,4,256,320]{3,4,2,1,0:T(8,128)(2,1)}, u32[]{:S(2)}) copy-start(bf16[1,1,4,256,320]{3,4,2,1,0:T(8,128)(2,1)} %param.13) | copy-start | bytes 1966084
  1.1 21.4 %collective-permute-start.1 = (bf16[2,320,256]{2,1,0:T(8,128)(2,1)S(1)}, bf16[2,320,256]{2,1,0:T(8,128)(2,1)S(1)}, u32[]{:S(2)}, u32[]{:S(2)}) collective-permute-start(bf16[2,320,256]{2,1,0:T(8,128)(2,1)S(1)} %edge.1), channel_id=1, source_target_pairs={{0,2},{2,0},{4,6},{6,4},{8,10},{10,8},{12,14},{14,12},{1,3},{3,1},... | collective-permute-start | bytes 983048 | tf_op jit(solution)/shard_map/ppermute | solution.py:388
  6.4 19.7 %copy-start = (bf16[3,3,320,320]{3,2,1,0:T(8,128)(2,1)S(1)}, bf16[3,3,320,320]{3,2,1,0:T(8,128)(2,1)}, u32[]{:S(2)}) copy-start(bf16[3,3,320,320]{3,2,1,0:T(8,128)(2,1)} %param.24) | copy-start | bytes 5529604
  6.4 2.0 %collective-permute-start.3 = (f32[8,128]{1,0:T(8,128)S(1)}, f32[8,128]{1,0:T(8,128)S(1)}, u32[]{:S(2)}, u32[]{:S(2)}) collective-permute-start(f32[8,128]{1,0:T(8,128)S(1)} %get-tuple-element.24), channel_id=1, source_target_pairs={{0,16},{16,0},{1,17},{17,1},{2,18},{18,2},{3,19},{19,3},{4,20},{20... | collective-permute-start | bytes 12296 | tf_op jit(solution)/shard_map/ppermute | solution.py:417
  6.5 16.0 %collective-permute-start.2 = (bf16[2,320,256]{2,1,0:T(8,128)(2,1)S(1)}, bf16[2,320,256]{2,1,0:T(8,128)(2,1)S(1)}, u32[]{:S(2)}, u32[]{:S(2)}) collective-permute-start(bf16[2,320,256]{2,1,0:T(8,128)(2,1)S(1)} %get-tuple-element.26), channel_id=1, source_target_pairs={{2,4},{6,8},{10,12},{4,2},{8,6},{12,10},{3,5},{7,9},{11,13},{5,3},... | collective-permute-start | bytes 983048 | tf_op jit(solution)/shard_map/ppermute | solution.py:419
  7.3 15.7 %collective-permute-start = (bf16[4,320,256]{2,1,0:T(8,128)(2,1)S(1)}, bf16[4,320,256]{2,1,0:T(8,128)(2,1)S(1)}, u32[]{:S(2)}, u32[]{:S(2)}) collective-permute-start(bf16[4,320,256]{2,1,0:T(8,128)(2,1)S(1)} %bitcast.13), channel_id=1, source_target_pairs={{0,16},{16,0},{1,17},{17,1},{2,18},{18,2},{3,19},{19,3},{4,20},{20... | collective-permute-start | bytes 1966088 | tf_op jit(solution)/shard_map/ppermute | solution.py:426
  22.5 3.6 %collective-permute-start.4 = (bf16[2,320,256]{2,1,0:T(8,128)(2,1)S(1)}, bf16[2,320,256]{2,1,0:T(8,128)(2,1)S(1)}, u32[]{:S(2)}, u32[]{:S(2)}) collective-permute-start(bf16[2,320,256]{2,1,0:T(8,128)(2,1)S(1)} %collective-permute-done.1.near_ref), channel_id=1, source_target_pairs={{0,16},{16,0},{1,17},{17,1},{2,18},{18,2},{3,19},{19,3},{4,20},{20... | collective-permute-start | bytes 983048 | tf_op jit(solution)/shard_map/ppermute | solution.py:428
  22.5 3.6 %collective-permute-start.5 = (bf16[2,320,256]{2,1,0:T(8,128)(2,1)S(1)}, bf16[2,320,256]{2,1,0:T(8,128)(2,1)S(1)}, u32[]{:S(2)}, u32[]{:S(2)}) collective-permute-start(bf16[2,320,256]{2,1,0:T(8,128)(2,1)S(1)} %collective-permute-done.2.next_ref), channel_id=1, source_target_pairs={{0,16},{16,0},{1,17},{17,1},{2,18},{18,2},{3,19},{19,3},{4,20},{20... | collective-permute-start | bytes 983048 | tf_op jit(solution)/shard_map/ppermute | solution.py:429

commit v16 on v15

--- a/solution.py
+++ b/solution.py
@@ -386,7 +386,8 @@
         name="edge",
     )(in_hbm(own))
     near = lax.ppermute(near_edge, "patch", [(i, i ^ 1) for i in range(patches)])
-    time_embed, _ = lax.optimization_barrier((time_embed, near_edge))
+    source, time_embed, _ = lax.optimization_barrier((own, time_embed, near_edge))
+    far = lax.ppermute(source, "cfg", swap)
     tile_one = tile_height(chans, 3)
     held, tile, next_edge, vectors, raw_one = pl.pallas_call(
         stats_kernel,
@@ -418,12 +419,9 @@
     steps = [(i, i + 1) for i in range(1, patches - 1, 2)]
     following = lax.ppermute(next_edge, "patch", steps + [(j, i) for i, j in steps])
     both = jnp.concatenate([tile, other], axis=0)
-    free = (jnp.arange(2 * tile_one) == tile_one - 1)[:, None] & (jnp.arange(LANES) == LANES - 1)
-    both = jnp.where(free, steer_scale[0], both)
+    both = both + jnp.pad(steer_scale.reshape(1, 1), ((tile_one - 1, tile_one), (LANES - 1, 0)))
     seen = everyone(jnp.broadcast_to(both, (patches,) + both.shape), "patch")
 
-    source, _ = lax.optimization_barrier((own, tile))
-    far = lax.ppermute(source, "cfg", swap)
     near, following, seen = lax.optimization_barrier((near, following, seen))
     far_near = lax.ppermute(near, "cfg", swap)
     far_next = lax.ppermute(following, "cfg", swap)

time: 43 us -> 43 us (level)
    ppermute x1, starting transfers between devices: 0.07 us -> 0.57 us  [body(): other = lax.ppermute(tile, 'cfg', swap)]
  transfers between devices with their start and end apart: 6 -> 6, of which waited for: 0 -> 1; matrix products, arithmetic and copies ran while one was open for 0% -> 0% of each run, Pallas kernels for 13% -> 13%
where the time goes in v16:
time: 43 us; the launch traced here: 42.7 us
  blocking collectives  23.4 us (54%)
  Pallas kernels  13.4 us (31%)
  starting transfers between devices  4.89 us (11%)
  between operations  0.73 us (2%)
    all_to_all x2, blocking collectives, everyone(): return lax.all_to_all(tiles, axes, 0, 0)  23.4 us
    pallas_call x1, Pallas kernels, body(): pl.pallas_call(second_kernel, out_shape=jax.ShapeDtypeStruct((rows, chans...  4.02 us
    pallas_call x1, Pallas kernels, body(): pl.pallas_call(inner_kernel, out_shape=[pltpu.VMEM((max(rows - 2, 1), cha...  3.07 us
    pallas_call x1, Pallas kernels, body(): pl.pallas_call(outer_kernel, out_shape=[pltpu.VMEM((2 * REACH, chans, col...  3.06 us
    ppermute x1, starting transfers between devices, body(): lax.ppermute(near_edge, 'patch', [(i, i ^ 1) for i in range(patches)])  3 us
    pallas_call x1, Pallas kernels, body(): pl.pallas_call(stats_kernel, out_shape=[pltpu.VMEM((rows, chans, cols), B...  2.31 us
    pallas_call x1, Pallas kernels, body(): pl.pallas_call(edge_kernel, out_shape=pltpu.VMEM((REACH, chans, cols), BF...  0.98 us
  transfers between devices with their start and end apart: 6, of which 1 were waited for; matrix products, arithmetic and copies ran while one was open for 0% of the time, Pallas kernels for 13%

profile of v16, /device:TPU:0, one launch (start us, length us, event | category | flops | bytes accessed | tf_op | source)
XLA Modules:
  0.0 42.7 jit_solution(11308113353750984237)
XLA Ops:
  0.0 1.0 %edge.1 = bf16[2,320,256]{2,1,0:T(8,128)(2,1)S(1)} custom-call(bf16[4,320,256]{2,1,0:T(8,128)(2,1)} %bitcast.11), custom_call_target="tpu_custom_call" | custom-call | tf_op jit(solution)/shard_map/edge/pallas_call | solution.py:379
  1.0 3.0 %collective-permute-start.1 = (bf16[2,320,256]{2,1,0:T(8,128)(2,1)S(1)}, bf16[2,320,256]{2,1,0:T(8,128)(2,1)S(1)}, u32[]{:S(2)}, u32[]{:S(2)}) collective-permute-start(bf16[2,320,256]{2,1,0:T(8,128)(2,1)S(1)} %edge.1), channel_id=1, source_target_pairs={{0,2},{2,0},{4,6},{6,4},{8,10},{10,8},{12,14},{14,12},{1,3},{3,1},... | collective-permute-start | bytes 983048 | tf_op jit(solution)/shard_map/ppermute | solution.py:388
  4.0 0.0 collective-permute-start
  4.0 2.3 %stats.1 = (bf16[4,320,256]{2,1,0:T(8,128)(2,1)S(1)}, f32[8,128]{1,0:T(8,128)S(1)}, bf16[2,320,256]{2,1,0:T(8,128)(2,1)S(1)}, f32[8,384]{1,0:T(8,128)S(1)}, bf16[2880,320]{1,0:T(8,128)(2,1)S(1)}) custom-call(bf16[4,320,256]{2,1,0:T(8,128)(2,1)} %bitcast.13, bf16[1,1280]{1,0:T(2,128)(2,1)} %embed_hbm, bf16[160,320]{1,0:T(8,128)(2,1)} %weight_hbm.1, ...), custom_call_target="tpu_custom_call" | custom-call | tf_op jit(solution)/shard_map/stats/pallas_call | solution.py:392
  6.3 0.0 copy-start
  6.3 0.8 %collective-permute-start.2 = (bf16[2,320,256]{2,1,0:T(8,128)(2,1)S(1)}, bf16[2,320,256]{2,1,0:T(8,128)(2,1)S(1)}, u32[]{:S(2)}, u32[]{:S(2)}) collective-permute-start(bf16[2,320,256]{2,1,0:T(8,128)(2,1)S(1)} %get-tuple-element.25), channel_id=1, source_target_pairs={{2,4},{6,8},{10,12},{4,2},{8,6},{12,10},{3,5},{7,9},{11,13},{5,3},... | collective-permute-start | bytes 983048 | tf_op jit(solution)/shard_map/ppermute | solution.py:420
  7.1 0.6 %collective-permute-start.3 = (f32[8,128]{1,0:T(8,128)S(1)}, f32[8,128]{1,0:T(8,128)S(1)}, u32[]{:S(2)}, u32[]{:S(2)}) collective-permute-start(f32[8,128]{1,0:T(8,128)S(1)} %get-tuple-element.26), channel_id=1, source_target_pairs={{0,16},{16,0},{1,17},{17,1},{2,18},{18,2},{3,19},{19,3},{4,20},{20... | collective-permute-start | bytes 12296 | tf_op jit(solution)/shard_map/ppermute | solution.py:418
  8.4 0.2 collective-permute-done.3
  8.5 0.1 maximum_add_fusion
  8.6 14.1 %all_to_all.10.seen_ref.steer_ref = f32[8,16,128]{2,1,0:T(8,128)S(1)} all-to-all(f32[8,16,128]{2,1,0:T(8,128)S(1)} %broadcast_in_dim.6), channel_id=1, replica_groups=mesh['cfg'=2,'patch'=8,'req'=2] {'patch'}, dimensions={0} | all-to-all | bytes 131072 | tf_op jit(solution)/shard_map/all_to_all | solution.py:356
  22.7 0.0 collective-permute-done.1.near_ref
  22.7 0.0 collective-permute-done.2.next_ref
  22.7 0.0 collective-permute-start.4
  22.7 0.5 %collective-permute-start.5 = (bf16[2,320,256]{2,1,0:T(8,128)(2,1)S(1)}, bf16[2,320,256]{2,1,0:T(8,128)(2,1)S(1)}, u32[]{:S(2)}, u32[]{:S(2)}) collective-permute-start(bf16[2,320,256]{2,1,0:T(8,128)(2,1)S(1)} %collective-permute-done.2.next_ref), channel_id=1, source_target_pairs={{0,16},{16,0},{1,17},{17,1},{2,18},{18,2},{3,19},{19,3},{4,20},{20... | collective-permute-start | bytes 983048 | tf_op jit(solution)/shard_map/ppermute | solution.py:427
  23.2 0.0 collective-permute-done.far_ref
  23.2 3.1 %inner.1 = (f32[2,320,256]{2,1,0:T(8,128)S(1)}, bf16[3840,256]{1,0:T(8,128)(2,1)S(1)}, f32[6,320,128]{2,1,0:T(8,128)S(1)}, bf16[320,2880]{1,0:T(8,128)(2,1)S(1)}) custom-call(bf16[4,320,256]{2,1,0:T(8,128)(2,1)S(1)} %get-tuple-element.23.own_ref.lat_ref, bf16[4,320,256]{2,1,0:T(8,128)(2,1)S(1)} %collective-permute-done.far_ref, ...), custom_call_target="tpu_custom_call" | custom-call | tf_op jit(solution)/shard_map/inner/pallas_call | solution.py:429
  26.3 0.0 collective-permute-done.4.far_near_ref
  26.3 0.0 collective-permute-done.5.far_next_ref
  26.3 0.0 copy-done
  26.4 3.1 %outer.1 = (f32[4,320,256]{2,1,0:T(8,128)S(1)}, f32[8,8,128]{2,1,0:T(8,128)S(1)}, bf16[320,2880]{1,0:T(8,128)(2,1)S(1)}) custom-call(bf16[2,320,256]{2,1,0:T(8,128)(2,1)S(1)} %collective-permute-done.1.near_ref, bf16[2,320,256]{2,1,0:T(8,128)(2,1)S(1)} %collective-permute-done.2.next_ref, bf16[2,320,256]{2,1,0:T(8,128)(2,1)S(1)} %collective-permute-done.4.far_near_ref, ...), custom_call_target="tpu_custom_call" | custom-call | tf_op jit(solution)/shard_map/outer/pallas_call | solution.py:443
  29.4 9.3 %all_to_all.11.seen_ref = f32[8,8,128]{2,1,0:T(8,128)S(1)} all-to-all(f32[8,8,128]{2,1,0:T(8,128)S(1)} %get-tuple-element.37), channel_id=1, replica_groups=mesh['cfg'=2,'patch'=8,'req'=2] {'patch'}, dimensions={0} | all-to-all | bytes 65536 | tf_op jit(solution)/shard_map/all_to_all | solution.py:356
  38.7 4.0 %second.1 = bf16[4,320,256]{2,1,0:T(8,128)(2,1)} custom-call(f32[2,320,256]{2,1,0:T(8,128)S(1)} %get-tuple-element.30.inner_ref, f32[4,320,256]{2,1,0:T(8,128)S(1)} %get-tuple-element.36.outer_ref, bf16[4,320,256]{2,1,0:T(8,128)(2,1)S(1)} %get-tuple-element.23.own_ref.lat_ref, f32[8,8,128]{2,1,0:T(8,128)S(1)} %all_to_all.11.seen_ref, ...), custom_call_target="tpu_custom_call" | custom-call | tf_op jit(solution)/shard_map/second/pallas_call | solution.py:463
  (1 shorter events, 0.0 us)
Async XLA Ops:
  1.0 21.7 %collective-permute-start.1 = (bf16[2,320,256]{2,1,0:T(8,128)(2,1)S(1)}, bf16[2,320,256]{2,1,0:T(8,128)(2,1)S(1)}, u32[]{:S(2)}, u32[]{:S(2)}) collective-permute-start(bf16[2,320,256]{2,1,0:T(8,128)(2,1)S(1)} %edge.1), channel_id=1, source_target_pairs={{0,2},{2,0},{4,6},{6,4},{8,10},{10,8},{12,14},{14,12},{1,3},{3,1},... | collective-permute-start | bytes 983048 | tf_op jit(solution)/shard_map/ppermute | solution.py:388
  4.0 19.3 %collective-permute-start = (bf16[4,320,256]{2,1,0:T(8,128)(2,1)}, bf16[4,320,256]{2,1,0:T(8,128)(2,1)S(1)}, u32[]{:S(2)}, u32[]{:S(2)}) collective-permute-start(bf16[4,320,256]{2,1,0:T(8,128)(2,1)} %bitcast.12), channel_id=1, source_target_pairs={{0,16},{16,0},{1,17},{17,1},{2,18},{18,2},{3,19},{19,3},{4,20},{20... | collective-permute-start | bytes 1966088 | tf_op jit(solution)/shard_map/ppermute | solution.py:390
  6.3 20.0 %copy-start = (bf16[3,3,320,320]{3,2,1,0:T(8,128)(2,1)S(1)}, bf16[3,3,320,320]{3,2,1,0:T(8,128)(2,1)}, u32[]{:S(2)}) copy-start(bf16[3,3,320,320]{3,2,1,0:T(8,128)(2,1)} %param.24) | copy-start | bytes 5529604
  6.3 16.4 %collective-permute-start.2 = (bf16[2,320,256]{2,1,0:T(8,128)(2,1)S(1)}, bf16[2,320,256]{2,1,0:T(8,128)(2,1)S(1)}, u32[]{:S(2)}, u32[]{:S(2)}) collective-permute-start(bf16[2,320,256]{2,1,0:T(8,128)(2,1)S(1)} %get-tuple-element.25), channel_id=1, source_target_pairs={{2,4},{6,8},{10,12},{4,2},{8,6},{12,10},{3,5},{7,9},{11,13},{5,3},... | collective-permute-start | bytes 983048 | tf_op jit(solution)/shard_map/ppermute | solution.py:420
  7.1 1.4 %collective-permute-start.3 = (f32[8,128]{1,0:T(8,128)S(1)}, f32[8,128]{1,0:T(8,128)S(1)}, u32[]{:S(2)}, u32[]{:S(2)}) collective-permute-start(f32[8,128]{1,0:T(8,128)S(1)} %get-tuple-element.26), channel_id=1, source_target_pairs={{0,16},{16,0},{1,17},{17,1},{2,18},{18,2},{3,19},{19,3},{4,20},{20... | collective-permute-start | bytes 12296 | tf_op jit(solution)/shard_map/ppermute | solution.py:418
  22.7 3.6 %collective-permute-start.4 = (bf16[2,320,256]{2,1,0:T(8,128)(2,1)S(1)}, bf16[2,320,256]{2,1,0:T(8,128)(2,1)S(1)}, u32[]{:S(2)}, u32[]{:S(2)}) collective-permute-start(bf16[2,320,256]{2,1,0:T(8,128)(2,1)S(1)} %collective-permute-done.1.near_ref), channel_id=1, source_target_pairs={{0,16},{16,0},{1,17},{17,1},{2,18},{18,2},{3,19},{19,3},{4,20},{20... | collective-permute-start | bytes 983048 | tf_op jit(solution)/shard_map/ppermute | solution.py:426
  22.7 3.6 %collective-permute-start.5 = (bf16[2,320,256]{2,1,0:T(8,128)(2,1)S(1)}, bf16[2,320,256]{2,1,0:T(8,128)(2,1)S(1)}, u32[]{:S(2)}, u32[]{:S(2)}) collective-permute-start(bf16[2,320,256]{2,1,0:T(8,128)(2,1)S(1)} %collective-permute-done.2.next_ref), channel_id=1, source_target_pairs={{0,16},{16,0},{1,17},{17,1},{2,18},{18,2},{3,19},{19,3},{4,20},{20... | collective-permute-start | bytes 983048 | tf_op jit(solution)/shard_map/ppermute | solution.py:427
